TPU v7x, 32 devices: a whole 2x2x4 slice. The times are simulated.
32 devices in a mesh: dp: 8 (over z, x), field: 4 (over y, core).
Axes of the slice: x: 2, y: 2, z: 4, core: 2. Of those that a mesh axis runs over, the one named last changes fastest.
Arguments:
- examples: float32 [16384, 512], P('dp', 'field'), may hold values from -6 to 6
- domain: int32 [16384], P('dp'), may hold values from 0 to 15
- labels: int32 [16384, 3], P('dp'), may hold values from 0 to 1
- row_counts: int32 [8], P('dp'), may hold values from 1 to 2048, as said below
- gate_weight: float32 [3, 512, 8], P(None, 'field'), may hold values from -0.25 to 0.25
- gate_bias: float32 [16, 24], replicated, may hold values from -1.5 to 1.5
- w_first: float32 [8, 512, 256], P(None, 'field'), may hold values from -0.25 to 0.25
- b_first: float32 [8, 256], replicated, may hold values from -1.5 to 1.5
- w_second: float32 [8, 256, 256], replicated, may hold values from -0.375 to 0.375
- b_second: float32 [8, 256], replicated, may hold values from -1.5 to 1.5
- tower_first: float32 [3, 256, 128], replicated, may hold values from -0.375 to 0.375
- tower_bias: float32 [3, 128], replicated, may hold values from -1.5 to 1.5
- tower_out: float32 [3, 128], replicated, may hold values from -0.5 to 0.5
- tower_out_bias: float32 [3], replicated, may hold values from -2 to 2
Outputs:
- loss: float32 [], replicated
- grad_examples: float32 [16384, 512], P('dp', 'field')
- grad_gate_weight: float32 [3, 512, 8], P(None, 'field')
- grad_gate_bias: float32 [16, 24], replicated
- grad_w_first: float32 [8, 512, 256], P(None, 'field')
- grad_b_first: float32 [8, 256], replicated
- grad_w_second: float32 [8, 256, 256], replicated
- grad_b_second: float32 [8, 256], replicated
- grad_tower_first: float32 [3, 256, 128], replicated
- grad_tower_bias: float32 [3, 128], replicated
- grad_tower_out: float32 [3, 128], replicated
- grad_tower_out_bias: float32 [3], replicated
Inputs may be any that keep to these rules, and one draw needn't show every extreme that they name: `row_counts`: the live rows of an index of dp are the first ones of its block; the last index of dp has all 2048 live.
All inputs are finite; a program needn't handle non-finite values.
Results may differ from a plain program's by a relative error of at most 0.00017.
Values sent between devices are 32-bit elements; how exact they have to be, the bound alone decides.
No kernel may reach another device: no remote copies, remote signals or barrier semaphores. Data moves between devices by JAX's collectives and lax.ppermute only.
A program may use at most 192 MiB of HBM per device.

v0:
```python
import jax
import jax.numpy as jnp
from jax import lax
from jax.sharding import PartitionSpec as P

HIGHEST = lax.Precision.HIGHEST


def gelu_exact(values):
    return jax.nn.gelu(values, approximate=False)


def per_device(
    examples,
    domain,
    labels,
    row_counts,
    gate_weight,
    gate_bias,
    w_first,
    b_first,
    w_second,
    b_second,
    tower_first,
    tower_bias,
    tower_out,
    tower_out_bias,
):
    rows = examples.shape[0]
    experts = w_first.shape[0]
    width = w_first.shape[2]
    tasks = gate_weight.shape[0]
    domains = gate_bias.shape[0]
    positions = jnp.arange(rows, dtype=jnp.int32)
    weights_live = (positions < row_counts[0]).astype(jnp.float32)
    count_here = jnp.sum(weights_live)
    total = lax.psum(count_here, "dp")
    factor = 1.0 / total
    part_first = jnp.einsum("tc,ech->teh", examples, w_first, precision=HIGHEST).reshape(
        rows, experts * width
    )
    part_gate = jnp.einsum("tc,kce->tke", examples, gate_weight, precision=HIGHEST).reshape(
        rows, tasks * experts
    )
    summed_first, summed_gate = lax.psum((part_first, part_gate), "field")
    onehot = (domain[:, None] == jnp.arange(domains, dtype=jnp.int32)[None, :]).astype(jnp.float32)
    targets = labels.astype(jnp.float32)
    pre_first = summed_first.reshape(rows, experts, width) + b_first
    hidden, hidden_back = jax.vjp(gelu_exact, pre_first)
    expert_out = jnp.einsum("teh,ehj->tej", hidden, w_second, precision=HIGHEST) + b_second
    logits = summed_gate.reshape(rows, tasks, experts)
    logits = logits + jnp.dot(onehot, gate_bias, precision=HIGHEST).reshape(rows, tasks, experts)
    gates = jax.nn.softmax(logits, axis=-1)
    mixture = jnp.einsum("tke,tej->tkj", gates, expert_out, precision=HIGHEST)
    tower_pre = jnp.einsum("tkj,kjm->tkm", mixture, tower_first, precision=HIGHEST) + tower_bias
    tower_act, tower_back = jax.vjp(gelu_exact, tower_pre)
    score = jnp.einsum("tkm,km->tk", tower_act, tower_out, precision=HIGHEST) + tower_out_bias
    per_item = jax.nn.softplus(score) - targets * score
    loss_part = jnp.sum(per_item * weights_live[:, None])
    grad_score = weights_live[:, None] * (jax.nn.sigmoid(score) - targets) * factor
    grad_out_bias = jnp.sum(grad_score, axis=0)
    grad_out = jnp.einsum("tk,tkm->km", grad_score, tower_act, precision=HIGHEST)
    grad_act = grad_score[:, :, None] * tower_out[None, :, :]
    grad_tower_pre = tower_back(grad_act)[0]
    grad_tbias = jnp.sum(grad_tower_pre, axis=0)
    grad_tfirst = jnp.einsum("tkj,tkm->kjm", mixture, grad_tower_pre, precision=HIGHEST)
    grad_mixture = jnp.einsum("tkm,kjm->tkj", grad_tower_pre, tower_first, precision=HIGHEST)
    grad_gates = jnp.einsum("tkj,tej->tke", grad_mixture, expert_out, precision=HIGHEST)
    grad_logits = gates * (grad_gates - jnp.sum(gates * grad_gates, axis=-1, keepdims=True))
    grad_gbias = jnp.dot(onehot.T, grad_logits.reshape(rows, tasks * experts), precision=HIGHEST)
    grad_expert_out = jnp.einsum("tke,tkj->tej", gates, grad_mixture, precision=HIGHEST)
    grad_bsecond = jnp.sum(grad_expert_out, axis=0)
    grad_wsecond = jnp.einsum("teh,tej->ehj", hidden, grad_expert_out, precision=HIGHEST)
    grad_hidden = jnp.einsum("tej,ehj->teh", grad_expert_out, w_second, precision=HIGHEST)
    grad_first = hidden_back(grad_hidden)[0]
    grad_bfirst = jnp.sum(grad_first, axis=0)
    grad_wfirst = jnp.einsum("tc,teh->ech", examples, grad_first, precision=HIGHEST)
    grad_gweight = jnp.einsum("tc,tke->kce", examples, grad_logits, precision=HIGHEST)
    grad_inputs = jnp.einsum("teh,ech->tc", grad_first, w_first, precision=HIGHEST)
    grad_inputs = grad_inputs + jnp.einsum(
        "tke,kce->tc", grad_logits, gate_weight, precision=HIGHEST
    )
    members = (
        grad_gweight,
        grad_gbias,
        grad_wfirst,
        grad_bfirst,
        grad_wsecond,
        grad_bsecond,
        grad_tfirst,
        grad_tbias,
        grad_out,
        grad_out_bias,
        loss_part,
    )
    summed = lax.psum(
        (
            members[0],
            members[1],
            members[2],
            members[3],
            members[4],
            members[5],
            members[6],
            members[7],
            members[8],
            members[9],
            members[10],
        ),
        "dp",
    )
    grads = list(summed[:10])
    loss = summed[10] / total
    return (
        loss,
        grad_inputs,
        grads[0],
        grads[1],
        grads[2],
        grads[3],
        grads[4],
        grads[5],
        grads[6],
        grads[7],
        grads[8],
        grads[9],
    )


def solution(mesh):
    placed = (
        P("dp", "field"),
        P("dp"),
        P("dp", None),
        P("dp"),
        P(None, "field", None),
        P(),
        P(None, "field", None),
        P(),
        P(),
        P(),
        P(),
        P(),
        P(),
        P(),
    )
    return jax.shard_map(
        per_device,
        mesh=mesh,
        in_specs=placed,
        out_specs=(
            P(),
            P("dp", "field"),
            P(None, "field", None),
            P(),
            P(None, "field", None),
            P(),
            P(),
            P(),
            P(),
            P(),
            P(),
            P(),
        ),
        check_vma=False,
    )
```

profile of v0, /device:TPU:0, one launch (start us, length us, event | category | flops | bytes accessed | tf_op | source)
XLA Modules:
  0.0 839.9 jit_solution(393494964639218448)
XLA Ops:
  7.2 0.0 copy-start
  7.2 0.0 all-reduce.8.cloned.1.call-start
  7.2 3.0 convolution_bitcast_fusion.3
  10.3 17.4 %fusion.53 = f32[2048,8,256]{2,0,1:T(8,128)} fusion(f32[8,128,256]{2,1,0:T(8,128)} %param.20, f32[2048,128]{1,0:T(8,128)} %param.14), kind=kOutput, calls=%fused_computation.84 | convolution fusion | flops 6442450944 | bytes 18874368 | tf_op jit(solution)/shard_map/tc,ech->teh/dot_general | solution.py:39
  27.6 0.0 all-reduce.8.cloned.1.call-update
  27.7 0.0 all-reduce.6.cloned.1.call-start
  28.4 0.6 fusion.73
  29.0 24.1 %psum.101 = f32[]{:T(128)} all-reduce(f32[]{:T(128)} %fusion.73), channel_id=1, replica_groups=mesh['dp'=8,'field'=4] {'dp'}, use_global_device_ids=true, to_apply=%region_7.8 | all-reduce | flops 1 | bytes 8 | tf_op jit(solution)/shard_map/psum | solution.py:37
  53.7 268.8 %all-reduce.8.cloned.1.call-done = (f32[2048,8,256]{2,0,1:T(8,128)}, f32[2048,24]{0,1:T(8,128)}) async-done(((f32[2048,8,256]{2,0,1:T(8,128)}, f32[2048,24]{0,1:T(8,128)}), (f32[2048,8,256]{2,0,1:T(8,128)}, f32[2048,24]{0,1:T(8,128)})) %all-reduce.8.cloned.1.call-update) | async-done | bytes 16973840 | tf_op jit(solution)/shard_map/psum | solution.py:45
  322.5 0.0 copy-done.20
  322.5 0.0 copy-done.21
  322.5 1.7 fusion.84
  324.2 0.4 copy.55
  324.6 0.0 copy-start.7
  324.6 3.1 copy.56
  327.7 29.9 %fusion.26 = f32[2048,3]{1,0:T(8,128)S(1)} fusion(f32[2048,3,8]{2,1,0:T(4,128)} %copy.56, f32[2048,3]{1,0:T(8,128)S(1)} %copy.55), kind=kLoop, calls=%fused_computation.44 | loop fusion | flops 92160 | bytes 245760 | tf_op jit(solution)/shard_map/reduce_sum | solution.py:53
  357.6 0.0 copy-done.12
  357.6 0.0 copy-start.17
  357.6 37.9 %fusion = f32[2048,8,256]{2,0,1:T(8,128)} fusion(f32[2048,8,256]{2,0,1:T(8,128)} %get-tuple-element.59, f32[8,256]{1,0:T(8,128)S(1)} %copy-done.12), kind=kLoop, calls=%fused_computation.1 | loop fusion | flops 264241152 | bytes 33562624 | tf_op jit(solution)/shard_map/jvp()/erfc | solution.py:10
  395.5 0.0 copy-done
  395.5 0.0 copy-done.17
  395.5 0.0 copy-start.1
  395.5 24.9 %add_bitcast_fusion = f32[2048,8,256]{2,0,1:T(8,128)} fusion(f32[8,256]{1,0:T(8,128)S(1)} %copy-done.17, f32[8,256,256]{2,1,0:T(8,128)S(1)} %copy-done, f32[2048,8,256]{2,0,1:T(8,128)} %fusion, f32[2048,8,256]{2,0,1:T(8,128)} %get-tuple-element.59, f32[8,256]{1,0:T(8,128)S(1)} %copy-done.12), kind=kOutput, calls=%fused_computation.10 | convolution fusion | flops 12901679104 | bytes 52445184 | tf_op jit(solution)/shard_map/teh,ehj->tej/dot_general | solution.py:50
  420.4 31.5 %fusion.18 = f32[2048,3,256]{2,1,0:T(4,128)} fusion(f32[2048,8,256]{2,0,1:T(8,128)} %add_bitcast_fusion, f32[2048,3,8]{2,1,0:T(4,128)S(1)} %copy-done.1, f32[2048,3]{1,0:T(8,128)S(1)} %fusion.26, f32[2048,3]{1,0:T(8,128)S(1)} %copy.55), kind=kOutput, calls=%fused_computation.30 | convolution fusion | flops 151093248 | bytes 23314432 | tf_op jit(solution)/shard_map/tke,tej->tkj/dot_general | solution.py:54
  451.9 9.1 %copy.69 = f32[2048,3,256]{0,2,1:T(8,128)} copy(f32[2048,3,256]{2,1,0:T(4,128)} %fusion.18) | data formatting | bytes 12582912 | tf_op jit(solution)/shard_map/tke,tej->tkj/dot_general | solution.py:54
  461.0 17.2 %fusion.33 = (f32[2048,3,128]{2,0,1:T(8,128)S(1)}, f32[3,2048,128]{2,1,0:T(8,128)S(1)}) fusion(f32[3,128]{1,0:T(4,128)} %param.25, f32[2048,3,256]{0,2,1:T(8,128)} %copy.69, f32[3,256,128]{2,1,0:T(8,128)S(1)} %copy-done.13), kind=kOutput, calls=%fused_computation.51 | convolution fusion | flops 2465464320 | bytes 12977664 | tf_op jit(solution)/shard_map/tkj,kjm->tkm/dot_general | solution.py:55
  478.2 0.0 copy-start.19
  478.2 0.0 copy-start.25
  478.3 0.0 copy-done.23
  478.3 0.0 slice-start
  478.3 2.9 fusion.50
  481.2 0.0 copy-done.19
  481.2 0.0 copy-done.25
  481.2 0.8 fusion.81
  482.0 1.6 fusion.82
  483.6 0.1 slice-done.1
  483.8 6.2 fusion.87
  489.9 6.9 convolution_bitcast_fusion
  496.9 45.6 %multiply_reduce_fusion = (f32[2048,3]{1,0:T(8,128)}, f32[2048,3,8]{2,1,0:T(4,128)}) fusion(f32[2048,3]{1,0:T(8,128)S(1)} %copy-done.10, f32[2048,3,8]{2,1,0:T(4,128)S(1)} %copy-done.2, f32[2048,3]{1,0:T(8,128)S(1)} %copy.55, f32[2048,8,256]{2,0,1:T(8,128)} %add_bitcast_fusion, f32[2048,3,256]{2,0,1:T(8,128)} %convolution_bitcast_fusion), kind=kOutput, calls=%fused_computation.40 | convolution fusion | flops 151185408 | bytes 23535616 | tf_op jit(solution)/shard_map/tkj,tej->tke/dot_general | solution.py:68
  542.5 32.2 %fusion.86 = (f32[8,256]{1,0:T(8,128)S(1)}, f32[2048,8,256]{2,1,0:T(8,128)}) fusion(f32[2048,3,256]{2,0,1:T(8,128)} %convolution_bitcast_fusion, f32[2048,3,8]{2,1,0:T(4,128)S(1)} %copy-done.2, f32[2048,3]{1,0:T(8,128)S(1)} %copy-done.10, f32[2048,3]{1,0:T(8,128)S(1)} %copy.55), kind=kOutput, calls=%fused_computation.124 | convolution fusion | flops 155285504 | bytes 23322624 | tf_op jit(solution)/shard_map/tke,tkj->tej/dot_general | solution.py:71
  574.6 42.5 %fusion.12 = f32[8,256,256]{2,1,0:T(8,128)} fusion(f32[2048,8,256]{2,1,0:T(8,128)} %get-tuple-element.75, f32[2048,8,256]{2,0,1:T(8,128)} %fusion, f32[2048,8,256]{2,0,1:T(8,128)} %get-tuple-element.59, f32[8,256]{1,0:T(8,128)S(1)} %copy-done.12), kind=kOutput, calls=%fused_computation.24 | convolution fusion | flops 12897484800 | bytes 52436992 | tf_op jit(solution)/shard_map/teh,tej->ehj/dot_general | solution.py:73
  617.1 37.1 %fusion.85 = (f32[8,256]{1,0:T(8,128)S(1)}, f32[2048,8,256]{2,0,1:T(8,128)}) fusion(f32[2048,8,256]{2,0,1:T(8,128)} %fusion, f32[8,256,256]{2,1,0:T(8,128)S(1)} %copy-done, f32[2048,8,256]{2,1,0:T(8,128)} %get-tuple-element.75, f32[2048,8,256]{2,0,1:T(8,128)} %get-tuple-element.59, f32[8,256]{1,0:T(8,128)S(1)} %copy-done.12), kind=kOutput, calls=%fused_computation.123 | convolution fusion | flops 12947814400 | bytes 69222400 | tf_op jit(solution)/shard_map/tej,ehj->teh/dot_general | solution.py:74
  654.2 29.7 %convolution_bitcast_fusion.4 = f32[8,128,256]{1,2,0:T(8,128)} fusion(f32[2048,8,256]{2,0,1:T(8,128)} %get-tuple-element.73, f32[2048,128]{1,0:T(8,128)S(1)} %copy-done.6), kind=kOutput, calls=%fused_computation.78 | convolution fusion | flops 6442450944 | bytes 18874368 | tf_op jit(solution)/shard_map/tc,teh->ech/dot_general | solution.py:77
  684.0 0.0 all-reduce.6.cloned.1.call-update
  684.0 0.0 copy-start.11
  684.0 0.0 copy-done.16
  684.0 4.0 fusion.49
  688.0 0.0 copy-done.3
  688.1 0.3 copy-done.8
  688.4 0.3 copy-done.11
  688.7 9.8 %subtract_multiply_fusion = f32[2048,3,8]{2,1,0:T(4,128)} fusion(f32[2048,3,8]{2,1,0:T(4,128)} %get-tuple-element.71, f32[2048,3]{1,0:T(8,128)} %get-tuple-element.70, f32[2048,3]{1,0:T(8,128)S(1)} %copy-done.11, f32[2048,3,8]{2,1,0:T(4,128)S(1)} %copy-done.3, f32[2048,3]{1,0:T(8,128)S(1)} %copy-done.8), kind=kLoop, calls=%fused_computation.39 | loop fusion | flops 196608 | bytes 663552 | tf_op jit(solution)/shard_map/mul | solution.py:69
  698.5 0.0 copy-start.22
  698.5 0.0 copy-start.24
  698.5 3.3 copy.63
  701.9 1.0 fusion.56
  702.9 0.6 convolution_bitcast_fusion.5
  703.6 40.6 %all-reduce = (f32[]{:T(128)}, f32[3,128,8]{1,2,0:T(8,128)}, f32[16,24]{1,0:T(8,128)}, f32[8,256]{1,0:T(8,128)}, f32[8,256]{1,0:T(8,128)}, /*index=5*/f32[3,128]{1,0:T(4,128)}, f32[3,128]{1,0:T(4,128)}, f32[3]{0:T(128)}) all-reduce(f32[]{:T(128)} %get-tuple-element.65, ...), channel_id=1, replica_groups=mesh['dp'=8,'field'=4] {'dp'}, use_global_device_ids=true, to_apply=%region_5.0 | all-reduce | flops 8324 | bytes 66592 | tf_op jit(solution)/shard_map/psum | solution.py:96
  745.5 0.0 copy-start.18
  745.5 16.8 %convolution_bitcast_fusion.2 = f32[2048,128]{1,0:T(8,128)S(1)} fusion(f32[2048,8,256]{2,0,1:T(8,128)} %get-tuple-element.73, f32[8,128,256]{2,1,0:T(8,128)} %param.20), kind=kOutput, calls=%fused_computation.73 | convolution fusion | flops 6442450944 | bytes 18874368 | tf_op jit(solution)/shard_map/teh,ech->tc/dot_general | solution.py:79
  762.3 2.8 fusion.47
  765.1 60.1 %all-reduce.6.cloned.1.call-done = (f32[8,128,256]{1,2,0:T(8,128)}, f32[8,256,256]{2,1,0:T(8,128)}, f32[3,256,128]{2,1,0:T(8,128)}) async-done(((f32[8,128,256]{1,2,0:T(8,128)}, f32[8,256,256]{2,1,0:T(8,128)}, f32[3,256,128]{2,1,0:T(8,128)}), (f32[8,128,256]{1,2,0:T(8,128)}, f32[8,256,256]{2,1,0:T(8,128)}, f32[3,256,128]{2,1,0:T(8,128)})) %all-reduce.6.cloned.1.call-update) | async-done | bytes 3538960 | tf_op jit(solution)/shard_map/psum | solution.py:96
  825.3 2.6 copy.70
  827.9 3.0 copy.118
  830.9 0.7 copy.119
  (35 shorter events, 0.1 us)
Async XLA Ops:
  7.2 388.3 %copy-start = (f32[8,256,256]{2,1,0:T(8,128)S(1)}, f32[8,256,256]{2,1,0:T(8,128)}, u32[]{:S(2)}) copy-start(f32[8,256,256]{2,1,0:T(8,128)} %param.22) | copy-start | bytes 6291460
  7.2 315.3 %all-reduce.8.cloned.1.call-start = ((), (), s32[]{:S(2)}) async-start(), calls=%async_computation.1 | async-start | bytes 33947648 | tf_op jit(solution)/shard_map/psum | solution.py:45
  27.6 294.9 %copy-start.20 = (f32[16,24]{1,0:T(8,128)S(1)}, f32[16,24]{1,0:T(8,128)}, u32[]{:S(2)}) copy-start(f32[16,24]{1,0:T(8,128)} %param.19) | copy-start | bytes 4612
  27.6 294.9 %copy-start.21 = (s32[2048]{0:T(1024)S(1)}, s32[2048]{0:T(1024)}, u32[]{:S(2)}) copy-start(s32[2048]{0:T(1024)} %param.15) | copy-start | bytes 24580
  27.7 797.6 %all-reduce.6.cloned.1.call-start = ((), (), s32[]{:S(2)}) async-start(), calls=%async_computation | async-start | bytes 7077888 | tf_op jit(solution)/shard_map/psum | solution.py:96
  324.6 217.9 %copy-start.7 = (f32[2048,3]{1,0:T(8,128)}, f32[2048,3]{1,0:T(8,128)S(1)}, u32[]{:S(2)}) copy-start(f32[2048,3]{1,0:T(8,128)S(1)} %copy.55) | copy-start | bytes 73732
  327.7 29.9 %copy-start.12 = (f32[8,256]{1,0:T(8,128)S(1)}, f32[8,256]{1,0:T(8,128)}, u32[]{:S(2)}) copy-start(f32[8,256]{1,0:T(8,128)} %param.21) | copy-start | bytes 24580
  357.6 62.8 %copy-start.9 = (f32[2048,3]{1,0:T(8,128)}, f32[2048,3]{1,0:T(8,128)S(1)}, u32[]{:S(2)}) copy-start(f32[2048,3]{1,0:T(8,128)S(1)} %fusion.26) | copy-start | bytes 73732
  357.6 37.9 %copy-start.17 = (f32[8,256]{1,0:T(8,128)S(1)}, f32[8,256]{1,0:T(8,128)}, u32[]{:S(2)}) copy-start(f32[8,256]{1,0:T(8,128)} %param.23) | copy-start | bytes 24580
  395.5 24.9 %copy-start.1 = (f32[2048,3,8]{2,1,0:T(4,128)S(1)}, f32[2048,3,8]{2,1,0:T(4,128)}, u32[]{:S(2)}) copy-start(f32[2048,3,8]{2,1,0:T(4,128)} %copy.56) | copy-start | bytes 589828
  451.9 9.1 %copy-start.13 = (f32[3,256,128]{2,1,0:T(8,128)S(1)}, f32[3,256,128]{2,1,0:T(8,128)}, u32[]{:S(2)}) copy-start(f32[3,256,128]{2,1,0:T(8,128)} %param.24) | copy-start | bytes 1179652
  461.0 17.3 %copy-start.23 = (f32[3,128]{1,0:T(4,128)S(1)}, f32[3,128]{1,0:T(4,128)}, u32[]{:S(2)}) copy-start(f32[3,128]{1,0:T(4,128)} %param.26) | copy-start | bytes 4612
  478.2 5.4 copy-start.4
  478.2 5.4 copy-start.5
  478.2 3.0 copy-start.19
  478.2 3.0 copy-start.25
  478.3 5.4 slice-start
  482.0 1.6 copy-start.15
  482.0 1.8 slice-start.1
  489.9 6.9 copy-start.2
  489.9 6.9 copy-start.10
  617.1 37.1 %copy-start.6 = (f32[2048,128]{1,0:T(8,128)S(1)}, f32[2048,128]{1,0:T(8,128)}, u32[]{:S(2)}) copy-start(f32[2048,128]{1,0:T(8,128)} %param.14) | copy-start | bytes 3145732
  654.2 29.8 %copy-start.16 = (f32[2048,3]{0,1:T(4,128)S(1)}, f32[2048,3]{0,1:T(4,128)}, u32[]{:S(2)}) copy-start(f32[2048,3]{0,1:T(4,128)} %copy-done.15) | copy-start | bytes 73732
  684.0 4.1 copy-start.3
  684.0 4.3 copy-start.8
  684.0 4.7 copy-start.11
  698.5 3.4 copy-start.22
  698.5 5.0 copy-start.24
  745.5 16.8 %copy-start.18 = (f32[3,128,8]{1,2,0:T(8,128)S(1)}, f32[3,128,8]{1,2,0:T(8,128)}, u32[]{:S(2)}) copy-start(f32[3,128,8]{1,2,0:T(8,128)} %param.18) | copy-start | bytes 36868
  825.3 5.6 copy-start.14
Sparse Core Ops, SparseCore 0:
  27.8 294.6 all-reduce.7
  684.1 141.1 all-reduce.5
where the time goes:
time: 845 us; the launch traced here: 840 us
  waiting for transfers between devices  329 us (39%)
  matrix products  324 us (38%)
  other arithmetic  80.6 us (10%)
  blocking collectives  64.7 us (8%)
  local copies, waits for them, and re-layouts  23.1 us (3%)
  between operations  18.4 us (2%)
    psum x1, waiting for transfers between devices, per_device(): summed_first, summed_gate = lax.psum((part_first, part_gate), 'field')  269 us
    psum x1, waiting for transfers between devices, per_device(): lax.psum((members[0], members[1], members[2], members[3], members[4], mem...  60.1 us
    dot_general x1, matrix products, per_device(): jnp.einsum('tkj,tej->tke', grad_mixture, expert_out, precision=HIGHEST)  45.6 us
    dot_general x1, matrix products, per_device(): jnp.einsum('teh,tej->ehj', hidden, grad_expert_out, precision=HIGHEST)  42.5 us
    psum x1, blocking collectives, per_device(): lax.psum((members[0], members[1], members[2], members[3], members[4], mem...  40.6 us
    another operation x1, other arithmetic, gelu_exact(): return jax.nn.gelu(values, approximate=False)  37.9 us
    dot_general x1, matrix products, per_device(): jnp.einsum('tej,ehj->teh', grad_expert_out, w_second, precision=HIGHEST)  37.1 us
    dot_general x1, matrix products, per_device(): jnp.einsum('tke,tkj->tej', gates, grad_mixture, precision=HIGHEST)  32.2 us
  transfers between devices with their start and end apart: 2, of which 2 were waited for; matrix products, arithmetic and copies ran while one was open for 5% of the time, Pallas kernels for 0%

commit v1 on v0

v1 whole, which is shorter than its diff:
```python
import functools

import jax
import jax.numpy as jnp
from jax import lax
from jax.experimental import pallas as pl
from jax.experimental.pallas import tpu as pltpu
from jax.sharding import PartitionSpec as P

F32 = jnp.float32
BF16 = jnp.bfloat16
ROOT_HALF = 0.7071067811865476
DENSITY = 0.3989422804014327
VMEM = pltpu.VMEM
PARAMS = pltpu.CompilerParams(vmem_limit_bytes=58 * 1024 * 1024)
NN, TN, NT = (1, 0), (0, 0), (1, 1)


def split(x):
    high = x.astype(BF16)
    return high, (x - high.astype(F32)).astype(BF16)


def one_dot(a, b, dims):
    return lax.dot_general(a, b, (((dims[0],), (dims[1],)), ((), ())), preferred_element_type=F32)


def dot3(a, b, dims):
    return one_dot(a[0], b[0], dims) + (one_dot(a[0], b[1], dims) + one_dot(a[1], b[0], dims))


def gelu_parts(v):
    cdf = 0.5 + 0.5 * lax.erf(v * ROOT_HALF)
    return v * cdf, cdf + v * (DENSITY * jnp.exp(-0.5 * v * v))


def pick(matrix, index):
    lane = lax.broadcasted_iota(jnp.int32, matrix.shape, 1)
    return jnp.sum(jnp.where(lane == index, matrix, 0.0), axis=1, keepdims=True)


def middle_kernel(
    place,
    factor,
    out_bias,
    x0,
    x1,
    x2,
    x3,
    w0,
    w1,
    w2,
    w3,
    domain,
    labels,
    gate_bias,
    b_first,
    w_second,
    b_second,
    t_first,
    t_bias,
    t_out,
    xt_high,
    xt_low,
    gf_high,
    gf_low,
    gate_rows,
    glog_out,
    s_keep,
    s_send,
    hid_high,
    hid_low,
    slope,
    e_out,
    gates,
    mix,
    gmix,
    ggate,
    b1_cols,
    b2_cols,
    summed,
    rest,
    sems,
):
    experts = w_second.shape[0]
    tasks, width, tower = t_first.shape
    hidden = w_second.shape[1]
    rows = domain.shape[1]
    domains = gate_bias.shape[1]
    cols = w0.shape[1]
    start, count, me, field = place[0], place[1], place[2], place[3]

    for k, ref in enumerate((x0, x1, x2, x3)):
        block = slice(k * cols, (k + 1) * cols)
        high, low = split(ref[0:rows, :].T)
        xt_high[block, :] = high
        xt_low[block, :] = low
        gate_rows[:, block] = ref[rows : rows + tasks * experts, :]
    hot = lax.broadcasted_iota(jnp.int32, (domains, rows), 0) == domain[...]
    onehot = jnp.where(hot, 1.0, 0.0).astype(BF16)
    bias_high, bias_low = split(gate_bias[...])
    logits = dot3(split(gate_rows[...]), (xt_high[...], xt_low[...]), NN)
    logits = logits + (one_dot(bias_high, onehot, NN) + one_dot(bias_low, onehot, NN))
    logits = logits.reshape(tasks, experts, rows)
    raised = jnp.exp(logits - jnp.max(logits, axis=1, keepdims=True))
    soft = raised / jnp.sum(raised, axis=1, keepdims=True)
    gates[...] = soft.reshape(tasks * experts, rows)
    mix[...] = jnp.zeros_like(mix)
    b1_cols[...] = jnp.zeros_like(b1_cols)
    b2_cols[...] = jnp.zeros_like(b2_cols)

    @pl.loop(0, experts)
    def _(e):
        weight = jnp.concatenate([w0[e], w1[e], w2[e], w3[e]], axis=0)
        pre = dot3(split(weight), (xt_high[...], xt_low[...]), TN) + pick(b_first[...], e)
        value, steep = gelu_parts(pre)
        slope[e] = steep
        value = split(value)
        hid_high[e], hid_low[e] = value
        result = dot3(split(w_second[e]), value, TN) + pick(b_second[...], e)
        e_out[e] = result
        for k in range(tasks):
            mix[k] += gates[pl.ds(k * experts + e, 1), :] * result

    position = start + lax.broadcasted_iota(jnp.int32, (1, rows), 1)
    live = jnp.where(position < count, 1.0, 0.0)
    loss = jnp.zeros((1, 1), F32)
    rest[...] = jnp.zeros_like(rest)
    small = width + tower + 4 * tasks * experts
    ones = jnp.ones((8, rows), BF16)
    row_of = lax.broadcasted_iota(jnp.int32, (8, rows), 0)
    lane_of = lax.broadcasted_iota(jnp.int32, (1, tower), 1)
    scalars = jnp.zeros((1, tower), F32)
    for k in range(tasks):
        mixed = split(mix[k])
        weight = split(t_first[k])
        pre = dot3(weight, mixed, TN) + t_bias[:, k : k + 1]
        value, steep = gelu_parts(pre)
        out_column = t_out[:, k : k + 1]
        score = jnp.sum(value * out_column, axis=0, keepdims=True) + out_bias[k]
        target = labels[k : k + 1, :].astype(F32)
        per_item = jnp.maximum(score, 0.0) + jnp.log1p(jnp.exp(-jnp.abs(score))) - target * score
        loss = loss + jnp.sum(per_item * live, axis=1, keepdims=True)
        gscore = live * (jax.nn.sigmoid(score) - target) * factor[0]
        gpre = split(gscore * out_column * steep)
        gweight = dot3(mixed, gpre, NT)
        gbias = one_dot(ones, gpre[0], NT) + one_dot(ones, gpre[1], NT)
        spread = split(jnp.where(row_of == 0, gscore, 0.0))
        gout = dot3(spread, split(value), NT)
        if k < 2:
            rest[0:width, k * tower : (k + 1) * tower] = gweight
        else:
            rest[width : width + tower, 0:tower] = gweight[0:tower]
            rest[width : width + tower, tower:] = gweight[tower:]
        misc = rest.shape[0] - 8
        at = k
        rest[misc + at // 2 : misc + at // 2 + 1, (at % 2) * tower : (at % 2 + 1) * tower] = gbias[0:1]
        at = tasks + k
        rest[misc + at // 2 : misc + at // 2 + 1, (at % 2) * tower : (at % 2 + 1) * tower] = gout[0:1]
        scalars = scalars + jnp.where(lane_of == k, jnp.sum(gscore, axis=1, keepdims=True), 0.0)
        gmix[k] = dot3(weight, gpre, NN)
    scalars = scalars + jnp.where(lane_of == tasks, loss, 0.0)
    rest[misc + tasks : misc + tasks + 1, 0:tower] = scalars

    @pl.loop(0, experts)
    def _(e):
        result = e_out[e]
        total = jnp.zeros_like(result)
        for k in range(tasks):
            down = gmix[k]
            ggate[pl.ds(k * experts + e, 1), :] = jnp.sum(down * result, axis=0, keepdims=True)
            total = total + gates[pl.ds(k * experts + e, 1), :] * down
        lane = lax.broadcasted_iota(jnp.int32, b1_cols.shape, 1)
        b2_cols[...] += jnp.where(lane == e, jnp.sum(total, axis=1, keepdims=True), 0.0)
        total = split(total)
        gweight = dot3((hid_high[e], hid_low[e]), total, NT)
        piece = hidden // 4
        for i in range(4):
            slot = (4 * e + i) ^ me
            summed[slot, 0:piece, :] = gweight[i * piece : (i + 1) * piece]
        gfirst = dot3(split(w_second[e]), total, NN) * slope[e]
        b1_cols[...] += jnp.where(lane == e, jnp.sum(gfirst, axis=1, keepdims=True), 0.0)
        high, low = split(gfirst)
        gf_high[e] = high
        gf_low[e] = low

    soft = gates[...].reshape(tasks, experts, rows)
    gsoft = ggate[...].reshape(tasks, experts, rows)
    glog = soft * (gsoft - jnp.sum(soft * gsoft, axis=1, keepdims=True))
    glog = glog.reshape(tasks * experts, rows)
    glog_out[...] = glog
    glog_parts = split(glog)
    ggw = dot3(glog_parts, (xt_high[...], xt_low[...]), NT)
    base = width + tower
    for k in range(4):
        rest[pl.ds(pl.multiple_of(base + (field ^ k) * tasks * experts, 8), tasks * experts), 0:tower] = ggw[
            :, k * cols : (k + 1) * cols
        ]
    b1_rows = b1_cols[...].T
    b2_rows = b2_cols[...].T
    rest[base : base + 8, tower:] = b1_rows[0:8, 0:tower]
    rest[base + 8 : base + 16, tower:] = b1_rows[0:8, tower:]
    base = base + 4 * tasks * experts
    rest[base : base + 8, :] = b2_rows[0:8]
    base = base + 8
    rest[base : base + domains, 0 : tasks * experts] = one_dot(onehot, glog_parts[0], NT) + one_dot(
        onehot, glog_parts[1], NT
    )
    tail = rest.shape[0] // 32
    for p in range(32):
        slot = p ^ me
        summed[slot, hidden // 4 :, :] = rest[p * tail : (p + 1) * tail, :]
    keep = pltpu.make_async_copy(summed.at[0:16], s_keep, sems.at[0])
    send = pltpu.make_async_copy(summed.at[16:32], s_send, sems.at[1])
    send.start()
    keep.start()
    send.wait()
    keep.wait()


def first_kernel(
    place, xt_high, xt_low, gf_high, gf_low, w0, w1, w2, w3, carried, *rest, first, last
):
    if last:
        keep, send, g0, g1, g2, g3, total = rest
    else:
        keep, send, total_out, total = rest
    step = pl.program_id(0)
    cols = w0.shape[1]
    piece = keep.shape[1] // 8
    halves = cols // piece
    me = place[0]
    parts = (gf_high[0], gf_low[0])
    weight = jnp.concatenate([w0[0], w1[0], w2[0], w3[0]], axis=0)
    gweight = dot3((xt_high[...], xt_low[...]), parts, NT)
    for k in range(4):
        target = (keep, send)[k % 2]
        for i in range(halves):
            slot = (halves * step + i) ^ me
            target[k // 2, pl.ds(pl.multiple_of(slot * piece, 8), piece), :] = gweight[
                k * cols + i * piece : k * cols + (i + 1) * piece
            ]

    @pl.when(step == 0)
    def _():
        if first:
            total[...] = dot3(split(carried[0][...]), split(carried[1][...]), TN)
        else:
            total[...] = carried[...]

    total[...] += dot3(split(weight), parts, NN)

    @pl.when(step == pl.num_programs(0) - 1)
    def _():
        if last:
            for k, ref in enumerate((g0, g1, g2, g3)):
                ref[...] = total[k * cols : (k + 1) * cols, :].T
        else:
            total_out[...] = total[...]


def finish_second_kernel(place, s0, s1, gw2, gtf, ggw, ggb, gb1, gb2, gtb, gto, scal, rest):
    me, field = place[0], place[1]
    hidden = gw2.shape[1]
    piece = hidden // 4
    tasks, width, tower = gtf.shape
    cols, experts = ggw.shape[1], ggw.shape[2]
    domains = ggb.shape[0]
    tail = rest.shape[0] // 32
    for p in range(32):
        slot = p ^ me
        low = slot % 16
        value = jnp.where(slot < 16, s0[low], s1[low])
        gw2[p // 4, (p % 4) * piece : (p % 4 + 1) * piece, :] = value[0:piece]
        rest[p * tail : (p + 1) * tail, :] = value[piece:]
    gtf[0] = rest[0:width, 0:tower]
    gtf[1] = rest[0:width, tower:]
    gtf[2, 0:tower] = rest[width : width + tower, 0:tower]
    gtf[2, tower:] = rest[width : width + tower, tower:]
    base = width + tower
    mine = rest[pl.ds(pl.multiple_of(base + field * tasks * experts, 8), tasks * experts), 0:tower]
    for k in range(tasks):
        ggw[k] = mine[k * experts : (k + 1) * experts].T
    gb1[:, 0:tower] = rest[base : base + 8, tower:]
    gb1[:, tower:] = rest[base + 8 : base + 16, tower:]
    base = base + 4 * tasks * experts
    gb2[...] = rest[base : base + 8, :]
    base = base + 8
    ggb[...] = rest[base : base + domains, 0 : tasks * experts]
    misc = rest.shape[0] - 8
    for k in range(tasks):
        at = k
        gtb[k : k + 1] = rest[misc + at // 2 : misc + at // 2 + 1, (at % 2) * tower : (at % 2 + 1) * tower]
        at = tasks + k
        gto[k : k + 1] = rest[misc + at // 2 : misc + at // 2 + 1, (at % 2) * tower : (at % 2 + 1) * tower]
    scal[...] = rest[misc + tasks : misc + tasks + 1, 0:tower]


def finish_first_kernel(place, a0, a1, b0, b1, out):
    me = place[0]
    half = out.shape[0] // 2
    cols = out.shape[1]
    piece = a0.shape[1]
    for c, (low_ref, high_ref) in enumerate(((a0, a1), (b0, b1))):
        for p in range(8):
            slot = p ^ me
            value = jnp.where(slot < 4, low_ref[slot % 4], high_ref[slot % 4])
            row = p * piece
            out[c * half + row // cols, row % cols : row % cols + piece, :] = value


def finish_inputs_kernel(place, g0, g1, g2, g3, out):
    field = place[0]
    rows = g0.shape[0]
    for k, ref in enumerate((g0, g1, g2, g3)):
        out[pl.ds(pl.multiple_of((field ^ k) * rows, 8), rows), :] = ref[...]


def whole():
    return pl.BlockSpec(memory_space=VMEM)


def scalars():
    return pl.BlockSpec(memory_space=pltpu.SMEM)


def like(shape, dtype=F32):
    return jax.ShapeDtypeStruct(shape, dtype)


def per_device(
    n_dp,
    examples,
    domain,
    labels,
    row_counts,
    gate_weight,
    gate_bias,
    w_first,
    b_first,
    w_second,
    b_second,
    tower_first,
    tower_bias,
    tower_out,
    tower_out_bias,
):
    all_rows, cols = examples.shape
    rows = all_rows // 4
    experts, _, hidden = w_first.shape
    tasks = gate_weight.shape[0]
    width = w_second.shape[2]
    tower = tower_first.shape[2]
    domains = gate_bias.shape[0]
    field = lax.axis_index("field").astype(jnp.int32)
    group = lax.axis_index("dp").astype(jnp.int32)

    def over_field(value, mask):
        return lax.ppermute(value, "field", [(d, d ^ mask) for d in range(4)])

    def over_dp(value, mask):
        return lax.ppermute(value, "dp", [(d, d ^ mask) for d in range(n_dp)])

    core, chip_y = field & 1, field >> 1
    chip_x, z_low, z_high = group & 1, (group >> 1) & 1, (group >> 2) & 1
    me5 = core * 16 + chip_x * 8 + chip_y * 4 + z_low * 2 + z_high
    me3 = chip_x * 4 + z_low * 2 + z_high

    count = row_counts[0]
    total = jnp.minimum(count, all_rows).astype(F32).reshape(1)
    mask = 1
    while mask < n_dp:
        total = total + over_dp(total, mask)
        mask *= 2
    factor = 1.0 / total

    gate_rows = jnp.transpose(gate_weight, (0, 2, 1)).reshape(tasks * experts, cols)
    blocks = []
    for k in range(4):
        mine = lax.dynamic_slice(examples, ((field ^ k) * rows, 0), (rows, cols))
        blocks.append(jnp.concatenate([mine, gate_rows], axis=0))
    blocks = [blocks[0]] + [over_field(blocks[k], k) for k in (1, 2, 3)]
    first_near = over_field(w_first, 1)
    first_far = over_field(w_first, 2)
    first_last = over_field(first_far, 1)
    firsts = (w_first, first_near, first_far, first_last)

    my_domain = lax.dynamic_slice(domain, (field * rows,), (rows,)).reshape(1, rows)
    my_labels = lax.dynamic_slice(labels, (field * rows, 0), (rows, tasks)).T

    units = experts * hidden
    place = jnp.stack([field * rows, count, me5, field]).astype(jnp.int32)
    outs = pl.pallas_call(
        middle_kernel,
        name="middle",
        out_shape=(
            like((4 * cols, rows), BF16),
            like((4 * cols, rows), BF16),
            like((experts, hidden, rows), BF16),
            like((experts, hidden, rows), BF16),
            like((tasks * experts, 4 * cols)),
            like((tasks * experts, rows)),
            like((16, 80, width)),
            like((16, 80, width)),
        ),
        in_specs=[scalars()] * 3 + [whole()] * 17,
        out_specs=[whole()] * 6 + [pl.BlockSpec(memory_space=pl.ANY)] * 2,
        scratch_shapes=[
            VMEM((experts, hidden, rows), BF16),
            VMEM((experts, hidden, rows), BF16),
            VMEM((experts, hidden, rows), F32),
            VMEM((experts, width, rows), F32),
            VMEM((tasks * experts, rows), F32),
            VMEM((tasks, width, rows), F32),
            VMEM((tasks, width, rows), F32),
            VMEM((tasks * experts, rows), F32),
            VMEM((hidden, 128), F32),
            VMEM((width, 128), F32),
            VMEM((32, 80, width), F32),
            VMEM((512, width), F32),
            pltpu.SemaphoreType.DMA((2,)),
        ],
        compiler_params=PARAMS,
        cost_estimate=pl.CostEstimate(
            flops=6 * rows * units * (4 * cols + 3 * width), bytes_accessed=24 << 20, transcendentals=2 * rows * units
        ),
    )(
        place,
        factor,
        tower_out_bias,
        *blocks,
        *firsts,
        my_domain,
        my_labels,
        gate_bias.T,
        b_first.T,
        w_second,
        b_second.T,
        tower_first,
        tower_bias.T,
        tower_out.T,
    )
    xt_high, xt_low, gf_high, gf_low, gate_all, glog, s_keep, s_send = outs

    half = experts // 2
    chunk_rows = half * cols
    place3 = me3.reshape(1)

    def first_call(index, carried):
        last = index == 1
        expert = lambda i: (i + index * half, 0, 0)
        tail_shapes = tuple(like((rows, cols)) for _ in range(4)) if last else (like((4 * cols, rows)),)
        n_carried = 1 if last else 2

        def body(place_ref, *refs):
            ins, others = refs[:8], refs[8:]
            given = others[:n_carried]
            first_kernel(
                place_ref,
                *ins,
                given[0] if last else given,
                *others[n_carried:],
                first=not last,
                last=last,
            )

        return pl.pallas_call(
            body,
            name="first_%d" % index,
            grid=(half,),
            out_shape=(like((2, chunk_rows, hidden)), like((2, chunk_rows, hidden))) + tail_shapes,
            in_specs=[scalars(), whole(), whole()]
            + [pl.BlockSpec((1, hidden, rows), expert)] * 2
            + [pl.BlockSpec((1, cols, hidden), expert)] * 4
            + [whole()] * n_carried,
            out_specs=[whole()] * (2 + len(tail_shapes)),
            scratch_shapes=[VMEM((4 * cols, rows), F32)],
            compiler_params=PARAMS,
            cost_estimate=pl.CostEstimate(
                flops=12 * rows * half * hidden * 4 * cols, bytes_accessed=12 << 20, transcendentals=0
            ),
        )(place3, xt_high, xt_low, gf_high, gf_low, *firsts, *carried)

    def over_rest(value):
        mask = 8
        while mask < n_dp:
            value = value + over_dp(value, mask)
            mask *= 2
        return value

    def halve(kept, got, move, mask):
        n = kept.shape[0] // 2
        send = kept[n:] + got[n:]
        stay = kept[:n] + got[:n]
        return stay, move(send, mask)

    def double(value, move, mask):
        return jnp.concatenate([value, move(value, mask)], axis=0)

    kept, got = s_keep, over_field(s_send, 1)
    kept, got = halve(kept, got, over_dp, 1)
    kept, got = halve(kept, got, over_field, 2)
    kept, got = halve(kept, got, over_dp, 2)
    kept, got = halve(kept, got, over_dp, 4)
    value = over_rest(kept + got)
    value = double(value, over_dp, 4)
    value = double(value, over_dp, 2)
    value = double(value, over_field, 2)
    value = double(value, over_dp, 1)
    other = over_field(value, 1)

    seconds = pl.pallas_call(
        finish_second_kernel,
        name="finish_second",
        out_shape=(
            like((experts, hidden, width)),
            like((tasks, width, tower)),
            like((tasks, cols, experts)),
            like((domains, tasks * experts)),
            like((experts, hidden)),
            like((experts, width)),
            like((tasks, tower)),
            like((tasks, tower)),
            like((1, tower)),
        ),
        in_specs=[scalars()] + [whole()] * 2,
        out_specs=[whole()] * 9,
        scratch_shapes=[VMEM((512, width), F32)],
        compiler_params=PARAMS,
    )(jnp.stack([me5, field]), value, other)
    grad_w_second, grad_tower_first, grad_gate_weight, grad_gate_bias = seconds[:4]
    grad_b_first, grad_b_second, grad_tower_bias, grad_tower_out, scal = seconds[4:]

    def sum_first(keep, send):
        got = over_field(send, 1)
        far = keep[1] + got[1]
        near = keep[0] + got[0]
        kept, got = near.reshape(8, -1, hidden), over_field(far, 2).reshape(8, -1, hidden)
        kept, got = halve(kept, got, over_dp, 1)
        kept, got = halve(kept, got, over_dp, 2)
        kept, got = halve(kept, got, over_dp, 4)
        value = over_rest(kept + got)
        value = double(value, over_dp, 4)
        value = double(value, over_dp, 2)
        return value, over_dp(value, 1)

    keep, send, carried = first_call(0, (gate_all, glog))
    pair_a = sum_first(keep, send)
    keep, send, g0, g1, g2, g3 = first_call(1, (carried,))
    pair_b = sum_first(keep, send)
    grad_w_first = pl.pallas_call(
        finish_first_kernel,
        name="finish_first",
        out_shape=like((experts, cols, hidden)),
        in_specs=[scalars()] + [whole()] * 4,
        out_specs=whole(),
        compiler_params=PARAMS,
    )(place3, *pair_a, *pair_b)

    back = [g0] + [over_field(g, k) for k, g in ((1, g1), (2, g2), (3, g3))]
    grad_examples = pl.pallas_call(
        finish_inputs_kernel,
        name="finish_inputs",
        out_shape=like((all_rows, cols)),
        in_specs=[scalars()] + [whole()] * 4,
        out_specs=whole(),
        compiler_params=PARAMS,
    )(field.reshape(1), *back)

    loss = scal[0, tasks] / total[0]
    return (
        loss,
        grad_examples,
        grad_gate_weight,
        grad_gate_bias,
        grad_w_first,
        grad_b_first,
        grad_w_second,
        grad_b_second,
        grad_tower_first,
        grad_tower_bias,
        grad_tower_out,
        scal[0, :tasks],
    )


def solution(mesh):
    placed = (
        P("dp", "field"),
        P("dp"),
        P("dp", None),
        P("dp"),
        P(None, "field", None),
        P(),
        P(None, "field", None),
        P(),
        P(),
        P(),
        P(),
        P(),
        P(),
        P(),
    )
    return jax.shard_map(
        functools.partial(per_device, mesh.shape["dp"]),
        mesh=mesh,
        in_specs=placed,
        out_specs=(
            P(),
            P("dp", "field"),
            P(None, "field", None),
            P(),
            P(None, "field", None),
            P(),
            P(),
            P(),
            P(),
            P(),
            P(),
            P(),
        ),
        check_vma=False,
    )
```

time: 845 us -> 225 us (0.27)
  matrix products: 324 us -> 0 us
  waiting for transfers between devices: 329 us -> 95.8 us
  other arithmetic: 80.6 us -> 2.95 us
  blocking collectives: 64.7 us -> 0 us
  Pallas kernels: 0 us -> 57.8 us
  starting transfers between devices: 0.08 us -> 47.3 us
  between operations: 18.4 us -> 5.59 us
    psum x2 -> x0, waiting for transfers between devices: 329 us -> none  [the longest x1 269 us: per_device(): summed_first, summed_gate = lax.psum((part_first, part_gate), 'field')]
    dot_general x18 -> x0, matrix products: 321 us -> none  [the longest x1 45.6 us: per_device(): jnp.einsum('tkj,tej->tke', grad_mixture, expert_out, precision=HIGHEST)]
    ppermute x0 -> x38, waiting for transfers between devices: none -> 95.8 us  [the longest x17 48.1 us: over_field(): return lax.ppermute(value, 'field', [(d, d ^ mask) for d in range(4)])]
    psum x2 -> x0, blocking collectives: 64.7 us -> none  [the longest x1 40.6 us: per_device(): lax.psum((members[0], members[1], members[2], members[3], members[4], mem...]
    pallas_call x0 -> x6, Pallas kernels: none -> 57.8 us  [the longest x1 28.5 us: per_device(): pl.pallas_call(middle_kernel, name='middle', out_shape=(like((4 * cols, r...]
    ppermute x0 -> x38, starting transfers between devices: none -> 47.3 us  [the longest x21 35.6 us: over_dp(): return lax.ppermute(value, 'dp', [(d, d ^ mask) for d in range(n_dp)])]
    another operation x1 -> x2, other arithmetic: 37.9 us -> 1.17 us  [the longest x1 0.59 us: per_device(): place = jnp.stack([field * rows, count, me5, field]).astype(jnp.int32)]
    reduce_sum x4 -> x0, other arithmetic: 32.8 us -> none  [the longest x1 29.9 us: per_device(): gates = jax.nn.softmax(logits, axis=-1)]
  transfers between devices with their start and end apart: 2 -> 38, of which waited for: 2 -> 20; matrix products, arithmetic and copies ran while one was open for 5% -> 4% of each run, Pallas kernels for 0% -> 11%
where the time goes in v1:
time: 225 us
  waiting for transfers between devices  95.8 us (43%)
  Pallas kernels  57.8 us (26%)
  starting transfers between devices  47.3 us (21%)
  local copies, waits for them, and re-layouts  15.4 us (7%)
  between operations  5.59 us (2%)
  other arithmetic  2.95 us (1%)
    ppermute x17, waiting for transfers between devices, over_field(): return lax.ppermute(value, 'field', [(d, d ^ mask) for d in range(4)])  48.1 us
    ppermute x21, waiting for transfers between devices, over_dp(): return lax.ppermute(value, 'dp', [(d, d ^ mask) for d in range(n_dp)])  47.7 us
    ppermute x21, starting transfers between devices, over_dp(): return lax.ppermute(value, 'dp', [(d, d ^ mask) for d in range(n_dp)])  35.6 us
    pallas_call x1, Pallas kernels, per_device(): pl.pallas_call(middle_kernel, name='middle', out_shape=(like((4 * cols, r...  28.5 us
    pallas_call x2, Pallas kernels, first_call(): pl.pallas_call(body, name='first_%d' % index, grid=(half,), out_shape=(li...  21.3 us
    ppermute x17, starting transfers between devices, over_field(): return lax.ppermute(value, 'field', [(d, d ^ mask) for d in range(4)])  11.7 us
    unnamed x61, local copies, waits for them, and re-layouts  9.67 us
  transfers between devices with their start and end apart: 38, of which 20 were waited for; matrix products, arithmetic and copies ran while one was open for 4% of the time, Pallas kernels for 11%

profile of v1, /device:TPU:0, one launch (start us, length us, event | category | flops | bytes accessed | tf_op | source)
XLA Modules:
  0.0 224.8 jit_solution(6286871919645788762)
XLA Ops:
  0.7 3.0 %collective-permute-start.7 = (f32[8,128,256]{2,1,0:T(8,128)}, f32[8,128,256]{2,1,0:T(8,128)S(1)}, u32[]{:S(2)}, u32[]{:S(2)}) collective-permute-start(f32[8,128,256]{2,1,0:T(8,128)} %refs_4_.3), channel_id=1, source_target_pairs={{0,2},{1,3},{2,0},{3,1},{4,6},{5,7},{6,4},{7,5},{8,10},{9,11},{10,... | collective-permute-start | bytes 3145736 | tf_op jit(solution)/shard_map/ppermute | solution.py:359
  3.7 23.4 %collective-permute-done.7.w2.refs_6_ = f32[8,128,256]{2,1,0:T(8,128)S(1)} collective-permute-done((f32[8,128,256]{2,1,0:T(8,128)}, f32[8,128,256]{2,1,0:T(8,128)S(1)}, u32[]{:S(2)}, u32[]{:S(2)}) %collective-permute-start.7) | collective-permute-done | bytes 1048608 | tf_op jit(solution)/shard_map/ppermute | solution.py:359
  27.7 3.1 %collective-permute-start = (f32[1]{0:T(128)}, f32[1]{0:T(128)}, u32[]{:S(2)}, u32[]{:S(2)}) collective-permute-start(f32[1]{0:T(128)} %convert_element_type.4), channel_id=1, source_target_pairs={{0,4},{4,0},{8,12},{12,8},{16,20},{20,16},{24,28},{28,24},{1,5},{5... | collective-permute-start | bytes 20 | tf_op jit(solution)/shard_map/ppermute | solution.py:362
  30.8 1.3 constant_dynamic-slice_fusion
  32.1 0.8 pad_maximum_fusion.1
  32.9 0.8 collective-permute-start.5
  33.7 0.9 collective-permute-start.3
  35.2 2.9 %collective-permute-start.1 = (f32[1]{0:T(128)}, f32[1]{0:T(128)}, u32[]{:S(2)}, u32[]{:S(2)}) collective-permute-start(f32[1]{0:T(128)} %add.142), channel_id=1, source_target_pairs={{0,8},{4,12},{8,0},{12,4},{16,24},{20,28},{24,16},{28,20},{1,9},{5... | collective-permute-start | bytes 20 | tf_op jit(solution)/shard_map/ppermute | solution.py:362
  38.2 0.6 collective-permute-done.1
  39.5 4.0 %collective-permute-start.2 = (f32[1]{0:T(128)}, f32[1]{0:T(128)}, u32[]{:S(2)}, u32[]{:S(2)}) collective-permute-start(f32[1]{0:T(128)} %add.143), channel_id=1, source_target_pairs={{0,16},{4,20},{8,24},{12,28},{16,0},{20,4},{24,8},{28,12},{1,17},{... | collective-permute-start | bytes 20 | tf_op jit(solution)/shard_map/ppermute | solution.py:362
  44.5 1.3 dynamic_slice.22
  45.8 0.7 copy.26
  46.5 0.7 copy.29
  47.2 0.8 copy.30
  48.0 0.8 copy.27
  48.8 0.8 copy.28
  49.6 0.6 pad_add_fusion.1.place
  50.1 0.6 dynamic-slice_bitcast_fusion.labels
  51.5 0.6 copy-done.22
  52.5 28.5 %middle.1 = (bf16[512,512]{1,0:T(8,128)(2,1)}, bf16[512,512]{1,0:T(8,128)(2,1)}, bf16[8,256,512]{2,1,0:T(8,128)(2,1)}, bf16[8,256,512]{2,1,0:T(8,128)(2,1)}, f32...) custom-call(s32[4]{0:T(128)} %pad_add_fusion.1.place, f32[1]{0:T(128)S(6)} %div.6.factor, ...), custom_call_target="tpu_custom_call" | custom-call | flops 8053063680 | bytes 25165824 | tf_op jit(solution)/shard_map/middle/pallas_call | solution.py:393
  81.1 9.0 %first_0.1 = (f32[2,512,256]{2,1,0:T(8,128)}, f32[2,512,256]{2,1,0:T(8,128)}, f32[512,512]{1,0:T(8,128)}) custom-call(s32[1]{0:T(128)} %bitcast.15.place_ref.place, bf16[512,512]{1,0:T(8,128)(2,1)} %get-tuple-element.41.refs_0_, bf16[512,512]{1,0:T(8,128)(2,1)} %get-tuple-element.42.refs_1_, bf16[8,256,512]{2,1,0:T(8,128)(2,1)} %get-tuple-element.43.refs_2_, ...), custom_call_target="tpu_custom_call" | custom-call | flops 3221225472 | bytes 12582912 | tf_op jit(solution)/shard_map/first_0/pallas_call | solution.py:467
  90.2 12.2 %first_1.1 = (f32[2,512,256]{2,1,0:T(8,128)}, f32[2,512,256]{2,1,0:T(8,128)}, f32[512,128]{1,0:T(8,128)}, f32[512,128]{1,0:T(8,128)}, f32[512,128]{1,0:T(8,128)}, /*index=5*/f32[512,128]{1,0:T(8,128)}) custom-call(s32[1]{0:T(128)} %bitcast.15.place_ref.place, bf16[512,512]{1,0:T(8,128)(2,1)} %get-tuple-element.41.refs_0_, ...), custom_call_target="tpu_custom_call" | custom-call | flops 3221225472 | bytes 12582912 | tf_op jit(solution)/shard_map/first_1/pallas_call | solution.py:467
  103.4 0.7 copy-done.21
  104.1 15.7 %collective-permute-done.10 = f32[8,80,256]{2,1,0:T(8,128)S(1)} collective-permute-done((f32[8,80,256]{2,1,0:T(8,128)S(1)}, f32[8,80,256]{2,1,0:T(8,128)S(1)}, u32[]{:S(2)}, u32[]{:S(2)}) %collective-permute-start.10) | collective-permute-done | bytes 655392 | tf_op jit(solution)/shard_map/ppermute | solution.py:362
  119.9 1.6 collective-permute-start.11
  122.2 8.4 %collective-permute-done.11 = f32[4,80,256]{2,1,0:T(8,128)S(1)} collective-permute-done((f32[4,80,256]{2,1,0:T(8,128)S(1)}, f32[4,80,256]{2,1,0:T(8,128)S(1)}, u32[]{:S(2)}, u32[]{:S(2)}) %collective-permute-start.11) | collective-permute-done | bytes 327712 | tf_op jit(solution)/shard_map/ppermute | solution.py:359
  130.7 1.6 collective-permute-start.12
  132.4 1.6 collective-permute-start.23
  134.0 2.9 %collective-permute-done.12 = f32[2,80,256]{2,1,0:T(8,128)S(1)} collective-permute-done((f32[2,80,256]{2,1,0:T(8,128)S(1)}, f32[2,80,256]{2,1,0:T(8,128)S(1)}, u32[]{:S(2)}, u32[]{:S(2)}) %collective-permute-start.12) | collective-permute-done | bytes 163872 | tf_op jit(solution)/shard_map/ppermute | solution.py:362
  136.9 2.5 %collective-permute-start.13 = (f32[1,80,256]{2,1,0:T(8,128)S(1)}, f32[1,80,256]{2,1,0:T(8,128)S(1)}, u32[]{:S(2)}, u32[]{:S(2)}) collective-permute-start(f32[1,80,256]{2,1,0:T(8,128)S(1)} %slice_add_fusion.18), channel_id=1, source_target_pairs={{0,16},{4,20},{8,24},{12,28},{16,0},{20,4},{24,8},{28,12},{1,17},{... | collective-permute-start | bytes 245768 | tf_op jit(solution)/shard_map/ppermute | solution.py:362
  139.5 2.4 %collective-permute-done.31 = f32[512,256]{1,0:T(8,128)S(1)} collective-permute-done((f32[512,256]{1,0:T(8,128)S(1)}, f32[512,256]{1,0:T(8,128)S(1)}, u32[]{:S(2)}, u32[]{:S(2)}) %collective-permute-start.31) | collective-permute-done | bytes 524320 | tf_op jit(solution)/shard_map/ppermute | solution.py:359
  142.3 2.0 collective-permute-done.13
  144.3 0.8 collective-permute-start.14
  145.2 6.1 %collective-permute-done.23 = f32[512,256]{1,0:T(8,128)S(1)} collective-permute-done((f32[512,256]{1,0:T(8,128)S(1)}, f32[512,256]{1,0:T(8,128)S(1)}, u32[]{:S(2)}, u32[]{:S(2)}) %collective-permute-start.23) | collective-permute-done | bytes 524320 | tf_op jit(solution)/shard_map/ppermute | solution.py:359
  151.3 1.6 collective-permute-start.15
  153.0 3.7 %collective-permute-done.15 = f32[2,80,256]{2,1,0:T(8,128)S(1)} collective-permute-done((f32[2,80,256]{2,1,0:T(8,128)S(1)}, f32[2,80,256]{2,1,0:T(8,128)S(1)}, u32[]{:S(2)}, u32[]{:S(2)}) %collective-permute-start.15) | collective-permute-done | bytes 163872 | tf_op jit(solution)/shard_map/ppermute | solution.py:362
  156.8 1.6 collective-permute-start.16
  159.0 1.6 collective-permute-start.33
  160.6 3.3 %collective-permute-done.16 = f32[4,80,256]{2,1,0:T(8,128)S(1)} collective-permute-done((f32[4,80,256]{2,1,0:T(8,128)S(1)}, f32[4,80,256]{2,1,0:T(8,128)S(1)}, u32[]{:S(2)}, u32[]{:S(2)}) %collective-permute-start.16) | collective-permute-done | bytes 327712 | tf_op jit(solution)/shard_map/ppermute | solution.py:359
  164.3 2.8 %collective-permute-done.24 = f32[4,64,256]{2,1,0:T(8,128)S(1)} collective-permute-done((f32[4,64,256]{2,1,0:T(8,128)S(1)}, f32[4,64,256]{2,1,0:T(8,128)S(1)}, u32[]{:S(2)}, u32[]{:S(2)}) %collective-permute-start.24) | collective-permute-done | bytes 262176 | tf_op jit(solution)/shard_map/ppermute | solution.py:362
  167.1 1.7 collective-permute-start.25
  168.8 2.6 %collective-permute-start.34 = (f32[1,64,256]{2,1,0:T(8,128)S(1)}, f32[1,64,256]{2,1,0:T(8,128)S(1)}, u32[]{:S(2)}, u32[]{:S(2)}) collective-permute-start(f32[1,64,256]{2,1,0:T(8,128)S(1)} %slice_add_fusion.20), channel_id=1, source_target_pairs={{0,16},{4,20},{8,24},{12,28},{16,0},{20,4},{24,8},{28,12},{1,17},{... | collective-permute-start | bytes 196616 | tf_op jit(solution)/shard_map/ppermute | solution.py:362
  171.5 7.3 %collective-permute-done.17 = f32[8,80,256]{2,1,0:T(8,128)S(1)} collective-permute-done((f32[8,80,256]{2,1,0:T(8,128)S(1)}, f32[8,80,256]{2,1,0:T(8,128)S(1)}, u32[]{:S(2)}, u32[]{:S(2)}) %collective-permute-start.17) | collective-permute-done | bytes 655392 | tf_op jit(solution)/shard_map/ppermute | solution.py:362
  179.0 2.6 %collective-permute-start.26 = (f32[1,64,256]{2,1,0:T(8,128)S(1)}, f32[1,64,256]{2,1,0:T(8,128)S(1)}, u32[]{:S(2)}, u32[]{:S(2)}) collective-permute-start(f32[1,64,256]{2,1,0:T(8,128)S(1)} %slice_add_fusion.22), channel_id=1, source_target_pairs={{0,16},{4,20},{8,24},{12,28},{16,0},{20,4},{24,8},{28,12},{1,17},{... | collective-permute-start | bytes 196616 | tf_op jit(solution)/shard_map/ppermute | solution.py:362
  182.1 4.0 %collective-permute-done.26 = f32[1,64,256]{2,1,0:T(8,128)S(1)} collective-permute-done((f32[1,64,256]{2,1,0:T(8,128)S(1)}, f32[1,64,256]{2,1,0:T(8,128)S(1)}, u32[]{:S(2)}, u32[]{:S(2)}) %collective-permute-start.26) | collective-permute-done | bytes 65568 | tf_op jit(solution)/shard_map/ppermute | solution.py:362
  186.1 1.5 collective-permute-start.27
  187.6 1.4 collective-permute-done.35
  189.0 2.5 %collective-permute-start.36 = (f32[2,64,256]{2,1,0:T(8,128)S(1)}, f32[2,64,256]{2,1,0:T(8,128)S(1)}, u32[]{:S(2)}, u32[]{:S(2)}) collective-permute-start(f32[2,64,256]{2,1,0:T(8,128)S(1)} %pad_maximum_fusion.10), channel_id=1, source_target_pairs={{0,8},{4,12},{8,0},{12,4},{16,24},{20,28},{24,16},{28,20},{1,9},{5... | collective-permute-start | bytes 393224 | tf_op jit(solution)/shard_map/ppermute | solution.py:362
  191.5 2.3 %collective-permute-start.28 = (f32[2,64,256]{2,1,0:T(8,128)S(1)}, f32[2,64,256]{2,1,0:T(8,128)S(1)}, u32[]{:S(2)}, u32[]{:S(2)}) collective-permute-start(f32[2,64,256]{2,1,0:T(8,128)S(1)} %pad_maximum_fusion.9), channel_id=1, source_target_pairs={{0,8},{4,12},{8,0},{12,4},{16,24},{20,28},{24,16},{28,20},{1,9},{5... | collective-permute-start | bytes 393224 | tf_op jit(solution)/shard_map/ppermute | solution.py:362
  194.3 0.8 collective-permute-done.36
  195.1 2.6 %collective-permute-done.28 = f32[2,64,256]{2,1,0:T(8,128)S(1)} collective-permute-done((f32[2,64,256]{2,1,0:T(8,128)S(1)}, f32[2,64,256]{2,1,0:T(8,128)S(1)}, u32[]{:S(2)}, u32[]{:S(2)}) %collective-permute-start.28) | collective-permute-done | bytes 131104 | tf_op jit(solution)/shard_map/ppermute | solution.py:362
  198.3 1.6 collective-permute-start.29
  200.5 2.6 %collective-permute-done.20.g2 = f32[512,128]{1,0:T(8,128)S(1)} collective-permute-done((f32[512,128]{1,0:T(8,128)S(1)}, f32[512,128]{1,0:T(8,128)S(1)}, u32[]{:S(2)}, u32[]{:S(2)}) %collective-permute-start.20) | collective-permute-done | bytes 262176 | tf_op jit(solution)/shard_map/ppermute | solution.py:359
  203.0 2.0 collective-permute-done.21.g3
  205.1 0.7 copy-done.10
  205.7 2.2 finish_inputs.1
  208.0 3.3 %collective-permute-done.29.a1 = f32[4,64,256]{2,1,0:T(8,128)S(1)} collective-permute-done((f32[4,64,256]{2,1,0:T(8,128)S(1)}, f32[4,64,256]{2,1,0:T(8,128)S(1)}, u32[]{:S(2)}, u32[]{:S(2)}) %collective-permute-start.29) | collective-permute-done | bytes 262176 | tf_op jit(solution)/shard_map/ppermute | solution.py:362
  211.3 0.7 copy-done.12
  212.0 2.3 %finish_first.1 = f32[8,128,256]{2,1,0:T(8,128)} custom-call(s32[1]{0:T(128)} %bitcast.15.place_ref.place, f32[4,64,256]{2,1,0:T(8,128)} %copy-done.7, f32[4,64,256]{2,1,0:T(8,128)} %copy-done.12, f32[4,64,256]{2,1,0:T(8,128)} %copy-done.6, f32[4,64,256]{2,1,0:T(8,128)} %copy-done.11), custom_call_target="tpu_custom_call" | custom-call | tf_op jit(solution)/shard_map/finish_first/pallas_call | solution.py:551
  214.3 1.1 copy-done.2
  215.4 3.6 %finish_second.1 = (f32[8,256,256]{2,1,0:T(8,128)}, f32[3,256,128]{2,1,0:T(8,128)}, f32[3,128,8]{2,1,0:T(8,128)}, f32[16,24]{1,0:T(8,128)}, f32[8,256]{1,0:T(8,1...) custom-call(s32[2]{0:T(128)} %pad_add_fusion.place, ...), custom_call_target="tpu_custom_call" | custom-call | tf_op jit(solution)/shard_map/finish_second/pallas_call | solution.py:512
  218.9 1.3 slice.198
  220.2 1.2 slice_bitcast_fusion.4
  221.4 1.6 copy.31
  (112 shorter events, 7.6 us)
Async XLA Ops:
  0.6 49.5 %copy-start = (s32[2048,3]{0,1:T(4,128)S(1)}, s32[2048,3]{0,1:T(4,128)}, u32[]{:S(2)}) copy-start(s32[2048,3]{0,1:T(4,128)} %param.16) | copy-start | bytes 73732
  0.7 31.5 %copy-start.13 = (f32[3,128,8]{1,2,0:T(8,128)S(1)}, f32[3,128,8]{1,2,0:T(8,128)}, u32[]{:S(2)}) copy-start(f32[3,128,8]{1,2,0:T(8,128)} %param.18) | copy-start | bytes 36868
  0.7 26.4 %collective-permute-start.7 = (f32[8,128,256]{2,1,0:T(8,128)}, f32[8,128,256]{2,1,0:T(8,128)S(1)}, u32[]{:S(2)}, u32[]{:S(2)}) collective-permute-start(f32[8,128,256]{2,1,0:T(8,128)} %refs_4_.3), channel_id=1, source_target_pairs={{0,2},{1,3},{2,0},{3,1},{4,6},{5,7},{6,4},{7,5},{8,10},{9,11},{10,... | collective-permute-start | bytes 3145736 | tf_op jit(solution)/shard_map/ppermute | solution.py:359
  3.7 47.8 %collective-permute-start.6 = (f32[8,128,256]{2,1,0:T(8,128)}, f32[8,128,256]{2,1,0:T(8,128)S(1)}, u32[]{:S(2)}, u32[]{:S(2)}) collective-permute-start(f32[8,128,256]{2,1,0:T(8,128)} %refs_4_.3), channel_id=1, source_target_pairs={{0,1},{1,0},{2,3},{3,2},{4,5},{5,4},{6,7},{7,6},{8,9},{9,8},{10,11... | collective-permute-start | bytes 3145736 | tf_op jit(solution)/shard_map/ppermute | solution.py:359
  27.1 5.9 %copy-start.19 = (f32[8,128,256]{2,1,0:T(8,128)}, f32[8,128,256]{2,1,0:T(8,128)S(1)}, u32[]{:S(2)}) copy-start(f32[8,128,256]{2,1,0:T(8,128)S(1)} %collective-permute-done.7.w2.refs_6_) | copy-start | bytes 3145732
  27.1 24.4 %collective-permute-start.8 = (f32[8,128,256]{2,1,0:T(8,128)S(1)}, f32[8,128,256]{2,1,0:T(8,128)}, u32[]{:S(2)}, u32[]{:S(2)}) collective-permute-start(f32[8,128,256]{2,1,0:T(8,128)S(1)} %collective-permute-done.7.w2.refs_6_), channel_id=1, source_target_pairs={{0,1},{1,0},{2,3},{3,2},{4,5},{5,4},{6,7},{7,6},{8,9},{9,8},{10,11... | collective-permute-start | bytes 3145736 | tf_op jit(solution)/shard_map/ppermute | solution.py:359
  27.7 6.8 %collective-permute-start = (f32[1]{0:T(128)}, f32[1]{0:T(128)}, u32[]{:S(2)}, u32[]{:S(2)}) collective-permute-start(f32[1]{0:T(128)} %convert_element_type.4), channel_id=1, source_target_pairs={{0,4},{4,0},{8,12},{12,8},{16,20},{20,16},{24,28},{28,24},{1,5},{5... | collective-permute-start | bytes 20 | tf_op jit(solution)/shard_map/ppermute | solution.py:362
  32.1 13.7 %copy-start.16 = (f32[16,24]{1,0:T(8,128)S(1)}, f32[16,24]{1,0:T(8,128)}, u32[]{:S(2)}) copy-start(f32[16,24]{1,0:T(8,128)} %param.19) | copy-start | bytes 4612
  32.1 14.4 %copy-start.17 = (f32[3,128]{1,0:T(4,128)S(1)}, f32[3,128]{1,0:T(4,128)}, u32[]{:S(2)}) copy-start(f32[3,128]{1,0:T(4,128)} %param.25) | copy-start | bytes 4612
  32.1 15.1 %copy-start.18 = (f32[3,128]{1,0:T(4,128)S(1)}, f32[3,128]{1,0:T(4,128)}, u32[]{:S(2)}) copy-start(f32[3,128]{1,0:T(4,128)} %param.26) | copy-start | bytes 4612
  32.1 15.9 %copy-start.14 = (f32[8,256]{1,0:T(8,128)S(1)}, f32[8,256]{1,0:T(8,128)}, u32[]{:S(2)}) copy-start(f32[8,256]{1,0:T(8,128)} %param.21) | copy-start | bytes 24580
  32.1 16.6 %copy-start.15 = (f32[8,256]{1,0:T(8,128)S(1)}, f32[8,256]{1,0:T(8,128)}, u32[]{:S(2)}) copy-start(f32[8,256]{1,0:T(8,128)} %param.23) | copy-start | bytes 24580
  32.9 18.5 %collective-permute-start.5 = (f32[536,128]{1,0:T(8,128)S(1)}, f32[536,128]{1,0:T(8,128)S(1)}, u32[]{:S(2)}, u32[]{:S(2)}) collective-permute-start(f32[536,128]{1,0:T(8,128)S(1)} %get-tuple-element.104), channel_id=1, source_target_pairs={{0,3},{1,2},{2,1},{3,0},{4,7},{5,6},{6,5},{7,4},{8,11},{9,10},{10,... | collective-permute-start | bytes 823304 | tf_op jit(solution)/shard_map/ppermute | solution.py:359
  33.7 17.7 %collective-permute-start.3 = (f32[536,128]{1,0:T(8,128)S(1)}, f32[536,128]{1,0:T(8,128)}, u32[]{:S(2)}, u32[]{:S(2)}) collective-permute-start(f32[536,128]{1,0:T(8,128)S(1)} %get-tuple-element.105), channel_id=1, source_target_pairs={{0,1},{1,0},{2,3},{3,2},{4,5},{5,4},{6,7},{7,6},{8,9},{9,8},{10,11... | collective-permute-start | bytes 823304 | tf_op jit(solution)/shard_map/ppermute | solution.py:359
  35.2 3.6 %collective-permute-start.1 = (f32[1]{0:T(128)}, f32[1]{0:T(128)}, u32[]{:S(2)}, u32[]{:S(2)}) collective-permute-start(f32[1]{0:T(128)} %add.142), channel_id=1, source_target_pairs={{0,8},{4,12},{8,0},{12,4},{16,24},{20,28},{24,16},{28,20},{1,9},{5... | collective-permute-start | bytes 20 | tf_op jit(solution)/shard_map/ppermute | solution.py:362
  39.5 4.5 %collective-permute-start.2 = (f32[1]{0:T(128)}, f32[1]{0:T(128)}, u32[]{:S(2)}, u32[]{:S(2)}) collective-permute-start(f32[1]{0:T(128)} %add.143), channel_id=1, source_target_pairs={{0,16},{4,20},{8,24},{12,28},{16,0},{20,4},{24,8},{28,12},{1,17},{... | collective-permute-start | bytes 20 | tf_op jit(solution)/shard_map/ppermute | solution.py:362
  43.9 7.5 %collective-permute-start.4 = (f32[536,128]{1,0:T(8,128)S(1)}, f32[536,128]{1,0:T(8,128)}, u32[]{:S(2)}, u32[]{:S(2)}) collective-permute-start(f32[536,128]{1,0:T(8,128)S(1)} %get-tuple-element.106), channel_id=1, source_target_pairs={{0,2},{1,3},{2,0},{3,1},{4,6},{5,7},{6,4},{7,5},{8,10},{9,11},{10,... | collective-permute-start | bytes 823304 | tf_op jit(solution)/shard_map/ppermute | solution.py:359
  51.4 0.7 copy-start.22
  51.5 1.0 copy-start.20
  81.0 21.9 %collective-permute-start.9 = (f32[16,80,256]{2,1,0:T(8,128)}, f32[16,80,256]{2,1,0:T(8,128)S(1)}, u32[]{:S(2)}, u32[]{:S(2)}) collective-permute-start(f32[16,80,256]{2,1,0:T(8,128)} %get-tuple-element.39), channel_id=1, source_target_pairs={{0,1},{1,0},{2,3},{3,2},{4,5},{5,4},{6,7},{7,6},{8,9},{9,8},{10,11... | collective-permute-start | bytes 3932168 | tf_op jit(solution)/shard_map/ppermute | solution.py:359
  90.2 12.7 %copy-start.3 = (f32[16,80,256]{2,1,0:T(8,128)S(1)}, f32[16,80,256]{2,1,0:T(8,128)}, u32[]{:S(2)}) copy-start(f32[16,80,256]{2,1,0:T(8,128)} %get-tuple-element.38) | copy-start | bytes 3932164
  102.4 19.1 %collective-permute-start.30 = (f32[2,512,256]{2,1,0:T(8,128)}, f32[2,512,256]{2,1,0:T(8,128)S(1)}, u32[]{:S(2)}, u32[]{:S(2)}) collective-permute-start(f32[2,512,256]{2,1,0:T(8,128)} %get-tuple-element.57), channel_id=1, source_target_pairs={{0,1},{1,0},{2,3},{3,2},{4,5},{5,4},{6,7},{7,6},{8,9},{9,8},{10,11... | collective-permute-start | bytes 3145736 | tf_op jit(solution)/shard_map/ppermute | solution.py:359
  102.9 1.2 copy-start.21
  103.0 18.4 %copy-start.5 = (f32[2,512,256]{2,1,0:T(8,128)S(1)}, f32[2,512,256]{2,1,0:T(8,128)}, u32[]{:S(2)}) copy-start(f32[2,512,256]{2,1,0:T(8,128)} %get-tuple-element.56) | copy-start | bytes 3145732
  103.1 16.7 %collective-permute-start.10 = (f32[8,80,256]{2,1,0:T(8,128)S(1)}, f32[8,80,256]{2,1,0:T(8,128)S(1)}, u32[]{:S(2)}, u32[]{:S(2)}) collective-permute-start(f32[8,80,256]{2,1,0:T(8,128)S(1)} %get-tuple-element.79), channel_id=1, source_target_pairs={{0,4},{4,0},{8,12},{12,8},{16,20},{20,16},{24,28},{28,24},{1,5},{5... | collective-permute-start | bytes 1966088 | tf_op jit(solution)/shard_map/ppermute | solution.py:362
  104.1 28.2 %collective-permute-start.22 = (f32[2,512,256]{2,1,0:T(8,128)S(1)}, f32[2,512,256]{2,1,0:T(8,128)S(1)}, u32[]{:S(2)}, u32[]{:S(2)}) collective-permute-start(f32[2,512,256]{2,1,0:T(8,128)S(1)} %copy-done.21), channel_id=1, source_target_pairs={{0,1},{1,0},{2,3},{3,2},{4,5},{5,4},{6,7},{7,6},{8,9},{9,8},{10,11... | collective-permute-start | bytes 3145736 | tf_op jit(solution)/shard_map/ppermute | solution.py:359
  119.9 10.7 %collective-permute-start.11 = (f32[4,80,256]{2,1,0:T(8,128)S(1)}, f32[4,80,256]{2,1,0:T(8,128)S(1)}, u32[]{:S(2)}, u32[]{:S(2)}) collective-permute-start(f32[4,80,256]{2,1,0:T(8,128)S(1)} %get-tuple-element.85), channel_id=1, source_target_pairs={{0,2},{1,3},{2,0},{3,1},{4,6},{5,7},{6,4},{7,5},{8,10},{9,11},{10,... | collective-permute-start | bytes 983048 | tf_op jit(solution)/shard_map/ppermute | solution.py:359
  121.5 10.8 %copy-start.4 = (f32[2,512,256]{2,1,0:T(8,128)S(1)}, f32[2,512,256]{2,1,0:T(8,128)}, u32[]{:S(2)}) copy-start(f32[2,512,256]{2,1,0:T(8,128)} %get-tuple-element.54) | copy-start | bytes 3145732
  121.6 20.2 %collective-permute-start.31 = (f32[512,256]{1,0:T(8,128)S(1)}, f32[512,256]{1,0:T(8,128)S(1)}, u32[]{:S(2)}, u32[]{:S(2)}) collective-permute-start(f32[512,256]{1,0:T(8,128)S(1)} %get-tuple-element.81), channel_id=1, source_target_pairs={{0,2},{1,3},{2,0},{3,1},{4,6},{5,7},{6,4},{7,5},{8,10},{9,11},{10,... | collective-permute-start | bytes 1572872 | tf_op jit(solution)/shard_map/ppermute | solution.py:359
  130.7 6.3 %collective-permute-start.12 = (f32[2,80,256]{2,1,0:T(8,128)S(1)}, f32[2,80,256]{2,1,0:T(8,128)S(1)}, u32[]{:S(2)}, u32[]{:S(2)}) collective-permute-start(f32[2,80,256]{2,1,0:T(8,128)S(1)} %get-tuple-element.95), channel_id=1, source_target_pairs={{0,8},{4,12},{8,0},{12,4},{16,24},{20,28},{24,16},{28,20},{1,9},{5... | collective-permute-start | bytes 491528 | tf_op jit(solution)/shard_map/ppermute | solution.py:362
  132.4 18.8 %collective-permute-start.23 = (f32[512,256]{1,0:T(8,128)S(1)}, f32[512,256]{1,0:T(8,128)S(1)}, u32[]{:S(2)}, u32[]{:S(2)}) collective-permute-start(f32[512,256]{1,0:T(8,128)S(1)} %get-tuple-element.83), channel_id=1, source_target_pairs={{0,2},{1,3},{2,0},{3,1},{4,6},{5,7},{6,4},{7,5},{8,10},{9,11},{10,... | collective-permute-start | bytes 1572872 | tf_op jit(solution)/shard_map/ppermute | solution.py:359
  136.9 7.4 %collective-permute-start.13 = (f32[1,80,256]{2,1,0:T(8,128)S(1)}, f32[1,80,256]{2,1,0:T(8,128)S(1)}, u32[]{:S(2)}, u32[]{:S(2)}) collective-permute-start(f32[1,80,256]{2,1,0:T(8,128)S(1)} %slice_add_fusion.18), channel_id=1, source_target_pairs={{0,16},{4,20},{8,24},{12,28},{16,0},{20,4},{24,8},{28,12},{1,17},{... | collective-permute-start | bytes 245768 | tf_op jit(solution)/shard_map/ppermute | solution.py:362
  141.9 17.0 %collective-permute-start.32 = (f32[4,64,256]{2,1,0:T(8,128)S(1)}, f32[4,64,256]{2,1,0:T(8,128)S(1)}, u32[]{:S(2)}, u32[]{:S(2)}) collective-permute-start(f32[4,64,256]{2,1,0:T(8,128)S(1)} %bitcast.49), channel_id=1, source_target_pairs={{0,4},{4,0},{8,12},{12,8},{16,20},{20,16},{24,28},{28,24},{1,5},{5... | collective-permute-start | bytes 786440 | tf_op jit(solution)/shard_map/ppermute | solution.py:362
  144.3 7.0 %collective-permute-start.14 = (f32[1,80,256]{2,1,0:T(8,128)S(1)}, f32[1,80,256]{2,1,0:T(8,128)S(1)}, u32[]{:S(2)}, u32[]{:S(2)}) collective-permute-start(f32[1,80,256]{2,1,0:T(8,128)S(1)} %get-tuple-element.77), channel_id=1, source_target_pairs={{0,16},{4,20},{8,24},{12,28},{16,0},{20,4},{24,8},{28,12},{1,17},{... | collective-permute-start | bytes 245768 | tf_op jit(solution)/shard_map/ppermute | solution.py:362
  151.3 5.4 %collective-permute-start.15 = (f32[2,80,256]{2,1,0:T(8,128)S(1)}, f32[2,80,256]{2,1,0:T(8,128)S(1)}, u32[]{:S(2)}, u32[]{:S(2)}) collective-permute-start(f32[2,80,256]{2,1,0:T(8,128)S(1)} %pad_maximum_fusion.8), channel_id=1, source_target_pairs={{0,8},{4,12},{8,0},{12,4},{16,24},{20,28},{24,16},{28,20},{1,9},{5... | collective-permute-start | bytes 491528 | tf_op jit(solution)/shard_map/ppermute | solution.py:362
  156.8 7.1 %collective-permute-start.16 = (f32[4,80,256]{2,1,0:T(8,128)S(1)}, f32[4,80,256]{2,1,0:T(8,128)S(1)}, u32[]{:S(2)}, u32[]{:S(2)}) collective-permute-start(f32[4,80,256]{2,1,0:T(8,128)S(1)} %pad_maximum_fusion.5), channel_id=1, source_target_pairs={{0,2},{1,3},{2,0},{3,1},{4,6},{5,7},{6,4},{7,5},{8,10},{9,11},{10,... | collective-permute-start | bytes 983048 | tf_op jit(solution)/shard_map/ppermute | solution.py:359
  158.4 8.7 %collective-permute-start.24 = (f32[4,64,256]{2,1,0:T(8,128)S(1)}, f32[4,64,256]{2,1,0:T(8,128)S(1)}, u32[]{:S(2)}, u32[]{:S(2)}) collective-permute-start(f32[4,64,256]{2,1,0:T(8,128)S(1)} %bitcast.50), channel_id=1, source_target_pairs={{0,4},{4,0},{8,12},{12,8},{16,20},{20,16},{24,28},{28,24},{1,5},{5... | collective-permute-start | bytes 786440 | tf_op jit(solution)/shard_map/ppermute | solution.py:362
  159.0 9.8 %collective-permute-start.33 = (f32[2,64,256]{2,1,0:T(8,128)S(1)}, f32[2,64,256]{2,1,0:T(8,128)S(1)}, u32[]{:S(2)}, u32[]{:S(2)}) collective-permute-start(f32[2,64,256]{2,1,0:T(8,128)S(1)} %get-tuple-element.97), channel_id=1, source_target_pairs={{0,8},{4,12},{8,0},{12,4},{16,24},{20,28},{24,16},{28,20},{1,9},{5... | collective-permute-start | bytes 393224 | tf_op jit(solution)/shard_map/ppermute | solution.py:362
  163.9 14.9 %collective-permute-start.17 = (f32[8,80,256]{2,1,0:T(8,128)S(1)}, f32[8,80,256]{2,1,0:T(8,128)S(1)}, u32[]{:S(2)}, u32[]{:S(2)}) collective-permute-start(f32[8,80,256]{2,1,0:T(8,128)S(1)} %pad_maximum_fusion), channel_id=1, source_target_pairs={{0,4},{4,0},{8,12},{12,8},{16,20},{20,16},{24,28},{28,24},{1,5},{5... | collective-permute-start | bytes 1966088 | tf_op jit(solution)/shard_map/ppermute | solution.py:362
  167.1 11.9 %collective-permute-start.25 = (f32[2,64,256]{2,1,0:T(8,128)S(1)}, f32[2,64,256]{2,1,0:T(8,128)S(1)}, u32[]{:S(2)}, u32[]{:S(2)}) collective-permute-start(f32[2,64,256]{2,1,0:T(8,128)S(1)} %get-tuple-element.101), channel_id=1, source_target_pairs={{0,8},{4,12},{8,0},{12,4},{16,24},{20,28},{24,16},{28,20},{1,9},{5... | collective-permute-start | bytes 393224 | tf_op jit(solution)/shard_map/ppermute | solution.py:362
  168.8 12.9 %collective-permute-start.34 = (f32[1,64,256]{2,1,0:T(8,128)S(1)}, f32[1,64,256]{2,1,0:T(8,128)S(1)}, u32[]{:S(2)}, u32[]{:S(2)}) collective-permute-start(f32[1,64,256]{2,1,0:T(8,128)S(1)} %slice_add_fusion.20), channel_id=1, source_target_pairs={{0,16},{4,20},{8,24},{12,28},{16,0},{20,4},{24,8},{28,12},{1,17},{... | collective-permute-start | bytes 196616 | tf_op jit(solution)/shard_map/ppermute | solution.py:362
  171.5 20.0 %copy-start.25 = (f32[512,128]{1,0:T(8,128)S(1)}, f32[512,128]{1,0:T(8,128)}, u32[]{:S(2)}) copy-start(f32[512,128]{1,0:T(8,128)} %get-tuple-element.49) | copy-start | bytes 786436
  171.5 22.3 %copy-start.24 = (f32[512,128]{1,0:T(8,128)S(1)}, f32[512,128]{1,0:T(8,128)}, u32[]{:S(2)}) copy-start(f32[512,128]{1,0:T(8,128)} %get-tuple-element.50) | copy-start | bytes 786436
  171.5 23.6 %copy-start.23 = (f32[512,128]{1,0:T(8,128)S(1)}, f32[512,128]{1,0:T(8,128)}, u32[]{:S(2)}) copy-start(f32[512,128]{1,0:T(8,128)} %get-tuple-element.51) | copy-start | bytes 786436
  178.9 29.1 %copy-start.1 = (f32[16,80,256]{2,1,0:T(8,128)}, f32[16,80,256]{2,1,0:T(8,128)S(1)}, u32[]{:S(2)}) copy-start(f32[16,80,256]{2,1,0:T(8,128)S(1)} %constant_dynamic-update-slice_fusion.s0) | copy-start | bytes 3932164
  178.9 35.4 %collective-permute-start.18 = (f32[16,80,256]{2,1,0:T(8,128)S(1)}, f32[16,80,256]{2,1,0:T(8,128)S(1)}, u32[]{:S(2)}, u32[]{:S(2)}) collective-permute-start(f32[16,80,256]{2,1,0:T(8,128)S(1)} %constant_dynamic-update-slice_fusion.s0), channel_id=1, source_target_pairs={{0,1},{1,0},{2,3},{3,2},{4,5},{5,4},{6,7},{7,6},{8,9},{9,8},{10,11... | collective-permute-start | bytes 3932168 | tf_op jit(solution)/shard_map/ppermute | solution.py:359
  179.0 7.1 %collective-permute-start.26 = (f32[1,64,256]{2,1,0:T(8,128)S(1)}, f32[1,64,256]{2,1,0:T(8,128)S(1)}, u32[]{:S(2)}, u32[]{:S(2)}) collective-permute-start(f32[1,64,256]{2,1,0:T(8,128)S(1)} %slice_add_fusion.22), channel_id=1, source_target_pairs={{0,16},{4,20},{8,24},{12,28},{16,0},{20,4},{24,8},{28,12},{1,17},{... | collective-permute-start | bytes 196616 | tf_op jit(solution)/shard_map/ppermute | solution.py:362
  181.7 7.3 %collective-permute-start.35 = (f32[1,64,256]{2,1,0:T(8,128)S(1)}, f32[1,64,256]{2,1,0:T(8,128)S(1)}, u32[]{:S(2)}, u32[]{:S(2)}) collective-permute-start(f32[1,64,256]{2,1,0:T(8,128)S(1)} %fusion.3), channel_id=1, source_target_pairs={{0,16},{4,20},{8,24},{12,28},{16,0},{20,4},{24,8},{28,12},{1,17},{... | collective-permute-start | bytes 196616 | tf_op jit(solution)/shard_map/ppermute | solution.py:362
  186.1 5.4 %collective-permute-start.27 = (f32[1,64,256]{2,1,0:T(8,128)S(1)}, f32[1,64,256]{2,1,0:T(8,128)S(1)}, u32[]{:S(2)}, u32[]{:S(2)}) collective-permute-start(f32[1,64,256]{2,1,0:T(8,128)S(1)} %fusion.4), channel_id=1, source_target_pairs={{0,16},{4,20},{8,24},{12,28},{16,0},{20,4},{24,8},{28,12},{1,17},{... | collective-permute-start | bytes 196616 | tf_op jit(solution)/shard_map/ppermute | solution.py:362
  189.0 6.1 %collective-permute-start.36 = (f32[2,64,256]{2,1,0:T(8,128)S(1)}, f32[2,64,256]{2,1,0:T(8,128)S(1)}, u32[]{:S(2)}, u32[]{:S(2)}) collective-permute-start(f32[2,64,256]{2,1,0:T(8,128)S(1)} %pad_maximum_fusion.10), channel_id=1, source_target_pairs={{0,8},{4,12},{8,0},{12,4},{16,24},{20,28},{24,16},{28,20},{1,9},{5... | collective-permute-start | bytes 393224 | tf_op jit(solution)/shard_map/ppermute | solution.py:362
  191.5 6.8 %collective-permute-start.19 = (f32[512,128]{1,0:T(8,128)S(1)}, f32[512,128]{1,0:T(8,128)S(1)}, u32[]{:S(2)}, u32[]{:S(2)}) collective-permute-start(f32[512,128]{1,0:T(8,128)S(1)} %copy-done.25), channel_id=1, source_target_pairs={{0,1},{1,0},{2,3},{3,2},{4,5},{5,4},{6,7},{7,6},{8,9},{9,8},{10,11... | collective-permute-start | bytes 786440 | tf_op jit(solution)/shard_map/ppermute | solution.py:359
  191.5 6.2 %collective-permute-start.28 = (f32[2,64,256]{2,1,0:T(8,128)S(1)}, f32[2,64,256]{2,1,0:T(8,128)S(1)}, u32[]{:S(2)}, u32[]{:S(2)}) collective-permute-start(f32[2,64,256]{2,1,0:T(8,128)S(1)} %pad_maximum_fusion.9), channel_id=1, source_target_pairs={{0,8},{4,12},{8,0},{12,4},{16,24},{20,28},{24,16},{28,20},{1,9},{5... | collective-permute-start | bytes 393224 | tf_op jit(solution)/shard_map/ppermute | solution.py:362
  193.8 9.2 %collective-permute-start.20 = (f32[512,128]{1,0:T(8,128)S(1)}, f32[512,128]{1,0:T(8,128)S(1)}, u32[]{:S(2)}, u32[]{:S(2)}) collective-permute-start(f32[512,128]{1,0:T(8,128)S(1)} %copy-done.24), channel_id=1, source_target_pairs={{0,2},{1,3},{2,0},{3,1},{4,6},{5,7},{6,4},{7,5},{8,10},{9,11},{10,... | collective-permute-start | bytes 786440 | tf_op jit(solution)/shard_map/ppermute | solution.py:359
  195.1 10.0 %collective-permute-start.21 = (f32[512,128]{1,0:T(8,128)S(1)}, f32[512,128]{1,0:T(8,128)S(1)}, u32[]{:S(2)}, u32[]{:S(2)}) collective-permute-start(f32[512,128]{1,0:T(8,128)S(1)} %copy-done.23), channel_id=1, source_target_pairs={{0,3},{1,2},{2,1},{3,0},{4,7},{5,6},{6,5},{7,4},{8,11},{9,10},{10,... | collective-permute-start | bytes 786440 | tf_op jit(solution)/shard_map/ppermute | solution.py:359
  195.1 12.9 %copy-start.6 = (f32[4,64,256]{2,1,0:T(8,128)}, f32[4,64,256]{2,1,0:T(8,128)S(1)}, u32[]{:S(2)}) copy-start(f32[4,64,256]{2,1,0:T(8,128)S(1)} %pad_maximum_fusion.7.b0) | copy-start | bytes 786436
  197.7 10.2 %collective-permute-start.37 = (f32[4,64,256]{2,1,0:T(8,128)S(1)}, f32[4,64,256]{2,1,0:T(8,128)S(1)}, u32[]{:S(2)}, u32[]{:S(2)}) collective-permute-start(f32[4,64,256]{2,1,0:T(8,128)S(1)} %pad_maximum_fusion.7.b0), channel_id=1, source_target_pairs={{0,4},{4,0},{8,12},{12,8},{16,20},{20,16},{24,28},{28,24},{1,5},{5... | collective-permute-start | bytes 786440 | tf_op jit(solution)/shard_map/ppermute | solution.py:362
  198.3 13.0 %copy-start.7 = (f32[4,64,256]{2,1,0:T(8,128)}, f32[4,64,256]{2,1,0:T(8,128)S(1)}, u32[]{:S(2)}) copy-start(f32[4,64,256]{2,1,0:T(8,128)S(1)} %pad_maximum_fusion.6.a0) | copy-start | bytes 786436
  198.3 6.7 %copy-start.8 = (f32[512,128]{1,0:T(8,128)}, f32[512,128]{1,0:T(8,128)S(1)}, u32[]{:S(2)}) copy-start(f32[512,128]{1,0:T(8,128)S(1)} %collective-permute-done.19.g1) | copy-start | bytes 786436
  198.3 13.0 %collective-permute-start.29 = (f32[4,64,256]{2,1,0:T(8,128)S(1)}, f32[4,64,256]{2,1,0:T(8,128)S(1)}, u32[]{:S(2)}, u32[]{:S(2)}) collective-permute-start(f32[4,64,256]{2,1,0:T(8,128)S(1)} %pad_maximum_fusion.6.a0), channel_id=1, source_target_pairs={{0,4},{4,0},{8,12},{12,8},{16,20},{20,16},{24,28},{28,24},{1,5},{5... | collective-permute-start | bytes 786440 | tf_op jit(solution)/shard_map/ppermute | solution.py:362
  203.0 2.0 copy-start.9
  205.0 0.7 copy-start.10
  208.0 3.3 %copy-start.11 = (f32[4,64,256]{2,1,0:T(8,128)}, f32[4,64,256]{2,1,0:T(8,128)S(1)}, u32[]{:S(2)}) copy-start(f32[4,64,256]{2,1,0:T(8,128)S(1)} %collective-permute-done.37.b1) | copy-start | bytes 786436
  211.3 0.7 copy-start.12
  214.3 1.1 copy-start.2

commit v2 on v1

v2 whole, which is shorter than its diff:
```python
import functools

import jax
import jax.numpy as jnp
from jax import lax
from jax.experimental import pallas as pl
from jax.experimental.pallas import tpu as pltpu
from jax.sharding import PartitionSpec as P

F32 = jnp.float32
BF16 = jnp.bfloat16
ROOT_HALF = 0.7071067811865476
DENSITY = 0.3989422804014327
VMEM = pltpu.VMEM
PARAMS = pltpu.CompilerParams(vmem_limit_bytes=58 * 1024 * 1024)
NN, TN, NT = (1, 0), (0, 0), (1, 1)


def split(x):
    high = x.astype(BF16)
    return high, (x - high.astype(F32)).astype(BF16)


def one_dot(a, b, dims):
    return lax.dot_general(a, b, (((dims[0],), (dims[1],)), ((), ())), preferred_element_type=F32)


def dot3(a, b, dims):
    return one_dot(a[0], b[0], dims) + (one_dot(a[0], b[1], dims) + one_dot(a[1], b[0], dims))


def gelu_parts(v):
    cdf = 0.5 + 0.5 * lax.erf(v * ROOT_HALF)
    return v * cdf, cdf + v * (DENSITY * jnp.exp(-0.5 * v * v))


def pick(matrix, index):
    lane = lax.broadcasted_iota(jnp.int32, matrix.shape, 1)
    return jnp.sum(jnp.where(lane == index, matrix, 0.0), axis=1, keepdims=True)


def middle_kernel(
    place,
    out_bias,
    x0,
    x1,
    x2,
    x3,
    gate_rows,
    near0,
    near1,
    fa0,
    fa1,
    fa2,
    fa3,
    fb0,
    fb1,
    fb2,
    fb3,
    domain,
    labels,
    gate_bias,
    b_first,
    w_second,
    b_second,
    t_first,
    t_bias,
    t_out,
    xt_high_out,
    xt_low_out,
    gf_high_out,
    gf_low_out,
    w_high_out,
    w_low_out,
    gate_all,
    glog_out,
    s_keep,
    s_send,
    w_in,
    w2_in,
    xt_high,
    xt_low,
    gf_high,
    gf_low,
    w_high,
    w_low,
    hid_high,
    hid_low,
    slope,
    e_out,
    gates,
    mix,
    gmix,
    ggate,
    b1_cols,
    b2_cols,
    summed,
    rest,
    sems,
):
    experts = w_second.shape[0]
    tasks, width, tower = t_first.shape
    hidden = w_second.shape[1]
    rows = domain.shape[1]
    domains = gate_bias.shape[0]
    cols = near0.shape[1]
    start, count, me, field, corner = place[0], place[1], place[2], place[3], place[4]
    units = tasks * experts
    quarter = experts // 4
    order = [(r ^ corner) * quarter + i for r in range(4) for i in range(quarter)]

    loads = []
    for n, e in enumerate(order):
        far_a, far_b = ((fa0, fb0), (fa1, fb1), (fa2, fb2), (fa3, fb3))[n // quarter]
        sources = (near0.at[e], near1.at[e], far_a.at[n % quarter], far_b.at[n % quarter])
        for k, source in enumerate(sources):
            target = w_in.at[n, k * cols : (k + 1) * cols]
            loads.append(pltpu.make_async_copy(source, target, sems.at[5 * n + k]))
        loads.append(pltpu.make_async_copy(w_second.at[e], w2_in.at[n], sems.at[5 * n + 4]))
    for load in loads:
        load.start()

    for k, ref in enumerate((x0, x1, x2, x3)):
        block = slice(k * cols, (k + 1) * cols)
        high, low = split(ref[0:rows, :].T)
        xt_high[block, :] = high
        xt_low[block, :] = low
        gate_all[:, block] = gate_rows[...] if k == 0 else ref[rows : rows + units, :]
    hot = lax.broadcasted_iota(jnp.int32, (domains, rows), 0) == domain[...]
    onehot = jnp.where(hot, 1.0, 0.0).astype(BF16)
    bias_high, bias_low = split(gate_bias[...])
    logits = dot3(split(gate_all[...]), (xt_high[...], xt_low[...]), NN)
    logits = logits + (one_dot(bias_high, onehot, TN) + one_dot(bias_low, onehot, TN))
    logits = logits.reshape(tasks, experts, rows)
    raised = jnp.exp(logits - jnp.max(logits, axis=1, keepdims=True))
    soft = raised / jnp.sum(raised, axis=1, keepdims=True)
    gates[...] = soft.reshape(units, rows)
    mix[...] = jnp.zeros_like(mix)
    b1_cols[...] = jnp.zeros_like(b1_cols)
    b2_cols[...] = jnp.zeros_like(b2_cols)
    b1_in = b_first[...].T
    b2_in = b_second[...].T
    rest[...] = jnp.zeros_like(rest)
    for load in loads:
        load.wait()

    def first_layer(n):
        weight = split(w_in[n])
        w_high[n], w_low[n] = weight
        return dot3(weight, (xt_high[...], xt_low[...]), TN)

    pre = first_layer(0)
    value = None
    for n in range(experts + 1):
        following = first_layer(n + 1) if n + 1 < experts else None
        if n < experts:
            raw, steep = gelu_parts(pre + pick(b1_in, order[n]))
            slope[n] = steep
        if n > 0:
            e = order[n - 1]
            result = dot3(split(w2_in[n - 1]), value, TN) + pick(b2_in, e)
            e_out[n - 1] = result
            for k in range(tasks):
                mix[k] += gates[pl.ds(k * experts + e, 1), :] * result
        if n < experts:
            value = split(raw)
            hid_high[n], hid_low[n] = value
        pre = following

    stores = [
        pltpu.make_async_copy(xt_high, xt_high_out, sems.at[0]),
        pltpu.make_async_copy(xt_low, xt_low_out, sems.at[1]),
    ]
    for n, e in enumerate(order):
        stores.append(pltpu.make_async_copy(w_high.at[n], w_high_out.at[e], sems.at[2 + 2 * n]))
        stores.append(pltpu.make_async_copy(w_low.at[n], w_low_out.at[e], sems.at[3 + 2 * n]))
    for store in stores:
        store.start()

    position = start + lax.broadcasted_iota(jnp.int32, (1, rows), 1)
    live = jnp.where(position < count, 1.0, 0.0)
    loss = jnp.zeros((1, 1), F32)
    ones = jnp.ones((8, rows), BF16)
    row_of = lax.broadcasted_iota(jnp.int32, (8, rows), 0)
    lane_of = lax.broadcasted_iota(jnp.int32, (1, tower), 1)
    scalars = jnp.where(lane_of == tasks + 1, jnp.sum(live, axis=1, keepdims=True), 0.0)
    eye = lax.broadcasted_iota(jnp.int32, (tasks, tower), 0) == lax.broadcasted_iota(jnp.int32, (tasks, tower), 1)
    eye = jnp.where(eye, 1.0, 0.0)
    tb_in = lax.dot_general(t_bias[...], eye, (((0,), (0,)), ((), ())), precision=lax.Precision.HIGHEST)
    to_in = lax.dot_general(t_out[...], eye, (((0,), (0,)), ((), ())), precision=lax.Precision.HIGHEST)
    misc = rest.shape[0] - 8
    for k in range(tasks):
        mixed = split(mix[k])
        weight = split(t_first[k])
        pre = dot3(weight, mixed, TN) + tb_in[:, k : k + 1]
        value, steep = gelu_parts(pre)
        out_column = to_in[:, k : k + 1]
        score = jnp.sum(value * out_column, axis=0, keepdims=True) + out_bias[k]
        target = labels[k : k + 1, :].astype(F32)
        per_item = jnp.maximum(score, 0.0) + jnp.log1p(jnp.exp(-jnp.abs(score))) - target * score
        loss = loss + jnp.sum(per_item * live, axis=1, keepdims=True)
        gscore = live * (jax.nn.sigmoid(score) - target)
        gpre = split(gscore * out_column * steep)
        gweight = dot3(mixed, gpre, NT)
        gbias = one_dot(ones, gpre[0], NT) + one_dot(ones, gpre[1], NT)
        spread = split(jnp.where(row_of == 0, gscore, 0.0))
        gout = dot3(spread, split(value), NT)
        if k < 2:
            rest[0:width, k * tower : (k + 1) * tower] = gweight
        else:
            rest[width : width + tower, 0:tower] = gweight[0:tower]
            rest[width : width + tower, tower:] = gweight[tower:]
        at = k
        rest[misc + at // 2 : misc + at // 2 + 1, (at % 2) * tower : (at % 2 + 1) * tower] = gbias[0:1]
        at = tasks + k
        rest[misc + at // 2 : misc + at // 2 + 1, (at % 2) * tower : (at % 2 + 1) * tower] = gout[0:1]
        scalars = scalars + jnp.where(lane_of == k, jnp.sum(gscore, axis=1, keepdims=True), 0.0)
        gmix[k] = dot3(weight, gpre, NN)
    scalars = scalars + jnp.where(lane_of == tasks, loss, 0.0)
    rest[misc + tasks : misc + tasks + 1, 0:tower] = scalars

    grads = []
    for n, e in enumerate(order):
        result = e_out[n]
        total = None
        for k in range(tasks):
            down = gmix[k]
            ggate[pl.ds(k * experts + e, 1), :] = jnp.sum(down * result, axis=0, keepdims=True)
            part = gates[pl.ds(k * experts + e, 1), :] * down
            total = part if total is None else total + part
        lane = lax.broadcasted_iota(jnp.int32, b1_cols.shape, 1)
        b2_cols[...] += jnp.where(lane == e, jnp.sum(total, axis=1, keepdims=True), 0.0)
        total = split(total)
        gweight = dot3((hid_high[n], hid_low[n]), total, NT)
        piece = hidden // 4
        for i in range(4):
            slot = (4 * e + i) ^ me
            summed[slot, 0:piece, :] = gweight[i * piece : (i + 1) * piece]
        gfirst = dot3(split(w2_in[n]), total, NN) * slope[n]
        b1_cols[...] += jnp.where(lane == e, jnp.sum(gfirst, axis=1, keepdims=True), 0.0)
        high, low = split(gfirst)
        gf_high[n] = high
        gf_low[n] = low
        grads.append(pltpu.make_async_copy(gf_high.at[n], gf_high_out.at[e], sems.at[20 + 2 * n]))
        grads.append(pltpu.make_async_copy(gf_low.at[n], gf_low_out.at[e], sems.at[21 + 2 * n]))
        if n % 4 == 3:
            for copy in grads[-8:]:
                copy.start()

    soft = gates[...].reshape(tasks, experts, rows)
    gsoft = ggate[...].reshape(tasks, experts, rows)
    glog = soft * (gsoft - jnp.sum(soft * gsoft, axis=1, keepdims=True))
    glog = glog.reshape(units, rows)
    glog_out[...] = glog
    glog_parts = split(glog)
    ggw = dot3(glog_parts, (xt_high[...], xt_low[...]), NT)
    base = width + tower
    for k in range(4):
        at = pl.multiple_of(base + (field ^ k) * units, 8)
        rest[pl.ds(at, units), 0:tower] = ggw[:, k * cols : (k + 1) * cols]
    b1_rows = b1_cols[...].T
    b2_rows = b2_cols[...].T
    rest[base : base + 8, tower:] = b1_rows[0:8, 0:tower]
    rest[base + 8 : base + 16, tower:] = b1_rows[0:8, tower:]
    base = base + 4 * units
    rest[base : base + 8, :] = b2_rows[0:8]
    base = base + 8
    rest[base : base + domains, 0:units] = one_dot(onehot, glog_parts[0], NT) + one_dot(onehot, glog_parts[1], NT)
    tail = rest.shape[0] // 32
    for p in range(32):
        slot = p ^ me
        summed[slot, hidden // 4 :, :] = rest[p * tail : (p + 1) * tail, :]
    last = [
        pltpu.make_async_copy(summed.at[16:32], s_send, sems.at[36]),
        pltpu.make_async_copy(summed.at[0:16], s_keep, sems.at[37]),
    ]
    for copy in last:
        copy.start()
    for copy in stores + grads + last:
        copy.wait()


def first_kernel(
    place, xt_high, xt_low, gate_all, glog, gf_high, gf_low, w_high, w_low, keep, send, g0, g1, g2, g3, total
):
    step = pl.program_id(0)
    cols = keep.shape[2]
    parts = (gf_high[0], gf_low[0])
    gweight = dot3((xt_high[...], xt_low[...]), parts, NT)
    slot = step ^ place[0]
    for k in range(4):
        target = (keep, send)[k % 2]
        target[k // 2, slot] = gweight[k * cols : (k + 1) * cols]

    @pl.when(step == 0)
    def _():
        total[...] = dot3(split(gate_all[...]), split(glog[...]), TN)

    total[...] += dot3((w_high[0], w_low[0]), parts, NN)

    @pl.when(step == pl.num_programs(0) - 1)
    def _():
        for k, ref in enumerate((g0, g1, g2, g3)):
            ref[...] = total[k * cols : (k + 1) * cols, :].T


def finish_second_kernel(
    place, a0, a1, a2, a3, b0, b1, b2, b3, gw2, gtf, ggw, ggb, gb1, gb2, gtb, gto, gtob, loss, factor_out, rest
):
    me, field = place[0], place[1]
    hidden = gw2.shape[1]
    piece = hidden // 4
    tasks, width, tower = gtf.shape
    experts = ggw.shape[1]
    units = tasks * experts
    domains = ggb.shape[0]
    tail = rest.shape[0] // 32
    held = (a0, a1, a2, a3, b0, b1, b2, b3)
    for s, ref in enumerate(held):
        for z in range(4):
            p = (s * 4 + z) ^ me
            rest[pl.ds(pl.multiple_of(p * tail, 8), tail), :] = ref[z, piece:]
    misc = rest.shape[0] - 8
    factor = 1.0 / rest[misc + tasks : misc + tasks + 1, tasks + 1 : tasks + 2]
    factor_out[...] = factor
    for s, ref in enumerate(held):
        for z in range(4):
            p = (s * 4 + z) ^ me
            gw2[p // 4, pl.ds(pl.multiple_of((p % 4) * piece, 8), piece), :] = ref[z, 0:piece] * factor
    rest[...] = rest[...] * factor
    gtf[0] = rest[0:width, 0:tower]
    gtf[1] = rest[0:width, tower:]
    gtf[2, 0:tower] = rest[width : width + tower, 0:tower]
    gtf[2, tower:] = rest[width : width + tower, tower:]
    base = width + tower
    mine = rest[pl.ds(pl.multiple_of(base + field * units, 8), units), 0:tower]
    for k in range(tasks):
        ggw[k] = mine[k * experts : (k + 1) * experts]
    gb1[:, 0:tower] = rest[base : base + 8, tower:]
    gb1[:, tower:] = rest[base + 8 : base + 16, tower:]
    base = base + 4 * units
    gb2[...] = rest[base : base + 8, :]
    base = base + 8
    ggb[...] = rest[base : base + domains, 0:units]
    for k in range(tasks):
        at = k
        gtb[k : k + 1] = rest[misc + at // 2 : misc + at // 2 + 1, (at % 2) * tower : (at % 2 + 1) * tower]
        at = tasks + k
        gto[k : k + 1] = rest[misc + at // 2 : misc + at // 2 + 1, (at % 2) * tower : (at % 2 + 1) * tower]
    gtob[...] = rest[misc + tasks : misc + tasks + 1, 0:tasks]
    loss[...] = rest[misc + tasks : misc + tasks + 1, tasks : tasks + 1]


def finish_first_kernel(place, factor, a0, a1, a2, a3, b, out):
    for z, ref in enumerate((a0, a1, a2, a3)):
        out[z ^ place[0]] = ref[...] * factor[...]
        out[(4 + z) ^ place[0]] = b[z] * factor[...]


def finish_inputs_kernel(place, factor, g0, g1, g2, g3, out):
    field = place[0]
    rows = g0.shape[0]
    for k, ref in enumerate((g0, g1, g2, g3)):
        out[pl.ds(pl.multiple_of((field ^ k) * rows, 8), rows), :] = ref[...] * factor[...]


def whole():
    return pl.BlockSpec(memory_space=VMEM)


def anywhere():
    return pl.BlockSpec(memory_space=pl.ANY)


def scalars():
    return pl.BlockSpec(memory_space=pltpu.SMEM)


def like(shape, dtype=F32):
    return jax.ShapeDtypeStruct(shape, dtype)


def after(value, *others):
    return lax.optimization_barrier((value, others))[0]


def per_device(
    n_dp,
    examples,
    domain,
    labels,
    row_counts,
    gate_weight,
    gate_bias,
    w_first,
    b_first,
    w_second,
    b_second,
    tower_first,
    tower_bias,
    tower_out,
    tower_out_bias,
):
    all_rows, cols = examples.shape
    rows = all_rows // 4
    experts, _, hidden = w_first.shape
    tasks = gate_weight.shape[0]
    width = w_second.shape[2]
    tower = tower_first.shape[2]
    domains = gate_bias.shape[0]
    units = tasks * experts
    field = lax.axis_index("field").astype(jnp.int32)
    group = lax.axis_index("dp").astype(jnp.int32)

    def move(value, dp_mask, field_mask):
        pairs = []
        for d in range(n_dp):
            for f in range(4):
                pairs.append((d * 4 + f, (d ^ dp_mask) * 4 + (f ^ field_mask)))
        return lax.ppermute(value, ("dp", "field"), pairs)

    def over_rest(value):
        mask = 8
        while mask < n_dp:
            value = value + move(value, mask, 0)
            mask *= 2
        return value

    core, chip_y = field & 1, field >> 1
    chip_x, chip_z = group & 1, (group >> 1) & 3
    me5 = core * 16 + chip_x * 8 + chip_y * 4 + chip_z
    me3 = chip_x * 4 + chip_z
    corner = group & 3

    count = row_counts[0]

    gate_rows = jnp.transpose(gate_weight, (0, 2, 1)).reshape(units, cols)
    quarter = experts // 4
    far = move(lax.dynamic_slice(w_first, (corner * quarter, 0, 0), (quarter, cols, hidden)), 0, 2)
    near = move(w_first, 0, 1)
    blocks = []
    for k in range(4):
        mine = lax.dynamic_slice(examples, ((field ^ k) * rows, 0), (rows, cols))
        blocks.append(mine if k == 0 else jnp.concatenate([mine, gate_rows], axis=0))
    blocks[1] = move(blocks[1], 0, 1)
    blocks[2] = move(after(blocks[2], far), 0, 2)
    blocks[3] = move(after(blocks[3], far), 0, 3)
    far_a = [far] + [move(far, r, 0) for r in (1, 2, 3)]
    far_b = [move(piece, 0, 1) for piece in far_a]

    my_domain = lax.dynamic_slice(domain, (field * rows,), (rows,)).reshape(1, rows)
    my_labels = lax.dynamic_slice(labels, (field * rows, 0), (rows, tasks)).T

    place = jnp.stack([field * rows, count, me5, field, corner]).astype(jnp.int32)
    outs = pl.pallas_call(
        middle_kernel,
        name="middle",
        out_shape=(
            like((4 * cols, rows), BF16),
            like((4 * cols, rows), BF16),
            like((experts, hidden, rows), BF16),
            like((experts, hidden, rows), BF16),
            like((experts, 4 * cols, hidden), BF16),
            like((experts, 4 * cols, hidden), BF16),
            like((units, 4 * cols)),
            like((units, rows)),
            like((16, 80, width)),
            like((16, 80, width)),
        ),
        in_specs=[scalars()] * 2
        + [whole()] * 5
        + [anywhere()] * 10
        + [whole()] * 4
        + [anywhere()]
        + [whole()] * 4,
        out_specs=[anywhere()] * 6 + [whole()] * 2 + [anywhere()] * 2,
        scratch_shapes=[
            VMEM((experts, 4 * cols, hidden), F32),
            VMEM((experts, hidden, width), F32),
            VMEM((4 * cols, rows), BF16),
            VMEM((4 * cols, rows), BF16),
            VMEM((experts, hidden, rows), BF16),
            VMEM((experts, hidden, rows), BF16),
            VMEM((experts, 4 * cols, hidden), BF16),
            VMEM((experts, 4 * cols, hidden), BF16),
            VMEM((experts, hidden, rows), BF16),
            VMEM((experts, hidden, rows), BF16),
            VMEM((experts, hidden, rows), F32),
            VMEM((experts, width, rows), F32),
            VMEM((units, rows), F32),
            VMEM((tasks, width, rows), F32),
            VMEM((tasks, width, rows), F32),
            VMEM((units, rows), F32),
            VMEM((hidden, 128), F32),
            VMEM((width, 128), F32),
            VMEM((32, 80, width), F32),
            VMEM((512, width), F32),
            pltpu.SemaphoreType.DMA((5 * experts,)),
        ],
        compiler_params=PARAMS,
    )(
        place,
        tower_out_bias,
        *blocks,
        gate_rows,
        w_first,
        near,
        *far_a,
        *far_b,
        my_domain,
        my_labels,
        gate_bias,
        b_first,
        w_second,
        b_second,
        tower_first,
        tower_bias,
        tower_out,
    )
    xt_high, xt_low, gf_high, gf_low, w_high, w_low, gate_all, glog, s_keep, s_send = outs

    got = move(s_send, 0, 1)
    s_parts = [s_keep[4 * q : 4 * q + 4] + got[4 * q : 4 * q + 4] for q in range(4)]
    s_parts = lax.optimization_barrier(s_parts)
    s_got = [move(s_parts[q], q >> 1, (q & 1) * 2) for q in (1, 2, 3)]

    place3 = me3.reshape(1)
    expert = lambda i: (i, 0, 0)
    w_keep, w_send, g0, g1, g2, g3 = pl.pallas_call(
        first_kernel,
        name="first",
        grid=(experts,),
        out_shape=(like((2, 8, cols, hidden)), like((2, 8, cols, hidden))) + (like((rows, cols)),) * 4,
        in_specs=[scalars()]
        + [whole()] * 4
        + [pl.BlockSpec((1, hidden, rows), expert)] * 2
        + [pl.BlockSpec((1, 4 * cols, hidden), expert)] * 2,
        out_specs=[whole()] * 6,
        scratch_shapes=[VMEM((4 * cols, rows), F32)],
        compiler_params=PARAMS,
        cost_estimate=pl.CostEstimate(flops=0, bytes_accessed=1 << 20, transcendentals=0),
    )(place3, xt_high, xt_low, gate_all, glog, after(gf_high, *s_parts), gf_low, w_high, w_low)

    got = move(after(w_send, *s_got), 0, 1)
    w_parts = [w_keep[q & 1, (q >> 1) * 4 : (q >> 1) * 4 + 4] + got[q & 1, (q >> 1) * 4 : (q >> 1) * 4 + 4] for q in range(4)]
    w_parts = lax.optimization_barrier(w_parts)
    w_got = [move(w_parts[q], q >> 1, (q & 1) * 2) for q in (1, 2, 3)]

    s_mine = s_parts[0] + s_got[0] + s_got[1] + s_got[2]
    s_got = [move(s_mine[z], 2 * z, 0) for z in (1, 2, 3)]
    s_piece = over_rest(s_mine[0] + s_got[0] + s_got[1] + s_got[2])
    s_line = jnp.stack([s_piece] + [move(s_piece, 2 * z, 0) for z in (1, 2, 3)])

    w_mine = w_parts[0] + w_got[0] + w_got[1] + w_got[2]
    w_mine, s_line = lax.optimization_barrier((w_mine, s_line))
    w_got = [move(w_mine[z], 2 * z, 0) for z in (1, 2, 3)]
    s_near = [s_line] + [move(s_line, q >> 1, (q & 1) * 2) for q in (1, 2, 3)]
    s_far = [move(part, 0, 1) for part in s_near]
    w_piece = over_rest(w_mine[0] + w_got[0] + w_got[1] + w_got[2])
    w_line = [w_piece] + [move(w_piece, 2 * z, 0) for z in (1, 2, 3)]
    w_other = move(jnp.stack(w_line), 1, 0)

    back = [g0] + [move(after(g, w_piece) if k > 1 else g, 0, k) for k, g in ((1, g1), (2, g2), (3, g3))]
    seconds = pl.pallas_call(
        finish_second_kernel,
        name="finish_second",
        out_shape=(
            like((experts, hidden, width)),
            like((tasks, width, tower)),
            like((tasks, experts, cols)),
            like((domains, units)),
            like((experts, hidden)),
            like((experts, width)),
            like((tasks, tower)),
            like((tasks, tower)),
            like((1, tasks)),
            like((1, 1)),
            like((1, 1)),
        ),
        in_specs=[scalars()] + [whole()] * 8,
        out_specs=[whole()] * 11,
        scratch_shapes=[VMEM((512, width), F32)],
        compiler_params=PARAMS,
    )(jnp.stack([me5, field]), *s_near, *s_far)
    grad_w_second, grad_tower_first, grad_gate_weight, grad_gate_bias = seconds[:4]
    grad_b_first, grad_b_second, grad_tower_bias, grad_tower_out, grad_out_bias, loss, factor = seconds[4:]

    grad_examples = pl.pallas_call(
        finish_inputs_kernel,
        name="finish_inputs",
        out_shape=like((all_rows, cols)),
        in_specs=[scalars()] + [whole()] * 5,
        out_specs=whole(),
        compiler_params=PARAMS,
    )(field.reshape(1), factor, *back)

    grad_w_first = pl.pallas_call(
        finish_first_kernel,
        name="finish_first",
        out_shape=like((experts, cols, hidden)),
        in_specs=[scalars()] + [whole()] * 6,
        out_specs=whole(),
        compiler_params=PARAMS,
    )(place3, factor, *w_line, w_other)

    return (
        loss[0, 0],
        grad_examples,
        jnp.transpose(grad_gate_weight, (0, 2, 1)),
        grad_gate_bias,
        grad_w_first,
        grad_b_first,
        grad_w_second,
        grad_b_second,
        grad_tower_first,
        grad_tower_bias,
        grad_tower_out,
        grad_out_bias[0],
    )


def solution(mesh):
    placed = (
        P("dp", "field"),
        P("dp"),
        P("dp", None),
        P("dp"),
        P(None, "field", None),
        P(),
        P(None, "field", None),
        P(),
        P(),
        P(),
        P(),
        P(),
        P(),
        P(),
    )
    return jax.shard_map(
        functools.partial(per_device, mesh.shape["dp"]),
        mesh=mesh,
        in_specs=placed,
        out_specs=(
            P(),
            P("dp", "field"),
            P(None, "field", None),
            P(),
            P(None, "field", None),
            P(),
            P(),
            P(),
            P(),
            P(),
            P(),
            P(),
        ),
        check_vma=False,
    )
```

time: 225 us -> 162 us (0.72)
  waiting for transfers between devices: 95.8 us -> 59 us
  Pallas kernels: 57.8 us -> 45.6 us
  local copies, waits for them, and re-layouts: 15.4 us -> 8.76 us
  starting transfers between devices: 47.3 us -> 41.8 us
  between operations: 5.59 us -> 1.78 us
    ppermute x38 -> x43, waiting for transfers between devices: 95.8 us -> 59 us  [move(): return lax.ppermute(value, ('dp', 'field'), pairs)]
    pallas_call x1, Pallas kernels: 28.5 us -> 21.6 us  [per_device(): pl.pallas_call(middle_kernel, name='middle', out_shape=(like((4 * cols, r...]
    pallas_call x2 -> x1, Pallas kernels: 21.3 us -> 14.7 us  [per_device(): pl.pallas_call(first_kernel, name='first', grid=(experts,), out_shape=(li...]
    unnamed x61 -> x62, local copies, waits for them, and re-layouts: 9.67 us -> 3.25 us
    ppermute x38 -> x43, starting transfers between devices: 47.3 us -> 41.8 us  [move(): return lax.ppermute(value, ('dp', 'field'), pairs)]
  transfers between devices with their start and end apart: 38 -> 43, of which waited for: 20 -> 17; matrix products, arithmetic and copies ran while one was open for 4% -> 4% of each run, Pallas kernels for 11% -> 13%
where the time goes in v2:
time: 162 us; the launch traced here: 160 us
  waiting for transfers between devices  59 us (36%)
  Pallas kernels  45.6 us (28%)
  starting transfers between devices  41.8 us (26%)
  local copies, waits for them, and re-layouts  8.76 us (5%)
  other arithmetic  2.79 us (2%)
  between operations  1.78 us (1%)
    ppermute x43, waiting for transfers between devices, move(): return lax.ppermute(value, ('dp', 'field'), pairs)  59 us
    ppermute x43, starting transfers between devices, move(): return lax.ppermute(value, ('dp', 'field'), pairs)  41.8 us
    pallas_call x1, Pallas kernels, per_device(): pl.pallas_call(middle_kernel, name='middle', out_shape=(like((4 * cols, r...  21.6 us
    pallas_call x1, Pallas kernels, per_device(): pl.pallas_call(first_kernel, name='first', grid=(experts,), out_shape=(li...  14.7 us
    pallas_call x1, Pallas kernels, per_device(): pl.pallas_call(finish_second_kernel, name='finish_second', out_shape=(lik...  3.37 us
    unnamed x62, local copies, waits for them, and re-layouts  3.25 us
  transfers between devices with their start and end apart: 43, of which 17 were waited for; matrix products, arithmetic and copies ran while one was open for 4% of the time, Pallas kernels for 13%

profile of v2, /device:TPU:0, one launch (start us, length us, event | category | flops | bytes accessed | tf_op | source)
XLA Modules:
  0.0 159.7 jit_solution(8101999060219958374)
XLA Ops:
  0.7 0.5 collective-permute-start.4
  1.2 1.0 constant_dynamic-slice_fusion.1
  2.2 2.6 %collective-permute-start.1 = (f32[2,128,256]{2,1,0:T(8,128)S(1)}, f32[2,128,256]{2,1,0:T(8,128)S(1)}, u32[]{:S(2)}, u32[]{:S(2)}) collective-permute-start(f32[2,128,256]{2,1,0:T(8,128)S(1)} %constant_dynamic-slice_fusion.1), channel_id=1, source_target_pairs={{0,2},{1,3},{2,0},{3,1},{4,6},{5,7},{6,4},{7,5},{8,10},{9,11},{10,... | collective-permute-start | bytes 786440 | tf_op jit(solution)/shard_map/ppermute | solution.py:420
  4.8 1.9 %constant_dynamic-slice_fusion = (f32[512,128]{1,0:T(8,128)S(1)}, f32[512,128]{1,0:T(8,128)S(1)}, f32[512,128]{1,0:T(8,128)}, f32[512,128]{1,0:T(8,128)S(1)}) fusion(f32[2048,128]{1,0:T(8,128)} %param.14, s32[]{:T(128)S(6)} %select_n.21, s32[]{:T(128)S(6)} %select_n.18, s32[]{:T(128)S(6)} %select_n.17, s32[]{:T(128)S(6)} %select_n.19), kind=kLoop, calls=%fused_computation.33 | loop fusion | bytes 2097168 | tf_op jit(solution)/shard_map/dynamic_slice | solution.py:443
  7.0 4.7 %collective-permute-done.1.fa0 = f32[2,128,256]{2,1,0:T(8,128)S(1)} collective-permute-done((f32[2,128,256]{2,1,0:T(8,128)S(1)}, f32[2,128,256]{2,1,0:T(8,128)S(1)}, u32[]{:S(2)}, u32[]{:S(2)}) %collective-permute-start.1) | collective-permute-done | bytes 262176 | tf_op jit(solution)/shard_map/ppermute | solution.py:420
  11.7 2.7 %collective-permute-start.7 = (f32[2,128,256]{2,1,0:T(8,128)S(1)}, f32[2,128,256]{2,1,0:T(8,128)S(1)}, u32[]{:S(2)}, u32[]{:S(2)}) collective-permute-start(f32[2,128,256]{2,1,0:T(8,128)S(1)} %collective-permute-done.1.fa0), channel_id=1, source_target_pairs={{0,12},{1,13},{2,14},{3,15},{4,8},{5,9},{6,10},{7,11},{8,4},{9,5},... | collective-permute-start | bytes 786440 | tf_op jit(solution)/shard_map/ppermute | solution.py:420
  14.5 1.5 collective-permute-start.2
  16.0 0.5 collective-permute-start.6
  16.4 0.5 collective-permute-start.5
  17.0 4.8 %collective-permute-done.7.fa3 = f32[2,128,256]{2,1,0:T(8,128)S(1)} collective-permute-done((f32[2,128,256]{2,1,0:T(8,128)S(1)}, f32[2,128,256]{2,1,0:T(8,128)S(1)}, u32[]{:S(2)}, u32[]{:S(2)}) %collective-permute-start.7) | collective-permute-done | bytes 262176 | tf_op jit(solution)/shard_map/ppermute | solution.py:420
  21.8 0.7 collective-permute-start.3
  22.5 4.8 %collective-permute-done.6.fa2 = f32[2,128,256]{2,1,0:T(8,128)S(1)} collective-permute-done((f32[2,128,256]{2,1,0:T(8,128)S(1)}, f32[2,128,256]{2,1,0:T(8,128)S(1)}, u32[]{:S(2)}, u32[]{:S(2)}) %collective-permute-start.6) | collective-permute-done | bytes 262176 | tf_op jit(solution)/shard_map/ppermute | solution.py:420
  27.3 0.5 collective-permute-start.10
  28.5 1.3 dynamic_slice.26
  29.9 0.6 stack.55.place
  30.5 0.6 dynamic-slice_bitcast_fusion.labels
  31.2 0.6 copy-done.18
  31.8 0.3 copy-done.4
  32.1 21.6 %middle.1 = (bf16[512,512]{1,0:T(8,128)(2,1)}, bf16[512,512]{1,0:T(8,128)(2,1)}, bf16[8,256,512]{2,1,0:T(8,128)(2,1)}, bf16[8,256,512]{2,1,0:T(8,128)(2,1)}, bf1...) custom-call(s32[5]{0:T(128)} %stack.55.place, ...), custom_call_target="tpu_custom_call" | custom-call | tf_op jit(solution)/shard_map/middle/pallas_call | solution.py:455
  53.7 0.5 collective-permute-start.12
  54.2 2.9 %collective-permute-done.12 = f32[16,80,256]{2,1,0:T(8,128)S(1)} collective-permute-done((f32[16,80,256]{2,1,0:T(8,128)}, f32[16,80,256]{2,1,0:T(8,128)S(1)}, u32[]{:S(2)}, u32[]{:S(2)}) %collective-permute-start.12) | collective-permute-done | bytes 1310752 | tf_op jit(solution)/shard_map/ppermute | solution.py:420
  57.1 1.4 slice_add_fusion.4
  58.5 1.6 %collective-permute-start.13 = (f32[4,80,256]{2,1,0:T(8,128)S(1)}, f32[4,80,256]{2,1,0:T(8,128)S(1)}, u32[]{:S(2)}, u32[]{:S(2)}) collective-permute-start(f32[4,80,256]{2,1,0:T(8,128)S(1)} %get-tuple-element.65), channel_id=1, source_target_pairs={{0,2},{1,3},{2,0},{3,1},{4,6},{5,7},{6,4},{7,5},{8,10},{9,11},{10,... | collective-permute-start | bytes 983048 | tf_op jit(solution)/shard_map/ppermute | solution.py:420
  60.1 1.3 collective-permute-start.14
  61.4 0.7 collective-permute-start.15
  62.1 14.7 %first.1 = (f32[2,8,128,256]{3,2,1,0:T(8,128)}, f32[2,8,128,256]{3,2,1,0:T(8,128)}, f32[512,128]{1,0:T(8,128)}, f32[512,128]{1,0:T(8,128)}, f32[512,128]{1,0:T(8,128)}, /*index=5*/f32[512,128]{1,0:T(8,128)}) custom-call(s32[1]{0:T(128)} %bitcast.2.place, bf16[512,512]{1,0:T(8,128)(2,1)} %get-tuple-element.57.xt_high, ...), custom_call_target="tpu_custom_call" | custom-call | bytes 1048576 | tf_op jit(solution)/shard_map/first/pallas_call | solution.py:529
  77.0 1.6 %collective-permute-start.20 = (f32[80,256]{1,0:T(8,128)S(1)}, f32[80,256]{1,0:T(8,128)S(1)}, u32[]{:S(2)}, u32[]{:S(2)}) collective-permute-start(f32[80,256]{1,0:T(8,128)S(1)} %get-tuple-element.113), channel_id=1, source_target_pairs={{0,8},{1,9},{2,10},{3,11},{4,12},{5,13},{6,14},{7,15},{8,0},{9,1},... | collective-permute-start | bytes 245768 | tf_op jit(solution)/shard_map/ppermute | solution.py:420
  78.7 2.5 %collective-permute-start.22 = (f32[80,256]{1,0:T(8,128)S(1)}, f32[80,256]{1,0:T(8,128)S(1)}, u32[]{:S(2)}, u32[]{:S(2)}) collective-permute-start(f32[80,256]{1,0:T(8,128)S(1)} %get-tuple-element.114), channel_id=1, source_target_pairs={{0,24},{1,25},{2,26},{3,27},{4,28},{5,29},{6,30},{7,31},{8,16},{9,... | collective-permute-start | bytes 245768 | tf_op jit(solution)/shard_map/ppermute | solution.py:420
  81.3 0.3 fusion
  81.6 1.6 collective-permute-start.17
  83.2 1.3 collective-permute-start.18
  84.4 0.7 collective-permute-start.19
  85.1 1.1 collective-permute-done.22
  86.2 3.1 %collective-permute-done.21 = f32[80,256]{1,0:T(8,128)S(1)} collective-permute-done((f32[80,256]{1,0:T(8,128)S(1)}, f32[80,256]{1,0:T(8,128)S(1)}, u32[]{:S(2)}, u32[]{:S(2)}) %collective-permute-start.21) | collective-permute-done | bytes 81952 | tf_op jit(solution)/shard_map/ppermute | solution.py:420
  89.4 2.7 %collective-permute-start.25 = (f32[80,256]{1,0:T(8,128)S(1)}, f32[80,256]{1,0:T(8,128)S(1)}, u32[]{:S(2)}, u32[]{:S(2)}) collective-permute-start(f32[80,256]{1,0:T(8,128)S(1)} %fusion.8), channel_id=1, source_target_pairs={{0,24},{1,25},{2,26},{3,27},{4,28},{5,29},{6,30},{7,31},{8,16},{9,... | collective-permute-start | bytes 245768 | tf_op jit(solution)/shard_map/ppermute | solution.py:420
  92.1 4.5 %collective-permute-done.25 = f32[80,256]{1,0:T(8,128)S(1)} collective-permute-done((f32[80,256]{1,0:T(8,128)S(1)}, f32[80,256]{1,0:T(8,128)S(1)}, u32[]{:S(2)}, u32[]{:S(2)}) %collective-permute-start.25) | collective-permute-done | bytes 81952 | tf_op jit(solution)/shard_map/ppermute | solution.py:420
  96.6 2.7 %collective-permute-done.24 = f32[80,256]{1,0:T(8,128)S(1)} collective-permute-done((f32[80,256]{1,0:T(8,128)S(1)}, f32[80,256]{1,0:T(8,128)S(1)}, u32[]{:S(2)}, u32[]{:S(2)}) %collective-permute-start.24) | collective-permute-done | bytes 81952 | tf_op jit(solution)/shard_map/ppermute | solution.py:420
  99.3 1.8 %collective-permute-done.23 = f32[80,256]{1,0:T(8,128)S(1)} collective-permute-done((f32[80,256]{1,0:T(8,128)S(1)}, f32[80,256]{1,0:T(8,128)S(1)}, u32[]{:S(2)}, u32[]{:S(2)}) %collective-permute-start.23) | collective-permute-done | bytes 81952 | tf_op jit(solution)/shard_map/ppermute | solution.py:420
  101.1 6.9 %collective-permute-done.19 = f32[4,128,256]{2,1,0:T(8,128)S(1)} collective-permute-done((f32[4,128,256]{2,1,0:T(8,128)S(1)}, f32[4,128,256]{2,1,0:T(8,128)S(1)}, u32[]{:S(2)}, u32[]{:S(2)}) %collective-permute-start.19) | collective-permute-done | bytes 524320 | tf_op jit(solution)/shard_map/ppermute | solution.py:420
  108.2 1.6 %collective-permute-start.34 = (f32[128,256]{1,0:T(8,128)S(1)}, f32[128,256]{1,0:T(8,128)S(1)}, u32[]{:S(2)}, u32[]{:S(2)}) collective-permute-start(f32[128,256]{1,0:T(8,128)S(1)} %get-tuple-element.110), channel_id=1, source_target_pairs={{0,8},{1,9},{2,10},{3,11},{4,12},{5,13},{6,14},{7,15},{8,0},{9,1},... | collective-permute-start | bytes 393224 | tf_op jit(solution)/shard_map/ppermute | solution.py:420
  109.9 2.5 %collective-permute-start.36 = (f32[128,256]{1,0:T(8,128)S(1)}, f32[128,256]{1,0:T(8,128)S(1)}, u32[]{:S(2)}, u32[]{:S(2)}) collective-permute-start(f32[128,256]{1,0:T(8,128)S(1)} %get-tuple-element.111), channel_id=1, source_target_pairs={{0,24},{1,25},{2,26},{3,27},{4,28},{5,29},{6,30},{7,31},{8,16},{9,... | collective-permute-start | bytes 393224 | tf_op jit(solution)/shard_map/ppermute | solution.py:420
  112.4 2.2 %collective-permute-start.28 = (f32[4,80,256]{2,1,0:T(8,128)S(1)}, f32[4,80,256]{2,1,0:T(8,128)S(1)}, u32[]{:S(2)}, u32[]{:S(2)}) collective-permute-start(f32[4,80,256]{2,1,0:T(8,128)S(1)} %pad_maximum_fusion.4.a0), channel_id=1, source_target_pairs={{0,6},{1,7},{2,4},{3,5},{4,2},{5,3},{6,0},{7,1},{8,14},{9,15},{10,... | collective-permute-start | bytes 983048 | tf_op jit(solution)/shard_map/ppermute | solution.py:420
  114.7 0.8 collective-permute-start.27
  115.4 3.3 %collective-permute-done.36 = f32[128,256]{1,0:T(8,128)S(1)} collective-permute-done((f32[128,256]{1,0:T(8,128)S(1)}, f32[128,256]{1,0:T(8,128)S(1)}, u32[]{:S(2)}, u32[]{:S(2)}) %collective-permute-start.36) | collective-permute-done | bytes 131104 | tf_op jit(solution)/shard_map/ppermute | solution.py:420
  118.7 4.5 %collective-permute-done.35 = f32[128,256]{1,0:T(8,128)S(1)} collective-permute-done((f32[128,256]{1,0:T(8,128)S(1)}, f32[128,256]{1,0:T(8,128)S(1)}, u32[]{:S(2)}, u32[]{:S(2)}) %collective-permute-start.35) | collective-permute-done | bytes 131104 | tf_op jit(solution)/shard_map/ppermute | solution.py:420
  123.3 3.3 %collective-permute-start.41 = (f32[128,256]{1,0:T(8,128)S(1)}, f32[128,256]{1,0:T(8,128)S(1)}, u32[]{:S(2)}, u32[]{:S(2)}) collective-permute-start(f32[128,256]{1,0:T(8,128)S(1)} %fusion.5.a0), channel_id=1, source_target_pairs={{0,24},{1,25},{2,26},{3,27},{4,28},{5,29},{6,30},{7,31},{8,16},{9,... | collective-permute-start | bytes 393224 | tf_op jit(solution)/shard_map/ppermute | solution.py:420
  126.6 1.1 collective-permute-start.39
  127.7 3.8 %collective-permute-done.41.a3 = f32[128,256]{1,0:T(8,128)S(1)} collective-permute-done((f32[128,256]{1,0:T(8,128)S(1)}, f32[128,256]{1,0:T(8,128)S(1)}, u32[]{:S(2)}, u32[]{:S(2)}) %collective-permute-start.41) | collective-permute-done | bytes 131104 | tf_op jit(solution)/shard_map/ppermute | solution.py:420
  131.6 1.5 collective-permute-start.26
  133.1 3.3 %collective-permute-done.40.a2 = f32[128,256]{1,0:T(8,128)S(1)} collective-permute-done((f32[128,256]{1,0:T(8,128)S(1)}, f32[128,256]{1,0:T(8,128)S(1)}, u32[]{:S(2)}, u32[]{:S(2)}) %collective-permute-start.40) | collective-permute-done | bytes 131104 | tf_op jit(solution)/shard_map/ppermute | solution.py:420
  136.4 0.5 collective-permute-start.32
  137.1 1.3 collective-permute-start.42
  138.4 0.3 collective-permute-done.26.a1
  138.7 0.6 collective-permute-start.33
  139.2 1.6 collective-permute-start.37
  140.9 0.6 pad_add_fusion.place
  141.6 0.7 copy-done.15
  142.3 3.4 %finish_second.1 = (f32[8,256,256]{2,1,0:T(8,128)}, f32[3,256,128]{2,1,0:T(8,128)}, f32[3,8,128]{2,1,0:T(8,128)}, f32[16,24]{1,0:T(8,128)}, f32[8,256]{1,0:T(8,1...) custom-call(s32[2]{0:T(128)} %pad_add_fusion.place, ...), custom_call_target="tpu_custom_call" | custom-call | tf_op jit(solution)/shard_map/finish_second/pallas_call | solution.py:564
  145.7 2.8 %collective-permute-done.37.g2 = f32[512,128]{1,0:T(8,128)S(1)} collective-permute-done((f32[512,128]{1,0:T(8,128)S(1)}, f32[512,128]{1,0:T(8,128)S(1)}, u32[]{:S(2)}, u32[]{:S(2)}) %collective-permute-start.37) | collective-permute-done | bytes 262176 | tf_op jit(solution)/shard_map/ppermute | solution.py:420
  148.5 3.8 %collective-permute-done.38.g3 = f32[512,128]{1,0:T(8,128)S(1)} collective-permute-done((f32[512,128]{1,0:T(8,128)S(1)}, f32[512,128]{1,0:T(8,128)S(1)}, u32[]{:S(2)}, u32[]{:S(2)}) %collective-permute-start.38) | collective-permute-done | bytes 262176 | tf_op jit(solution)/shard_map/ppermute | solution.py:420
  152.3 0.7 copy-done.26
  153.0 2.9 %finish_inputs.1 = f32[2048,128]{1,0:T(8,128)} custom-call(s32[1]{0:T(128)} %bitcast.1.place, f32[1,1]{1,0:T(1,128)} %get-tuple-element.81.factor, f32[512,128]{1,0:T(8,128)} %get-tuple-element.82.g0, f32[512,128]{1,0:T(8,128)} %copy-done.24, f32[512,128]{1,0:T(8,128)} %copy-done.25, f32[512,128]{1,0:T(8,128)} %copy-done.26), custom_call_target="tpu_custom_call" | custom-call | tf_op jit(solution)/shard_map/finish_inputs/pallas_call | solution.py:588
  155.9 0.8 copy-done.5
  156.7 3.1 %finish_first.1 = f32[8,128,256]{2,1,0:T(8,128)} custom-call(s32[1]{0:T(128)} %bitcast.2.place, f32[1,1]{1,0:T(1,128)} %get-tuple-element.81.factor, f32[128,256]{1,0:T(8,128)} %copy-done.3, f32[128,256]{1,0:T(8,128)} %copy-done.8, f32[128,256]{1,0:T(8,128)} %copy-done.7, f32[128,256]{1,0:T(8,128)} %copy-done.6, f32[4,128,256]{2,1,0:T(8,128)} %copy-done.5), custom_call_target="tpu_custom_call" | custom-call | tf_op jit(solution)/shard_map/finish_first/pallas_call | solution.py:597
  (106 shorter events, 1.4 us)
Async XLA Ops:
  0.6 29.8 %copy-start = (s32[2048,3]{0,1:T(4,128)S(1)}, s32[2048,3]{0,1:T(4,128)}, u32[]{:S(2)}) copy-start(s32[2048,3]{0,1:T(4,128)} %param.16) | copy-start | bytes 73732
  0.7 6.1 %copy-start.27 = (f32[3,128,8]{1,2,0:T(8,128)S(1)}, f32[3,128,8]{1,2,0:T(8,128)}, u32[]{:S(2)}) copy-start(f32[3,128,8]{1,2,0:T(8,128)} %param.18) | copy-start | bytes 36868
  0.7 30.4 %collective-permute-start.4 = (f32[8,128,256]{2,1,0:T(8,128)}, f32[8,128,256]{2,1,0:T(8,128)S(1)}, u32[]{:S(2)}, u32[]{:S(2)}) collective-permute-start(f32[8,128,256]{2,1,0:T(8,128)} %near0.1), channel_id=1, source_target_pairs={{0,1},{1,0},{2,3},{3,2},{4,5},{5,4},{6,7},{7,6},{8,9},{9,8},{10,11... | collective-permute-start | bytes 3145736 | tf_op jit(solution)/shard_map/ppermute | solution.py:420
  2.2 9.6 %collective-permute-start.1 = (f32[2,128,256]{2,1,0:T(8,128)S(1)}, f32[2,128,256]{2,1,0:T(8,128)S(1)}, u32[]{:S(2)}, u32[]{:S(2)}) collective-permute-start(f32[2,128,256]{2,1,0:T(8,128)S(1)} %constant_dynamic-slice_fusion.1), channel_id=1, source_target_pairs={{0,2},{1,3},{2,0},{3,1},{4,6},{5,7},{6,4},{7,5},{8,10},{9,11},{10,... | collective-permute-start | bytes 786440 | tf_op jit(solution)/shard_map/ppermute | solution.py:420
  6.8 9.2 %collective-permute-start = (f32[536,128]{1,0:T(8,128)S(1)}, f32[536,128]{1,0:T(8,128)S(1)}, u32[]{:S(2)}, u32[]{:S(2)}) collective-permute-start(f32[536,128]{1,0:T(8,128)S(1)} %get-tuple-element.118), channel_id=1, source_target_pairs={{0,1},{1,0},{2,3},{3,2},{4,5},{5,4},{6,7},{7,6},{8,9},{9,8},{10,11... | collective-permute-start | bytes 823304 | tf_op jit(solution)/shard_map/ppermute | solution.py:420
  11.7 19.4 %copy-start.19 = (f32[2,128,256]{2,1,0:T(8,128)}, f32[2,128,256]{2,1,0:T(8,128)S(1)}, u32[]{:S(2)}) copy-start(f32[2,128,256]{2,1,0:T(8,128)S(1)} %collective-permute-done.1.fa0) | copy-start | bytes 786436
  11.7 4.7 %collective-permute-start.8 = (f32[2,128,256]{2,1,0:T(8,128)S(1)}, f32[2,128,256]{2,1,0:T(8,128)S(1)}, u32[]{:S(2)}, u32[]{:S(2)}) collective-permute-start(f32[2,128,256]{2,1,0:T(8,128)S(1)} %collective-permute-done.1.fa0), channel_id=1, source_target_pairs={{0,1},{1,0},{2,3},{3,2},{4,5},{5,4},{6,7},{7,6},{8,9},{9,8},{10,11... | collective-permute-start | bytes 786440 | tf_op jit(solution)/shard_map/ppermute | solution.py:420
  11.7 10.0 %collective-permute-start.7 = (f32[2,128,256]{2,1,0:T(8,128)S(1)}, f32[2,128,256]{2,1,0:T(8,128)S(1)}, u32[]{:S(2)}, u32[]{:S(2)}) collective-permute-start(f32[2,128,256]{2,1,0:T(8,128)S(1)} %collective-permute-done.1.fa0), channel_id=1, source_target_pairs={{0,12},{1,13},{2,14},{3,15},{4,8},{5,9},{6,10},{7,11},{8,4},{9,5},... | collective-permute-start | bytes 786440 | tf_op jit(solution)/shard_map/ppermute | solution.py:420
  14.5 13.3 %collective-permute-start.2 = (f32[536,128]{1,0:T(8,128)S(1)}, f32[536,128]{1,0:T(8,128)S(1)}, u32[]{:S(2)}, u32[]{:S(2)}) collective-permute-start(f32[536,128]{1,0:T(8,128)S(1)} %get-tuple-element.55), channel_id=1, source_target_pairs={{0,2},{1,3},{2,0},{3,1},{4,6},{5,7},{6,4},{7,5},{8,10},{9,11},{10,... | collective-permute-start | bytes 823304 | tf_op jit(solution)/shard_map/ppermute | solution.py:420
  16.0 15.2 %copy-start.16 = (f32[536,128]{1,0:T(8,128)}, f32[536,128]{1,0:T(8,128)S(1)}, u32[]{:S(2)}) copy-start(f32[536,128]{1,0:T(8,128)S(1)} %collective-permute-done.x1) | copy-start | bytes 823300
  16.0 11.3 %collective-permute-start.6 = (f32[2,128,256]{2,1,0:T(8,128)S(1)}, f32[2,128,256]{2,1,0:T(8,128)S(1)}, u32[]{:S(2)}, u32[]{:S(2)}) collective-permute-start(f32[2,128,256]{2,1,0:T(8,128)S(1)} %collective-permute-done.1.fa0), channel_id=1, source_target_pairs={{0,8},{1,9},{2,10},{3,11},{4,12},{5,13},{6,14},{7,15},{8,0},{9,1},... | collective-permute-start | bytes 786440 | tf_op jit(solution)/shard_map/ppermute | solution.py:420
  16.4 14.7 %copy-start.20 = (f32[2,128,256]{2,1,0:T(8,128)}, f32[2,128,256]{2,1,0:T(8,128)S(1)}, u32[]{:S(2)}) copy-start(f32[2,128,256]{2,1,0:T(8,128)S(1)} %collective-permute-done.8.fb0) | copy-start | bytes 786436
  16.4 10.8 %collective-permute-start.5 = (f32[2,128,256]{2,1,0:T(8,128)S(1)}, f32[2,128,256]{2,1,0:T(8,128)S(1)}, u32[]{:S(2)}, u32[]{:S(2)}) collective-permute-start(f32[2,128,256]{2,1,0:T(8,128)S(1)} %collective-permute-done.1.fa0), channel_id=1, source_target_pairs={{0,4},{1,5},{2,6},{3,7},{4,0},{5,1},{6,2},{7,3},{8,12},{9,13},{10,... | collective-permute-start | bytes 786440 | tf_op jit(solution)/shard_map/ppermute | solution.py:420
  21.8 9.4 %copy-start.21 = (f32[2,128,256]{2,1,0:T(8,128)}, f32[2,128,256]{2,1,0:T(8,128)S(1)}, u32[]{:S(2)}) copy-start(f32[2,128,256]{2,1,0:T(8,128)S(1)} %collective-permute-done.7.fa3) | copy-start | bytes 786436
  21.8 9.3 %collective-permute-start.3 = (f32[536,128]{1,0:T(8,128)S(1)}, f32[536,128]{1,0:T(8,128)S(1)}, u32[]{:S(2)}, u32[]{:S(2)}) collective-permute-start(f32[536,128]{1,0:T(8,128)S(1)} %get-tuple-element.56), channel_id=1, source_target_pairs={{0,3},{1,2},{2,1},{3,0},{4,7},{5,6},{6,5},{7,4},{8,11},{9,10},{10,... | collective-permute-start | bytes 823304 | tf_op jit(solution)/shard_map/ppermute | solution.py:420
  27.3 3.9 %copy-start.22 = (f32[2,128,256]{2,1,0:T(8,128)}, f32[2,128,256]{2,1,0:T(8,128)S(1)}, u32[]{:S(2)}) copy-start(f32[2,128,256]{2,1,0:T(8,128)S(1)} %collective-permute-done.6.fa2) | copy-start | bytes 786436
  27.3 3.8 %collective-permute-start.11 = (f32[2,128,256]{2,1,0:T(8,128)S(1)}, f32[2,128,256]{2,1,0:T(8,128)}, u32[]{:S(2)}, u32[]{:S(2)}) collective-permute-start(f32[2,128,256]{2,1,0:T(8,128)S(1)} %collective-permute-done.7.fa3), channel_id=1, source_target_pairs={{0,1},{1,0},{2,3},{3,2},{4,5},{5,4},{6,7},{7,6},{8,9},{9,8},{10,11... | collective-permute-start | bytes 786440 | tf_op jit(solution)/shard_map/ppermute | solution.py:420
  27.3 3.9 %copy-start.23 = (f32[2,128,256]{2,1,0:T(8,128)}, f32[2,128,256]{2,1,0:T(8,128)S(1)}, u32[]{:S(2)}) copy-start(f32[2,128,256]{2,1,0:T(8,128)S(1)} %collective-permute-done.5.fa1) | copy-start | bytes 786436
  27.3 3.8 %collective-permute-start.10 = (f32[2,128,256]{2,1,0:T(8,128)S(1)}, f32[2,128,256]{2,1,0:T(8,128)}, u32[]{:S(2)}, u32[]{:S(2)}) collective-permute-start(f32[2,128,256]{2,1,0:T(8,128)S(1)} %collective-permute-done.6.fa2), channel_id=1, source_target_pairs={{0,1},{1,0},{2,3},{3,2},{4,5},{5,4},{6,7},{7,6},{8,9},{9,8},{10,11... | collective-permute-start | bytes 786440 | tf_op jit(solution)/shard_map/ppermute | solution.py:420
  27.8 3.3 %collective-permute-start.9 = (f32[2,128,256]{2,1,0:T(8,128)S(1)}, f32[2,128,256]{2,1,0:T(8,128)}, u32[]{:S(2)}, u32[]{:S(2)}) collective-permute-start(f32[2,128,256]{2,1,0:T(8,128)S(1)} %collective-permute-done.5.fa1), channel_id=1, source_target_pairs={{0,1},{1,0},{2,3},{3,2},{4,5},{5,4},{6,7},{7,6},{8,9},{9,8},{10,11... | collective-permute-start | bytes 786440 | tf_op jit(solution)/shard_map/ppermute | solution.py:420
  53.7 3.3 %collective-permute-start.12 = (f32[16,80,256]{2,1,0:T(8,128)}, f32[16,80,256]{2,1,0:T(8,128)S(1)}, u32[]{:S(2)}, u32[]{:S(2)}) collective-permute-start(f32[16,80,256]{2,1,0:T(8,128)} %get-tuple-element.63), channel_id=1, source_target_pairs={{0,1},{1,0},{2,3},{3,2},{4,5},{5,4},{6,7},{7,6},{8,9},{9,8},{10,11... | collective-permute-start | bytes 3932168 | tf_op jit(solution)/shard_map/ppermute | solution.py:420
  58.5 18.3 %collective-permute-start.13 = (f32[4,80,256]{2,1,0:T(8,128)S(1)}, f32[4,80,256]{2,1,0:T(8,128)S(1)}, u32[]{:S(2)}, u32[]{:S(2)}) collective-permute-start(f32[4,80,256]{2,1,0:T(8,128)S(1)} %get-tuple-element.65), channel_id=1, source_target_pairs={{0,2},{1,3},{2,0},{3,1},{4,6},{5,7},{6,4},{7,5},{8,10},{9,11},{10,... | collective-permute-start | bytes 983048 | tf_op jit(solution)/shard_map/ppermute | solution.py:420
  60.1 16.7 %collective-permute-start.14 = (f32[4,80,256]{2,1,0:T(8,128)S(1)}, f32[4,80,256]{2,1,0:T(8,128)S(1)}, u32[]{:S(2)}, u32[]{:S(2)}) collective-permute-start(f32[4,80,256]{2,1,0:T(8,128)S(1)} %get-tuple-element.66), channel_id=1, source_target_pairs={{0,4},{1,5},{2,6},{3,7},{4,0},{5,1},{6,2},{7,3},{8,12},{9,13},{10,... | collective-permute-start | bytes 983048 | tf_op jit(solution)/shard_map/ppermute | solution.py:420
  61.4 15.4 %collective-permute-start.15 = (f32[4,80,256]{2,1,0:T(8,128)S(1)}, f32[4,80,256]{2,1,0:T(8,128)S(1)}, u32[]{:S(2)}, u32[]{:S(2)}) collective-permute-start(f32[4,80,256]{2,1,0:T(8,128)S(1)} %get-tuple-element.67), channel_id=1, source_target_pairs={{0,6},{1,7},{2,4},{3,5},{4,2},{5,3},{6,0},{7,1},{8,14},{9,15},{10,... | collective-permute-start | bytes 983048 | tf_op jit(solution)/shard_map/ppermute | solution.py:420
  76.8 4.5 %copy-start.1 = (f32[2,8,128,256]{3,2,1,0:T(8,128)S(1)}, f32[2,8,128,256]{3,2,1,0:T(8,128)}, u32[]{:S(2)}) copy-start(f32[2,8,128,256]{3,2,1,0:T(8,128)} %get-tuple-element.72) | copy-start | bytes 6291460
  76.8 4.4 %collective-permute-start.16 = (f32[2,8,128,256]{3,2,1,0:T(8,128)}, f32[2,8,128,256]{3,2,1,0:T(8,128)S(1)}, u32[]{:S(2)}, u32[]{:S(2)}) collective-permute-start(f32[2,8,128,256]{3,2,1,0:T(8,128)} %get-tuple-element.74), channel_id=1, source_target_pairs={{0,1},{1,0},{2,3},{3,2},{4,5},{5,4},{6,7},{7,6},{8,9},{9,8},{10,11... | collective-permute-start | bytes 6291464 | tf_op jit(solution)/shard_map/ppermute | solution.py:420
  77.0 7.4 %collective-permute-start.20 = (f32[80,256]{1,0:T(8,128)S(1)}, f32[80,256]{1,0:T(8,128)S(1)}, u32[]{:S(2)}, u32[]{:S(2)}) collective-permute-start(f32[80,256]{1,0:T(8,128)S(1)} %get-tuple-element.113), channel_id=1, source_target_pairs={{0,8},{1,9},{2,10},{3,11},{4,12},{5,13},{6,14},{7,15},{8,0},{9,1},... | collective-permute-start | bytes 245768 | tf_op jit(solution)/shard_map/ppermute | solution.py:420
  78.7 7.6 %collective-permute-start.22 = (f32[80,256]{1,0:T(8,128)S(1)}, f32[80,256]{1,0:T(8,128)S(1)}, u32[]{:S(2)}, u32[]{:S(2)}) collective-permute-start(f32[80,256]{1,0:T(8,128)S(1)} %get-tuple-element.114), channel_id=1, source_target_pairs={{0,24},{1,25},{2,26},{3,27},{4,28},{5,29},{6,30},{7,31},{8,16},{9,... | collective-permute-start | bytes 245768 | tf_op jit(solution)/shard_map/ppermute | solution.py:420
  81.2 8.2 %collective-permute-start.21 = (f32[80,256]{1,0:T(8,128)S(1)}, f32[80,256]{1,0:T(8,128)S(1)}, u32[]{:S(2)}, u32[]{:S(2)}) collective-permute-start(f32[80,256]{1,0:T(8,128)S(1)} %get-tuple-element.115), channel_id=1, source_target_pairs={{0,16},{1,17},{2,18},{3,19},{4,20},{5,21},{6,22},{7,23},{8,24},{9,... | collective-permute-start | bytes 245768 | tf_op jit(solution)/shard_map/ppermute | solution.py:420
  81.6 19.6 %collective-permute-start.17 = (f32[4,128,256]{2,1,0:T(8,128)S(1)}, f32[4,128,256]{2,1,0:T(8,128)S(1)}, u32[]{:S(2)}, u32[]{:S(2)}) collective-permute-start(f32[4,128,256]{2,1,0:T(8,128)S(1)} %get-tuple-element.76), channel_id=1, source_target_pairs={{0,2},{1,3},{2,0},{3,1},{4,6},{5,7},{6,4},{7,5},{8,10},{9,11},{10,... | collective-permute-start | bytes 1572872 | tf_op jit(solution)/shard_map/ppermute | solution.py:420
  83.2 18.0 %collective-permute-start.18 = (f32[4,128,256]{2,1,0:T(8,128)S(1)}, f32[4,128,256]{2,1,0:T(8,128)S(1)}, u32[]{:S(2)}, u32[]{:S(2)}) collective-permute-start(f32[4,128,256]{2,1,0:T(8,128)S(1)} %get-tuple-element.77), channel_id=1, source_target_pairs={{0,4},{1,5},{2,6},{3,7},{4,0},{5,1},{6,2},{7,3},{8,12},{9,13},{10,... | collective-permute-start | bytes 1572872 | tf_op jit(solution)/shard_map/ppermute | solution.py:420
  84.4 23.6 %collective-permute-start.19 = (f32[4,128,256]{2,1,0:T(8,128)S(1)}, f32[4,128,256]{2,1,0:T(8,128)S(1)}, u32[]{:S(2)}, u32[]{:S(2)}) collective-permute-start(f32[4,128,256]{2,1,0:T(8,128)S(1)} %get-tuple-element.78), channel_id=1, source_target_pairs={{0,6},{1,7},{2,4},{3,5},{4,2},{5,3},{6,0},{7,1},{8,14},{9,15},{10,... | collective-permute-start | bytes 1572872 | tf_op jit(solution)/shard_map/ppermute | solution.py:420
  89.4 7.3 %collective-permute-start.25 = (f32[80,256]{1,0:T(8,128)S(1)}, f32[80,256]{1,0:T(8,128)S(1)}, u32[]{:S(2)}, u32[]{:S(2)}) collective-permute-start(f32[80,256]{1,0:T(8,128)S(1)} %fusion.8), channel_id=1, source_target_pairs={{0,24},{1,25},{2,26},{3,27},{4,28},{5,29},{6,30},{7,31},{8,16},{9,... | collective-permute-start | bytes 245768 | tf_op jit(solution)/shard_map/ppermute | solution.py:420
  92.1 7.2 %collective-permute-start.24 = (f32[80,256]{1,0:T(8,128)S(1)}, f32[80,256]{1,0:T(8,128)S(1)}, u32[]{:S(2)}, u32[]{:S(2)}) collective-permute-start(f32[80,256]{1,0:T(8,128)S(1)} %fusion.8), channel_id=1, source_target_pairs={{0,16},{1,17},{2,18},{3,19},{4,20},{5,21},{6,22},{7,23},{8,24},{9,... | collective-permute-start | bytes 245768 | tf_op jit(solution)/shard_map/ppermute | solution.py:420
  96.6 4.4 %collective-permute-start.23 = (f32[80,256]{1,0:T(8,128)S(1)}, f32[80,256]{1,0:T(8,128)S(1)}, u32[]{:S(2)}, u32[]{:S(2)}) collective-permute-start(f32[80,256]{1,0:T(8,128)S(1)} %fusion.8), channel_id=1, source_target_pairs={{0,8},{1,9},{2,10},{3,11},{4,12},{5,13},{6,14},{7,15},{8,0},{9,1},... | collective-permute-start | bytes 245768 | tf_op jit(solution)/shard_map/ppermute | solution.py:420
  101.1 36.0 %copy-start.2 = (f32[4,80,256]{2,1,0:T(8,128)}, f32[4,80,256]{2,1,0:T(8,128)S(1)}, u32[]{:S(2)}) copy-start(f32[4,80,256]{2,1,0:T(8,128)S(1)} %pad_maximum_fusion.4.a0) | copy-start | bytes 983044
  101.1 37.6 %copy-start.30 = (f32[512,128]{1,0:T(8,128)S(1)}, f32[512,128]{1,0:T(8,128)}, u32[]{:S(2)}) copy-start(f32[512,128]{1,0:T(8,128)} %get-tuple-element.83) | copy-start | bytes 786436
  101.1 38.1 %copy-start.29 = (f32[512,128]{1,0:T(8,128)S(1)}, f32[512,128]{1,0:T(8,128)}, u32[]{:S(2)}) copy-start(f32[512,128]{1,0:T(8,128)} %get-tuple-element.86) | copy-start | bytes 786436
  101.1 39.7 %copy-start.28 = (f32[512,128]{1,0:T(8,128)S(1)}, f32[512,128]{1,0:T(8,128)}, u32[]{:S(2)}) copy-start(f32[512,128]{1,0:T(8,128)} %get-tuple-element.88) | copy-start | bytes 786436
  108.2 7.2 %collective-permute-start.34 = (f32[128,256]{1,0:T(8,128)S(1)}, f32[128,256]{1,0:T(8,128)S(1)}, u32[]{:S(2)}, u32[]{:S(2)}) collective-permute-start(f32[128,256]{1,0:T(8,128)S(1)} %get-tuple-element.110), channel_id=1, source_target_pairs={{0,8},{1,9},{2,10},{3,11},{4,12},{5,13},{6,14},{7,15},{8,0},{9,1},... | collective-permute-start | bytes 393224 | tf_op jit(solution)/shard_map/ppermute | solution.py:420
  109.9 8.9 %collective-permute-start.36 = (f32[128,256]{1,0:T(8,128)S(1)}, f32[128,256]{1,0:T(8,128)S(1)}, u32[]{:S(2)}, u32[]{:S(2)}) collective-permute-start(f32[128,256]{1,0:T(8,128)S(1)} %get-tuple-element.111), channel_id=1, source_target_pairs={{0,24},{1,25},{2,26},{3,27},{4,28},{5,29},{6,30},{7,31},{8,16},{9,... | collective-permute-start | bytes 393224 | tf_op jit(solution)/shard_map/ppermute | solution.py:420
  112.4 10.9 %collective-permute-start.35 = (f32[128,256]{1,0:T(8,128)S(1)}, f32[128,256]{1,0:T(8,128)S(1)}, u32[]{:S(2)}, u32[]{:S(2)}) collective-permute-start(f32[128,256]{1,0:T(8,128)S(1)} %get-tuple-element.112), channel_id=1, source_target_pairs={{0,16},{1,17},{2,18},{3,19},{4,20},{5,21},{6,22},{7,23},{8,24},{9,... | collective-permute-start | bytes 393224 | tf_op jit(solution)/shard_map/ppermute | solution.py:420
  112.4 24.0 %collective-permute-start.28 = (f32[4,80,256]{2,1,0:T(8,128)S(1)}, f32[4,80,256]{2,1,0:T(8,128)S(1)}, u32[]{:S(2)}, u32[]{:S(2)}) collective-permute-start(f32[4,80,256]{2,1,0:T(8,128)S(1)} %pad_maximum_fusion.4.a0), channel_id=1, source_target_pairs={{0,6},{1,7},{2,4},{3,5},{4,2},{5,3},{6,0},{7,1},{8,14},{9,15},{10,... | collective-permute-start | bytes 983048 | tf_op jit(solution)/shard_map/ppermute | solution.py:420
  114.7 22.3 %collective-permute-start.27 = (f32[4,80,256]{2,1,0:T(8,128)S(1)}, f32[4,80,256]{2,1,0:T(8,128)S(1)}, u32[]{:S(2)}, u32[]{:S(2)}) collective-permute-start(f32[4,80,256]{2,1,0:T(8,128)S(1)} %pad_maximum_fusion.4.a0), channel_id=1, source_target_pairs={{0,4},{1,5},{2,6},{3,7},{4,0},{5,1},{6,2},{7,3},{8,12},{9,13},{10,... | collective-permute-start | bytes 983048 | tf_op jit(solution)/shard_map/ppermute | solution.py:420
  123.3 32.6 %copy-start.3 = (f32[128,256]{1,0:T(8,128)}, f32[128,256]{1,0:T(8,128)S(1)}, u32[]{:S(2)}) copy-start(f32[128,256]{1,0:T(8,128)S(1)} %fusion.5.a0) | copy-start | bytes 393220
  123.3 8.3 %collective-permute-start.41 = (f32[128,256]{1,0:T(8,128)S(1)}, f32[128,256]{1,0:T(8,128)S(1)}, u32[]{:S(2)}, u32[]{:S(2)}) collective-permute-start(f32[128,256]{1,0:T(8,128)S(1)} %fusion.5.a0), channel_id=1, source_target_pairs={{0,24},{1,25},{2,26},{3,27},{4,28},{5,29},{6,30},{7,31},{8,16},{9,... | collective-permute-start | bytes 393224 | tf_op jit(solution)/shard_map/ppermute | solution.py:420
  126.6 9.8 %collective-permute-start.40 = (f32[128,256]{1,0:T(8,128)S(1)}, f32[128,256]{1,0:T(8,128)S(1)}, u32[]{:S(2)}, u32[]{:S(2)}) collective-permute-start(f32[128,256]{1,0:T(8,128)S(1)} %fusion.5.a0), channel_id=1, source_target_pairs={{0,16},{1,17},{2,18},{3,19},{4,20},{5,21},{6,22},{7,23},{8,24},{9,... | collective-permute-start | bytes 393224 | tf_op jit(solution)/shard_map/ppermute | solution.py:420
  126.6 10.4 %collective-permute-start.39 = (f32[128,256]{1,0:T(8,128)S(1)}, f32[128,256]{1,0:T(8,128)S(1)}, u32[]{:S(2)}, u32[]{:S(2)}) collective-permute-start(f32[128,256]{1,0:T(8,128)S(1)} %fusion.5.a0), channel_id=1, source_target_pairs={{0,8},{1,9},{2,10},{3,11},{4,12},{5,13},{6,14},{7,15},{8,0},{9,1},... | collective-permute-start | bytes 393224 | tf_op jit(solution)/shard_map/ppermute | solution.py:420
  131.6 24.3 %copy-start.6 = (f32[128,256]{1,0:T(8,128)}, f32[128,256]{1,0:T(8,128)S(1)}, u32[]{:S(2)}) copy-start(f32[128,256]{1,0:T(8,128)S(1)} %collective-permute-done.41.a3) | copy-start | bytes 393220
  131.6 7.1 %collective-permute-start.26 = (f32[4,80,256]{2,1,0:T(8,128)S(1)}, f32[4,80,256]{2,1,0:T(8,128)S(1)}, u32[]{:S(2)}, u32[]{:S(2)}) collective-permute-start(f32[4,80,256]{2,1,0:T(8,128)S(1)} %pad_maximum_fusion.4.a0), channel_id=1, source_target_pairs={{0,2},{1,3},{2,0},{3,1},{4,6},{5,7},{6,4},{7,5},{8,10},{9,11},{10,... | collective-permute-start | bytes 983048 | tf_op jit(solution)/shard_map/ppermute | solution.py:420
  136.4 19.5 %copy-start.7 = (f32[128,256]{1,0:T(8,128)}, f32[128,256]{1,0:T(8,128)S(1)}, u32[]{:S(2)}) copy-start(f32[128,256]{1,0:T(8,128)S(1)} %collective-permute-done.40.a2) | copy-start | bytes 393220
  136.4 2.3 %collective-permute-start.29 = (f32[4,80,256]{2,1,0:T(8,128)S(1)}, f32[4,80,256]{2,1,0:T(8,128)S(1)}, u32[]{:S(2)}, u32[]{:S(2)}) collective-permute-start(f32[4,80,256]{2,1,0:T(8,128)S(1)} %pad_maximum_fusion.4.a0), channel_id=1, source_target_pairs={{0,1},{1,0},{2,3},{3,2},{4,5},{5,4},{6,7},{7,6},{8,9},{9,8},{10,11... | collective-permute-start | bytes 983048 | tf_op jit(solution)/shard_map/ppermute | solution.py:420
  136.4 5.1 %copy-start.9 = (f32[4,80,256]{2,1,0:T(8,128)}, f32[4,80,256]{2,1,0:T(8,128)S(1)}, u32[]{:S(2)}) copy-start(f32[4,80,256]{2,1,0:T(8,128)S(1)} %collective-permute-done.28.a3) | copy-start | bytes 983044
  136.4 2.8 %collective-permute-start.32 = (f32[4,80,256]{2,1,0:T(8,128)S(1)}, f32[4,80,256]{2,1,0:T(8,128)S(1)}, u32[]{:S(2)}, u32[]{:S(2)}) collective-permute-start(f32[4,80,256]{2,1,0:T(8,128)S(1)} %collective-permute-done.28.a3), channel_id=1, source_target_pairs={{0,1},{1,0},{2,3},{3,2},{4,5},{5,4},{6,7},{7,6},{8,9},{9,8},{10,11... | collective-permute-start | bytes 983048 | tf_op jit(solution)/shard_map/ppermute | solution.py:420
  136.9 4.6 %copy-start.10 = (f32[4,80,256]{2,1,0:T(8,128)}, f32[4,80,256]{2,1,0:T(8,128)S(1)}, u32[]{:S(2)}) copy-start(f32[4,80,256]{2,1,0:T(8,128)S(1)} %collective-permute-done.27.a2) | copy-start | bytes 983044
  136.9 3.9 %collective-permute-start.31 = (f32[4,80,256]{2,1,0:T(8,128)S(1)}, f32[4,80,256]{2,1,0:T(8,128)S(1)}, u32[]{:S(2)}, u32[]{:S(2)}) collective-permute-start(f32[4,80,256]{2,1,0:T(8,128)S(1)} %collective-permute-done.27.a2), channel_id=1, source_target_pairs={{0,1},{1,0},{2,3},{3,2},{4,5},{5,4},{6,7},{7,6},{8,9},{9,8},{10,11... | collective-permute-start | bytes 983048 | tf_op jit(solution)/shard_map/ppermute | solution.py:420
  137.0 18.9 %copy-start.8 = (f32[128,256]{1,0:T(8,128)}, f32[128,256]{1,0:T(8,128)S(1)}, u32[]{:S(2)}) copy-start(f32[128,256]{1,0:T(8,128)S(1)} %collective-permute-done.39.a1) | copy-start | bytes 393220
  137.1 18.8 %collective-permute-start.42 = (f32[4,128,256]{2,1,0:T(8,128)S(1)}, f32[4,128,256]{2,1,0:T(8,128)S(1)}, u32[]{:S(2)}, u32[]{:S(2)}) collective-permute-start(f32[4,128,256]{2,1,0:T(8,128)S(1)} %pad_maximum_fusion), channel_id=1, source_target_pairs={{0,4},{1,5},{2,6},{3,7},{4,0},{5,1},{6,2},{7,3},{8,12},{9,13},{10,... | collective-permute-start | bytes 1572872 | tf_op jit(solution)/shard_map/ppermute | solution.py:420
  138.7 2.9 %collective-permute-start.30 = (f32[4,80,256]{2,1,0:T(8,128)S(1)}, f32[4,80,256]{2,1,0:T(8,128)S(1)}, u32[]{:S(2)}, u32[]{:S(2)}) collective-permute-start(f32[4,80,256]{2,1,0:T(8,128)S(1)} %collective-permute-done.26.a1), channel_id=1, source_target_pairs={{0,1},{1,0},{2,3},{3,2},{4,5},{5,4},{6,7},{7,6},{8,9},{9,8},{10,11... | collective-permute-start | bytes 983048 | tf_op jit(solution)/shard_map/ppermute | solution.py:420
  138.7 7.0 %collective-permute-start.33 = (f32[512,128]{1,0:T(8,128)S(1)}, f32[512,128]{1,0:T(8,128)S(1)}, u32[]{:S(2)}, u32[]{:S(2)}) collective-permute-start(f32[512,128]{1,0:T(8,128)S(1)} %copy-done.30), channel_id=1, source_target_pairs={{0,1},{1,0},{2,3},{3,2},{4,5},{5,4},{6,7},{7,6},{8,9},{9,8},{10,11... | collective-permute-start | bytes 786440 | tf_op jit(solution)/shard_map/ppermute | solution.py:420
  139.2 9.2 %collective-permute-start.37 = (f32[512,128]{1,0:T(8,128)S(1)}, f32[512,128]{1,0:T(8,128)S(1)}, u32[]{:S(2)}, u32[]{:S(2)}) collective-permute-start(f32[512,128]{1,0:T(8,128)S(1)} %copy-done.29), channel_id=1, source_target_pairs={{0,2},{1,3},{2,0},{3,1},{4,6},{5,7},{6,4},{7,5},{8,10},{9,11},{10,... | collective-permute-start | bytes 786440 | tf_op jit(solution)/shard_map/ppermute | solution.py:420
  140.8 11.4 %collective-permute-start.38 = (f32[512,128]{1,0:T(8,128)S(1)}, f32[512,128]{1,0:T(8,128)S(1)}, u32[]{:S(2)}, u32[]{:S(2)}) collective-permute-start(f32[512,128]{1,0:T(8,128)S(1)} %copy-done.28), channel_id=1, source_target_pairs={{0,3},{1,2},{2,1},{3,0},{4,7},{5,6},{6,5},{7,4},{8,11},{9,10},{10,... | collective-permute-start | bytes 786440 | tf_op jit(solution)/shard_map/ppermute | solution.py:420
  145.7 6.6 %copy-start.24 = (f32[512,128]{1,0:T(8,128)}, f32[512,128]{1,0:T(8,128)S(1)}, u32[]{:S(2)}) copy-start(f32[512,128]{1,0:T(8,128)S(1)} %collective-permute-done.33.g1) | copy-start | bytes 786436
  148.5 3.8 %copy-start.25 = (f32[512,128]{1,0:T(8,128)}, f32[512,128]{1,0:T(8,128)S(1)}, u32[]{:S(2)}) copy-start(f32[512,128]{1,0:T(8,128)S(1)} %collective-permute-done.37.g2) | copy-start | bytes 786436
  (10 other events, 16.2 us)

commit v3 on v2

v3 whole, which is shorter than its diff:
```python
import functools

import jax
import jax.numpy as jnp
from jax import lax
from jax.experimental import pallas as pl
from jax.experimental.pallas import tpu as pltpu
from jax.sharding import PartitionSpec as P

F32 = jnp.float32
BF16 = jnp.bfloat16
ROOT_HALF = 0.7071067811865476
DENSITY = 0.3989422804014327
VMEM = pltpu.VMEM
PARAMS = pltpu.CompilerParams(vmem_limit_bytes=58 * 1024 * 1024)
SMALL = pltpu.CompilerParams(vmem_limit_bytes=12 * 1024 * 1024)
NN, TN, NT = (1, 0), (0, 0), (1, 1)


def split(x):
    high = x.astype(BF16)
    return high, (x - high.astype(F32)).astype(BF16)


def one_dot(a, b, dims):
    return lax.dot_general(a, b, (((dims[0],), (dims[1],)), ((), ())), preferred_element_type=F32)


def dot3(a, b, dims):
    return one_dot(a[0], b[0], dims) + (one_dot(a[0], b[1], dims) + one_dot(a[1], b[0], dims))


def gelu_parts(v):
    cdf = 0.5 + 0.5 * lax.erf(v * ROOT_HALF)
    return v * cdf, cdf + v * (DENSITY * jnp.exp(-0.5 * v * v))


def middle_kernel(
    place,
    out_bias,
    x0,
    x1,
    x2,
    x3,
    gate_rows,
    near0,
    near1,
    fa0,
    fa1,
    fa2,
    fa3,
    fb0,
    fb1,
    fb2,
    fb3,
    domain,
    labels,
    gate_bias,
    b_first,
    w_second,
    b_second,
    t_first,
    t_bias,
    t_out,
    xt_high_out,
    xt_low_out,
    gf_high_out,
    gf_low_out,
    w_high_out,
    w_low_out,
    gate_all,
    glog_out,
    s_keep,
    s_send,
    w_in,
    w2_in,
    xt_high,
    xt_low,
    gf_high,
    gf_low,
    w_high,
    w_low,
    hid_high,
    hid_low,
    slope,
    e_out,
    gates,
    soft_rows,
    bias_rows,
    mix,
    gmix,
    ggate,
    scores,
    targets,
    summed,
    rest,
    sems,
):
    experts = w_second.shape[0]
    tasks, width, tower = t_first.shape
    hidden = w_second.shape[1]
    rows = domain.shape[1]
    domains = gate_bias.shape[0]
    cols = near0.shape[1]
    start, count, me, field, corner = place[0], place[1], place[2], place[3], place[4]
    units = tasks * experts
    quarter = experts // 4
    order = [(r ^ corner) * quarter + i for r in range(4) for i in range(quarter)]

    loads = []
    for n, e in enumerate(order):
        far_a, far_b = ((fa0, fb0), (fa1, fb1), (fa2, fb2), (fa3, fb3))[n // quarter]
        sources = (near0.at[e], near1.at[e], far_a.at[n % quarter], far_b.at[n % quarter])
        for k, source in enumerate(sources):
            target = w_in.at[n, k * cols : (k + 1) * cols]
            loads.append(pltpu.make_async_copy(source, target, sems.at[5 * n + k]))
        loads.append(pltpu.make_async_copy(w_second.at[e], w2_in.at[n], sems.at[5 * n + 4]))
    for load in loads:
        load.start()

    wide = tasks * experts
    starts = (0, 0, 0, rows)
    gate_starts = (0, rows, 2 * rows, 2 * rows)
    for k, ref in enumerate((x0, x1, x2, x3)):
        block = slice(k * cols, (k + 1) * cols)
        high, low = split(ref[starts[k] : starts[k] + rows, :].T)
        xt_high[block, :] = high
        xt_low[block, :] = low
        gate_all[:, block] = gate_rows[...] if k == 0 else ref[gate_starts[k] : gate_starts[k] + wide, :]
    hot = lax.broadcasted_iota(jnp.int32, (domains, rows), 0) == domain[pl.ds(field, 1), :]
    onehot = jnp.where(hot, 1.0, 0.0).astype(BF16)
    bias_high, bias_low = split(gate_bias[...])
    logits = dot3(split(gate_all[...]), (xt_high[...], xt_low[...]), NN)
    logits = logits + (one_dot(bias_high, onehot, TN) + one_dot(bias_low, onehot, TN))
    logits = logits.reshape(tasks, experts, rows)
    raised = jnp.exp(logits - jnp.max(logits, axis=1, keepdims=True))
    soft = raised / jnp.sum(raised, axis=1, keepdims=True)
    soft_rows[...] = soft.reshape(units, rows)
    for n, e in enumerate(order):
        for k in range(tasks):
            gates[k * experts + n : k * experts + n + 1, :] = soft_rows[pl.ds(k * experts + e, 1), :]
        bias_rows[n : n + 1, :] = b_first[pl.ds(e, 1), :]
        bias_rows[experts + n : experts + n + 1, :] = b_second[pl.ds(e, 1), :]
    targets[...] = jnp.zeros_like(targets)
    targets[0:tasks, :] = labels[:, pl.ds(pl.multiple_of(field * rows, 128), rows)].astype(F32)
    mix[...] = jnp.zeros_like(mix)
    bias_cols = bias_rows[...].T
    rest[...] = jnp.zeros_like(rest)
    eye = lax.broadcasted_iota(jnp.int32, (tasks, tower), 0) == lax.broadcasted_iota(jnp.int32, (tasks, tower), 1)
    eye = jnp.where(eye, 1.0, 0.0)
    tb_in = lax.dot_general(t_bias[...], eye, (((0,), (0,)), ((), ())), precision=lax.Precision.HIGHEST)
    to_in = lax.dot_general(t_out[...], eye, (((0,), (0,)), ((), ())), precision=lax.Precision.HIGHEST)
    for load in loads:
        load.wait()

    def first_layer(n):
        weight = split(w_in[n])
        w_high[n], w_low[n] = weight
        return dot3(weight, (xt_high[...], xt_low[...]), TN)

    pre = first_layer(0)
    value = None
    for n in range(experts + 1):
        following = first_layer(n + 1) if n + 1 < experts else None
        if n < experts:
            raw, steep = gelu_parts(pre + bias_cols[:, n : n + 1])
            slope[n] = steep
        if n > 0:
            at = experts + n - 1
            result = dot3(split(w2_in[n - 1]), value, TN) + bias_cols[:, at : at + 1]
            e_out[n - 1] = result
            for k in range(tasks):
                mix[k] += gates[k * experts + n - 1 : k * experts + n, :] * result
        if n < experts:
            value = split(raw)
            hid_high[n], hid_low[n] = value
        pre = following

    stores = [
        pltpu.make_async_copy(xt_high, xt_high_out, sems.at[0]),
        pltpu.make_async_copy(xt_low, xt_low_out, sems.at[1]),
    ]
    for n, e in enumerate(order):
        stores.append(pltpu.make_async_copy(w_high.at[n], w_high_out.at[e], sems.at[2 + 2 * n]))
        stores.append(pltpu.make_async_copy(w_low.at[n], w_low_out.at[e], sems.at[3 + 2 * n]))
    for store in stores:
        store.start()

    position = start + lax.broadcasted_iota(jnp.int32, (1, rows), 1)
    live = jnp.where(position < count, 1.0, 0.0)
    row_of = lax.broadcasted_iota(jnp.int32, (8, rows), 0)
    misc = rest.shape[0] - 8
    scores[...] = jnp.zeros_like(scores)
    acts, steeps, mixed, weights = [], [], [], []
    for k in range(tasks):
        mixed.append(split(mix[k]))
        weights.append(split(t_first[k]))
        value, steep = gelu_parts(dot3(weights[k], mixed[k], TN) + tb_in[:, k : k + 1])
        out_column = to_in[:, k : k + 1]
        scores[k : k + 1, :] = jnp.sum(value * out_column, axis=0, keepdims=True) + out_bias[k]
        acts.append(value)
        steeps.append(out_column * steep)
    score = scores[...]
    target = targets[...]
    task_live = jnp.where(row_of < tasks, live, 0.0)
    per_item = jnp.maximum(score, 0.0) + jnp.log1p(jnp.exp(-jnp.abs(score))) - target * score
    gscores = task_live * (jax.nn.sigmoid(score) - target)
    sums = jnp.sum(gscores, axis=1, keepdims=True)
    losses = jnp.sum(per_item * task_live, axis=(0, 1), keepdims=True)
    t_sums = []
    for k in range(tasks):
        gpre = gscores[k : k + 1, :] * steeps[k]
        t_sums.append(jnp.sum(gpre, axis=1, keepdims=True))
        t_sums.append(jnp.sum(gscores[k : k + 1, :] * acts[k], axis=1, keepdims=True))
        gpre = split(gpre)
        gmix[k] = dot3(weights[k], gpre, NN)
        gweight = dot3(mixed[k], gpre, NT)
        if k < 2:
            rest[0:width, k * tower : (k + 1) * tower] = gweight
        else:
            rest[width : width + tower, 0:tower] = gweight[0:tower]
            rest[width : width + tower, tower:] = gweight[tower:]
        rest[misc + tasks : misc + tasks + 1, k : k + 1] = sums[k : k + 1, :]
    rest[misc + tasks : misc + tasks + 1, tasks : tasks + 1] = losses

    grads = []
    b1_sums, b2_sums = [], []
    for n, e in enumerate(order):
        result = e_out[n]
        total = None
        for k in range(tasks):
            down = gmix[k]
            at = k * experts + n
            ggate[at : at + 1, :] = jnp.sum(down * result, axis=0, keepdims=True)
            part = gates[at : at + 1, :] * down
            total = part if total is None else total + part
        b2_sums.append(jnp.sum(total, axis=1, keepdims=True))
        total = split(total)
        gweight = dot3((hid_high[n], hid_low[n]), total, NT)
        piece = hidden // 4
        for i in range(4):
            slot = (4 * e + i) ^ me
            summed[slot, 0:piece, :] = gweight[i * piece : (i + 1) * piece]
        gfirst = dot3(split(w2_in[n]), total, NN) * slope[n]
        b1_sums.append(jnp.sum(gfirst, axis=1, keepdims=True))
        high, low = split(gfirst)
        gf_high[n] = high
        gf_low[n] = low
        grads.append(pltpu.make_async_copy(gf_high.at[n], gf_high_out.at[e], sems.at[20 + 2 * n]))
        grads.append(pltpu.make_async_copy(gf_low.at[n], gf_low_out.at[e], sems.at[21 + 2 * n]))
        if n % 2 == 1:
            for copy in grads[-4:]:
                copy.start()

    piece = hidden // 4
    last = [
        pltpu.make_async_copy(summed.at[16:32, 0:piece], s_send.at[:, 0:piece], sems.at[36]),
        pltpu.make_async_copy(summed.at[0:16, 0:piece], s_keep.at[:, 0:piece], sems.at[37]),
        pltpu.make_async_copy(summed.at[16:32, piece:], s_send.at[:, piece:], sems.at[38]),
        pltpu.make_async_copy(summed.at[0:16, piece:], s_keep.at[:, piece:], sems.at[39]),
    ]
    last[0].start()
    last[1].start()

    lane = lax.broadcasted_iota(jnp.int32, (width, 128), 1)
    lane_t = lax.broadcasted_iota(jnp.int32, (tower, tower), 1)
    t_cols = jnp.zeros((tower, tower), F32)
    for n, column in enumerate(t_sums):
        t_cols = jnp.where(lane_t == n, column, t_cols)
    t_cols = t_cols.T
    for k in range(tasks):
        for at, n in ((k, 2 * k), (tasks + k, 2 * k + 1)):
            side = slice((at % 2) * tower, (at % 2 + 1) * tower)
            rest[misc + at // 2 : misc + at // 2 + 1, side] = t_cols[n : n + 1, :]
    sums = jnp.zeros((width, 128), F32)
    for n in range(experts):
        sums = jnp.where(lane == n, b1_sums[n], sums)
        sums = jnp.where(lane == experts + n, b2_sums[n], sums)
    sums = sums.T
    soft = gates[...].reshape(tasks, experts, rows)
    gsoft = ggate[...].reshape(tasks, experts, rows)
    glog = soft * (gsoft - jnp.sum(soft * gsoft, axis=1, keepdims=True))
    gates[...] = glog.reshape(units, rows)
    base = 2 * tower + tower + 2 * units
    for n, e in enumerate(order):
        for k in range(tasks):
            glog_out[pl.ds(k * experts + e, 1), :] = gates[k * experts + n : k * experts + n + 1, :]
        rest[pl.ds(base + e, 1), :] = sums[n : n + 1, :]
        rest[pl.ds(base + experts + e, 1), :] = sums[experts + n : experts + n + 1, :]
    glog_parts = split(glog_out[...])
    ggw = dot3(glog_parts, (xt_high[...], xt_low[...]), NT)
    base = width + tower
    for k in range(4):
        at = pl.multiple_of(base + ((field ^ k) >> 1) * units, 8)
        part = ggw[:, k * cols : (k + 1) * cols]
        low_side = ((field ^ k) & 1) == 0
        rest[pl.ds(at, units), 0:tower] = jnp.where(low_side, part, rest[pl.ds(at, units), 0:tower])
        rest[pl.ds(at, units), tower:] = jnp.where(low_side, rest[pl.ds(at, units), tower:], part)
    base = base + 2 * units + 2 * experts
    rest[base : base + domains, 0:units] = one_dot(onehot, glog_parts[0], NT) + one_dot(onehot, glog_parts[1], NT)
    alive = jnp.broadcast_to(jnp.sum(live, axis=1, keepdims=True), (1, width))
    tail = rest.shape[0] // 32
    for p in range(32):
        slot = p ^ me
        summed[slot, hidden // 4 :, :] = jnp.concatenate([rest[p * tail : (p + 1) * tail, :], alive], axis=0)
    last[2].start()
    last[3].start()
    for copy in stores + grads + last:
        copy.wait()


def first_kernel(
    place,
    xt_high_in,
    xt_low_in,
    gf_high_in,
    gf_low_in,
    keep_a,
    send_a,
    keep_b,
    send_b,
    xt_high,
    xt_low,
    gf_high,
    gf_low,
    keep,
    send,
    sems,
):
    experts, cols = keep.shape[0], keep.shape[2]
    loads = [
        pltpu.make_async_copy(xt_high_in, xt_high, sems.at[0]),
        pltpu.make_async_copy(xt_low_in, xt_low, sems.at[1]),
    ]
    for n in range(experts):
        loads.append(pltpu.make_async_copy(gf_high_in.at[n], gf_high.at[n], sems.at[2 + 2 * n]))
        loads.append(pltpu.make_async_copy(gf_low_in.at[n], gf_low.at[n], sems.at[3 + 2 * n]))
    for copy in loads:
        copy.start()
    for copy in loads[0:2]:
        copy.wait()
    stores = []
    for n in range(experts):
        if n % 2 == 0:
            for copy in loads[2 + 2 * n : 6 + 2 * n]:
                copy.wait()
        gweight = dot3((xt_high[...], xt_low[...]), (gf_high[n], gf_low[n]), NT)
        slot = n ^ place[0]
        for k in range(4):
            held, outs = ((keep, (keep_a, keep_b)), (send, (send_a, send_b)))[k % 2]
            held[n, k // 2] = gweight[k * cols : (k + 1) * cols]
            for h, out in enumerate(outs):
                at = sems.at[2 + 2 * experts + 8 * n + 2 * k + h]
                part = held.at[n, k // 2, h * (cols // 2) : (h + 1) * (cols // 2)]
                stores.append(pltpu.make_async_copy(part, out.at[k // 2, slot], at))
        if n % 2 == 1:
            for copy in stores[-16:]:
                copy.start()
    for copy in stores:
        copy.wait()


def inputs_kernel(
    gate_all, glog, gf_high_in, gf_low_in, w_high_in, w_low_in, g0, gc, gy, gf_high, gf_low, w_high, w_low, total, sems
):
    experts = gf_high.shape[0]
    rows, cols = g0.shape
    loads = []
    sources = ((gf_high_in, gf_high), (gf_low_in, gf_low), (w_high_in, w_high), (w_low_in, w_low))
    for n in range(experts):
        for m, (source, target) in enumerate(sources):
            loads.append(pltpu.make_async_copy(source.at[n], target.at[n], sems.at[4 * n + m]))
    for copy in loads:
        copy.start()
    total[...] = dot3(split(gate_all[...]), split(glog[...]), TN)
    for n in range(experts):
        if n % 2 == 0:
            for copy in loads[4 * n : 4 * n + 8]:
                copy.wait()
        total[...] += dot3((w_high[n], w_low[n]), (gf_high[n], gf_low[n]), NN)
    g0[...] = total[0:cols, :].T
    gc[0:rows, :] = total[cols : 2 * cols, :].T
    gc[rows:, :] = total[3 * cols :, :].T
    gy[...] = total[2 * cols : 3 * cols, :].T


def finish_second_kernel(
    place, a0, a1, a2, a3, b0, b1, b2, b3, gw2, gtf, ggw, ggb, gb1, gb2, gtb, gto, gtob, loss, parts, rest
):
    me, field = place[0], place[1]
    hidden = gw2.shape[1]
    piece = hidden // 4
    tasks, width, tower = gtf.shape
    experts = ggw.shape[1]
    units = tasks * experts
    domains = ggb.shape[0]
    tail = rest.shape[0] // 32
    half = (piece + tail + 1) // 2
    for s, (ref_a, ref_b) in enumerate(((a0, a1), (a2, a3), (b0, b1), (b2, b3))):
        for i in range(2):
            for z in range(4):
                p = ((s // 2) * 16 + ((s % 2) * 2 + i) * 4 + z) ^ me
                gw2[p // 4, pl.ds(pl.multiple_of((p % 4) * piece, 8), half), :] = ref_a[i, z]
                p = ((s // 2) * 16 + ((s % 2) + 2 * i) * 4 + z) ^ me
                at = pl.multiple_of((p % 4) * piece + half, 8)
                gw2[p // 4, pl.ds(at, piece - half), :] = ref_b[i, z, 0 : piece - half]
                parts[p] = ref_b[i, z, piece - half :]
    for p in range(32):
        rest[p * tail : (p + 1) * tail, :] = parts[p, 0:tail]
    gtf[0] = rest[0:width, 0:tower]
    gtf[1] = rest[0:width, tower:]
    gtf[2, 0:tower] = rest[width : width + tower, 0:tower]
    gtf[2, tower:] = rest[width : width + tower, tower:]
    base = width + tower
    mine = rest[pl.ds(pl.multiple_of(base + (field >> 1) * units, 8), units), :]
    mine = jnp.where((field & 1) == 0, mine[:, 0:tower], mine[:, tower:])
    for k in range(tasks):
        ggw[k] = mine[k * experts : (k + 1) * experts]
    base = base + 2 * units
    gb1[...] = rest[base : base + experts, :]
    gb2[...] = rest[base + experts : base + 2 * experts, :]
    base = base + 2 * experts
    ggb[...] = rest[base : base + domains, 0:units]
    misc = rest.shape[0] - 8
    for k in range(tasks):
        at = k
        gtb[k : k + 1] = rest[misc + at // 2 : misc + at // 2 + 1, (at % 2) * tower : (at % 2 + 1) * tower]
        at = tasks + k
        gto[k : k + 1] = rest[misc + at // 2 : misc + at // 2 + 1, (at % 2) * tower : (at % 2 + 1) * tower]
    gtob[...] = rest[misc + tasks : misc + tasks + 1, 0:tasks]
    loss[...] = rest[misc + tasks : misc + tasks + 1, tasks : tasks + 1]


def place_near_kernel(place, a0, a1, a2, a3, out, sems):
    copies = [
        pltpu.make_async_copy(ref, out.at[z ^ place[0]], sems.at[z]) for z, ref in enumerate((a0, a1, a2, a3))
    ]
    for copy in copies:
        copy.start()
    for copy in copies:
        copy.wait()


def place_far_kernel(place, b, begun, out, sems):
    copies = [pltpu.make_async_copy(b.at[z], out.at[(4 + z) ^ place[0]], sems.at[z]) for z in range(4)]
    for copy in copies:
        copy.start()
    for copy in copies:
        copy.wait()


def finish_inputs_kernel(place, factor, g0, gc, gy, out):
    field = place[0]
    rows = g0.shape[0]
    for k, ref in enumerate((g0, gc, gy, gy)):
        at = rows if k == 3 else 0
        out[pl.ds(pl.multiple_of((field ^ k) * rows, 8), rows), :] = ref[at : at + rows, :] * factor[...]


def whole():
    return pl.BlockSpec(memory_space=VMEM)


def anywhere():
    return pl.BlockSpec(memory_space=pl.ANY)


def scalars():
    return pl.BlockSpec(memory_space=pltpu.SMEM)


def like(shape, dtype=F32):
    return jax.ShapeDtypeStruct(shape, dtype)


def after(value, *others):
    return lax.optimization_barrier((value, others))[0]


def per_device(
    n_dp,
    examples,
    domain,
    labels,
    row_counts,
    gate_weight,
    gate_bias,
    w_first,
    b_first,
    w_second,
    b_second,
    tower_first,
    tower_bias,
    tower_out,
    tower_out_bias,
):
    all_rows, cols = examples.shape
    rows = all_rows // 4
    experts, _, hidden = w_first.shape
    tasks = gate_weight.shape[0]
    width = w_second.shape[2]
    tower = tower_first.shape[2]
    domains = gate_bias.shape[0]
    units = tasks * experts
    field = lax.axis_index("field").astype(jnp.int32)
    group = lax.axis_index("dp").astype(jnp.int32)

    def move(value, dp_mask, field_mask):
        pairs = []
        for d in range(n_dp):
            for f in range(4):
                pairs.append((d * 4 + f, (d ^ dp_mask) * 4 + (f ^ field_mask)))
        return lax.ppermute(value, ("dp", "field"), pairs)

    def over_rest(value):
        mask = 8
        while mask < n_dp:
            value = value + move(value, mask, 0)
            mask *= 2
        return value

    core, chip_y = field & 1, field >> 1
    chip_x, chip_z = group & 1, (group >> 1) & 3
    me5 = core * 16 + chip_x * 8 + chip_y * 4 + chip_z
    me3 = chip_x * 4 + chip_z
    corner = group & 3

    count = row_counts[0]

    gate_rows = jnp.transpose(gate_weight, (0, 2, 1)).reshape(units, cols)
    quarter = experts // 4

    def rows_for(k):
        return lax.dynamic_slice(examples, ((field ^ k) * rows, 0), (rows, cols))

    far = move(lax.dynamic_slice(w_first, (corner * quarter, 0, 0), (quarter, cols, hidden)), 0, 2)
    near = move(w_first, 0, 1)
    place = jnp.stack([field * rows, count, me5, field, corner]).astype(jnp.int32)
    domain = domain.reshape(4, rows)
    x0 = rows_for(0)
    near_rows = jnp.concatenate([rows_for(1), gate_rows], axis=0)
    y_rows = jnp.concatenate([rows_for(2), rows_for(3), gate_rows], axis=0)
    early = (far, near, near_rows, y_rows, x0, place, domain)
    far, near, near_rows, y_rows, x0, place, domain = lax.optimization_barrier(early)

    x2 = move(y_rows, 0, 2)
    x1 = move(near_rows, 0, 1)
    far_a = [far] + [move(far, r, 0) for r in (1, 2, 3)]
    x1, x2, far_a = lax.optimization_barrier((x1, x2, far_a))

    x3 = move(x2, 0, 1)
    far_b = [move(piece, 0, 1) for piece in far_a]

    outs = pl.pallas_call(
        middle_kernel,
        name="middle",
        out_shape=(
            like((4 * cols, rows), BF16),
            like((4 * cols, rows), BF16),
            like((experts, hidden, rows), BF16),
            like((experts, hidden, rows), BF16),
            like((experts, 4 * cols, hidden), BF16),
            like((experts, 4 * cols, hidden), BF16),
            like((units, 4 * cols)),
            like((units, rows)),
            like((16, 80, width)),
            like((16, 80, width)),
        ),
        in_specs=[scalars()] * 2
        + [whole()] * 5
        + [anywhere()] * 10
        + [whole()] * 4
        + [anywhere()]
        + [whole()] * 4,
        out_specs=[anywhere()] * 6 + [whole()] * 2 + [anywhere()] * 2,
        scratch_shapes=[
            VMEM((experts, 4 * cols, hidden), F32),
            VMEM((experts, hidden, width), F32),
            VMEM((4 * cols, rows), BF16),
            VMEM((4 * cols, rows), BF16),
            VMEM((experts, hidden, rows), BF16),
            VMEM((experts, hidden, rows), BF16),
            VMEM((experts, 4 * cols, hidden), BF16),
            VMEM((experts, 4 * cols, hidden), BF16),
            VMEM((experts, hidden, rows), BF16),
            VMEM((experts, hidden, rows), BF16),
            VMEM((experts, hidden, rows), F32),
            VMEM((experts, width, rows), F32),
            VMEM((units, rows), F32),
            VMEM((units, rows), F32),
            VMEM((2 * experts, hidden), F32),
            VMEM((tasks, width, rows), F32),
            VMEM((tasks, width, rows), F32),
            VMEM((units, rows), F32),
            VMEM((8, rows), F32),
            VMEM((8, rows), F32),
            VMEM((32, 80, width), F32),
            VMEM((480, width), F32),
            pltpu.SemaphoreType.DMA((5 * experts,)),
        ],
        compiler_params=PARAMS,
    )(
        place,
        tower_out_bias,
        x0,
        x1,
        x2,
        x3,
        gate_rows,
        w_first,
        near,
        *far_a,
        *far_b,
        domain,
        labels.T,
        gate_bias,
        b_first,
        w_second,
        b_second,
        tower_first,
        tower_bias,
        tower_out,
    )
    xt_high, xt_low, gf_high, gf_low, w_high, w_low, gate_all, glog, s_keep, s_send = outs

    place3 = me3.reshape(1)
    cheap = pl.CostEstimate(flops=0, bytes_accessed=1 << 20, transcendentals=0)

    def fold(keep, got, axis):
        held = keep + got
        return lax.index_in_dim(held, 0, axis, False), lax.index_in_dim(held, 1, axis, False)

    s_keep = s_keep.reshape(2, 2, 4, 80, width)
    s_got = move(s_send, 0, 1).reshape(2, 2, 4, 80, width)
    sa, sa_out = fold(s_keep[:, :, :, 0:40], s_got[:, :, :, 0:40], 0)
    sb, sb_out = fold(s_keep[:, :, :, 40:80], s_got[:, :, :, 40:80], 1)
    sa, sa_out, sb, sb_out, gf_high = lax.optimization_barrier((sa, sa_out, sb, sb_out, gf_high))

    sa_got, sb_got = move(sa_out, 1, 0), move(sb_out, 0, 2)
    wa_keep, wa_send, wb_keep, wb_send = pl.pallas_call(
        first_kernel,
        name="first",
        out_shape=tuple(like((2, 8, cols // 2, hidden)) for _ in range(4)),
        in_specs=[scalars()] + [anywhere()] * 4,
        out_specs=[anywhere()] * 4,
        scratch_shapes=[
            VMEM((4 * cols, rows), BF16),
            VMEM((4 * cols, rows), BF16),
            VMEM((experts, hidden, rows), BF16),
            VMEM((experts, hidden, rows), BF16),
            VMEM((experts, 2, cols, hidden), F32),
            VMEM((experts, 2, cols, hidden), F32),
            pltpu.SemaphoreType.DMA((10 * experts + 2,)),
        ],
        compiler_params=PARAMS,
        cost_estimate=cheap,
    )(place3, xt_high, xt_low, gf_high, gf_low)
    wa_got, wb_got = move(wa_send, 0, 1), move(wb_send, 0, 1)
    sa, sa_out = fold(sa, sa_got, 0)
    sb, sb_out = fold(sb, sb_got, 0)
    sa_got, sb_got = move(sa_out, 0, 2), move(sb_out, 1, 0)
    s_mine = jnp.concatenate([sa + sa_got, sb + sb_got], axis=1)
    slots = (2, 2, 4, cols // 2, hidden)
    wa, wa_out = fold(wa_keep.reshape(slots), wa_got.reshape(slots), 0)
    wb, wb_out = fold(wb_keep.reshape(slots), wb_got.reshape(slots), 1)
    stage = (wa, wa_out, wb, wb_out, s_mine, gf_low)
    wa, wa_out, wb, wb_out, s_mine, gf_low = lax.optimization_barrier(stage)

    wa_got, wb_got = move(wa_out, 0, 2), move(wb_out, 1, 0)
    s_got = [move(s_mine[z], 2 * z, 0) for z in (1, 2, 3)]
    wa, wa_out = fold(wa, wa_got, 0)
    wb, wb_out = fold(wb, wb_got, 0)
    wa_got, wb_got = move(wa_out, 1, 0), move(wb_out, 0, 2)
    s_piece = over_rest(s_mine[0] + s_got[0] + s_got[1] + s_got[2])
    factor = 1.0 / s_piece[79:80, 0:1]
    s_piece = s_piece * factor
    s_line = jnp.stack([s_piece] + [move(s_piece, 2 * z, 0) for z in (1, 2, 3)])
    w_mine = jnp.concatenate([wa + wa_got, wb + wb_got], axis=1)
    w_mine, s_line, gf_low = lax.optimization_barrier((w_mine, s_line, gf_low))

    g0, gc, gy = pl.pallas_call(
        inputs_kernel,
        name="inputs",
        out_shape=(like((rows, cols)), like((2 * rows, cols)), like((rows, cols))),
        in_specs=[whole()] * 2 + [anywhere()] * 4,
        out_specs=[whole()] * 3,
        scratch_shapes=[
            VMEM((experts, hidden, rows), BF16),
            VMEM((experts, hidden, rows), BF16),
            VMEM((experts, 4 * cols, hidden), BF16),
            VMEM((experts, 4 * cols, hidden), BF16),
            VMEM((4 * cols, rows), F32),
            pltpu.SemaphoreType.DMA((4 * experts,)),
        ],
        compiler_params=PARAMS,
        cost_estimate=cheap,
    )(gate_all, glog, gf_high, gf_low, w_high, w_low)
    w_got = [move(w_mine[z], 2 * z, 0) for z in (1, 2, 3)]
    sa, sb = s_line[:, 0:40], s_line[:, 40:80]
    sa = jnp.stack([sa, move(sa, 0, 2)])
    sb = jnp.stack([sb, move(sb, 1, 0)])
    w_piece = over_rest(w_mine[0] + w_got[0] + w_got[1] + w_got[2]) * factor
    w_piece, sa, sb, g0, gc, gy = lax.optimization_barrier((w_piece, sa, sb, g0, gc, gy))

    gc = move(gc, 0, 1)
    w_line = [w_piece] + [move(w_piece, 2 * z, 0) for z in (1, 2, 3)]
    s_near = [sa, sb, move(sa, 1, 0), move(sb, 0, 2)]
    gy = jnp.concatenate([gy, gc[rows:]], axis=0)
    w_line, s_near, gy = lax.optimization_barrier((w_line, s_near, gy))

    w_other = move(jnp.stack(w_line), 1, 0)
    gy = move(gy, 0, 2)
    s_far = [move(part, 0, 1) for part in s_near]

    seconds = pl.pallas_call(
        finish_second_kernel,
        name="finish_second",
        out_shape=(
            like((experts, hidden, width)),
            like((tasks, width, tower)),
            like((tasks, experts, cols)),
            like((domains, units)),
            like((experts, hidden)),
            like((experts, width)),
            like((tasks, tower)),
            like((tasks, tower)),
            like((1, tasks)),
            like((1, 1)),
        ),
        in_specs=[scalars()] + [whole()] * 8,
        out_specs=[whole()] * 10,
        scratch_shapes=[VMEM((32, 16, width), F32), VMEM((480, width), F32)],
        compiler_params=SMALL,
    )(jnp.stack([me5, field]), *s_near, *s_far)
    grad_w_second, grad_tower_first, grad_gate_weight, grad_gate_bias = seconds[:4]
    grad_b_first, grad_b_second, grad_tower_bias, grad_tower_out, grad_out_bias, loss = seconds[4:]

    grad_examples = pl.pallas_call(
        finish_inputs_kernel,
        name="finish_inputs",
        out_shape=like((all_rows, cols)),
        in_specs=[scalars()] + [whole()] * 4,
        out_specs=whole(),
        compiler_params=SMALL,
    )(field.reshape(1), factor, g0, gc, gy)

    begun = pl.pallas_call(
        place_near_kernel,
        name="place_near",
        out_shape=like((experts, cols, hidden)),
        in_specs=[scalars()] + [anywhere()] * 4,
        out_specs=anywhere(),
        scratch_shapes=[pltpu.SemaphoreType.DMA((4,))],
        compiler_params=SMALL,
    )(place3, *w_line)
    grad_w_first = pl.pallas_call(
        place_far_kernel,
        name="place_far",
        out_shape=like((experts, cols, hidden)),
        in_specs=[scalars(), anywhere(), anywhere()],
        out_specs=anywhere(),
        scratch_shapes=[pltpu.SemaphoreType.DMA((4,))],
        input_output_aliases={2: 0},
        compiler_params=SMALL,
    )(place3, w_other, after(begun, grad_examples, grad_w_second))

    return (
        loss[0, 0],
        grad_examples,
        jnp.transpose(grad_gate_weight, (0, 2, 1)),
        grad_gate_bias,
        grad_w_first,
        grad_b_first,
        grad_w_second,
        grad_b_second,
        grad_tower_first,
        grad_tower_bias,
        grad_tower_out,
        grad_out_bias[0],
    )


def solution(mesh):
    placed = (
        P("dp", "field"),
        P("dp"),
        P("dp", None),
        P("dp"),
        P(None, "field", None),
        P(),
        P(None, "field", None),
        P(),
        P(),
        P(),
        P(),
        P(),
        P(),
        P(),
    )
    return jax.shard_map(
        functools.partial(per_device, mesh.shape["dp"]),
        mesh=mesh,
        in_specs=placed,
        out_specs=(
            P(),
            P("dp", "field"),
            P(None, "field", None),
            P(),
            P(None, "field", None),
            P(),
            P(),
            P(),
            P(),
            P(),
            P(),
            P(),
        ),
        check_vma=False,
    )
```

time: 162 us -> 152 us (0.938)
  Pallas kernels: 45.6 us -> 41.4 us
  waiting for transfers between devices: 59 us -> 56 us
  local copies, waits for them, and re-layouts: 8.76 us -> 6.9 us
    ppermute x43 -> x46, waiting for transfers between devices: 59 us -> 56 us  [move(): return lax.ppermute(value, ('dp', 'field'), pairs)]
    pallas_call x1, Pallas kernels: 2.92 us -> 1.11 us  [per_device(): pl.pallas_call(finish_inputs_kernel, name='finish_inputs', out_shape=like...]
    pallas_call x2 -> x4, Pallas kernels: 17.7 us -> 16.1 us  [the longest x1 7.25 us: per_device(): pl.pallas_call(inputs_kernel, name='inputs', out_shape=(like((rows, cols)...]
    unnamed x62 -> x36, local copies, waits for them, and re-layouts: 3.25 us -> 1.81 us
    dynamic_slice x2 -> x1, local copies, waits for them, and re-layouts: 3.29 us -> 1.94 us  [rows_for(): return lax.dynamic_slice(examples, ((field ^ k) * rows, 0), (rows, cols))]
    ppermute x43 -> x46, starting transfers between devices: 41.8 us -> 41.7 us  [move(): return lax.ppermute(value, ('dp', 'field'), pairs)]
  transfers between devices with their start and end apart: 43 -> 46, of which waited for: 17 -> 24; matrix products, arithmetic and copies ran while one was open for 4% -> 4% of each run, Pallas kernels for 13% -> 12%
where the time goes in v3:
time: 152 us; the launch traced here: 151 us
  waiting for transfers between devices  56 us (37%)
  starting transfers between devices  41.7 us (27%)
  Pallas kernels  41.4 us (27%)
  local copies, waits for them, and re-layouts  6.9 us (5%)
  between operations  2.71 us (2%)
  other arithmetic  2.63 us (2%)
    ppermute x46, waiting for transfers between devices, move(): return lax.ppermute(value, ('dp', 'field'), pairs)  56 us
    ppermute x46, starting transfers between devices, move(): return lax.ppermute(value, ('dp', 'field'), pairs)  41.7 us
    pallas_call x1, Pallas kernels, per_device(): pl.pallas_call(middle_kernel, name='middle', out_shape=(like((4 * cols, r...  21.8 us
    pallas_call x1, Pallas kernels, per_device(): pl.pallas_call(inputs_kernel, name='inputs', out_shape=(like((rows, cols)...  7.25 us
    pallas_call x1, Pallas kernels, per_device(): pl.pallas_call(first_kernel, name='first', out_shape=tuple((like((2, 8, c...  7.2 us
  transfers between devices with their start and end apart: 46, of which 24 were waited for; matrix products, arithmetic and copies ran while one was open for 4% of the time, Pallas kernels for 12%

profile of v3, /device:TPU:0, one launch (start us, length us, event | category | flops | bytes accessed | tf_op | source)
XLA Modules:
  0.0 151.3 jit_solution(17790160166954575270)
XLA Ops:
  0.7 0.5 collective-permute-start.1
  1.2 1.0 constant_dynamic-slice_fusion.4
  2.2 2.6 %collective-permute-start = (f32[2,128,256]{2,1,0:T(8,128)S(1)}, f32[2,128,256]{2,1,0:T(8,128)S(1)}, u32[]{:S(2)}, u32[]{:S(2)}) collective-permute-start(f32[2,128,256]{2,1,0:T(8,128)S(1)} %constant_dynamic-slice_fusion.4), channel_id=1, source_target_pairs={{0,2},{1,3},{2,0},{3,1},{4,6},{5,7},{6,4},{7,5},{8,10},{9,11},{10,... | collective-permute-start | bytes 786440 | tf_op jit(solution)/shard_map/ppermute | solution.py:513
  4.8 1.9 %constant_dynamic-slice_fusion = (f32[512,128]{1,0:T(8,128)}, f32[512,128]{1,0:T(8,128)S(1)}, f32[512,128]{1,0:T(8,128)S(1)}, f32[512,128]{1,0:T(8,128)S(1)}) fusion(f32[2048,128]{1,0:T(8,128)} %param.14, s32[]{:T(128)S(6)} %select_n.19, s32[]{:T(128)S(6)} %select_n.17, s32[]{:T(128)S(6)} %select_n.16, s32[]{:T(128)S(6)} %select_n.18), kind=kLoop, calls=%fused_computation.43 | loop fusion | bytes 2097168 | tf_op jit(solution)/shard_map/dynamic_slice | solution.py:534
  7.4 0.6 reshape.52.domain
  8.0 0.6 stack.73.place
  8.6 3.1 %collective-permute-done.fa0 = f32[2,128,256]{2,1,0:T(8,128)S(1)} collective-permute-done((f32[2,128,256]{2,1,0:T(8,128)S(1)}, f32[2,128,256]{2,1,0:T(8,128)S(1)}, u32[]{:S(2)}, u32[]{:S(2)}) %collective-permute-start) | collective-permute-done | bytes 262176 | tf_op jit(solution)/shard_map/ppermute | solution.py:513
  11.7 1.8 %collective-permute-start.3 = (f32[1048,128]{1,0:T(8,128)S(1)}, f32[1048,128]{1,0:T(8,128)S(1)}, u32[]{:S(2)}, u32[]{:S(2)}) collective-permute-start(f32[1048,128]{1,0:T(8,128)S(1)} %pad_maximum_fusion), channel_id=1, source_target_pairs={{0,2},{1,3},{2,0},{3,1},{4,6},{5,7},{6,4},{7,5},{8,10},{9,11},{10,... | collective-permute-start | bytes 1609736 | tf_op jit(solution)/shard_map/ppermute | solution.py:513
  13.5 2.5 %collective-permute-start.6 = (f32[2,128,256]{2,1,0:T(8,128)S(1)}, f32[2,128,256]{2,1,0:T(8,128)S(1)}, u32[]{:S(2)}, u32[]{:S(2)}) collective-permute-start(f32[2,128,256]{2,1,0:T(8,128)S(1)} %collective-permute-done.fa0), channel_id=1, source_target_pairs={{0,12},{1,13},{2,14},{3,15},{4,8},{5,9},{6,10},{7,11},{8,4},{9,5},... | collective-permute-start | bytes 786440 | tf_op jit(solution)/shard_map/ppermute | solution.py:513
  16.5 0.5 collective-permute-start.4
  17.0 6.6 %collective-permute-done.6.fa3 = f32[2,128,256]{2,1,0:T(8,128)S(1)} collective-permute-done((f32[2,128,256]{2,1,0:T(8,128)S(1)}, f32[2,128,256]{2,1,0:T(8,128)S(1)}, u32[]{:S(2)}, u32[]{:S(2)}) %collective-permute-start.6) | collective-permute-done | bytes 262176 | tf_op jit(solution)/shard_map/ppermute | solution.py:513
  23.6 5.3 %collective-permute-done.5.fa2 = f32[2,128,256]{2,1,0:T(8,128)S(1)} collective-permute-done((f32[2,128,256]{2,1,0:T(8,128)S(1)}, f32[2,128,256]{2,1,0:T(8,128)S(1)}, u32[]{:S(2)}, u32[]{:S(2)}) %collective-permute-start.5) | collective-permute-done | bytes 262176 | tf_op jit(solution)/shard_map/ppermute | solution.py:513
  29.0 0.5 collective-permute-start.8
  30.0 1.2 collective-permute-done.8.fb0
  33.3 21.8 %middle.1 = (bf16[512,512]{1,0:T(8,128)(2,1)}, bf16[512,512]{1,0:T(8,128)(2,1)}, bf16[8,256,512]{2,1,0:T(8,128)(2,1)}, bf16[8,256,512]{2,1,0:T(8,128)(2,1)}, bf1...) custom-call(s32[5]{0:T(128)} %stack.73.place, ...), custom_call_target="tpu_custom_call" | custom-call | tf_op jit(solution)/shard_map/middle/pallas_call | solution.py:554
  55.3 3.1 %collective-permute-done.12 = f32[16,80,256]{2,1,0:T(8,128)S(1)} collective-permute-done((f32[16,80,256]{2,1,0:T(8,128)}, f32[16,80,256]{2,1,0:T(8,128)S(1)}, u32[]{:S(2)}, u32[]{:S(2)}) %collective-permute-start.12) | collective-permute-done | bytes 1310752 | tf_op jit(solution)/shard_map/ppermute | solution.py:513
  58.4 1.5 fusion.9
  60.1 1.5 collective-permute-start.15
  61.6 0.5 collective-permute-start.17
  62.1 7.2 %first.1 = (f32[2,8,64,256]{3,2,1,0:T(8,128)}, f32[2,8,64,256]{3,2,1,0:T(8,128)}, f32[2,8,64,256]{3,2,1,0:T(8,128)}, f32[2,8,64,256]{3,2,1,0:T(8,128)}) custom-call(s32[1]{0:T(128)} %bitcast.2.place, bf16[512,512]{1,0:T(8,128)(2,1)} %get-tuple-element.95.xt_high_in, bf16[512,512]{1,0:T(8,128)(2,1)} %get-tuple-element.96.xt_low_in, ...), custom_call_target="tpu_custom_call" | custom-call | bytes 1048576 | tf_op jit(solution)/shard_map/first/pallas_call | solution.py:640
  69.4 0.5 collective-permute-start.14
  70.0 1.5 %collective-permute-start.16 = (f32[4,40,256]{2,1,0:T(8,128)S(1)}, f32[4,40,256]{2,1,0:T(8,128)S(1)}, u32[]{:S(2)}, u32[]{:S(2)}) collective-permute-start(f32[4,40,256]{2,1,0:T(8,128)S(1)} %slice_bitcast_fusion.12), channel_id=1, source_target_pairs={{0,2},{1,3},{2,0},{3,1},{4,6},{5,7},{6,4},{7,5},{8,10},{9,11},{10,... | collective-permute-start | bytes 491528 | tf_op jit(solution)/shard_map/ppermute | solution.py:513
  71.6 0.7 collective-permute-start.18
  72.3 3.9 %collective-permute-done.16 = f32[4,40,256]{2,1,0:T(8,128)S(1)} collective-permute-done((f32[4,40,256]{2,1,0:T(8,128)S(1)}, f32[4,40,256]{2,1,0:T(8,128)S(1)}, u32[]{:S(2)}, u32[]{:S(2)}) %collective-permute-start.16) | collective-permute-done | bytes 163872 | tf_op jit(solution)/shard_map/ppermute | solution.py:513
  76.2 1.4 collective-permute-done.18
  77.9 0.9 copy-done.1
  79.1 1.6 %collective-permute-start.23 = (f32[80,256]{1,0:T(8,128)S(1)}, f32[80,256]{1,0:T(8,128)S(1)}, u32[]{:S(2)}, u32[]{:S(2)}) collective-permute-start(f32[80,256]{1,0:T(8,128)S(1)} %get-tuple-element.174), channel_id=1, source_target_pairs={{0,8},{1,9},{2,10},{3,11},{4,12},{5,13},{6,14},{7,15},{8,0},{9,1},... | collective-permute-start | bytes 245768 | tf_op jit(solution)/shard_map/ppermute | solution.py:513
  80.8 2.5 %collective-permute-start.25 = (f32[80,256]{1,0:T(8,128)S(1)}, f32[80,256]{1,0:T(8,128)S(1)}, u32[]{:S(2)}, u32[]{:S(2)}) collective-permute-start(f32[80,256]{1,0:T(8,128)S(1)} %get-tuple-element.175), channel_id=1, source_target_pairs={{0,24},{1,25},{2,26},{3,27},{4,28},{5,29},{6,30},{7,31},{8,16},{9,... | collective-permute-start | bytes 245768 | tf_op jit(solution)/shard_map/ppermute | solution.py:513
  83.4 0.5 collective-permute-start.19
  83.9 0.9 collective-permute-start.21
  84.8 2.7 %collective-permute-done.25 = f32[80,256]{1,0:T(8,128)S(1)} collective-permute-done((f32[80,256]{1,0:T(8,128)S(1)}, f32[80,256]{1,0:T(8,128)S(1)}, u32[]{:S(2)}, u32[]{:S(2)}) %collective-permute-start.25) | collective-permute-done | bytes 81952 | tf_op jit(solution)/shard_map/ppermute | solution.py:513
  87.4 2.7 %collective-permute-done.24 = f32[80,256]{1,0:T(8,128)S(1)} collective-permute-done((f32[80,256]{1,0:T(8,128)S(1)}, f32[80,256]{1,0:T(8,128)S(1)}, u32[]{:S(2)}, u32[]{:S(2)}) %collective-permute-start.24) | collective-permute-done | bytes 81952 | tf_op jit(solution)/shard_map/ppermute | solution.py:513
  90.2 0.5 slice.150
  91.4 0.7 collective-permute-start.27
  92.1 2.3 %collective-permute-start.26 = (f32[80,256]{1,0:T(8,128)S(1)}, f32[80,256]{1,0:T(8,128)S(1)}, u32[]{:S(2)}, u32[]{:S(2)}) collective-permute-start(f32[80,256]{1,0:T(8,128)S(1)} %broadcast_multiply_fusion), channel_id=1, source_target_pairs={{0,8},{1,9},{2,10},{3,11},{4,12},{5,13},{6,14},{7,15},{8,0},{9,1},... | collective-permute-start | bytes 245768 | tf_op jit(solution)/shard_map/ppermute | solution.py:513
  94.5 1.4 collective-permute-start.28
  96.0 0.7 collective-permute-start.20
  96.8 0.8 collective-permute-start.22
  97.6 1.2 collective-permute-done.27
  98.8 1.9 %collective-permute-done.28 = f32[80,256]{1,0:T(8,128)S(1)} collective-permute-done((f32[80,256]{1,0:T(8,128)S(1)}, f32[80,256]{1,0:T(8,128)S(1)}, u32[]{:S(2)}, u32[]{:S(2)}) %collective-permute-start.28) | collective-permute-done | bytes 81952 | tf_op jit(solution)/shard_map/ppermute | solution.py:513
  100.7 2.2 %collective-permute-done.20 = f32[4,64,256]{2,1,0:T(8,128)S(1)} collective-permute-done((f32[4,64,256]{2,1,0:T(8,128)S(1)}, f32[4,64,256]{2,1,0:T(8,128)S(1)}, u32[]{:S(2)}, u32[]{:S(2)}) %collective-permute-start.20) | collective-permute-done | bytes 262176 | tf_op jit(solution)/shard_map/ppermute | solution.py:513
  102.9 0.5 collective-permute-done.22
  103.5 1.3 collective-permute-start.29
  104.8 2.5 %collective-permute-start.31 = (f32[128,256]{1,0:T(8,128)S(1)}, f32[128,256]{1,0:T(8,128)S(1)}, u32[]{:S(2)}, u32[]{:S(2)}) collective-permute-start(f32[128,256]{1,0:T(8,128)S(1)} %get-tuple-element.168), channel_id=1, source_target_pairs={{0,24},{1,25},{2,26},{3,27},{4,28},{5,29},{6,30},{7,31},{8,16},{9,... | collective-permute-start | bytes 393224 | tf_op jit(solution)/shard_map/ppermute | solution.py:513
  107.3 1.3 collective-permute-start.33
  108.6 1.7 %collective-permute-start.32 = (f32[4,40,256]{2,1,0:T(8,128)S(1)}, f32[4,40,256]{2,1,0:T(8,128)S(1)}, u32[]{:S(2)}, u32[]{:S(2)}) collective-permute-start(f32[4,40,256]{2,1,0:T(8,128)S(1)} %get-tuple-element.173), channel_id=1, source_target_pairs={{0,2},{1,3},{2,0},{3,1},{4,6},{5,7},{6,4},{7,5},{8,10},{9,11},{10,... | collective-permute-start | bytes 491528 | tf_op jit(solution)/shard_map/ppermute | solution.py:513
  110.3 7.2 %inputs.1 = (f32[512,128]{1,0:T(8,128)}, f32[1024,128]{1,0:T(8,128)}, f32[512,128]{1,0:T(8,128)}) custom-call(f32[24,512]{1,0:T(8,128)} %get-tuple-element.118.gate_all, f32[24,512]{1,0:T(8,128)} %get-tuple-element.119.glog, bf16[8,256,512]{2,1,0:T(8,128)(2,1)} %get-tuple-element.100.gf_high_in, bf16[8,256,512]{2,1,0:T(8,128)(2,1)} %get-tuple-element.120.gf_low_in, ...), custom_call_target="tpu_custom_call" | custom-call | bytes 1048576 | tf_op jit(solution)/shard_map/inputs/pallas_call | solution.py:681
  117.8 1.2 collective-permute-start.37
  119.0 2.1 %collective-permute-start.36 = (f32[128,256]{1,0:T(8,128)S(1)}, f32[128,256]{1,0:T(8,128)S(1)}, u32[]{:S(2)}, u32[]{:S(2)}) collective-permute-start(f32[128,256]{1,0:T(8,128)S(1)} %fusion.6.a0), channel_id=1, source_target_pairs={{0,24},{1,25},{2,26},{3,27},{4,28},{5,29},{6,30},{7,31},{8,16},{9,... | collective-permute-start | bytes 393224 | tf_op jit(solution)/shard_map/ppermute | solution.py:513
  121.1 1.3 collective-permute-start.35
  122.4 1.0 collective-permute-start.34
  123.5 3.8 %collective-permute-done.36.a3 = f32[128,256]{1,0:T(8,128)S(1)} collective-permute-done((f32[128,256]{1,0:T(8,128)S(1)}, f32[128,256]{1,0:T(8,128)S(1)}, u32[]{:S(2)}, u32[]{:S(2)}) %collective-permute-start.36) | collective-permute-done | bytes 131104 | tf_op jit(solution)/shard_map/ppermute | solution.py:513
  127.2 7.1 %collective-permute-done.35.a2 = f32[128,256]{1,0:T(8,128)S(1)} collective-permute-done((f32[128,256]{1,0:T(8,128)S(1)}, f32[128,256]{1,0:T(8,128)S(1)}, u32[]{:S(2)}, u32[]{:S(2)}) %collective-permute-start.35) | collective-permute-done | bytes 131104 | tf_op jit(solution)/shard_map/ppermute | solution.py:513
  134.5 1.8 %collective-permute-start.44 = (f32[1024,128]{1,0:T(8,128)S(1)}, f32[1024,128]{1,0:T(8,128)S(1)}, u32[]{:S(2)}, u32[]{:S(2)}) collective-permute-start(f32[1024,128]{1,0:T(8,128)S(1)} %pad_maximum_fusion.2), channel_id=1, source_target_pairs={{0,2},{1,3},{2,0},{3,1},{4,6},{5,7},{6,4},{7,5},{8,10},{9,11},{10,... | collective-permute-start | bytes 1572872 | tf_op jit(solution)/shard_map/ppermute | solution.py:513
  136.3 0.9 collective-permute-start.45
  137.2 0.5 collective-permute-start.42
  137.8 0.8 place_near.1.begun
  138.9 0.5 collective-permute-done.42.b2
  139.3 0.5 collective-permute-done.43.b3
  139.8 2.4 %finish_second.1 = (f32[8,256,256]{2,1,0:T(8,128)}, f32[3,256,128]{2,1,0:T(8,128)}, f32[3,8,128]{2,1,0:T(8,128)}, f32[16,24]{1,0:T(8,128)}, f32[8,256]{1,0:T(8,1...) custom-call(s32[2]{0:T(128)S(1)} %pad_add_fusion.place, ...), custom_call_target="tpu_custom_call" | custom-call | tf_op jit(solution)/shard_map/finish_second/pallas_call | solution.py:715
  142.2 6.6 %collective-permute-done.44.gy = f32[1024,128]{1,0:T(8,128)S(1)} collective-permute-done((f32[1024,128]{1,0:T(8,128)S(1)}, f32[1024,128]{1,0:T(8,128)S(1)}, u32[]{:S(2)}, u32[]{:S(2)}) %collective-permute-start.44) | collective-permute-done | bytes 524320 | tf_op jit(solution)/shard_map/ppermute | solution.py:513
  148.8 1.1 finish_inputs.1
  149.9 0.5 collective-permute-done.45.b
  150.4 0.8 place_far.1
  (114 shorter events, 5.6 us)
Async XLA Ops:
  0.6 6.1 %copy-start.16 = (f32[3,128,8]{1,2,0:T(8,128)S(1)}, f32[3,128,8]{1,2,0:T(8,128)}, u32[]{:S(2)}) copy-start(f32[3,128,8]{1,2,0:T(8,128)} %param.18) | copy-start | bytes 36868
  0.7 6.7 %copy-start.17 = (s32[2048]{0:T(1024)S(1)}, s32[2048]{0:T(1024)}, u32[]{:S(2)}) copy-start(s32[2048]{0:T(1024)} %param.15) | copy-start | bytes 24580
  0.7 11.1 %collective-permute-start.1 = (f32[8,128,256]{2,1,0:T(8,128)}, f32[8,128,256]{2,1,0:T(8,128)S(1)}, u32[]{:S(2)}, u32[]{:S(2)}) collective-permute-start(f32[8,128,256]{2,1,0:T(8,128)} %near0.1), channel_id=1, source_target_pairs={{0,1},{1,0},{2,3},{3,2},{4,5},{5,4},{6,7},{7,6},{8,9},{9,8},{10,11... | collective-permute-start | bytes 3145736 | tf_op jit(solution)/shard_map/ppermute | solution.py:513
  2.2 9.6 %collective-permute-start = (f32[2,128,256]{2,1,0:T(8,128)S(1)}, f32[2,128,256]{2,1,0:T(8,128)S(1)}, u32[]{:S(2)}, u32[]{:S(2)}) collective-permute-start(f32[2,128,256]{2,1,0:T(8,128)S(1)} %constant_dynamic-slice_fusion.4), channel_id=1, source_target_pairs={{0,2},{1,3},{2,0},{3,1},{4,6},{5,7},{6,4},{7,5},{8,10},{9,11},{10,... | collective-permute-start | bytes 786440 | tf_op jit(solution)/shard_map/ppermute | solution.py:513
  11.7 20.7 %copy-start.7 = (f32[2,128,256]{2,1,0:T(8,128)}, f32[2,128,256]{2,1,0:T(8,128)S(1)}, u32[]{:S(2)}) copy-start(f32[2,128,256]{2,1,0:T(8,128)S(1)} %collective-permute-done.fa0) | copy-start | bytes 786436
  11.7 20.7 %copy-start.3 = (f32[8,128,256]{2,1,0:T(8,128)}, f32[8,128,256]{2,1,0:T(8,128)S(1)}, u32[]{:S(2)}) copy-start(f32[8,128,256]{2,1,0:T(8,128)S(1)} %collective-permute-done.1.near1) | copy-start | bytes 3145732
  11.7 17.1 %collective-permute-start.3 = (f32[1048,128]{1,0:T(8,128)S(1)}, f32[1048,128]{1,0:T(8,128)S(1)}, u32[]{:S(2)}, u32[]{:S(2)}) collective-permute-start(f32[1048,128]{1,0:T(8,128)S(1)} %pad_maximum_fusion), channel_id=1, source_target_pairs={{0,2},{1,3},{2,0},{3,1},{4,6},{5,7},{6,4},{7,5},{8,10},{9,11},{10,... | collective-permute-start | bytes 1609736 | tf_op jit(solution)/shard_map/ppermute | solution.py:513
  13.5 15.3 %collective-permute-start.2 = (f32[536,128]{1,0:T(8,128)S(1)}, f32[536,128]{1,0:T(8,128)S(1)}, u32[]{:S(2)}, u32[]{:S(2)}) collective-permute-start(f32[536,128]{1,0:T(8,128)S(1)} %pad_maximum_fusion.8), channel_id=1, source_target_pairs={{0,1},{1,0},{2,3},{3,2},{4,5},{5,4},{6,7},{7,6},{8,9},{9,8},{10,11... | collective-permute-start | bytes 823304 | tf_op jit(solution)/shard_map/ppermute | solution.py:513
  13.5 10.0 %collective-permute-start.6 = (f32[2,128,256]{2,1,0:T(8,128)S(1)}, f32[2,128,256]{2,1,0:T(8,128)S(1)}, u32[]{:S(2)}, u32[]{:S(2)}) collective-permute-start(f32[2,128,256]{2,1,0:T(8,128)S(1)} %collective-permute-done.fa0), channel_id=1, source_target_pairs={{0,12},{1,13},{2,14},{3,15},{4,8},{5,9},{6,10},{7,11},{8,4},{9,5},... | collective-permute-start | bytes 786440 | tf_op jit(solution)/shard_map/ppermute | solution.py:513
  16.0 12.8 %collective-permute-start.5 = (f32[2,128,256]{2,1,0:T(8,128)S(1)}, f32[2,128,256]{2,1,0:T(8,128)S(1)}, u32[]{:S(2)}, u32[]{:S(2)}) collective-permute-start(f32[2,128,256]{2,1,0:T(8,128)S(1)} %collective-permute-done.fa0), channel_id=1, source_target_pairs={{0,8},{1,9},{2,10},{3,11},{4,12},{5,13},{6,14},{7,15},{8,0},{9,1},... | collective-permute-start | bytes 786440 | tf_op jit(solution)/shard_map/ppermute | solution.py:513
  16.5 12.4 %collective-permute-start.4 = (f32[2,128,256]{2,1,0:T(8,128)S(1)}, f32[2,128,256]{2,1,0:T(8,128)S(1)}, u32[]{:S(2)}, u32[]{:S(2)}) collective-permute-start(f32[2,128,256]{2,1,0:T(8,128)S(1)} %collective-permute-done.fa0), channel_id=1, source_target_pairs={{0,4},{1,5},{2,6},{3,7},{4,0},{5,1},{6,2},{7,3},{8,12},{9,13},{10,... | collective-permute-start | bytes 786440 | tf_op jit(solution)/shard_map/ppermute | solution.py:513
  23.6 8.8 %copy-start.8 = (f32[2,128,256]{2,1,0:T(8,128)}, f32[2,128,256]{2,1,0:T(8,128)S(1)}, u32[]{:S(2)}) copy-start(f32[2,128,256]{2,1,0:T(8,128)S(1)} %collective-permute-done.6.fa3) | copy-start | bytes 786436
  28.8 3.6 %copy-start.9 = (f32[2,128,256]{2,1,0:T(8,128)}, f32[2,128,256]{2,1,0:T(8,128)S(1)}, u32[]{:S(2)}) copy-start(f32[2,128,256]{2,1,0:T(8,128)S(1)} %collective-permute-done.5.fa2) | copy-start | bytes 786436
  28.8 3.6 %copy-start.10 = (f32[2,128,256]{2,1,0:T(8,128)}, f32[2,128,256]{2,1,0:T(8,128)S(1)}, u32[]{:S(2)}) copy-start(f32[2,128,256]{2,1,0:T(8,128)S(1)} %collective-permute-done.4.fa1) | copy-start | bytes 786436
  28.8 3.6 %copy-start.6 = (f32[536,128]{1,0:T(8,128)}, f32[536,128]{1,0:T(8,128)S(1)}, u32[]{:S(2)}) copy-start(f32[536,128]{1,0:T(8,128)S(1)} %collective-permute-done.2.x1) | copy-start | bytes 823300
  28.9 3.6 %copy-start.4 = (f32[1048,128]{1,0:T(8,128)}, f32[1048,128]{1,0:T(8,128)S(1)}, u32[]{:S(2)}) copy-start(f32[1048,128]{1,0:T(8,128)S(1)} %collective-permute-done.3.x2) | copy-start | bytes 1609732
  28.9 3.5 %collective-permute-start.7 = (f32[1048,128]{1,0:T(8,128)S(1)}, f32[1048,128]{1,0:T(8,128)S(1)}, u32[]{:S(2)}, u32[]{:S(2)}) collective-permute-start(f32[1048,128]{1,0:T(8,128)S(1)} %collective-permute-done.3.x2), channel_id=1, source_target_pairs={{0,1},{1,0},{2,3},{3,2},{4,5},{5,4},{6,7},{7,6},{8,9},{9,8},{10,11... | collective-permute-start | bytes 1609736 | tf_op jit(solution)/shard_map/ppermute | solution.py:513
  29.0 2.3 %collective-permute-start.8 = (f32[2,128,256]{2,1,0:T(8,128)S(1)}, f32[2,128,256]{2,1,0:T(8,128)S(1)}, u32[]{:S(2)}, u32[]{:S(2)}) collective-permute-start(f32[2,128,256]{2,1,0:T(8,128)S(1)} %collective-permute-done.fa0), channel_id=1, source_target_pairs={{0,1},{1,0},{2,3},{3,2},{4,5},{5,4},{6,7},{7,6},{8,9},{9,8},{10,11... | collective-permute-start | bytes 786440 | tf_op jit(solution)/shard_map/ppermute | solution.py:513
  29.5 2.2 %collective-permute-start.9 = (f32[2,128,256]{2,1,0:T(8,128)S(1)}, f32[2,128,256]{2,1,0:T(8,128)S(1)}, u32[]{:S(2)}, u32[]{:S(2)}) collective-permute-start(f32[2,128,256]{2,1,0:T(8,128)S(1)} %collective-permute-done.4.fa1), channel_id=1, source_target_pairs={{0,1},{1,0},{2,3},{3,2},{4,5},{5,4},{6,7},{7,6},{8,9},{9,8},{10,11... | collective-permute-start | bytes 786440 | tf_op jit(solution)/shard_map/ppermute | solution.py:513
  29.5 2.5 %collective-permute-start.10 = (f32[2,128,256]{2,1,0:T(8,128)S(1)}, f32[2,128,256]{2,1,0:T(8,128)S(1)}, u32[]{:S(2)}, u32[]{:S(2)}) collective-permute-start(f32[2,128,256]{2,1,0:T(8,128)S(1)} %collective-permute-done.5.fa2), channel_id=1, source_target_pairs={{0,1},{1,0},{2,3},{3,2},{4,5},{5,4},{6,7},{7,6},{8,9},{9,8},{10,11... | collective-permute-start | bytes 786440 | tf_op jit(solution)/shard_map/ppermute | solution.py:513
  30.0 2.4 %collective-permute-start.11 = (f32[2,128,256]{2,1,0:T(8,128)S(1)}, f32[2,128,256]{2,1,0:T(8,128)S(1)}, u32[]{:S(2)}, u32[]{:S(2)}) collective-permute-start(f32[2,128,256]{2,1,0:T(8,128)S(1)} %collective-permute-done.6.fa3), channel_id=1, source_target_pairs={{0,1},{1,0},{2,3},{3,2},{4,5},{5,4},{6,7},{7,6},{8,9},{9,8},{10,11... | collective-permute-start | bytes 786440 | tf_op jit(solution)/shard_map/ppermute | solution.py:513
  31.3 1.2 copy-start.11
  31.6 0.8 copy-start.12
  32.0 0.7 copy-start.13
  32.4 0.7 copy-start.14
  32.4 0.9 copy-start.5
  55.1 3.3 %collective-permute-start.12 = (f32[16,80,256]{2,1,0:T(8,128)}, f32[16,80,256]{2,1,0:T(8,128)S(1)}, u32[]{:S(2)}, u32[]{:S(2)}) collective-permute-start(f32[16,80,256]{2,1,0:T(8,128)} %get-tuple-element.98), channel_id=1, source_target_pairs={{0,1},{1,0},{2,3},{3,2},{4,5},{5,4},{6,7},{7,6},{8,9},{9,8},{10,11... | collective-permute-start | bytes 3932168 | tf_op jit(solution)/shard_map/ppermute | solution.py:513
  60.1 9.8 %collective-permute-start.15 = (f32[2,4,40,256]{3,2,1,0:T(8,128)S(1)}, f32[2,4,40,256]{3,2,1,0:T(8,128)S(1)}, u32[]{:S(2)}, u32[]{:S(2)}) collective-permute-start(f32[2,4,40,256]{3,2,1,0:T(8,128)S(1)} %get-tuple-element.107), channel_id=1, source_target_pairs={{0,4},{1,5},{2,6},{3,7},{4,0},{5,1},{6,2},{7,3},{8,12},{9,13},{10,... | collective-permute-start | bytes 983048 | tf_op jit(solution)/shard_map/ppermute | solution.py:513
  61.6 9.9 %collective-permute-start.17 = (f32[2,4,40,256]{3,2,1,0:T(8,128)S(1)}, f32[2,4,40,256]{3,2,1,0:T(8,128)S(1)}, u32[]{:S(2)}, u32[]{:S(2)}) collective-permute-start(f32[2,4,40,256]{3,2,1,0:T(8,128)S(1)} %get-tuple-element.109), channel_id=1, source_target_pairs={{0,2},{1,3},{2,0},{3,1},{4,6},{5,7},{6,4},{7,5},{8,10},{9,11},{10,... | collective-permute-start | bytes 983048 | tf_op jit(solution)/shard_map/ppermute | solution.py:513
  69.3 8.3 %collective-permute-start.13 = (f32[2,8,64,256]{3,2,1,0:T(8,128)}, f32[2,8,64,256]{3,2,1,0:T(8,128)S(1)}, u32[]{:S(2)}, u32[]{:S(2)}) collective-permute-start(f32[2,8,64,256]{3,2,1,0:T(8,128)} %get-tuple-element.103), channel_id=1, source_target_pairs={{0,1},{1,0},{2,3},{3,2},{4,5},{5,4},{6,7},{7,6},{8,9},{9,8},{10,11... | collective-permute-start | bytes 3145736 | tf_op jit(solution)/shard_map/ppermute | solution.py:513
  69.3 8.3 %copy-start.2 = (f32[2,8,64,256]{3,2,1,0:T(8,128)S(1)}, f32[2,8,64,256]{3,2,1,0:T(8,128)}, u32[]{:S(2)}) copy-start(f32[2,8,64,256]{3,2,1,0:T(8,128)} %get-tuple-element.102) | copy-start | bytes 3145732
  69.4 8.5 %collective-permute-start.14 = (f32[2,8,64,256]{3,2,1,0:T(8,128)}, f32[2,8,64,256]{3,2,1,0:T(8,128)S(1)}, u32[]{:S(2)}, u32[]{:S(2)}) collective-permute-start(f32[2,8,64,256]{3,2,1,0:T(8,128)} %get-tuple-element.105), channel_id=1, source_target_pairs={{0,1},{1,0},{2,3},{3,2},{4,5},{5,4},{6,7},{7,6},{8,9},{9,8},{10,11... | collective-permute-start | bytes 3145736 | tf_op jit(solution)/shard_map/ppermute | solution.py:513
  70.0 6.2 %collective-permute-start.16 = (f32[4,40,256]{2,1,0:T(8,128)S(1)}, f32[4,40,256]{2,1,0:T(8,128)S(1)}, u32[]{:S(2)}, u32[]{:S(2)}) collective-permute-start(f32[4,40,256]{2,1,0:T(8,128)S(1)} %slice_bitcast_fusion.12), channel_id=1, source_target_pairs={{0,2},{1,3},{2,0},{3,1},{4,6},{5,7},{6,4},{7,5},{8,10},{9,11},{10,... | collective-permute-start | bytes 491528 | tf_op jit(solution)/shard_map/ppermute | solution.py:513
  71.6 6.0 %collective-permute-start.18 = (f32[4,40,256]{2,1,0:T(8,128)S(1)}, f32[4,40,256]{2,1,0:T(8,128)S(1)}, u32[]{:S(2)}, u32[]{:S(2)}) collective-permute-start(f32[4,40,256]{2,1,0:T(8,128)S(1)} %slice_bitcast_fusion.10), channel_id=1, source_target_pairs={{0,4},{1,5},{2,6},{3,7},{4,0},{5,1},{6,2},{7,3},{8,12},{9,13},{10,... | collective-permute-start | bytes 491528 | tf_op jit(solution)/shard_map/ppermute | solution.py:513
  77.6 1.2 copy-start.1
  79.1 5.6 %collective-permute-start.23 = (f32[80,256]{1,0:T(8,128)S(1)}, f32[80,256]{1,0:T(8,128)S(1)}, u32[]{:S(2)}, u32[]{:S(2)}) collective-permute-start(f32[80,256]{1,0:T(8,128)S(1)} %get-tuple-element.174), channel_id=1, source_target_pairs={{0,8},{1,9},{2,10},{3,11},{4,12},{5,13},{6,14},{7,15},{8,0},{9,1},... | collective-permute-start | bytes 245768 | tf_op jit(solution)/shard_map/ppermute | solution.py:513
  80.8 6.6 %collective-permute-start.25 = (f32[80,256]{1,0:T(8,128)S(1)}, f32[80,256]{1,0:T(8,128)S(1)}, u32[]{:S(2)}, u32[]{:S(2)}) collective-permute-start(f32[80,256]{1,0:T(8,128)S(1)} %get-tuple-element.175), channel_id=1, source_target_pairs={{0,24},{1,25},{2,26},{3,27},{4,28},{5,29},{6,30},{7,31},{8,16},{9,... | collective-permute-start | bytes 245768 | tf_op jit(solution)/shard_map/ppermute | solution.py:513
  83.3 6.9 %collective-permute-start.24 = (f32[80,256]{1,0:T(8,128)S(1)}, f32[80,256]{1,0:T(8,128)S(1)}, u32[]{:S(2)}, u32[]{:S(2)}) collective-permute-start(f32[80,256]{1,0:T(8,128)S(1)} %get-tuple-element.176), channel_id=1, source_target_pairs={{0,16},{1,17},{2,18},{3,19},{4,20},{5,21},{6,22},{7,23},{8,24},{9,... | collective-permute-start | bytes 245768 | tf_op jit(solution)/shard_map/ppermute | solution.py:513
  83.4 12.5 %collective-permute-start.19 = (f32[2,4,64,256]{3,2,1,0:T(8,128)S(1)}, f32[2,4,64,256]{3,2,1,0:T(8,128)S(1)}, u32[]{:S(2)}, u32[]{:S(2)}) collective-permute-start(f32[2,4,64,256]{3,2,1,0:T(8,128)S(1)} %bitcast.107), channel_id=1, source_target_pairs={{0,2},{1,3},{2,0},{3,1},{4,6},{5,7},{6,4},{7,5},{8,10},{9,11},{10,... | collective-permute-start | bytes 1572872 | tf_op jit(solution)/shard_map/ppermute | solution.py:513
  83.9 12.8 %collective-permute-start.21 = (f32[2,4,64,256]{3,2,1,0:T(8,128)S(1)}, f32[2,4,64,256]{3,2,1,0:T(8,128)S(1)}, u32[]{:S(2)}, u32[]{:S(2)}) collective-permute-start(f32[2,4,64,256]{3,2,1,0:T(8,128)S(1)} %get-tuple-element.113), channel_id=1, source_target_pairs={{0,4},{1,5},{2,6},{3,7},{4,0},{5,1},{6,2},{7,3},{8,12},{9,13},{10,... | collective-permute-start | bytes 1572872 | tf_op jit(solution)/shard_map/ppermute | solution.py:513
  91.4 7.4 %collective-permute-start.27 = (f32[80,256]{1,0:T(8,128)S(1)}, f32[80,256]{1,0:T(8,128)S(1)}, u32[]{:S(2)}, u32[]{:S(2)}) collective-permute-start(f32[80,256]{1,0:T(8,128)S(1)} %broadcast_multiply_fusion), channel_id=1, source_target_pairs={{0,16},{1,17},{2,18},{3,19},{4,20},{5,21},{6,22},{7,23},{8,24},{9,... | collective-permute-start | bytes 245768 | tf_op jit(solution)/shard_map/ppermute | solution.py:513
  92.1 6.7 %collective-permute-start.26 = (f32[80,256]{1,0:T(8,128)S(1)}, f32[80,256]{1,0:T(8,128)S(1)}, u32[]{:S(2)}, u32[]{:S(2)}) collective-permute-start(f32[80,256]{1,0:T(8,128)S(1)} %broadcast_multiply_fusion), channel_id=1, source_target_pairs={{0,8},{1,9},{2,10},{3,11},{4,12},{5,13},{6,14},{7,15},{8,0},{9,1},... | collective-permute-start | bytes 245768 | tf_op jit(solution)/shard_map/ppermute | solution.py:513
  94.5 6.2 %collective-permute-start.28 = (f32[80,256]{1,0:T(8,128)S(1)}, f32[80,256]{1,0:T(8,128)S(1)}, u32[]{:S(2)}, u32[]{:S(2)}) collective-permute-start(f32[80,256]{1,0:T(8,128)S(1)} %broadcast_multiply_fusion), channel_id=1, source_target_pairs={{0,24},{1,25},{2,26},{3,27},{4,28},{5,29},{6,30},{7,31},{8,16},{9,... | collective-permute-start | bytes 245768 | tf_op jit(solution)/shard_map/ppermute | solution.py:513
  96.0 6.9 %collective-permute-start.20 = (f32[4,64,256]{2,1,0:T(8,128)S(1)}, f32[4,64,256]{2,1,0:T(8,128)S(1)}, u32[]{:S(2)}, u32[]{:S(2)}) collective-permute-start(f32[4,64,256]{2,1,0:T(8,128)S(1)} %slice_bitcast_fusion.8), channel_id=1, source_target_pairs={{0,4},{1,5},{2,6},{3,7},{4,0},{5,1},{6,2},{7,3},{8,12},{9,13},{10,... | collective-permute-start | bytes 786440 | tf_op jit(solution)/shard_map/ppermute | solution.py:513
  96.8 6.6 %collective-permute-start.22 = (f32[4,64,256]{2,1,0:T(8,128)S(1)}, f32[4,64,256]{2,1,0:T(8,128)S(1)}, u32[]{:S(2)}, u32[]{:S(2)}) collective-permute-start(f32[4,64,256]{2,1,0:T(8,128)S(1)} %slice_bitcast_fusion.6), channel_id=1, source_target_pairs={{0,2},{1,3},{2,0},{3,1},{4,6},{5,7},{6,4},{7,5},{8,10},{9,11},{10,... | collective-permute-start | bytes 786440 | tf_op jit(solution)/shard_map/ppermute | solution.py:513
  103.5 14.0 %collective-permute-start.29 = (f32[128,256]{1,0:T(8,128)S(1)}, f32[128,256]{1,0:T(8,128)S(1)}, u32[]{:S(2)}, u32[]{:S(2)}) collective-permute-start(f32[128,256]{1,0:T(8,128)S(1)} %get-tuple-element.167), channel_id=1, source_target_pairs={{0,8},{1,9},{2,10},{3,11},{4,12},{5,13},{6,14},{7,15},{8,0},{9,1},... | collective-permute-start | bytes 393224 | tf_op jit(solution)/shard_map/ppermute | solution.py:513
  104.8 12.8 %collective-permute-start.31 = (f32[128,256]{1,0:T(8,128)S(1)}, f32[128,256]{1,0:T(8,128)S(1)}, u32[]{:S(2)}, u32[]{:S(2)}) collective-permute-start(f32[128,256]{1,0:T(8,128)S(1)} %get-tuple-element.168), channel_id=1, source_target_pairs={{0,24},{1,25},{2,26},{3,27},{4,28},{5,29},{6,30},{7,31},{8,16},{9,... | collective-permute-start | bytes 393224 | tf_op jit(solution)/shard_map/ppermute | solution.py:513
  107.3 10.3 %collective-permute-start.30 = (f32[128,256]{1,0:T(8,128)S(1)}, f32[128,256]{1,0:T(8,128)S(1)}, u32[]{:S(2)}, u32[]{:S(2)}) collective-permute-start(f32[128,256]{1,0:T(8,128)S(1)} %get-tuple-element.169), channel_id=1, source_target_pairs={{0,16},{1,17},{2,18},{3,19},{4,20},{5,21},{6,22},{7,23},{8,24},{9,... | collective-permute-start | bytes 393224 | tf_op jit(solution)/shard_map/ppermute | solution.py:513
  107.3 10.3 %collective-permute-start.33 = (f32[4,40,256]{2,1,0:T(8,128)S(1)}, f32[4,40,256]{2,1,0:T(8,128)S(1)}, u32[]{:S(2)}, u32[]{:S(2)}) collective-permute-start(f32[4,40,256]{2,1,0:T(8,128)S(1)} %get-tuple-element.172), channel_id=1, source_target_pairs={{0,4},{1,5},{2,6},{3,7},{4,0},{5,1},{6,2},{7,3},{8,12},{9,13},{10,... | collective-permute-start | bytes 491528 | tf_op jit(solution)/shard_map/ppermute | solution.py:513
  108.6 9.1 %collective-permute-start.32 = (f32[4,40,256]{2,1,0:T(8,128)S(1)}, f32[4,40,256]{2,1,0:T(8,128)S(1)}, u32[]{:S(2)}, u32[]{:S(2)}) collective-permute-start(f32[4,40,256]{2,1,0:T(8,128)S(1)} %get-tuple-element.173), channel_id=1, source_target_pairs={{0,2},{1,3},{2,0},{3,1},{4,6},{5,7},{6,4},{7,5},{8,10},{9,11},{10,... | collective-permute-start | bytes 491528 | tf_op jit(solution)/shard_map/ppermute | solution.py:513
  117.5 5.9 %copy-start.15 = (f32[512,128]{1,0:T(8,128)S(1)}, f32[512,128]{1,0:T(8,128)}, u32[]{:S(2)}) copy-start(f32[512,128]{1,0:T(8,128)} %get-tuple-element.129) | copy-start | bytes 786436
  117.7 4.7 %collective-permute-start.39 = (f32[1024,128]{1,0:T(8,128)}, f32[1024,128]{1,0:T(8,128)S(1)}, u32[]{:S(2)}, u32[]{:S(2)}) collective-permute-start(f32[1024,128]{1,0:T(8,128)} %get-tuple-element.130), channel_id=1, source_target_pairs={{0,1},{1,0},{2,3},{3,2},{4,5},{5,4},{6,7},{7,6},{8,9},{9,8},{10,11... | collective-permute-start | bytes 1572872 | tf_op jit(solution)/shard_map/ppermute | solution.py:513
  117.8 16.6 %collective-permute-start.37 = (f32[2,4,40,256]{3,2,1,0:T(8,128)S(1)}, f32[2,4,40,256]{3,2,1,0:T(8,128)S(1)}, u32[]{:S(2)}, u32[]{:S(2)}) collective-permute-start(f32[2,4,40,256]{3,2,1,0:T(8,128)S(1)} %pad_maximum_fusion.6.a0), channel_id=1, source_target_pairs={{0,4},{1,5},{2,6},{3,7},{4,0},{5,1},{6,2},{7,3},{8,12},{9,13},{10,... | collective-permute-start | bytes 983048 | tf_op jit(solution)/shard_map/ppermute | solution.py:513
  119.0 15.4 %collective-permute-start.38 = (f32[2,4,40,256]{3,2,1,0:T(8,128)S(1)}, f32[2,4,40,256]{3,2,1,0:T(8,128)S(1)}, u32[]{:S(2)}, u32[]{:S(2)}) collective-permute-start(f32[2,4,40,256]{3,2,1,0:T(8,128)S(1)} %pad_maximum_fusion.7.a1), channel_id=1, source_target_pairs={{0,2},{1,3},{2,0},{3,1},{4,6},{5,7},{6,4},{7,5},{8,10},{9,11},{10,... | collective-permute-start | bytes 983048 | tf_op jit(solution)/shard_map/ppermute | solution.py:513
  119.0 8.2 %collective-permute-start.36 = (f32[128,256]{1,0:T(8,128)S(1)}, f32[128,256]{1,0:T(8,128)S(1)}, u32[]{:S(2)}, u32[]{:S(2)}) collective-permute-start(f32[128,256]{1,0:T(8,128)S(1)} %fusion.6.a0), channel_id=1, source_target_pairs={{0,24},{1,25},{2,26},{3,27},{4,28},{5,29},{6,30},{7,31},{8,16},{9,... | collective-permute-start | bytes 393224 | tf_op jit(solution)/shard_map/ppermute | solution.py:513
  121.1 13.3 %collective-permute-start.35 = (f32[128,256]{1,0:T(8,128)S(1)}, f32[128,256]{1,0:T(8,128)S(1)}, u32[]{:S(2)}, u32[]{:S(2)}) collective-permute-start(f32[128,256]{1,0:T(8,128)S(1)} %fusion.6.a0), channel_id=1, source_target_pairs={{0,16},{1,17},{2,18},{3,19},{4,20},{5,21},{6,22},{7,23},{8,24},{9,... | collective-permute-start | bytes 393224 | tf_op jit(solution)/shard_map/ppermute | solution.py:513
  122.4 12.0 %collective-permute-start.34 = (f32[128,256]{1,0:T(8,128)S(1)}, f32[128,256]{1,0:T(8,128)S(1)}, u32[]{:S(2)}, u32[]{:S(2)}) collective-permute-start(f32[128,256]{1,0:T(8,128)S(1)} %fusion.6.a0), channel_id=1, source_target_pairs={{0,8},{1,9},{2,10},{3,11},{4,12},{5,13},{6,14},{7,15},{8,0},{9,1},... | collective-permute-start | bytes 393224 | tf_op jit(solution)/shard_map/ppermute | solution.py:513
  134.4 3.4 %collective-permute-start.40 = (f32[2,4,40,256]{3,2,1,0:T(8,128)S(1)}, f32[2,4,40,256]{3,2,1,0:T(8,128)S(1)}, u32[]{:S(2)}, u32[]{:S(2)}) collective-permute-start(f32[2,4,40,256]{3,2,1,0:T(8,128)S(1)} %pad_maximum_fusion.6.a0), channel_id=1, source_target_pairs={{0,1},{1,0},{2,3},{3,2},{4,5},{5,4},{6,7},{7,6},{8,9},{9,8},{10,11... | collective-permute-start | bytes 983048 | tf_op jit(solution)/shard_map/ppermute | solution.py:513
  134.5 14.3 %collective-permute-start.44 = (f32[1024,128]{1,0:T(8,128)S(1)}, f32[1024,128]{1,0:T(8,128)S(1)}, u32[]{:S(2)}, u32[]{:S(2)}) collective-permute-start(f32[1024,128]{1,0:T(8,128)S(1)} %pad_maximum_fusion.2), channel_id=1, source_target_pairs={{0,2},{1,3},{2,0},{3,1},{4,6},{5,7},{6,4},{7,5},{8,10},{9,11},{10,... | collective-permute-start | bytes 1572872 | tf_op jit(solution)/shard_map/ppermute | solution.py:513
  136.3 14.1 %collective-permute-start.45 = (f32[4,128,256]{2,1,0:T(8,128)S(1)}, f32[4,128,256]{2,1,0:T(8,128)S(1)}, u32[]{:S(2)}, u32[]{:S(2)}) collective-permute-start(f32[4,128,256]{2,1,0:T(8,128)S(1)} %pad_maximum_fusion.3), channel_id=1, source_target_pairs={{0,4},{1,5},{2,6},{3,7},{4,0},{5,1},{6,2},{7,3},{8,12},{9,13},{10,... | collective-permute-start | bytes 1572872 | tf_op jit(solution)/shard_map/ppermute | solution.py:513
  137.2 1.6 %collective-permute-start.41 = (f32[2,4,40,256]{3,2,1,0:T(8,128)S(1)}, f32[2,4,40,256]{3,2,1,0:T(8,128)S(1)}, u32[]{:S(2)}, u32[]{:S(2)}) collective-permute-start(f32[2,4,40,256]{3,2,1,0:T(8,128)S(1)} %pad_maximum_fusion.7.a1), channel_id=1, source_target_pairs={{0,1},{1,0},{2,3},{3,2},{4,5},{5,4},{6,7},{7,6},{8,9},{9,8},{10,11... | collective-permute-start | bytes 983048 | tf_op jit(solution)/shard_map/ppermute | solution.py:513
  137.2 2.1 %collective-permute-start.42 = (f32[2,4,40,256]{3,2,1,0:T(8,128)S(1)}, f32[2,4,40,256]{3,2,1,0:T(8,128)S(1)}, u32[]{:S(2)}, u32[]{:S(2)}) collective-permute-start(f32[2,4,40,256]{3,2,1,0:T(8,128)S(1)} %collective-permute-done.37.a2), channel_id=1, source_target_pairs={{0,1},{1,0},{2,3},{3,2},{4,5},{5,4},{6,7},{7,6},{8,9},{9,8},{10,11... | collective-permute-start | bytes 983048 | tf_op jit(solution)/shard_map/ppermute | solution.py:513
  137.7 2.1 %collective-permute-start.43 = (f32[2,4,40,256]{3,2,1,0:T(8,128)S(1)}, f32[2,4,40,256]{3,2,1,0:T(8,128)S(1)}, u32[]{:S(2)}, u32[]{:S(2)}) collective-permute-start(f32[2,4,40,256]{3,2,1,0:T(8,128)S(1)} %collective-permute-done.38.a3), channel_id=1, source_target_pairs={{0,1},{1,0},{2,3},{3,2},{4,5},{5,4},{6,7},{7,6},{8,9},{9,8},{10,11... | collective-permute-start | bytes 983048 | tf_op jit(solution)/shard_map/ppermute | solution.py:513
  137.8 11.0 %copy-start = (f32[512,128]{1,0:T(8,128)S(1)}, f32[512,128]{1,0:T(8,128)}, u32[]{:S(2)}) copy-start(f32[512,128]{1,0:T(8,128)} %get-tuple-element.136.g0) | copy-start | bytes 786436

commit v4 on v3

--- a/solution.py
+++ b/solution.py
@@ -13,6 +13,7 @@
 DENSITY = 0.3989422804014327
 VMEM = pltpu.VMEM
 PARAMS = pltpu.CompilerParams(vmem_limit_bytes=58 * 1024 * 1024)
+MEDIUM = pltpu.CompilerParams(vmem_limit_bytes=24 * 1024 * 1024)
 SMALL = pltpu.CompilerParams(vmem_limit_bytes=12 * 1024 * 1024)
 NN, TN, NT = (1, 0), (0, 0), (1, 1)
 
@@ -66,20 +67,18 @@
     xt_low_out,
     gf_high_out,
     gf_low_out,
-    w_high_out,
-    w_low_out,
     gate_all,
     glog_out,
     s_keep,
     s_send,
-    w_in,
+    x_in,
+    near_in,
+    far_in,
     w2_in,
     xt_high,
     xt_low,
     gf_high,
     gf_low,
-    w_high,
-    w_low,
     hid_high,
     hid_low,
     slope,
@@ -92,6 +91,7 @@
     ggate,
     scores,
     targets,
+    tower_rows,
     summed,
     rest,
     sems,
@@ -107,26 +107,34 @@
     quarter = experts // 4
     order = [(r ^ corner) * quarter + i for r in range(4) for i in range(quarter)]
 
-    loads = []
-    for n, e in enumerate(order):
-        far_a, far_b = ((fa0, fb0), (fa1, fb1), (fa2, fb2), (fa3, fb3))[n // quarter]
-        sources = (near0.at[e], near1.at[e], far_a.at[n % quarter], far_b.at[n % quarter])
-        for k, source in enumerate(sources):
-            target = w_in.at[n, k * cols : (k + 1) * cols]
-            loads.append(pltpu.make_async_copy(source, target, sems.at[5 * n + k]))
-        loads.append(pltpu.make_async_copy(w_second.at[e], w2_in.at[n], sems.at[5 * n + 4]))
-    for load in loads:
+    loads = [
+        pltpu.make_async_copy(near0, near_in.at[:, 0:cols], sems.at[0]),
+        pltpu.make_async_copy(near1, near_in.at[:, cols : 2 * cols], sems.at[1]),
+        pltpu.make_async_copy(w_second, w2_in, sems.at[2]),
+    ]
+    for r, (far_a, far_b) in enumerate(((fa0, fb0), (fa1, fb1), (fa2, fb2), (fa3, fb3))):
+        target = far_in.at[r * quarter : (r + 1) * quarter]
+        loads.append(pltpu.make_async_copy(far_a, target.at[:, 0:cols], sems.at[3 + 2 * r]))
+        loads.append(pltpu.make_async_copy(far_b, target.at[:, cols : 2 * cols], sems.at[4 + 2 * r]))
+    x_loads = [
+        pltpu.make_async_copy(x0, x_in.at[0, 0:rows], sems.at[11]),
+        pltpu.make_async_copy(x1, x_in.at[1], sems.at[12]),
+        pltpu.make_async_copy(x2.at[0:rows], x_in.at[2, 0:rows], sems.at[13]),
+        pltpu.make_async_copy(x2.at[2 * rows :], x_in.at[2, rows:], sems.at[14]),
+        pltpu.make_async_copy(x3.at[rows:], x_in.at[3], sems.at[15]),
+    ]
+    for load in x_loads + loads:
         load.start()
 
     wide = tasks * experts
-    starts = (0, 0, 0, rows)
-    gate_starts = (0, rows, 2 * rows, 2 * rows)
-    for k, ref in enumerate((x0, x1, x2, x3)):
+    for copy in x_loads:
+        copy.wait()
+    for k, ref in enumerate((x_in.at[0], x_in.at[1], x_in.at[2], x_in.at[3])):
         block = slice(k * cols, (k + 1) * cols)
-        high, low = split(ref[starts[k] : starts[k] + rows, :].T)
+        high, low = split(ref[0:rows, :].T)
         xt_high[block, :] = high
         xt_low[block, :] = low
-        gate_all[:, block] = gate_rows[...] if k == 0 else ref[gate_starts[k] : gate_starts[k] + wide, :]
+        gate_all[:, block] = gate_rows[...] if k == 0 else ref[rows : rows + wide, :]
     hot = lax.broadcasted_iota(jnp.int32, (domains, rows), 0) == domain[pl.ds(field, 1), :]
     onehot = jnp.where(hot, 1.0, 0.0).astype(BF16)
     bias_high, bias_low = split(gate_bias[...])
@@ -143,19 +151,18 @@
         bias_rows[experts + n : experts + n + 1, :] = b_second[pl.ds(e, 1), :]
     targets[...] = jnp.zeros_like(targets)
     targets[0:tasks, :] = labels[:, pl.ds(pl.multiple_of(field * rows, 128), rows)].astype(F32)
-    mix[...] = jnp.zeros_like(mix)
     bias_cols = bias_rows[...].T
     rest[...] = jnp.zeros_like(rest)
-    eye = lax.broadcasted_iota(jnp.int32, (tasks, tower), 0) == lax.broadcasted_iota(jnp.int32, (tasks, tower), 1)
-    eye = jnp.where(eye, 1.0, 0.0)
-    tb_in = lax.dot_general(t_bias[...], eye, (((0,), (0,)), ((), ())), precision=lax.Precision.HIGHEST)
-    to_in = lax.dot_general(t_out[...], eye, (((0,), (0,)), ((), ())), precision=lax.Precision.HIGHEST)
+    tower_rows[...] = jnp.zeros_like(tower_rows)
+    tower_rows[0:tasks, :] = t_bias[...]
+    tower_rows[tasks : 2 * tasks, :] = t_out[...]
+    tower_cols = tower_rows[...].T
     for load in loads:
         load.wait()
 
     def first_layer(n):
-        weight = split(w_in[n])
-        w_high[n], w_low[n] = weight
+        e = order[n]
+        weight = split(jnp.concatenate([near_in[e], far_in[n]], axis=0))
         return dot3(weight, (xt_high[...], xt_low[...]), TN)
 
     pre = first_layer(0)
@@ -167,10 +174,14 @@
             slope[n] = steep
         if n > 0:
             at = experts + n - 1
-            result = dot3(split(w2_in[n - 1]), value, TN) + bias_cols[:, at : at + 1]
+            result = dot3(split(w2_in[order[n - 1]]), value, TN) + bias_cols[:, at : at + 1]
             e_out[n - 1] = result
-            for k in range(tasks):
-                mix[k] += gates[k * experts + n - 1 : k * experts + n, :] * result
+            if n % 4 == 0:
+                for k in range(tasks):
+                    part = gates[k * experts + n - 1 : k * experts + n, :] * result
+                    for m in range(n - 4, n - 1):
+                        part = part + gates[k * experts + m : k * experts + m + 1, :] * e_out[m]
+                    mix[k] = part if n == 4 else mix[k] + part
         if n < experts:
             value = split(raw)
             hid_high[n], hid_low[n] = value
@@ -180,9 +191,6 @@
         pltpu.make_async_copy(xt_high, xt_high_out, sems.at[0]),
         pltpu.make_async_copy(xt_low, xt_low_out, sems.at[1]),
     ]
-    for n, e in enumerate(order):
-        stores.append(pltpu.make_async_copy(w_high.at[n], w_high_out.at[e], sems.at[2 + 2 * n]))
-        stores.append(pltpu.make_async_copy(w_low.at[n], w_low_out.at[e], sems.at[3 + 2 * n]))
     for store in stores:
         store.start()
 
@@ -195,8 +203,8 @@
     for k in range(tasks):
         mixed.append(split(mix[k]))
         weights.append(split(t_first[k]))
-        value, steep = gelu_parts(dot3(weights[k], mixed[k], TN) + tb_in[:, k : k + 1])
-        out_column = to_in[:, k : k + 1]
+        value, steep = gelu_parts(dot3(weights[k], mixed[k], TN) + tower_cols[:, k : k + 1])
+        out_column = tower_cols[:, tasks + k : tasks + k + 1]
         scores[k : k + 1, :] = jnp.sum(value * out_column, axis=0, keepdims=True) + out_bias[k]
         acts.append(value)
         steeps.append(out_column * steep)
@@ -241,23 +249,24 @@
         for i in range(4):
             slot = (4 * e + i) ^ me
             summed[slot, 0:piece, :] = gweight[i * piece : (i + 1) * piece]
-        gfirst = dot3(split(w2_in[n]), total, NN) * slope[n]
+        gfirst = dot3(split(w2_in[e]), total, NN) * slope[n]
         b1_sums.append(jnp.sum(gfirst, axis=1, keepdims=True))
         high, low = split(gfirst)
-        gf_high[n] = high
-        gf_low[n] = low
-        grads.append(pltpu.make_async_copy(gf_high.at[n], gf_high_out.at[e], sems.at[20 + 2 * n]))
-        grads.append(pltpu.make_async_copy(gf_low.at[n], gf_low_out.at[e], sems.at[21 + 2 * n]))
-        if n % 2 == 1:
-            for copy in grads[-4:]:
-                copy.start()
+        gf_high[e] = high
+        gf_low[e] = low
+        if n % 4 == 3:
+            half = pl.ds(((corner >> 1) ^ (n // 4)) * 4, 4)
+            grads.append(pltpu.make_async_copy(gf_high.at[half], gf_high_out.at[half], sems.at[4 + n // 2]))
+            grads.append(pltpu.make_async_copy(gf_low.at[half], gf_low_out.at[half], sems.at[5 + n // 2]))
+            grads[-2].start()
+            grads[-1].start()
 
     piece = hidden // 4
     last = [
-        pltpu.make_async_copy(summed.at[16:32, 0:piece], s_send.at[:, 0:piece], sems.at[36]),
-        pltpu.make_async_copy(summed.at[0:16, 0:piece], s_keep.at[:, 0:piece], sems.at[37]),
-        pltpu.make_async_copy(summed.at[16:32, piece:], s_send.at[:, piece:], sems.at[38]),
-        pltpu.make_async_copy(summed.at[0:16, piece:], s_keep.at[:, piece:], sems.at[39]),
+        pltpu.make_async_copy(summed.at[16:32, 0:piece], s_send.at[:, 0:piece], sems.at[8]),
+        pltpu.make_async_copy(summed.at[0:16, 0:piece], s_keep.at[:, 0:piece], sems.at[9]),
+        pltpu.make_async_copy(summed.at[16:32, piece:], s_send.at[:, piece:], sems.at[10]),
+        pltpu.make_async_copy(summed.at[0:16, piece:], s_keep.at[:, piece:], sems.at[11]),
     ]
     last[0].start()
     last[1].start()
@@ -327,61 +336,95 @@
     send,
     sems,
 ):
-    experts, cols = keep.shape[0], keep.shape[2]
+    experts, cols = keep.shape[1], keep.shape[2]
+    half = experts // 2
+    first_part, second_part = slice(0, half), slice(half, experts)
     loads = [
         pltpu.make_async_copy(xt_high_in, xt_high, sems.at[0]),
         pltpu.make_async_copy(xt_low_in, xt_low, sems.at[1]),
+        pltpu.make_async_copy(gf_high_in.at[first_part], gf_high.at[first_part], sems.at[2]),
+        pltpu.make_async_copy(gf_low_in.at[first_part], gf_low.at[first_part], sems.at[3]),
+        pltpu.make_async_copy(gf_high_in.at[second_part], gf_high.at[second_part], sems.at[4]),
+        pltpu.make_async_copy(gf_low_in.at[second_part], gf_low.at[second_part], sems.at[5]),
     ]
-    for n in range(experts):
-        loads.append(pltpu.make_async_copy(gf_high_in.at[n], gf_high.at[n], sems.at[2 + 2 * n]))
-        loads.append(pltpu.make_async_copy(gf_low_in.at[n], gf_low.at[n], sems.at[3 + 2 * n]))
     for copy in loads:
         copy.start()
-    for copy in loads[0:2]:
+    for copy in loads[0:4]:
         copy.wait()
     stores = []
     for n in range(experts):
-        if n % 2 == 0:
-            for copy in loads[2 + 2 * n : 6 + 2 * n]:
+        if n == half:
+            for copy in loads[4:6]:
                 copy.wait()
         gweight = dot3((xt_high[...], xt_low[...]), (gf_high[n], gf_low[n]), NT)
         slot = n ^ place[0]
         for k in range(4):
-            held, outs = ((keep, (keep_a, keep_b)), (send, (send_a, send_b)))[k % 2]
-            held[n, k // 2] = gweight[k * cols : (k + 1) * cols]
-            for h, out in enumerate(outs):
-                at = sems.at[2 + 2 * experts + 8 * n + 2 * k + h]
-                part = held.at[n, k // 2, h * (cols // 2) : (h + 1) * (cols // 2)]
-                stores.append(pltpu.make_async_copy(part, out.at[k // 2, slot], at))
-        if n % 2 == 1:
-            for copy in stores[-16:]:
-                copy.start()
+            held = (keep, send)[k % 2]
+            held[k // 2, slot] = gweight[k * cols : (k + 1) * cols]
+        if n % half == half - 1:
+            done = pl.ds(((place[0] >> 2) ^ (n // half)) * half, half)
+            lower, upper = slice(0, cols // 2), slice(cols // 2, cols)
+            pairs = ((send, send_a, lower), (send, send_b, upper), (keep, keep_a, lower), (keep, keep_b, upper))
+            for held, out, part in pairs:
+                at = sems.at[6 + len(stores)]
+                stores.append(pltpu.make_async_copy(held.at[:, done, part], out.at[:, done], at))
+                stores[-1].start()
     for copy in stores:
         copy.wait()
 
 
 def inputs_kernel(
-    gate_all, glog, gf_high_in, gf_low_in, w_high_in, w_low_in, g0, gc, gy, gf_high, gf_low, w_high, w_low, total, sems
+    place,
+    gate_all,
+    glog,
+    gf_high_in,
+    gf_low_in,
+    near0,
+    near1,
+    fa0,
+    fa1,
+    fa2,
+    fa3,
+    fb0,
+    fb1,
+    fb2,
+    fb3,
+    g0,
+    g1,
+    g2,
+    g3,
+    gf_high,
+    gf_low,
+    near_in,
+    far_in,
+    total,
+    sems,
 ):
     experts = gf_high.shape[0]
     rows, cols = g0.shape
-    loads = []
-    sources = ((gf_high_in, gf_high), (gf_low_in, gf_low), (w_high_in, w_high), (w_low_in, w_low))
-    for n in range(experts):
-        for m, (source, target) in enumerate(sources):
-            loads.append(pltpu.make_async_copy(source.at[n], target.at[n], sems.at[4 * n + m]))
+    quarter = experts // 4
+    corner = place[4]
+    order = [(r ^ corner) * quarter + i for r in range(4) for i in range(quarter)]
+    loads = [
+        pltpu.make_async_copy(gf_high_in, gf_high, sems.at[0]),
+        pltpu.make_async_copy(gf_low_in, gf_low, sems.at[1]),
+        pltpu.make_async_copy(near0, near_in.at[:, 0:cols], sems.at[2]),
+        pltpu.make_async_copy(near1, near_in.at[:, cols : 2 * cols], sems.at[3]),
+    ]
+    for r, (far_a, far_b) in enumerate(((fa0, fb0), (fa1, fb1), (fa2, fb2), (fa3, fb3))):
+        target = far_in.at[r * quarter : (r + 1) * quarter]
+        loads.append(pltpu.make_async_copy(far_a, target.at[:, 0:cols], sems.at[4 + 2 * r]))
+        loads.append(pltpu.make_async_copy(far_b, target.at[:, cols : 2 * cols], sems.at[5 + 2 * r]))
     for copy in loads:
         copy.start()
     total[...] = dot3(split(gate_all[...]), split(glog[...]), TN)
-    for n in range(experts):
-        if n % 2 == 0:
-            for copy in loads[4 * n : 4 * n + 8]:
-                copy.wait()
-        total[...] += dot3((w_high[n], w_low[n]), (gf_high[n], gf_low[n]), NN)
-    g0[...] = total[0:cols, :].T
-    gc[0:rows, :] = total[cols : 2 * cols, :].T
-    gc[rows:, :] = total[3 * cols :, :].T
-    gy[...] = total[2 * cols : 3 * cols, :].T
+    for copy in loads:
+        copy.wait()
+    for n, e in enumerate(order):
+        weight = split(jnp.concatenate([near_in[e], far_in[n]], axis=0))
+        total[...] += dot3(weight, (gf_high[e], gf_low[e]), NN)
+    for k, ref in enumerate((g0, g1, g2, g3)):
+        ref[...] = total[k * cols : (k + 1) * cols, :].T
 
 
 def finish_second_kernel(
@@ -449,12 +492,11 @@
         copy.wait()
 
 
-def finish_inputs_kernel(place, factor, g0, gc, gy, out):
+def finish_inputs_kernel(place, factor, g0, g1, g2, g3, out):
     field = place[0]
     rows = g0.shape[0]
-    for k, ref in enumerate((g0, gc, gy, gy)):
-        at = rows if k == 3 else 0
-        out[pl.ds(pl.multiple_of((field ^ k) * rows, 8), rows), :] = ref[at : at + rows, :] * factor[...]
+    for k, ref in enumerate((g0, g1, g2, g3)):
+        out[pl.ds(pl.multiple_of((field ^ k) * rows, 8), rows), :] = ref[...] * factor[...]
 
 
 def whole():
@@ -559,29 +601,28 @@
             like((4 * cols, rows), BF16),
             like((experts, hidden, rows), BF16),
             like((experts, hidden, rows), BF16),
-            like((experts, 4 * cols, hidden), BF16),
-            like((experts, 4 * cols, hidden), BF16),
             like((units, 4 * cols)),
             like((units, rows)),
             like((16, 80, width)),
             like((16, 80, width)),
         ),
         in_specs=[scalars()] * 2
-        + [whole()] * 5
+        + [anywhere()] * 4
+        + [whole()]
         + [anywhere()] * 10
         + [whole()] * 4
         + [anywhere()]
         + [whole()] * 4,
-        out_specs=[anywhere()] * 6 + [whole()] * 2 + [anywhere()] * 2,
+        out_specs=[anywhere()] * 4 + [whole()] * 2 + [anywhere()] * 2,
         scratch_shapes=[
-            VMEM((experts, 4 * cols, hidden), F32),
+            VMEM((4, rows + units, cols), F32),
+            VMEM((experts, 2 * cols, hidden), F32),
+            VMEM((experts, 2 * cols, hidden), F32),
             VMEM((experts, hidden, width), F32),
             VMEM((4 * cols, rows), BF16),
             VMEM((4 * cols, rows), BF16),
             VMEM((experts, hidden, rows), BF16),
             VMEM((experts, hidden, rows), BF16),
-            VMEM((experts, 4 * cols, hidden), BF16),
-            VMEM((experts, 4 * cols, hidden), BF16),
             VMEM((experts, hidden, rows), BF16),
             VMEM((experts, hidden, rows), BF16),
             VMEM((experts, hidden, rows), F32),
@@ -594,9 +635,10 @@
             VMEM((units, rows), F32),
             VMEM((8, rows), F32),
             VMEM((8, rows), F32),
+            VMEM((8, tower), F32),
             VMEM((32, 80, width), F32),
             VMEM((480, width), F32),
-            pltpu.SemaphoreType.DMA((5 * experts,)),
+            pltpu.SemaphoreType.DMA((16,)),
         ],
         compiler_params=PARAMS,
     )(
@@ -621,7 +663,7 @@
         tower_bias,
         tower_out,
     )
-    xt_high, xt_low, gf_high, gf_low, w_high, w_low, gate_all, glog, s_keep, s_send = outs
+    xt_high, xt_low, gf_high, gf_low, gate_all, glog, s_keep, s_send = outs
 
     place3 = me3.reshape(1)
     cheap = pl.CostEstimate(flops=0, bytes_accessed=1 << 20, transcendentals=0)
@@ -648,9 +690,9 @@
             VMEM((4 * cols, rows), BF16),
             VMEM((experts, hidden, rows), BF16),
             VMEM((experts, hidden, rows), BF16),
-            VMEM((experts, 2, cols, hidden), F32),
-            VMEM((experts, 2, cols, hidden), F32),
-            pltpu.SemaphoreType.DMA((10 * experts + 2,)),
+            VMEM((2, experts, cols, hidden), F32),
+            VMEM((2, experts, cols, hidden), F32),
+            pltpu.SemaphoreType.DMA((14,)),
         ],
         compiler_params=PARAMS,
         cost_estimate=cheap,
@@ -678,38 +720,39 @@
     w_mine = jnp.concatenate([wa + wa_got, wb + wb_got], axis=1)
     w_mine, s_line, gf_low = lax.optimization_barrier((w_mine, s_line, gf_low))
 
-    g0, gc, gy = pl.pallas_call(
+    g0, g1, g2, g3 = pl.pallas_call(
         inputs_kernel,
         name="inputs",
-        out_shape=(like((rows, cols)), like((2 * rows, cols)), like((rows, cols))),
-        in_specs=[whole()] * 2 + [anywhere()] * 4,
-        out_specs=[whole()] * 3,
+        out_shape=tuple(like((rows, cols)) for _ in range(4)),
+        in_specs=[scalars()] + [whole()] * 2 + [anywhere()] * 12,
+        out_specs=[whole()] * 4,
         scratch_shapes=[
             VMEM((experts, hidden, rows), BF16),
             VMEM((experts, hidden, rows), BF16),
-            VMEM((experts, 4 * cols, hidden), BF16),
-            VMEM((experts, 4 * cols, hidden), BF16),
+            VMEM((experts, 2 * cols, hidden), F32),
+            VMEM((experts, 2 * cols, hidden), F32),
             VMEM((4 * cols, rows), F32),
-            pltpu.SemaphoreType.DMA((4 * experts,)),
+            pltpu.SemaphoreType.DMA((12,)),
         ],
-        compiler_params=PARAMS,
+        compiler_params=MEDIUM,
         cost_estimate=cheap,
-    )(gate_all, glog, gf_high, gf_low, w_high, w_low)
+    )(place, gate_all, glog, gf_high, gf_low, w_first, near, *far_a, *far_b)
     w_got = [move(w_mine[z], 2 * z, 0) for z in (1, 2, 3)]
     sa, sb = s_line[:, 0:40], s_line[:, 40:80]
     sa = jnp.stack([sa, move(sa, 0, 2)])
     sb = jnp.stack([sb, move(sb, 1, 0)])
     w_piece = over_rest(w_mine[0] + w_got[0] + w_got[1] + w_got[2]) * factor
-    w_piece, sa, sb, g0, gc, gy = lax.optimization_barrier((w_piece, sa, sb, g0, gc, gy))
-
-    gc = move(gc, 0, 1)
+    w_piece, sa, sb, g0, g1, g2, g3 = lax.optimization_barrier((w_piece, sa, sb, g0, g1, g2, g3))
+
+    g1 = move(g1, 0, 1)
     w_line = [w_piece] + [move(w_piece, 2 * z, 0) for z in (1, 2, 3)]
     s_near = [sa, sb, move(sa, 1, 0), move(sb, 0, 2)]
-    gy = jnp.concatenate([gy, gc[rows:]], axis=0)
-    w_line, s_near, gy = lax.optimization_barrier((w_line, s_near, gy))
+    tick = move(w_line[1][0:8] + w_line[2][0:8] + w_line[3][0:8], 0, 1)
+    s_near, g2, g3, tick = lax.optimization_barrier((s_near, g2, g3, tick))
 
     w_other = move(jnp.stack(w_line), 1, 0)
-    gy = move(gy, 0, 2)
+    g2 = move(g2, 0, 2)
+    g3 = move(g3, 0, 3)
     s_far = [move(part, 0, 1) for part in s_near]
 
     seconds = pl.pallas_call(
@@ -739,10 +782,10 @@
         finish_inputs_kernel,
         name="finish_inputs",
         out_shape=like((all_rows, cols)),
-        in_specs=[scalars()] + [whole()] * 4,
+        in_specs=[scalars()] + [whole()] * 5,
         out_specs=whole(),
         compiler_params=SMALL,
-    )(field.reshape(1), factor, g0, gc, gy)
+    )(field.reshape(1), factor, g0, g1, g2, g3)
 
     begun = pl.pallas_call(
         place_near_kernel,

time: 152 us -> 144 us (0.947)
  waiting for transfers between devices: 56 us -> 50 us
  Pallas kernels: 41.4 us -> 38.4 us
    ppermute x46 -> x47, waiting for transfers between devices: 56 us -> 50 us  [move(): return lax.ppermute(value, ('dp', 'field'), pairs)]
    pallas_call x1, Pallas kernels: 7.25 us -> 5.56 us  [per_device(): pl.pallas_call(inputs_kernel, name='inputs', out_shape=tuple((like((rows,...]
    ppermute x46 -> x47, starting transfers between devices: 41.7 us -> 42.6 us  [move(): return lax.ppermute(value, ('dp', 'field'), pairs)]
  transfers between devices with their start and end apart: 46 -> 47, of which waited for: 24 -> 22; matrix products, arithmetic and copies ran while one was open for 4% -> 4% of each run, Pallas kernels for 12% -> 12%
where the time goes in v4:
time: 144 us
  waiting for transfers between devices  50 us (35%)
  starting transfers between devices  42.6 us (30%)
  Pallas kernels  38.4 us (27%)
  local copies, waits for them, and re-layouts  7.1 us (5%)
  between operations  2.85 us (2%)
  other arithmetic  2.55 us (2%)
    ppermute x47, waiting for transfers between devices, move(): return lax.ppermute(value, ('dp', 'field'), pairs)  50 us
    ppermute x47, starting transfers between devices, move(): return lax.ppermute(value, ('dp', 'field'), pairs)  42.6 us
    pallas_call x1, Pallas kernels, per_device(): pl.pallas_call(middle_kernel, name='middle', out_shape=(like((4 * cols, r...  20.7 us
    pallas_call x1, Pallas kernels, per_device(): pl.pallas_call(first_kernel, name='first', out_shape=tuple((like((2, 8, c...  7.04 us
    pallas_call x1, Pallas kernels, per_device(): pl.pallas_call(inputs_kernel, name='inputs', out_shape=tuple((like((rows,...  5.56 us
  transfers between devices with their start and end apart: 47, of which 22 were waited for; matrix products, arithmetic and copies ran while one was open for 4% of the time, Pallas kernels for 12%

profile of v4, /device:TPU:0, one launch (start us, length us, event | category | flops | bytes accessed | tf_op | source)
XLA Modules:
  0.0 143.5 jit_solution(16552391054296049357)
XLA Ops:
  0.6 0.5 collective-permute-start.1
  1.2 1.0 constant_dynamic-slice_fusion.4
  2.1 2.6 %collective-permute-start = (f32[2,128,256]{2,1,0:T(8,128)S(1)}, f32[2,128,256]{2,1,0:T(8,128)S(1)}, u32[]{:S(2)}, u32[]{:S(2)}) collective-permute-start(f32[2,128,256]{2,1,0:T(8,128)S(1)} %constant_dynamic-slice_fusion.4), channel_id=1, source_target_pairs={{0,2},{1,3},{2,0},{3,1},{4,6},{5,7},{6,4},{7,5},{8,10},{9,11},{10,... | collective-permute-start | bytes 786440 | tf_op jit(solution)/shard_map/ppermute | solution.py:555
  4.8 2.0 %constant_dynamic-slice_fusion = (f32[512,128]{1,0:T(8,128)}, f32[512,128]{1,0:T(8,128)S(1)}, f32[512,128]{1,0:T(8,128)S(1)}, f32[512,128]{1,0:T(8,128)S(1)}) fusion(f32[2048,128]{1,0:T(8,128)} %param.14, s32[]{:T(128)S(6)} %select_n.19, s32[]{:T(128)S(6)} %select_n.17, s32[]{:T(128)S(6)} %select_n.16, s32[]{:T(128)S(6)} %select_n.18), kind=kLoop, calls=%fused_computation.42 | loop fusion | bytes 2097168 | tf_op jit(solution)/shard_map/dynamic_slice | solution.py:576
  7.4 0.6 reshape.52.domain
  8.0 0.6 stack.73.place
  8.7 3.1 %collective-permute-done.fa0 = f32[2,128,256]{2,1,0:T(8,128)S(1)} collective-permute-done((f32[2,128,256]{2,1,0:T(8,128)S(1)}, f32[2,128,256]{2,1,0:T(8,128)S(1)}, u32[]{:S(2)}, u32[]{:S(2)}) %collective-permute-start) | collective-permute-done | bytes 262176 | tf_op jit(solution)/shard_map/ppermute | solution.py:555
  11.7 1.8 %collective-permute-start.3 = (f32[1048,128]{1,0:T(8,128)S(1)}, f32[1048,128]{1,0:T(8,128)S(1)}, u32[]{:S(2)}, u32[]{:S(2)}) collective-permute-start(f32[1048,128]{1,0:T(8,128)S(1)} %pad_maximum_fusion), channel_id=1, source_target_pairs={{0,2},{1,3},{2,0},{3,1},{4,6},{5,7},{6,4},{7,5},{8,10},{9,11},{10,... | collective-permute-start | bytes 1609736 | tf_op jit(solution)/shard_map/ppermute | solution.py:555
  13.5 2.5 %collective-permute-start.6 = (f32[2,128,256]{2,1,0:T(8,128)S(1)}, f32[2,128,256]{2,1,0:T(8,128)S(1)}, u32[]{:S(2)}, u32[]{:S(2)}) collective-permute-start(f32[2,128,256]{2,1,0:T(8,128)S(1)} %collective-permute-done.fa0), channel_id=1, source_target_pairs={{0,12},{1,13},{2,14},{3,15},{4,8},{5,9},{6,10},{7,11},{8,4},{9,5},... | collective-permute-start | bytes 786440 | tf_op jit(solution)/shard_map/ppermute | solution.py:555
  16.5 0.5 collective-permute-start.4
  17.0 6.6 %collective-permute-done.6.fa3 = f32[2,128,256]{2,1,0:T(8,128)S(1)} collective-permute-done((f32[2,128,256]{2,1,0:T(8,128)S(1)}, f32[2,128,256]{2,1,0:T(8,128)S(1)}, u32[]{:S(2)}, u32[]{:S(2)}) %collective-permute-start.6) | collective-permute-done | bytes 262176 | tf_op jit(solution)/shard_map/ppermute | solution.py:555
  23.6 5.3 %collective-permute-done.5.fa2 = f32[2,128,256]{2,1,0:T(8,128)S(1)} collective-permute-done((f32[2,128,256]{2,1,0:T(8,128)S(1)}, f32[2,128,256]{2,1,0:T(8,128)S(1)}, u32[]{:S(2)}, u32[]{:S(2)}) %collective-permute-start.5) | collective-permute-done | bytes 262176 | tf_op jit(solution)/shard_map/ppermute | solution.py:555
  29.0 0.5 collective-permute-start.8
  30.0 1.2 collective-permute-done.8.fb0
  33.3 20.7 %middle.1 = (bf16[512,512]{1,0:T(8,128)(2,1)}, bf16[512,512]{1,0:T(8,128)(2,1)}, bf16[8,256,512]{2,1,0:T(8,128)(2,1)}, bf16[8,256,512]{2,1,0:T(8,128)(2,1)}, f32...) custom-call(s32[5]{0:T(128)} %stack.73.place, f32[3]{0:T(128)} %out_bias.1, ...), custom_call_target="tpu_custom_call" | custom-call | tf_op jit(solution)/shard_map/middle/pallas_call | solution.py:596
  54.1 3.1 %collective-permute-done.12 = f32[16,80,256]{2,1,0:T(8,128)S(1)} collective-permute-done((f32[16,80,256]{2,1,0:T(8,128)}, f32[16,80,256]{2,1,0:T(8,128)S(1)}, u32[]{:S(2)}, u32[]{:S(2)}) %collective-permute-start.12) | collective-permute-done | bytes 1310752 | tf_op jit(solution)/shard_map/ppermute | solution.py:555
  57.2 1.5 %fusion.9 = (f32[2,2,4,40,256]{4,3,2,1,0:T(8,128)S(1)}, f32[2,2,4,40,256]{4,3,2,1,0:T(8,128)S(1)}, f32[2,2,4,40,256]{4,3,2,1,0:T(8,128)S(1)}) fusion(f32[2,2,4,80,256]{4,3,2,1,0:T(8,128)} %bitcast.105, f32[2,2,4,80,256]{4,3,2,1,0:T(8,128)S(1)} %bitcast.106), kind=kLoop, calls=%fused_computation.50 | loop fusion | flops 163840 | bytes 4587520 | tf_op jit(solution)/shard_map/slice | solution.py:678
  58.9 1.5 %collective-permute-start.15 = (f32[2,4,40,256]{3,2,1,0:T(8,128)S(1)}, f32[2,4,40,256]{3,2,1,0:T(8,128)S(1)}, u32[]{:S(2)}, u32[]{:S(2)}) collective-permute-start(f32[2,4,40,256]{3,2,1,0:T(8,128)S(1)} %get-tuple-element.104), channel_id=1, source_target_pairs={{0,4},{1,5},{2,6},{3,7},{4,0},{5,1},{6,2},{7,3},{8,12},{9,13},{10,... | collective-permute-start | bytes 983048 | tf_op jit(solution)/shard_map/ppermute | solution.py:555
  60.4 0.5 collective-permute-start.17
  60.9 7.0 %first.1 = (f32[2,8,64,256]{3,2,1,0:T(8,128)}, f32[2,8,64,256]{3,2,1,0:T(8,128)}, f32[2,8,64,256]{3,2,1,0:T(8,128)}, f32[2,8,64,256]{3,2,1,0:T(8,128)}) custom-call(s32[1]{0:T(128)} %bitcast.2.place, bf16[512,512]{1,0:T(8,128)(2,1)} %get-tuple-element.92.xt_high_in, bf16[512,512]{1,0:T(8,128)(2,1)} %get-tuple-element.93.xt_low_in, ...), custom_call_target="tpu_custom_call" | custom-call | bytes 1048576 | tf_op jit(solution)/shard_map/first/pallas_call | solution.py:682
  68.0 0.5 collective-permute-start.14
  68.8 1.4 collective-permute-start.16
  70.3 0.7 collective-permute-start.18
  70.9 3.9 %collective-permute-done.16 = f32[4,40,256]{2,1,0:T(8,128)S(1)} collective-permute-done((f32[4,40,256]{2,1,0:T(8,128)S(1)}, f32[4,40,256]{2,1,0:T(8,128)S(1)}, u32[]{:S(2)}, u32[]{:S(2)}) %collective-permute-start.16) | collective-permute-done | bytes 163872 | tf_op jit(solution)/shard_map/ppermute | solution.py:555
  74.9 1.4 collective-permute-done.18
  76.6 1.1 copy-done.24
  77.9 1.6 %collective-permute-start.23 = (f32[80,256]{1,0:T(8,128)S(1)}, f32[80,256]{1,0:T(8,128)S(1)}, u32[]{:S(2)}, u32[]{:S(2)}) collective-permute-start(f32[80,256]{1,0:T(8,128)S(1)} %get-tuple-element.168), channel_id=1, source_target_pairs={{0,8},{1,9},{2,10},{3,11},{4,12},{5,13},{6,14},{7,15},{8,0},{9,1},... | collective-permute-start | bytes 245768 | tf_op jit(solution)/shard_map/ppermute | solution.py:555
  79.6 2.5 %collective-permute-start.25 = (f32[80,256]{1,0:T(8,128)S(1)}, f32[80,256]{1,0:T(8,128)S(1)}, u32[]{:S(2)}, u32[]{:S(2)}) collective-permute-start(f32[80,256]{1,0:T(8,128)S(1)} %get-tuple-element.169), channel_id=1, source_target_pairs={{0,24},{1,25},{2,26},{3,27},{4,28},{5,29},{6,30},{7,31},{8,16},{9,... | collective-permute-start | bytes 245768 | tf_op jit(solution)/shard_map/ppermute | solution.py:555
  82.2 0.5 collective-permute-start.19
  82.7 1.0 collective-permute-start.21
  83.7 2.5 %collective-permute-done.25 = f32[80,256]{1,0:T(8,128)S(1)} collective-permute-done((f32[80,256]{1,0:T(8,128)S(1)}, f32[80,256]{1,0:T(8,128)S(1)}, u32[]{:S(2)}, u32[]{:S(2)}) %collective-permute-start.25) | collective-permute-done | bytes 81952 | tf_op jit(solution)/shard_map/ppermute | solution.py:555
  86.2 2.7 %collective-permute-done.24 = f32[80,256]{1,0:T(8,128)S(1)} collective-permute-done((f32[80,256]{1,0:T(8,128)S(1)}, f32[80,256]{1,0:T(8,128)S(1)}, u32[]{:S(2)}, u32[]{:S(2)}) %collective-permute-start.24) | collective-permute-done | bytes 81952 | tf_op jit(solution)/shard_map/ppermute | solution.py:555
  89.0 0.5 slice.149
  90.2 0.7 collective-permute-start.27
  90.9 2.3 %collective-permute-start.26 = (f32[80,256]{1,0:T(8,128)S(1)}, f32[80,256]{1,0:T(8,128)S(1)}, u32[]{:S(2)}, u32[]{:S(2)}) collective-permute-start(f32[80,256]{1,0:T(8,128)S(1)} %broadcast_multiply_fusion), channel_id=1, source_target_pairs={{0,8},{1,9},{2,10},{3,11},{4,12},{5,13},{6,14},{7,15},{8,0},{9,1},... | collective-permute-start | bytes 245768 | tf_op jit(solution)/shard_map/ppermute | solution.py:555
  93.2 1.4 collective-permute-start.28
  94.9 0.6 collective-permute-start.20
  95.6 0.8 collective-permute-start.22
  96.4 1.2 collective-permute-done.27
  97.6 1.9 %collective-permute-done.28 = f32[80,256]{1,0:T(8,128)S(1)} collective-permute-done((f32[80,256]{1,0:T(8,128)S(1)}, f32[80,256]{1,0:T(8,128)S(1)}, u32[]{:S(2)}, u32[]{:S(2)}) %collective-permute-start.28) | collective-permute-done | bytes 81952 | tf_op jit(solution)/shard_map/ppermute | solution.py:555
  99.5 2.2 %collective-permute-done.20 = f32[4,64,256]{2,1,0:T(8,128)S(1)} collective-permute-done((f32[4,64,256]{2,1,0:T(8,128)S(1)}, f32[4,64,256]{2,1,0:T(8,128)S(1)}, u32[]{:S(2)}, u32[]{:S(2)}) %collective-permute-start.20) | collective-permute-done | bytes 262176 | tf_op jit(solution)/shard_map/ppermute | solution.py:555
  101.8 0.5 collective-permute-done.22
  102.4 1.2 collective-permute-start.29
  103.6 2.5 %collective-permute-start.31 = (f32[128,256]{1,0:T(8,128)S(1)}, f32[128,256]{1,0:T(8,128)S(1)}, u32[]{:S(2)}, u32[]{:S(2)}) collective-permute-start(f32[128,256]{1,0:T(8,128)S(1)} %get-tuple-element.162), channel_id=1, source_target_pairs={{0,24},{1,25},{2,26},{3,27},{4,28},{5,29},{6,30},{7,31},{8,16},{9,... | collective-permute-start | bytes 393224 | tf_op jit(solution)/shard_map/ppermute | solution.py:555
  106.1 1.4 collective-permute-start.33
  107.5 1.6 %collective-permute-start.32 = (f32[4,40,256]{2,1,0:T(8,128)S(1)}, f32[4,40,256]{2,1,0:T(8,128)S(1)}, u32[]{:S(2)}, u32[]{:S(2)}) collective-permute-start(f32[4,40,256]{2,1,0:T(8,128)S(1)} %get-tuple-element.167), channel_id=1, source_target_pairs={{0,2},{1,3},{2,0},{3,1},{4,6},{5,7},{6,4},{7,5},{8,10},{9,11},{10,... | collective-permute-start | bytes 491528 | tf_op jit(solution)/shard_map/ppermute | solution.py:555
  109.2 5.6 %inputs.1 = (f32[512,128]{1,0:T(8,128)S(1)}, f32[512,128]{1,0:T(8,128)S(1)}, f32[512,128]{1,0:T(8,128)S(1)}, f32[512,128]{1,0:T(8,128)S(1)}) custom-call(s32[5]{0:T(128)S(1)} %copy-done.23, f32[24,512]{1,0:T(8,128)S(1)} %copy-done.21, f32[24,512]{1,0:T(8,128)S(1)} %copy-done.22, bf16[8,256,512]{2,1,0:T(8,128)(2,1)S(1)} %copy-done, ...), custom_call_target="tpu_custom_call" | custom-call | bytes 1048576 | tf_op jit(solution)/shard_map/inputs/pallas_call | solution.py:723
  115.0 1.5 %collective-permute-start.34 = (f32[2,4,40,256]{3,2,1,0:T(8,128)S(1)}, f32[2,4,40,256]{3,2,1,0:T(8,128)S(1)}, u32[]{:S(2)}, u32[]{:S(2)}) collective-permute-start(f32[2,4,40,256]{3,2,1,0:T(8,128)S(1)} %pad_maximum_fusion.5.a0), channel_id=1, source_target_pairs={{0,4},{1,5},{2,6},{3,7},{4,0},{5,1},{6,2},{7,3},{8,12},{9,13},{10,... | collective-permute-start | bytes 983048 | tf_op jit(solution)/shard_map/ppermute | solution.py:555
  116.5 0.5 collective-permute-start.35
  117.0 1.8 %collective-permute-start.45 = (f32[128,256]{1,0:T(8,128)S(1)}, f32[128,256]{1,0:T(8,128)S(1)}, u32[]{:S(2)}, u32[]{:S(2)}) collective-permute-start(f32[128,256]{1,0:T(8,128)S(1)} %fusion.6.a0), channel_id=1, source_target_pairs={{0,24},{1,25},{2,26},{3,27},{4,28},{5,29},{6,30},{7,31},{8,16},{9,... | collective-permute-start | bytes 393224 | tf_op jit(solution)/shard_map/ppermute | solution.py:555
  118.7 0.8 collective-permute-start.44
  119.6 1.8 %collective-permute-start.43 = (f32[128,256]{1,0:T(8,128)S(1)}, f32[128,256]{1,0:T(8,128)S(1)}, u32[]{:S(2)}, u32[]{:S(2)}) collective-permute-start(f32[128,256]{1,0:T(8,128)S(1)} %fusion.6.a0), channel_id=1, source_target_pairs={{0,8},{1,9},{2,10},{3,11},{4,12},{5,13},{6,14},{7,15},{8,0},{9,1},... | collective-permute-start | bytes 393224 | tf_op jit(solution)/shard_map/ppermute | solution.py:555
  121.4 2.3 %collective-permute-done.34.a2 = f32[2,4,40,256]{3,2,1,0:T(8,128)S(1)} collective-permute-done((f32[2,4,40,256]{3,2,1,0:T(8,128)S(1)}, f32[2,4,40,256]{3,2,1,0:T(8,128)S(1)}, u32[]{:S(2)}, u32[]{:S(2)}) %collective-permute-start.34) | collective-permute-done | bytes 327712 | tf_op jit(solution)/shard_map/ppermute | solution.py:555
  123.6 1.2 collective-permute-done.35.a3
  125.5 3.1 %collective-permute-done.44.a2 = f32[128,256]{1,0:T(8,128)S(1)} collective-permute-done((f32[128,256]{1,0:T(8,128)S(1)}, f32[128,256]{1,0:T(8,128)S(1)}, u32[]{:S(2)}, u32[]{:S(2)}) %collective-permute-start.44) | collective-permute-done | bytes 131104 | tf_op jit(solution)/shard_map/ppermute | solution.py:555
  128.6 0.6 collective-permute-start.46
  129.2 0.5 collective-permute-start.37
  129.7 4.3 %collective-permute-done.41.g2 = f32[512,128]{1,0:T(8,128)S(1)} collective-permute-done((f32[512,128]{1,0:T(8,128)S(1)}, f32[512,128]{1,0:T(8,128)S(1)}, u32[]{:S(2)}, u32[]{:S(2)}) %collective-permute-start.41) | collective-permute-done | bytes 262176 | tf_op jit(solution)/shard_map/ppermute | solution.py:555
  134.1 2.2 %collective-permute-done.42.g3 = f32[512,128]{1,0:T(8,128)S(1)} collective-permute-done((f32[512,128]{1,0:T(8,128)S(1)}, f32[512,128]{1,0:T(8,128)S(1)}, u32[]{:S(2)}, u32[]{:S(2)}) %collective-permute-start.42) | collective-permute-done | bytes 262176 | tf_op jit(solution)/shard_map/ppermute | solution.py:555
  136.3 1.8 %collective-permute-start.39 = (f32[2,4,40,256]{3,2,1,0:T(8,128)S(1)}, f32[2,4,40,256]{3,2,1,0:T(8,128)S(1)}, u32[]{:S(2)}, u32[]{:S(2)}) collective-permute-start(f32[2,4,40,256]{3,2,1,0:T(8,128)S(1)} %collective-permute-done.35.a3), channel_id=1, source_target_pairs={{0,1},{1,0},{2,3},{3,2},{4,5},{5,4},{6,7},{7,6},{8,9},{9,8},{10,11... | collective-permute-start | bytes 983048 | tf_op jit(solution)/shard_map/ppermute | solution.py:555
  138.2 0.8 place_near.1.begun
  139.0 1.1 finish_inputs.1
  140.1 2.4 %finish_second.1 = (f32[8,256,256]{2,1,0:T(8,128)}, f32[3,256,128]{2,1,0:T(8,128)}, f32[3,8,128]{2,1,0:T(8,128)}, f32[16,24]{1,0:T(8,128)}, f32[8,256]{1,0:T(8,1...) custom-call(s32[2]{0:T(128)S(1)} %pad_add_fusion.place, ...), custom_call_target="tpu_custom_call" | custom-call | tf_op jit(solution)/shard_map/finish_second/pallas_call | solution.py:758
  142.5 0.8 place_far.1
  (140 shorter events, 6.0 us)
Async XLA Ops:
  0.6 11.1 %collective-permute-start.1 = (f32[8,128,256]{2,1,0:T(8,128)}, f32[8,128,256]{2,1,0:T(8,128)S(1)}, u32[]{:S(2)}, u32[]{:S(2)}) collective-permute-start(f32[8,128,256]{2,1,0:T(8,128)} %near0.3), channel_id=1, source_target_pairs={{0,1},{1,0},{2,3},{3,2},{4,5},{5,4},{6,7},{7,6},{8,9},{9,8},{10,11... | collective-permute-start | bytes 3145736 | tf_op jit(solution)/shard_map/ppermute | solution.py:555
  2.1 9.6 %collective-permute-start = (f32[2,128,256]{2,1,0:T(8,128)S(1)}, f32[2,128,256]{2,1,0:T(8,128)S(1)}, u32[]{:S(2)}, u32[]{:S(2)}) collective-permute-start(f32[2,128,256]{2,1,0:T(8,128)S(1)} %constant_dynamic-slice_fusion.4), channel_id=1, source_target_pairs={{0,2},{1,3},{2,0},{3,1},{4,6},{5,7},{6,4},{7,5},{8,10},{9,11},{10,... | collective-permute-start | bytes 786440 | tf_op jit(solution)/shard_map/ppermute | solution.py:555
  11.7 20.7 %copy-start.5 = (f32[2,128,256]{2,1,0:T(8,128)}, f32[2,128,256]{2,1,0:T(8,128)S(1)}, u32[]{:S(2)}) copy-start(f32[2,128,256]{2,1,0:T(8,128)S(1)} %collective-permute-done.fa0) | copy-start | bytes 786436
  11.7 20.7 %copy-start.3 = (f32[8,128,256]{2,1,0:T(8,128)}, f32[8,128,256]{2,1,0:T(8,128)S(1)}, u32[]{:S(2)}) copy-start(f32[8,128,256]{2,1,0:T(8,128)S(1)} %collective-permute-done.1.near1) | copy-start | bytes 3145732
  11.7 17.1 %collective-permute-start.3 = (f32[1048,128]{1,0:T(8,128)S(1)}, f32[1048,128]{1,0:T(8,128)S(1)}, u32[]{:S(2)}, u32[]{:S(2)}) collective-permute-start(f32[1048,128]{1,0:T(8,128)S(1)} %pad_maximum_fusion), channel_id=1, source_target_pairs={{0,2},{1,3},{2,0},{3,1},{4,6},{5,7},{6,4},{7,5},{8,10},{9,11},{10,... | collective-permute-start | bytes 1609736 | tf_op jit(solution)/shard_map/ppermute | solution.py:555
  13.5 15.3 %collective-permute-start.2 = (f32[536,128]{1,0:T(8,128)S(1)}, f32[536,128]{1,0:T(8,128)S(1)}, u32[]{:S(2)}, u32[]{:S(2)}) collective-permute-start(f32[536,128]{1,0:T(8,128)S(1)} %pad_maximum_fusion.7), channel_id=1, source_target_pairs={{0,1},{1,0},{2,3},{3,2},{4,5},{5,4},{6,7},{7,6},{8,9},{9,8},{10,11... | collective-permute-start | bytes 823304 | tf_op jit(solution)/shard_map/ppermute | solution.py:555
  13.5 10.0 %collective-permute-start.6 = (f32[2,128,256]{2,1,0:T(8,128)S(1)}, f32[2,128,256]{2,1,0:T(8,128)S(1)}, u32[]{:S(2)}, u32[]{:S(2)}) collective-permute-start(f32[2,128,256]{2,1,0:T(8,128)S(1)} %collective-permute-done.fa0), channel_id=1, source_target_pairs={{0,12},{1,13},{2,14},{3,15},{4,8},{5,9},{6,10},{7,11},{8,4},{9,5},... | collective-permute-start | bytes 786440 | tf_op jit(solution)/shard_map/ppermute | solution.py:555
  16.0 12.8 %collective-permute-start.5 = (f32[2,128,256]{2,1,0:T(8,128)S(1)}, f32[2,128,256]{2,1,0:T(8,128)S(1)}, u32[]{:S(2)}, u32[]{:S(2)}) collective-permute-start(f32[2,128,256]{2,1,0:T(8,128)S(1)} %collective-permute-done.fa0), channel_id=1, source_target_pairs={{0,8},{1,9},{2,10},{3,11},{4,12},{5,13},{6,14},{7,15},{8,0},{9,1},... | collective-permute-start | bytes 786440 | tf_op jit(solution)/shard_map/ppermute | solution.py:555
  16.5 12.4 %collective-permute-start.4 = (f32[2,128,256]{2,1,0:T(8,128)S(1)}, f32[2,128,256]{2,1,0:T(8,128)S(1)}, u32[]{:S(2)}, u32[]{:S(2)}) collective-permute-start(f32[2,128,256]{2,1,0:T(8,128)S(1)} %collective-permute-done.fa0), channel_id=1, source_target_pairs={{0,4},{1,5},{2,6},{3,7},{4,0},{5,1},{6,2},{7,3},{8,12},{9,13},{10,... | collective-permute-start | bytes 786440 | tf_op jit(solution)/shard_map/ppermute | solution.py:555
  23.6 8.8 %copy-start.7 = (f32[2,128,256]{2,1,0:T(8,128)}, f32[2,128,256]{2,1,0:T(8,128)S(1)}, u32[]{:S(2)}) copy-start(f32[2,128,256]{2,1,0:T(8,128)S(1)} %collective-permute-done.6.fa3) | copy-start | bytes 786436
  28.9 3.5 %collective-permute-start.7 = (f32[1048,128]{1,0:T(8,128)S(1)}, f32[1048,128]{1,0:T(8,128)S(1)}, u32[]{:S(2)}, u32[]{:S(2)}) collective-permute-start(f32[1048,128]{1,0:T(8,128)S(1)} %collective-permute-done.3.x2), channel_id=1, source_target_pairs={{0,1},{1,0},{2,3},{3,2},{4,5},{5,4},{6,7},{7,6},{8,9},{9,8},{10,11... | collective-permute-start | bytes 1609736 | tf_op jit(solution)/shard_map/ppermute | solution.py:555
  29.0 2.3 %collective-permute-start.8 = (f32[2,128,256]{2,1,0:T(8,128)S(1)}, f32[2,128,256]{2,1,0:T(8,128)S(1)}, u32[]{:S(2)}, u32[]{:S(2)}) collective-permute-start(f32[2,128,256]{2,1,0:T(8,128)S(1)} %collective-permute-done.fa0), channel_id=1, source_target_pairs={{0,1},{1,0},{2,3},{3,2},{4,5},{5,4},{6,7},{7,6},{8,9},{9,8},{10,11... | collective-permute-start | bytes 786440 | tf_op jit(solution)/shard_map/ppermute | solution.py:555
  29.5 2.2 %collective-permute-start.9 = (f32[2,128,256]{2,1,0:T(8,128)S(1)}, f32[2,128,256]{2,1,0:T(8,128)S(1)}, u32[]{:S(2)}, u32[]{:S(2)}) collective-permute-start(f32[2,128,256]{2,1,0:T(8,128)S(1)} %collective-permute-done.4.fa1), channel_id=1, source_target_pairs={{0,1},{1,0},{2,3},{3,2},{4,5},{5,4},{6,7},{7,6},{8,9},{9,8},{10,11... | collective-permute-start | bytes 786440 | tf_op jit(solution)/shard_map/ppermute | solution.py:555
  29.5 2.5 %collective-permute-start.10 = (f32[2,128,256]{2,1,0:T(8,128)S(1)}, f32[2,128,256]{2,1,0:T(8,128)S(1)}, u32[]{:S(2)}, u32[]{:S(2)}) collective-permute-start(f32[2,128,256]{2,1,0:T(8,128)S(1)} %collective-permute-done.5.fa2), channel_id=1, source_target_pairs={{0,1},{1,0},{2,3},{3,2},{4,5},{5,4},{6,7},{7,6},{8,9},{9,8},{10,11... | collective-permute-start | bytes 786440 | tf_op jit(solution)/shard_map/ppermute | solution.py:555
  30.0 2.4 %collective-permute-start.11 = (f32[2,128,256]{2,1,0:T(8,128)S(1)}, f32[2,128,256]{2,1,0:T(8,128)S(1)}, u32[]{:S(2)}, u32[]{:S(2)}) collective-permute-start(f32[2,128,256]{2,1,0:T(8,128)S(1)} %collective-permute-done.6.fa3), channel_id=1, source_target_pairs={{0,1},{1,0},{2,3},{3,2},{4,5},{5,4},{6,7},{7,6},{8,9},{9,8},{10,11... | collective-permute-start | bytes 786440 | tf_op jit(solution)/shard_map/ppermute | solution.py:555
  53.9 3.3 %collective-permute-start.12 = (f32[16,80,256]{2,1,0:T(8,128)}, f32[16,80,256]{2,1,0:T(8,128)S(1)}, u32[]{:S(2)}, u32[]{:S(2)}) collective-permute-start(f32[16,80,256]{2,1,0:T(8,128)} %get-tuple-element.95), channel_id=1, source_target_pairs={{0,1},{1,0},{2,3},{3,2},{4,5},{5,4},{6,7},{7,6},{8,9},{9,8},{10,11... | collective-permute-start | bytes 3932168 | tf_op jit(solution)/shard_map/ppermute | solution.py:555
  58.9 9.8 %collective-permute-start.15 = (f32[2,4,40,256]{3,2,1,0:T(8,128)S(1)}, f32[2,4,40,256]{3,2,1,0:T(8,128)S(1)}, u32[]{:S(2)}, u32[]{:S(2)}) collective-permute-start(f32[2,4,40,256]{3,2,1,0:T(8,128)S(1)} %get-tuple-element.104), channel_id=1, source_target_pairs={{0,4},{1,5},{2,6},{3,7},{4,0},{5,1},{6,2},{7,3},{8,12},{9,13},{10,... | collective-permute-start | bytes 983048 | tf_op jit(solution)/shard_map/ppermute | solution.py:555
  60.4 9.8 %collective-permute-start.17 = (f32[2,4,40,256]{3,2,1,0:T(8,128)S(1)}, f32[2,4,40,256]{3,2,1,0:T(8,128)S(1)}, u32[]{:S(2)}, u32[]{:S(2)}) collective-permute-start(f32[2,4,40,256]{3,2,1,0:T(8,128)S(1)} %get-tuple-element.106), channel_id=1, source_target_pairs={{0,2},{1,3},{2,0},{3,1},{4,6},{5,7},{6,4},{7,5},{8,10},{9,11},{10,... | collective-permute-start | bytes 983048 | tf_op jit(solution)/shard_map/ppermute | solution.py:555
  68.0 8.3 %collective-permute-start.13 = (f32[2,8,64,256]{3,2,1,0:T(8,128)}, f32[2,8,64,256]{3,2,1,0:T(8,128)S(1)}, u32[]{:S(2)}, u32[]{:S(2)}) collective-permute-start(f32[2,8,64,256]{3,2,1,0:T(8,128)} %get-tuple-element.100), channel_id=1, source_target_pairs={{0,1},{1,0},{2,3},{3,2},{4,5},{5,4},{6,7},{7,6},{8,9},{9,8},{10,11... | collective-permute-start | bytes 3145736 | tf_op jit(solution)/shard_map/ppermute | solution.py:555
  68.0 8.5 %collective-permute-start.14 = (f32[2,8,64,256]{3,2,1,0:T(8,128)}, f32[2,8,64,256]{3,2,1,0:T(8,128)S(1)}, u32[]{:S(2)}, u32[]{:S(2)}) collective-permute-start(f32[2,8,64,256]{3,2,1,0:T(8,128)} %get-tuple-element.102), channel_id=1, source_target_pairs={{0,1},{1,0},{2,3},{3,2},{4,5},{5,4},{6,7},{7,6},{8,9},{9,8},{10,11... | collective-permute-start | bytes 3145736 | tf_op jit(solution)/shard_map/ppermute | solution.py:555
  68.8 7.5 %copy-start.25 = (f32[2,8,64,256]{3,2,1,0:T(8,128)S(1)}, f32[2,8,64,256]{3,2,1,0:T(8,128)}, u32[]{:S(2)}) copy-start(f32[2,8,64,256]{3,2,1,0:T(8,128)} %get-tuple-element.99) | copy-start | bytes 3145732
  68.8 6.0 %collective-permute-start.16 = (f32[4,40,256]{2,1,0:T(8,128)S(1)}, f32[4,40,256]{2,1,0:T(8,128)S(1)}, u32[]{:S(2)}, u32[]{:S(2)}) collective-permute-start(f32[4,40,256]{2,1,0:T(8,128)S(1)} %slice_bitcast_fusion.12), channel_id=1, source_target_pairs={{0,2},{1,3},{2,0},{3,1},{4,6},{5,7},{6,4},{7,5},{8,10},{9,11},{10,... | collective-permute-start | bytes 491528 | tf_op jit(solution)/shard_map/ppermute | solution.py:555
  70.3 6.0 %collective-permute-start.18 = (f32[4,40,256]{2,1,0:T(8,128)S(1)}, f32[4,40,256]{2,1,0:T(8,128)S(1)}, u32[]{:S(2)}, u32[]{:S(2)}) collective-permute-start(f32[4,40,256]{2,1,0:T(8,128)S(1)} %slice_bitcast_fusion.10), channel_id=1, source_target_pairs={{0,4},{1,5},{2,6},{3,7},{4,0},{5,1},{6,2},{7,3},{8,12},{9,13},{10,... | collective-permute-start | bytes 491528 | tf_op jit(solution)/shard_map/ppermute | solution.py:555
  77.9 5.8 %collective-permute-start.23 = (f32[80,256]{1,0:T(8,128)S(1)}, f32[80,256]{1,0:T(8,128)S(1)}, u32[]{:S(2)}, u32[]{:S(2)}) collective-permute-start(f32[80,256]{1,0:T(8,128)S(1)} %get-tuple-element.168), channel_id=1, source_target_pairs={{0,8},{1,9},{2,10},{3,11},{4,12},{5,13},{6,14},{7,15},{8,0},{9,1},... | collective-permute-start | bytes 245768 | tf_op jit(solution)/shard_map/ppermute | solution.py:555
  79.6 6.6 %collective-permute-start.25 = (f32[80,256]{1,0:T(8,128)S(1)}, f32[80,256]{1,0:T(8,128)S(1)}, u32[]{:S(2)}, u32[]{:S(2)}) collective-permute-start(f32[80,256]{1,0:T(8,128)S(1)} %get-tuple-element.169), channel_id=1, source_target_pairs={{0,24},{1,25},{2,26},{3,27},{4,28},{5,29},{6,30},{7,31},{8,16},{9,... | collective-permute-start | bytes 245768 | tf_op jit(solution)/shard_map/ppermute | solution.py:555
  82.1 6.9 %collective-permute-start.24 = (f32[80,256]{1,0:T(8,128)S(1)}, f32[80,256]{1,0:T(8,128)S(1)}, u32[]{:S(2)}, u32[]{:S(2)}) collective-permute-start(f32[80,256]{1,0:T(8,128)S(1)} %get-tuple-element.170), channel_id=1, source_target_pairs={{0,16},{1,17},{2,18},{3,19},{4,20},{5,21},{6,22},{7,23},{8,24},{9,... | collective-permute-start | bytes 245768 | tf_op jit(solution)/shard_map/ppermute | solution.py:555
  82.2 12.5 %collective-permute-start.19 = (f32[2,4,64,256]{3,2,1,0:T(8,128)S(1)}, f32[2,4,64,256]{3,2,1,0:T(8,128)S(1)}, u32[]{:S(2)}, u32[]{:S(2)}) collective-permute-start(f32[2,4,64,256]{3,2,1,0:T(8,128)S(1)} %bitcast.107), channel_id=1, source_target_pairs={{0,2},{1,3},{2,0},{3,1},{4,6},{5,7},{6,4},{7,5},{8,10},{9,11},{10,... | collective-permute-start | bytes 1572872 | tf_op jit(solution)/shard_map/ppermute | solution.py:555
  82.7 12.8 %collective-permute-start.21 = (f32[2,4,64,256]{3,2,1,0:T(8,128)S(1)}, f32[2,4,64,256]{3,2,1,0:T(8,128)S(1)}, u32[]{:S(2)}, u32[]{:S(2)}) collective-permute-start(f32[2,4,64,256]{3,2,1,0:T(8,128)S(1)} %get-tuple-element.110), channel_id=1, source_target_pairs={{0,4},{1,5},{2,6},{3,7},{4,0},{5,1},{6,2},{7,3},{8,12},{9,13},{10,... | collective-permute-start | bytes 1572872 | tf_op jit(solution)/shard_map/ppermute | solution.py:555
  90.2 7.4 %collective-permute-start.27 = (f32[80,256]{1,0:T(8,128)S(1)}, f32[80,256]{1,0:T(8,128)S(1)}, u32[]{:S(2)}, u32[]{:S(2)}) collective-permute-start(f32[80,256]{1,0:T(8,128)S(1)} %broadcast_multiply_fusion), channel_id=1, source_target_pairs={{0,16},{1,17},{2,18},{3,19},{4,20},{5,21},{6,22},{7,23},{8,24},{9,... | collective-permute-start | bytes 245768 | tf_op jit(solution)/shard_map/ppermute | solution.py:555
  90.9 6.7 %collective-permute-start.26 = (f32[80,256]{1,0:T(8,128)S(1)}, f32[80,256]{1,0:T(8,128)S(1)}, u32[]{:S(2)}, u32[]{:S(2)}) collective-permute-start(f32[80,256]{1,0:T(8,128)S(1)} %broadcast_multiply_fusion), channel_id=1, source_target_pairs={{0,8},{1,9},{2,10},{3,11},{4,12},{5,13},{6,14},{7,15},{8,0},{9,1},... | collective-permute-start | bytes 245768 | tf_op jit(solution)/shard_map/ppermute | solution.py:555
  93.2 6.2 %collective-permute-start.28 = (f32[80,256]{1,0:T(8,128)S(1)}, f32[80,256]{1,0:T(8,128)S(1)}, u32[]{:S(2)}, u32[]{:S(2)}) collective-permute-start(f32[80,256]{1,0:T(8,128)S(1)} %broadcast_multiply_fusion), channel_id=1, source_target_pairs={{0,24},{1,25},{2,26},{3,27},{4,28},{5,29},{6,30},{7,31},{8,16},{9,... | collective-permute-start | bytes 245768 | tf_op jit(solution)/shard_map/ppermute | solution.py:555
  94.7 14.4 %copy-start.16 = (f32[2,128,256]{2,1,0:T(8,128)S(1)}, f32[2,128,256]{2,1,0:T(8,128)}, u32[]{:S(2)}) copy-start(f32[2,128,256]{2,1,0:T(8,128)} %copy-done.15) | copy-start | bytes 786436
  94.7 14.4 %copy-start.18 = (f32[2,128,256]{2,1,0:T(8,128)S(1)}, f32[2,128,256]{2,1,0:T(8,128)}, u32[]{:S(2)}) copy-start(f32[2,128,256]{2,1,0:T(8,128)} %copy-done.17) | copy-start | bytes 786436
  94.7 14.4 %copy-start.20 = (f32[2,128,256]{2,1,0:T(8,128)S(1)}, f32[2,128,256]{2,1,0:T(8,128)}, u32[]{:S(2)}) copy-start(f32[2,128,256]{2,1,0:T(8,128)} %copy-done.19) | copy-start | bytes 786436
  94.7 14.4 %copy-start.22 = (f32[24,512]{1,0:T(8,128)S(1)}, f32[24,512]{1,0:T(8,128)}, u32[]{:S(2)}) copy-start(f32[24,512]{1,0:T(8,128)} %get-tuple-element.116.glog) | copy-start | bytes 147460
  94.8 14.3 %copy-start.12 = (f32[2,128,256]{2,1,0:T(8,128)S(1)}, f32[2,128,256]{2,1,0:T(8,128)}, u32[]{:S(2)}) copy-start(f32[2,128,256]{2,1,0:T(8,128)} %copy-done.11) | copy-start | bytes 786436
  94.8 14.3 %copy-start.14 = (f32[2,128,256]{2,1,0:T(8,128)S(1)}, f32[2,128,256]{2,1,0:T(8,128)}, u32[]{:S(2)}) copy-start(f32[2,128,256]{2,1,0:T(8,128)} %copy-done.13) | copy-start | bytes 786436
  94.9 6.9 %collective-permute-start.20 = (f32[4,64,256]{2,1,0:T(8,128)S(1)}, f32[4,64,256]{2,1,0:T(8,128)S(1)}, u32[]{:S(2)}, u32[]{:S(2)}) collective-permute-start(f32[4,64,256]{2,1,0:T(8,128)S(1)} %slice_bitcast_fusion.8), channel_id=1, source_target_pairs={{0,4},{1,5},{2,6},{3,7},{4,0},{5,1},{6,2},{7,3},{8,12},{9,13},{10,... | collective-permute-start | bytes 786440 | tf_op jit(solution)/shard_map/ppermute | solution.py:555
  95.5 13.6 %copy-start.2 = (f32[8,128,256]{2,1,0:T(8,128)S(1)}, f32[8,128,256]{2,1,0:T(8,128)}, u32[]{:S(2)}) copy-start(f32[8,128,256]{2,1,0:T(8,128)} %near0.3) | copy-start | bytes 3145732
  95.5 13.6 %copy-start.8 = (f32[2,128,256]{2,1,0:T(8,128)S(1)}, f32[2,128,256]{2,1,0:T(8,128)}, u32[]{:S(2)}) copy-start(f32[2,128,256]{2,1,0:T(8,128)} %copy-done.7) | copy-start | bytes 786436
  95.5 13.6 %copy-start.10 = (f32[2,128,256]{2,1,0:T(8,128)S(1)}, f32[2,128,256]{2,1,0:T(8,128)}, u32[]{:S(2)}) copy-start(f32[2,128,256]{2,1,0:T(8,128)} %copy-done.9) | copy-start | bytes 786436
  95.6 13.6 %copy-start.4 = (f32[8,128,256]{2,1,0:T(8,128)S(1)}, f32[8,128,256]{2,1,0:T(8,128)}, u32[]{:S(2)}) copy-start(f32[8,128,256]{2,1,0:T(8,128)} %copy-done.3) | copy-start | bytes 3145732
  95.6 6.6 %collective-permute-start.22 = (f32[4,64,256]{2,1,0:T(8,128)S(1)}, f32[4,64,256]{2,1,0:T(8,128)S(1)}, u32[]{:S(2)}, u32[]{:S(2)}) collective-permute-start(f32[4,64,256]{2,1,0:T(8,128)S(1)} %slice_bitcast_fusion.6), channel_id=1, source_target_pairs={{0,2},{1,3},{2,0},{3,1},{4,6},{5,7},{6,4},{7,5},{8,10},{9,11},{10,... | collective-permute-start | bytes 786440 | tf_op jit(solution)/shard_map/ppermute | solution.py:555
  99.5 9.7 %copy-start.6 = (f32[2,128,256]{2,1,0:T(8,128)S(1)}, f32[2,128,256]{2,1,0:T(8,128)}, u32[]{:S(2)}) copy-start(f32[2,128,256]{2,1,0:T(8,128)} %copy-done.5) | copy-start | bytes 786436
  101.7 7.5 %copy-start.1 = (bf16[8,256,512]{2,1,0:T(8,128)(2,1)S(1)}, bf16[8,256,512]{2,1,0:T(8,128)(2,1)}, u32[]{:S(2)}) copy-start(bf16[8,256,512]{2,1,0:T(8,128)(2,1)} %get-tuple-element.117.gf_low_in) | copy-start | bytes 6291460
  102.3 6.9 %copy-start = (bf16[8,256,512]{2,1,0:T(8,128)(2,1)S(1)}, bf16[8,256,512]{2,1,0:T(8,128)(2,1)}, u32[]{:S(2)}) copy-start(bf16[8,256,512]{2,1,0:T(8,128)(2,1)} %get-tuple-element.97.gf_high_in) | copy-start | bytes 6291460
  102.4 12.4 %collective-permute-start.29 = (f32[128,256]{1,0:T(8,128)S(1)}, f32[128,256]{1,0:T(8,128)S(1)}, u32[]{:S(2)}, u32[]{:S(2)}) collective-permute-start(f32[128,256]{1,0:T(8,128)S(1)} %get-tuple-element.161), channel_id=1, source_target_pairs={{0,8},{1,9},{2,10},{3,11},{4,12},{5,13},{6,14},{7,15},{8,0},{9,1},... | collective-permute-start | bytes 393224 | tf_op jit(solution)/shard_map/ppermute | solution.py:555
  103.6 11.2 %collective-permute-start.31 = (f32[128,256]{1,0:T(8,128)S(1)}, f32[128,256]{1,0:T(8,128)S(1)}, u32[]{:S(2)}, u32[]{:S(2)}) collective-permute-start(f32[128,256]{1,0:T(8,128)S(1)} %get-tuple-element.162), channel_id=1, source_target_pairs={{0,24},{1,25},{2,26},{3,27},{4,28},{5,29},{6,30},{7,31},{8,16},{9,... | collective-permute-start | bytes 393224 | tf_op jit(solution)/shard_map/ppermute | solution.py:555
  106.1 8.8 %collective-permute-start.30 = (f32[128,256]{1,0:T(8,128)S(1)}, f32[128,256]{1,0:T(8,128)S(1)}, u32[]{:S(2)}, u32[]{:S(2)}) collective-permute-start(f32[128,256]{1,0:T(8,128)S(1)} %get-tuple-element.163), channel_id=1, source_target_pairs={{0,16},{1,17},{2,18},{3,19},{4,20},{5,21},{6,22},{7,23},{8,24},{9,... | collective-permute-start | bytes 393224 | tf_op jit(solution)/shard_map/ppermute | solution.py:555
  106.1 8.7 %collective-permute-start.33 = (f32[4,40,256]{2,1,0:T(8,128)S(1)}, f32[4,40,256]{2,1,0:T(8,128)S(1)}, u32[]{:S(2)}, u32[]{:S(2)}) collective-permute-start(f32[4,40,256]{2,1,0:T(8,128)S(1)} %get-tuple-element.166), channel_id=1, source_target_pairs={{0,4},{1,5},{2,6},{3,7},{4,0},{5,1},{6,2},{7,3},{8,12},{9,13},{10,... | collective-permute-start | bytes 491528 | tf_op jit(solution)/shard_map/ppermute | solution.py:555
  107.5 7.4 %collective-permute-start.32 = (f32[4,40,256]{2,1,0:T(8,128)S(1)}, f32[4,40,256]{2,1,0:T(8,128)S(1)}, u32[]{:S(2)}, u32[]{:S(2)}) collective-permute-start(f32[4,40,256]{2,1,0:T(8,128)S(1)} %get-tuple-element.167), channel_id=1, source_target_pairs={{0,2},{1,3},{2,0},{3,1},{4,6},{5,7},{6,4},{7,5},{8,10},{9,11},{10,... | collective-permute-start | bytes 491528 | tf_op jit(solution)/shard_map/ppermute | solution.py:555
  115.0 8.7 %collective-permute-start.34 = (f32[2,4,40,256]{3,2,1,0:T(8,128)S(1)}, f32[2,4,40,256]{3,2,1,0:T(8,128)S(1)}, u32[]{:S(2)}, u32[]{:S(2)}) collective-permute-start(f32[2,4,40,256]{3,2,1,0:T(8,128)S(1)} %pad_maximum_fusion.5.a0), channel_id=1, source_target_pairs={{0,4},{1,5},{2,6},{3,7},{4,0},{5,1},{6,2},{7,3},{8,12},{9,13},{10,... | collective-permute-start | bytes 983048 | tf_op jit(solution)/shard_map/ppermute | solution.py:555
  116.5 8.3 %collective-permute-start.35 = (f32[2,4,40,256]{3,2,1,0:T(8,128)S(1)}, f32[2,4,40,256]{3,2,1,0:T(8,128)S(1)}, u32[]{:S(2)}, u32[]{:S(2)}) collective-permute-start(f32[2,4,40,256]{3,2,1,0:T(8,128)S(1)} %pad_maximum_fusion.6.a1), channel_id=1, source_target_pairs={{0,2},{1,3},{2,0},{3,1},{4,6},{5,7},{6,4},{7,5},{8,10},{9,11},{10,... | collective-permute-start | bytes 983048 | tf_op jit(solution)/shard_map/ppermute | solution.py:555
  117.0 8.2 %collective-permute-start.45 = (f32[128,256]{1,0:T(8,128)S(1)}, f32[128,256]{1,0:T(8,128)S(1)}, u32[]{:S(2)}, u32[]{:S(2)}) collective-permute-start(f32[128,256]{1,0:T(8,128)S(1)} %fusion.6.a0), channel_id=1, source_target_pairs={{0,24},{1,25},{2,26},{3,27},{4,28},{5,29},{6,30},{7,31},{8,16},{9,... | collective-permute-start | bytes 393224 | tf_op jit(solution)/shard_map/ppermute | solution.py:555
  118.7 9.9 %collective-permute-start.44 = (f32[128,256]{1,0:T(8,128)S(1)}, f32[128,256]{1,0:T(8,128)S(1)}, u32[]{:S(2)}, u32[]{:S(2)}) collective-permute-start(f32[128,256]{1,0:T(8,128)S(1)} %fusion.6.a0), channel_id=1, source_target_pairs={{0,16},{1,17},{2,18},{3,19},{4,20},{5,21},{6,22},{7,23},{8,24},{9,... | collective-permute-start | bytes 393224 | tf_op jit(solution)/shard_map/ppermute | solution.py:555
  119.6 9.0 %collective-permute-start.43 = (f32[128,256]{1,0:T(8,128)S(1)}, f32[128,256]{1,0:T(8,128)S(1)}, u32[]{:S(2)}, u32[]{:S(2)}) collective-permute-start(f32[128,256]{1,0:T(8,128)S(1)} %fusion.6.a0), channel_id=1, source_target_pairs={{0,8},{1,9},{2,10},{3,11},{4,12},{5,13},{6,14},{7,15},{8,0},{9,1},... | collective-permute-start | bytes 393224 | tf_op jit(solution)/shard_map/ppermute | solution.py:555
  123.6 5.6 %collective-permute-start.40 = (f32[512,128]{1,0:T(8,128)S(1)}, f32[512,128]{1,0:T(8,128)S(1)}, u32[]{:S(2)}, u32[]{:S(2)}) collective-permute-start(f32[512,128]{1,0:T(8,128)S(1)} %get-tuple-element.132), channel_id=1, source_target_pairs={{0,1},{1,0},{2,3},{3,2},{4,5},{5,4},{6,7},{7,6},{8,9},{9,8},{10,11... | collective-permute-start | bytes 786440 | tf_op jit(solution)/shard_map/ppermute | solution.py:555
  124.8 9.2 %collective-permute-start.41 = (f32[512,128]{1,0:T(8,128)S(1)}, f32[512,128]{1,0:T(8,128)S(1)}, u32[]{:S(2)}, u32[]{:S(2)}) collective-permute-start(f32[512,128]{1,0:T(8,128)S(1)} %get-tuple-element.133), channel_id=1, source_target_pairs={{0,2},{1,3},{2,0},{3,1},{4,6},{5,7},{6,4},{7,5},{8,10},{9,11},{10,... | collective-permute-start | bytes 786440 | tf_op jit(solution)/shard_map/ppermute | solution.py:555
  125.2 11.1 %collective-permute-start.42 = (f32[512,128]{1,0:T(8,128)S(1)}, f32[512,128]{1,0:T(8,128)S(1)}, u32[]{:S(2)}, u32[]{:S(2)}) collective-permute-start(f32[512,128]{1,0:T(8,128)S(1)} %get-tuple-element.134), channel_id=1, source_target_pairs={{0,3},{1,2},{2,1},{3,0},{4,7},{5,6},{6,5},{7,4},{8,11},{9,10},{10,... | collective-permute-start | bytes 786440 | tf_op jit(solution)/shard_map/ppermute | solution.py:555
  128.6 13.9 %collective-permute-start.46 = (f32[4,128,256]{2,1,0:T(8,128)S(1)}, f32[4,128,256]{2,1,0:T(8,128)S(1)}, u32[]{:S(2)}, u32[]{:S(2)}) collective-permute-start(f32[4,128,256]{2,1,0:T(8,128)S(1)} %pad_maximum_fusion.2), channel_id=1, source_target_pairs={{0,4},{1,5},{2,6},{3,7},{4,0},{5,1},{6,2},{7,3},{8,12},{9,13},{10,... | collective-permute-start | bytes 1572872 | tf_op jit(solution)/shard_map/ppermute | solution.py:555
  129.2 10.9 %collective-permute-start.36 = (f32[2,4,40,256]{3,2,1,0:T(8,128)S(1)}, f32[2,4,40,256]{3,2,1,0:T(8,128)S(1)}, u32[]{:S(2)}, u32[]{:S(2)}) collective-permute-start(f32[2,4,40,256]{3,2,1,0:T(8,128)S(1)} %pad_maximum_fusion.5.a0), channel_id=1, source_target_pairs={{0,1},{1,0},{2,3},{3,2},{4,5},{5,4},{6,7},{7,6},{8,9},{9,8},{10,11... | collective-permute-start | bytes 983048 | tf_op jit(solution)/shard_map/ppermute | solution.py:555
  129.2 10.9 %collective-permute-start.37 = (f32[2,4,40,256]{3,2,1,0:T(8,128)S(1)}, f32[2,4,40,256]{3,2,1,0:T(8,128)S(1)}, u32[]{:S(2)}, u32[]{:S(2)}) collective-permute-start(f32[2,4,40,256]{3,2,1,0:T(8,128)S(1)} %pad_maximum_fusion.6.a1), channel_id=1, source_target_pairs={{0,1},{1,0},{2,3},{3,2},{4,5},{5,4},{6,7},{7,6},{8,9},{9,8},{10,11... | collective-permute-start | bytes 983048 | tf_op jit(solution)/shard_map/ppermute | solution.py:555
  134.0 6.1 %collective-permute-start.38 = (f32[2,4,40,256]{3,2,1,0:T(8,128)S(1)}, f32[2,4,40,256]{3,2,1,0:T(8,128)S(1)}, u32[]{:S(2)}, u32[]{:S(2)}) collective-permute-start(f32[2,4,40,256]{3,2,1,0:T(8,128)S(1)} %collective-permute-done.34.a2), channel_id=1, source_target_pairs={{0,1},{1,0},{2,3},{3,2},{4,5},{5,4},{6,7},{7,6},{8,9},{9,8},{10,11... | collective-permute-start | bytes 983048 | tf_op jit(solution)/shard_map/ppermute | solution.py:555
  136.3 3.8 %collective-permute-start.39 = (f32[2,4,40,256]{3,2,1,0:T(8,128)S(1)}, f32[2,4,40,256]{3,2,1,0:T(8,128)S(1)}, u32[]{:S(2)}, u32[]{:S(2)}) collective-permute-start(f32[2,4,40,256]{3,2,1,0:T(8,128)S(1)} %collective-permute-done.35.a3), channel_id=1, source_target_pairs={{0,1},{1,0},{2,3},{3,2},{4,5},{5,4},{6,7},{7,6},{8,9},{9,8},{10,11... | collective-permute-start | bytes 983048 | tf_op jit(solution)/shard_map/ppermute | solution.py:555
  (14 other events, 41.9 us)

commit v5 on v4

--- a/solution.py
+++ b/solution.py
@@ -69,8 +69,11 @@
     gf_low_out,
     gate_all,
     glog_out,
-    s_keep,
-    s_send,
+    sa_keep,
+    sa_send,
+    sb_keep,
+    sb_send,
+    begun,
     x_in,
     near_in,
     far_in,
@@ -157,11 +160,19 @@
     tower_rows[0:tasks, :] = t_bias[...]
     tower_rows[tasks : 2 * tasks, :] = t_out[...]
     tower_cols = tower_rows[...].T
-    for load in loads:
+    for load in loads[0:2]:
+        load.wait()
+    ahead = 4
+    for n in range(ahead):
+        begun[n] = dot3(split(near_in[order[n]]), (xt_high[0 : 2 * cols], xt_low[0 : 2 * cols]), TN)
+    for load in loads[2:]:
         load.wait()
 
     def first_layer(n):
         e = order[n]
+        if n < ahead:
+            weight = split(far_in[n])
+            return begun[n] + dot3(weight, (xt_high[2 * cols :], xt_low[2 * cols :]), TN)
         weight = split(jnp.concatenate([near_in[e], far_in[n]], axis=0))
         return dot3(weight, (xt_high[...], xt_low[...]), TN)
 
@@ -262,11 +273,12 @@
             grads[-1].start()
 
     piece = hidden // 4
+    half = summed.shape[1] // 2
     last = [
-        pltpu.make_async_copy(summed.at[16:32, 0:piece], s_send.at[:, 0:piece], sems.at[8]),
-        pltpu.make_async_copy(summed.at[0:16, 0:piece], s_keep.at[:, 0:piece], sems.at[9]),
-        pltpu.make_async_copy(summed.at[16:32, piece:], s_send.at[:, piece:], sems.at[10]),
-        pltpu.make_async_copy(summed.at[0:16, piece:], s_keep.at[:, piece:], sems.at[11]),
+        pltpu.make_async_copy(summed.at[16:32, 0:half], sa_send, sems.at[8]),
+        pltpu.make_async_copy(summed.at[0:16, 0:half], sa_keep, sems.at[9]),
+        pltpu.make_async_copy(summed.at[16:32, half:], sb_send, sems.at[10]),
+        pltpu.make_async_copy(summed.at[0:16, half:], sb_keep, sems.at[11]),
     ]
     last[0].start()
     last[1].start()
@@ -603,8 +615,10 @@
             like((experts, hidden, rows), BF16),
             like((units, 4 * cols)),
             like((units, rows)),
-            like((16, 80, width)),
-            like((16, 80, width)),
+            like((16, 40, width)),
+            like((16, 40, width)),
+            like((16, 40, width)),
+            like((16, 40, width)),
         ),
         in_specs=[scalars()] * 2
         + [anywhere()] * 4
@@ -613,8 +627,9 @@
         + [whole()] * 4
         + [anywhere()]
         + [whole()] * 4,
-        out_specs=[anywhere()] * 4 + [whole()] * 2 + [anywhere()] * 2,
+        out_specs=[anywhere()] * 4 + [whole()] * 2 + [anywhere()] * 4,
         scratch_shapes=[
+            VMEM((4, hidden, rows), F32),
             VMEM((4, rows + units, cols), F32),
             VMEM((experts, 2 * cols, hidden), F32),
             VMEM((experts, 2 * cols, hidden), F32),
@@ -663,7 +678,7 @@
         tower_bias,
         tower_out,
     )
-    xt_high, xt_low, gf_high, gf_low, gate_all, glog, s_keep, s_send = outs
+    xt_high, xt_low, gf_high, gf_low, gate_all, glog, sa_keep, sa_send, sb_keep, sb_send = outs
 
     place3 = me3.reshape(1)
     cheap = pl.CostEstimate(flops=0, bytes_accessed=1 << 20, transcendentals=0)
@@ -672,10 +687,9 @@
         held = keep + got
         return lax.index_in_dim(held, 0, axis, False), lax.index_in_dim(held, 1, axis, False)
 
-    s_keep = s_keep.reshape(2, 2, 4, 80, width)
-    s_got = move(s_send, 0, 1).reshape(2, 2, 4, 80, width)
-    sa, sa_out = fold(s_keep[:, :, :, 0:40], s_got[:, :, :, 0:40], 0)
-    sb, sb_out = fold(s_keep[:, :, :, 40:80], s_got[:, :, :, 40:80], 1)
+    slots = (2, 2, 4, 40, width)
+    sa, sa_out = fold(sa_keep.reshape(slots), move(sa_send, 0, 1).reshape(slots), 0)
+    sb, sb_out = fold(sb_keep.reshape(slots), move(sb_send, 0, 1).reshape(slots), 1)
     sa, sa_out, sb, sb_out, gf_high = lax.optimization_barrier((sa, sa_out, sb, sb_out, gf_high))
 
     sa_got, sb_got = move(sa_out, 1, 0), move(sb_out, 0, 2)
@@ -747,8 +761,7 @@
     g1 = move(g1, 0, 1)
     w_line = [w_piece] + [move(w_piece, 2 * z, 0) for z in (1, 2, 3)]
     s_near = [sa, sb, move(sa, 1, 0), move(sb, 0, 2)]
-    tick = move(w_line[1][0:8] + w_line[2][0:8] + w_line[3][0:8], 0, 1)
-    s_near, g2, g3, tick = lax.optimization_barrier((s_near, g2, g3, tick))
+    s_near, g2, g3 = lax.optimization_barrier((s_near, g2, g3))
 
     w_other = move(jnp.stack(w_line), 1, 0)
     g2 = move(g2, 0, 2)

time: 144 us -> 142 us (0.986)
    slice x1 -> x0, other arithmetic: 1.48 us -> none  [per_device(): sb, sb_out = fold(s_keep[:, :, :, 40:80], s_got[:, :, :, 40:80], 1)]
    ppermute x47 -> x48, waiting for transfers between devices: 50 us -> 48.7 us  [move(): return lax.ppermute(value, ('dp', 'field'), pairs)]
    ppermute x47 -> x48, starting transfers between devices: 42.6 us -> 43 us  [move(): return lax.ppermute(value, ('dp', 'field'), pairs)]
  transfers between devices with their start and end apart: 47 -> 48, of which waited for: 22 -> 23; matrix products, arithmetic and copies ran while one was open for 4% -> 5% of each run, Pallas kernels for 12% -> 12%
where the time goes in v5:
time: 142 us; the launch traced here: 141 us
  waiting for transfers between devices  48.7 us (34%)
  starting transfers between devices  43 us (30%)
  Pallas kernels  37.7 us (27%)
  local copies, waits for them, and re-layouts  6.95 us (5%)
  between operations  2.89 us (2%)
  other arithmetic  2.27 us (2%)
    ppermute x48, waiting for transfers between devices, move(): return lax.ppermute(value, ('dp', 'field'), pairs)  48.7 us
    ppermute x48, starting transfers between devices, move(): return lax.ppermute(value, ('dp', 'field'), pairs)  43 us
    pallas_call x1, Pallas kernels, per_device(): pl.pallas_call(middle_kernel, name='middle', out_shape=(like((4 * cols, r...  19.9 us
    pallas_call x1, Pallas kernels, per_device(): pl.pallas_call(first_kernel, name='first', out_shape=tuple((like((2, 8, c...  7.02 us
    pallas_call x1, Pallas kernels, per_device(): pl.pallas_call(inputs_kernel, name='inputs', out_shape=tuple((like((rows,...  5.56 us
  transfers between devices with their start and end apart: 48, of which 23 were waited for; matrix products, arithmetic and copies ran while one was open for 5% of the time, Pallas kernels for 12%

profile of v5, /device:TPU:0, one launch (start us, length us, event | category | flops | bytes accessed | tf_op | source)
XLA Modules:
  0.0 141.4 jit_solution(4973171971998860508)
XLA Ops:
  0.7 0.5 collective-permute-start.1
  1.2 1.0 constant_dynamic-slice_fusion.4
  2.2 2.6 %collective-permute-start = (f32[2,128,256]{2,1,0:T(8,128)S(1)}, f32[2,128,256]{2,1,0:T(8,128)S(1)}, u32[]{:S(2)}, u32[]{:S(2)}) collective-permute-start(f32[2,128,256]{2,1,0:T(8,128)S(1)} %constant_dynamic-slice_fusion.4), channel_id=1, source_target_pairs={{0,2},{1,3},{2,0},{3,1},{4,6},{5,7},{6,4},{7,5},{8,10},{9,11},{10,... | collective-permute-start | bytes 786440 | tf_op jit(solution)/shard_map/ppermute | solution.py:567
  4.8 2.0 %constant_dynamic-slice_fusion = (f32[512,128]{1,0:T(8,128)}, f32[512,128]{1,0:T(8,128)S(1)}, f32[512,128]{1,0:T(8,128)S(1)}, f32[512,128]{1,0:T(8,128)S(1)}) fusion(f32[2048,128]{1,0:T(8,128)} %param.14, s32[]{:T(128)S(6)} %select_n.19, s32[]{:T(128)S(6)} %select_n.17, s32[]{:T(128)S(6)} %select_n.16, s32[]{:T(128)S(6)} %select_n.18), kind=kLoop, calls=%fused_computation.38 | loop fusion | bytes 2097168 | tf_op jit(solution)/shard_map/dynamic_slice | solution.py:588
  7.4 0.6 reshape.56.domain
  8.0 0.6 stack.73.place
  8.7 3.1 %collective-permute-done.fa0 = f32[2,128,256]{2,1,0:T(8,128)S(1)} collective-permute-done((f32[2,128,256]{2,1,0:T(8,128)S(1)}, f32[2,128,256]{2,1,0:T(8,128)S(1)}, u32[]{:S(2)}, u32[]{:S(2)}) %collective-permute-start) | collective-permute-done | bytes 262176 | tf_op jit(solution)/shard_map/ppermute | solution.py:567
  11.7 1.8 %collective-permute-start.3 = (f32[1048,128]{1,0:T(8,128)S(1)}, f32[1048,128]{1,0:T(8,128)S(1)}, u32[]{:S(2)}, u32[]{:S(2)}) collective-permute-start(f32[1048,128]{1,0:T(8,128)S(1)} %pad_maximum_fusion), channel_id=1, source_target_pairs={{0,2},{1,3},{2,0},{3,1},{4,6},{5,7},{6,4},{7,5},{8,10},{9,11},{10,... | collective-permute-start | bytes 1609736 | tf_op jit(solution)/shard_map/ppermute | solution.py:567
  13.5 2.5 %collective-permute-start.6 = (f32[2,128,256]{2,1,0:T(8,128)S(1)}, f32[2,128,256]{2,1,0:T(8,128)S(1)}, u32[]{:S(2)}, u32[]{:S(2)}) collective-permute-start(f32[2,128,256]{2,1,0:T(8,128)S(1)} %collective-permute-done.fa0), channel_id=1, source_target_pairs={{0,12},{1,13},{2,14},{3,15},{4,8},{5,9},{6,10},{7,11},{8,4},{9,5},... | collective-permute-start | bytes 786440 | tf_op jit(solution)/shard_map/ppermute | solution.py:567
  16.5 0.5 collective-permute-start.4
  17.0 6.6 %collective-permute-done.6.fa3 = f32[2,128,256]{2,1,0:T(8,128)S(1)} collective-permute-done((f32[2,128,256]{2,1,0:T(8,128)S(1)}, f32[2,128,256]{2,1,0:T(8,128)S(1)}, u32[]{:S(2)}, u32[]{:S(2)}) %collective-permute-start.6) | collective-permute-done | bytes 262176 | tf_op jit(solution)/shard_map/ppermute | solution.py:567
  23.6 5.3 %collective-permute-done.5.fa2 = f32[2,128,256]{2,1,0:T(8,128)S(1)} collective-permute-done((f32[2,128,256]{2,1,0:T(8,128)S(1)}, f32[2,128,256]{2,1,0:T(8,128)S(1)}, u32[]{:S(2)}, u32[]{:S(2)}) %collective-permute-start.5) | collective-permute-done | bytes 262176 | tf_op jit(solution)/shard_map/ppermute | solution.py:567
  29.0 0.5 collective-permute-start.8
  30.0 1.2 collective-permute-done.8.fb0
  33.3 19.9 %middle.1 = (bf16[512,512]{1,0:T(8,128)(2,1)}, bf16[512,512]{1,0:T(8,128)(2,1)}, bf16[8,256,512]{2,1,0:T(8,128)(2,1)}, bf16[8,256,512]{2,1,0:T(8,128)(2,1)}, f32...) custom-call(s32[5]{0:T(128)} %stack.73.place, ...), custom_call_target="tpu_custom_call" | custom-call | tf_op jit(solution)/shard_map/middle/pallas_call | solution.py:608
  53.8 1.8 %collective-permute-done.12 = f32[16,40,256]{2,1,0:T(8,128)S(1)} collective-permute-done((f32[16,40,256]{2,1,0:T(8,128)}, f32[16,40,256]{2,1,0:T(8,128)S(1)}, u32[]{:S(2)}, u32[]{:S(2)}) %collective-permute-start.12) | collective-permute-done | bytes 655392 | tf_op jit(solution)/shard_map/ppermute | solution.py:567
  55.6 1.2 add.98
  57.0 1.5 %collective-permute-start.16 = (f32[2,4,40,256]{3,2,1,0:T(8,128)S(1)}, f32[2,4,40,256]{3,2,1,0:T(8,128)S(1)}, u32[]{:S(2)}, u32[]{:S(2)}) collective-permute-start(f32[2,4,40,256]{3,2,1,0:T(8,128)S(1)} %bitcast.109), channel_id=1, source_target_pairs={{0,4},{1,5},{2,6},{3,7},{4,0},{5,1},{6,2},{7,3},{8,12},{9,13},{10,... | collective-permute-start | bytes 983048 | tf_op jit(solution)/shard_map/ppermute | solution.py:567
  58.5 0.5 collective-permute-start.18
  59.0 7.0 %first.1 = (f32[2,8,64,256]{3,2,1,0:T(8,128)}, f32[2,8,64,256]{3,2,1,0:T(8,128)}, f32[2,8,64,256]{3,2,1,0:T(8,128)}, f32[2,8,64,256]{3,2,1,0:T(8,128)}) custom-call(s32[1]{0:T(128)} %bitcast.2.place, bf16[512,512]{1,0:T(8,128)(2,1)} %get-tuple-element.94.xt_high_in, bf16[512,512]{1,0:T(8,128)(2,1)} %get-tuple-element.95.xt_low_in, ...), custom_call_target="tpu_custom_call" | custom-call | bytes 1048576 | tf_op jit(solution)/shard_map/first/pallas_call | solution.py:696
  66.1 0.5 collective-permute-start.15
  66.9 1.3 collective-permute-start.17
  68.3 0.7 collective-permute-start.19
  69.0 3.9 %collective-permute-done.17 = f32[4,40,256]{2,1,0:T(8,128)S(1)} collective-permute-done((f32[4,40,256]{2,1,0:T(8,128)S(1)}, f32[4,40,256]{2,1,0:T(8,128)S(1)}, u32[]{:S(2)}, u32[]{:S(2)}) %collective-permute-start.17) | collective-permute-done | bytes 163872 | tf_op jit(solution)/shard_map/ppermute | solution.py:567
  72.9 1.3 collective-permute-done.19
  74.6 1.0 copy-done.24
  75.9 1.6 %collective-permute-start.24 = (f32[80,256]{1,0:T(8,128)S(1)}, f32[80,256]{1,0:T(8,128)S(1)}, u32[]{:S(2)}, u32[]{:S(2)}) collective-permute-start(f32[80,256]{1,0:T(8,128)S(1)} %get-tuple-element.169), channel_id=1, source_target_pairs={{0,8},{1,9},{2,10},{3,11},{4,12},{5,13},{6,14},{7,15},{8,0},{9,1},... | collective-permute-start | bytes 245768 | tf_op jit(solution)/shard_map/ppermute | solution.py:567
  77.5 2.5 %collective-permute-start.26 = (f32[80,256]{1,0:T(8,128)S(1)}, f32[80,256]{1,0:T(8,128)S(1)}, u32[]{:S(2)}, u32[]{:S(2)}) collective-permute-start(f32[80,256]{1,0:T(8,128)S(1)} %get-tuple-element.170), channel_id=1, source_target_pairs={{0,24},{1,25},{2,26},{3,27},{4,28},{5,29},{6,30},{7,31},{8,16},{9,... | collective-permute-start | bytes 245768 | tf_op jit(solution)/shard_map/ppermute | solution.py:567
  80.1 0.5 collective-permute-start.20
  80.6 1.0 collective-permute-start.22
  81.7 2.5 %collective-permute-done.26 = f32[80,256]{1,0:T(8,128)S(1)} collective-permute-done((f32[80,256]{1,0:T(8,128)S(1)}, f32[80,256]{1,0:T(8,128)S(1)}, u32[]{:S(2)}, u32[]{:S(2)}) %collective-permute-start.26) | collective-permute-done | bytes 81952 | tf_op jit(solution)/shard_map/ppermute | solution.py:567
  84.2 2.7 %collective-permute-done.25 = f32[80,256]{1,0:T(8,128)S(1)} collective-permute-done((f32[80,256]{1,0:T(8,128)S(1)}, f32[80,256]{1,0:T(8,128)S(1)}, u32[]{:S(2)}, u32[]{:S(2)}) %collective-permute-start.25) | collective-permute-done | bytes 81952 | tf_op jit(solution)/shard_map/ppermute | solution.py:567
  86.9 0.5 slice.128
  88.2 0.7 collective-permute-start.28
  88.9 2.3 %collective-permute-start.27 = (f32[80,256]{1,0:T(8,128)S(1)}, f32[80,256]{1,0:T(8,128)S(1)}, u32[]{:S(2)}, u32[]{:S(2)}) collective-permute-start(f32[80,256]{1,0:T(8,128)S(1)} %broadcast_multiply_fusion), channel_id=1, source_target_pairs={{0,8},{1,9},{2,10},{3,11},{4,12},{5,13},{6,14},{7,15},{8,0},{9,1},... | collective-permute-start | bytes 245768 | tf_op jit(solution)/shard_map/ppermute | solution.py:567
  91.2 1.4 %collective-permute-start.29 = (f32[80,256]{1,0:T(8,128)S(1)}, f32[80,256]{1,0:T(8,128)S(1)}, u32[]{:S(2)}, u32[]{:S(2)}) collective-permute-start(f32[80,256]{1,0:T(8,128)S(1)} %broadcast_multiply_fusion), channel_id=1, source_target_pairs={{0,24},{1,25},{2,26},{3,27},{4,28},{5,29},{6,30},{7,31},{8,16},{9,... | collective-permute-start | bytes 245768 | tf_op jit(solution)/shard_map/ppermute | solution.py:567
  92.8 0.7 collective-permute-start.21
  93.6 0.8 collective-permute-start.23
  94.3 1.2 collective-permute-done.28
  95.5 1.9 %collective-permute-done.29 = f32[80,256]{1,0:T(8,128)S(1)} collective-permute-done((f32[80,256]{1,0:T(8,128)S(1)}, f32[80,256]{1,0:T(8,128)S(1)}, u32[]{:S(2)}, u32[]{:S(2)}) %collective-permute-start.29) | collective-permute-done | bytes 81952 | tf_op jit(solution)/shard_map/ppermute | solution.py:567
  97.5 2.2 %collective-permute-done.21 = f32[4,64,256]{2,1,0:T(8,128)S(1)} collective-permute-done((f32[4,64,256]{2,1,0:T(8,128)S(1)}, f32[4,64,256]{2,1,0:T(8,128)S(1)}, u32[]{:S(2)}, u32[]{:S(2)}) %collective-permute-start.21) | collective-permute-done | bytes 262176 | tf_op jit(solution)/shard_map/ppermute | solution.py:567
  99.7 0.5 collective-permute-done.23
  100.3 1.2 collective-permute-start.30
  101.5 2.5 %collective-permute-start.32 = (f32[128,256]{1,0:T(8,128)S(1)}, f32[128,256]{1,0:T(8,128)S(1)}, u32[]{:S(2)}, u32[]{:S(2)}) collective-permute-start(f32[128,256]{1,0:T(8,128)S(1)} %get-tuple-element.163), channel_id=1, source_target_pairs={{0,24},{1,25},{2,26},{3,27},{4,28},{5,29},{6,30},{7,31},{8,16},{9,... | collective-permute-start | bytes 393224 | tf_op jit(solution)/shard_map/ppermute | solution.py:567
  104.0 1.4 collective-permute-start.34
  105.4 1.6 %collective-permute-start.33 = (f32[4,40,256]{2,1,0:T(8,128)S(1)}, f32[4,40,256]{2,1,0:T(8,128)S(1)}, u32[]{:S(2)}, u32[]{:S(2)}) collective-permute-start(f32[4,40,256]{2,1,0:T(8,128)S(1)} %get-tuple-element.168), channel_id=1, source_target_pairs={{0,2},{1,3},{2,0},{3,1},{4,6},{5,7},{6,4},{7,5},{8,10},{9,11},{10,... | collective-permute-start | bytes 491528 | tf_op jit(solution)/shard_map/ppermute | solution.py:567
  107.1 5.6 %inputs.1 = (f32[512,128]{1,0:T(8,128)S(1)}, f32[512,128]{1,0:T(8,128)S(1)}, f32[512,128]{1,0:T(8,128)S(1)}, f32[512,128]{1,0:T(8,128)S(1)}) custom-call(s32[5]{0:T(128)S(1)} %copy-done.23, f32[24,512]{1,0:T(8,128)S(1)} %copy-done.21, f32[24,512]{1,0:T(8,128)S(1)} %copy-done.22, bf16[8,256,512]{2,1,0:T(8,128)(2,1)S(1)} %copy-done, ...), custom_call_target="tpu_custom_call" | custom-call | bytes 1048576 | tf_op jit(solution)/shard_map/inputs/pallas_call | solution.py:737
  112.9 1.6 %collective-permute-start.35 = (f32[2,4,40,256]{3,2,1,0:T(8,128)S(1)}, f32[2,4,40,256]{3,2,1,0:T(8,128)S(1)}, u32[]{:S(2)}, u32[]{:S(2)}) collective-permute-start(f32[2,4,40,256]{3,2,1,0:T(8,128)S(1)} %pad_maximum_fusion.5.a0), channel_id=1, source_target_pairs={{0,4},{1,5},{2,6},{3,7},{4,0},{5,1},{6,2},{7,3},{8,12},{9,13},{10,... | collective-permute-start | bytes 983048 | tf_op jit(solution)/shard_map/ppermute | solution.py:567
  114.4 0.5 collective-permute-start.36
  114.9 1.8 %collective-permute-start.46 = (f32[128,256]{1,0:T(8,128)S(1)}, f32[128,256]{1,0:T(8,128)S(1)}, u32[]{:S(2)}, u32[]{:S(2)}) collective-permute-start(f32[128,256]{1,0:T(8,128)S(1)} %fusion.6.a0), channel_id=1, source_target_pairs={{0,24},{1,25},{2,26},{3,27},{4,28},{5,29},{6,30},{7,31},{8,16},{9,... | collective-permute-start | bytes 393224 | tf_op jit(solution)/shard_map/ppermute | solution.py:567
  116.7 0.8 collective-permute-start.45
  117.5 1.8 %collective-permute-start.44 = (f32[128,256]{1,0:T(8,128)S(1)}, f32[128,256]{1,0:T(8,128)S(1)}, u32[]{:S(2)}, u32[]{:S(2)}) collective-permute-start(f32[128,256]{1,0:T(8,128)S(1)} %fusion.6.a0), channel_id=1, source_target_pairs={{0,8},{1,9},{2,10},{3,11},{4,12},{5,13},{6,14},{7,15},{8,0},{9,1},... | collective-permute-start | bytes 393224 | tf_op jit(solution)/shard_map/ppermute | solution.py:567
  119.3 2.3 %collective-permute-done.35.a2 = f32[2,4,40,256]{3,2,1,0:T(8,128)S(1)} collective-permute-done((f32[2,4,40,256]{3,2,1,0:T(8,128)S(1)}, f32[2,4,40,256]{3,2,1,0:T(8,128)S(1)}, u32[]{:S(2)}, u32[]{:S(2)}) %collective-permute-start.35) | collective-permute-done | bytes 327712 | tf_op jit(solution)/shard_map/ppermute | solution.py:567
  121.5 1.2 collective-permute-done.36.a3
  123.4 3.1 %collective-permute-done.45.a2 = f32[128,256]{1,0:T(8,128)S(1)} collective-permute-done((f32[128,256]{1,0:T(8,128)S(1)}, f32[128,256]{1,0:T(8,128)S(1)}, u32[]{:S(2)}, u32[]{:S(2)}) %collective-permute-start.45) | collective-permute-done | bytes 131104 | tf_op jit(solution)/shard_map/ppermute | solution.py:567
  126.5 0.6 collective-permute-start.47
  127.1 0.5 collective-permute-start.38
  127.6 4.4 %collective-permute-done.42.g2 = f32[512,128]{1,0:T(8,128)S(1)} collective-permute-done((f32[512,128]{1,0:T(8,128)S(1)}, f32[512,128]{1,0:T(8,128)S(1)}, u32[]{:S(2)}, u32[]{:S(2)}) %collective-permute-start.42) | collective-permute-done | bytes 262176 | tf_op jit(solution)/shard_map/ppermute | solution.py:567
  132.0 2.2 %collective-permute-done.43.g3 = f32[512,128]{1,0:T(8,128)S(1)} collective-permute-done((f32[512,128]{1,0:T(8,128)S(1)}, f32[512,128]{1,0:T(8,128)S(1)}, u32[]{:S(2)}, u32[]{:S(2)}) %collective-permute-start.43) | collective-permute-done | bytes 262176 | tf_op jit(solution)/shard_map/ppermute | solution.py:567
  134.2 1.8 %collective-permute-start.40 = (f32[2,4,40,256]{3,2,1,0:T(8,128)S(1)}, f32[2,4,40,256]{3,2,1,0:T(8,128)S(1)}, u32[]{:S(2)}, u32[]{:S(2)}) collective-permute-start(f32[2,4,40,256]{3,2,1,0:T(8,128)S(1)} %collective-permute-done.36.a3), channel_id=1, source_target_pairs={{0,1},{1,0},{2,3},{3,2},{4,5},{5,4},{6,7},{7,6},{8,9},{9,8},{10,11... | collective-permute-start | bytes 983048 | tf_op jit(solution)/shard_map/ppermute | solution.py:567
  136.1 0.8 place_near.1.begun
  136.9 1.1 finish_inputs.1
  138.0 2.4 %finish_second.1 = (f32[8,256,256]{2,1,0:T(8,128)}, f32[3,256,128]{2,1,0:T(8,128)}, f32[3,8,128]{2,1,0:T(8,128)}, f32[16,24]{1,0:T(8,128)}, f32[8,256]{1,0:T(8,1...) custom-call(s32[2]{0:T(128)S(1)} %pad_add_fusion.place, ...), custom_call_target="tpu_custom_call" | custom-call | tf_op jit(solution)/shard_map/finish_second/pallas_call | solution.py:771
  140.4 0.8 place_far.1
  (144 shorter events, 6.4 us)
Async XLA Ops:
  0.7 11.1 %collective-permute-start.1 = (f32[8,128,256]{2,1,0:T(8,128)}, f32[8,128,256]{2,1,0:T(8,128)S(1)}, u32[]{:S(2)}, u32[]{:S(2)}) collective-permute-start(f32[8,128,256]{2,1,0:T(8,128)} %near0.3), channel_id=1, source_target_pairs={{0,1},{1,0},{2,3},{3,2},{4,5},{5,4},{6,7},{7,6},{8,9},{9,8},{10,11... | collective-permute-start | bytes 3145736 | tf_op jit(solution)/shard_map/ppermute | solution.py:567
  2.2 9.6 %collective-permute-start = (f32[2,128,256]{2,1,0:T(8,128)S(1)}, f32[2,128,256]{2,1,0:T(8,128)S(1)}, u32[]{:S(2)}, u32[]{:S(2)}) collective-permute-start(f32[2,128,256]{2,1,0:T(8,128)S(1)} %constant_dynamic-slice_fusion.4), channel_id=1, source_target_pairs={{0,2},{1,3},{2,0},{3,1},{4,6},{5,7},{6,4},{7,5},{8,10},{9,11},{10,... | collective-permute-start | bytes 786440 | tf_op jit(solution)/shard_map/ppermute | solution.py:567
  11.7 20.7 %copy-start.5 = (f32[2,128,256]{2,1,0:T(8,128)}, f32[2,128,256]{2,1,0:T(8,128)S(1)}, u32[]{:S(2)}) copy-start(f32[2,128,256]{2,1,0:T(8,128)S(1)} %collective-permute-done.fa0) | copy-start | bytes 786436
  11.7 20.7 %copy-start.3 = (f32[8,128,256]{2,1,0:T(8,128)}, f32[8,128,256]{2,1,0:T(8,128)S(1)}, u32[]{:S(2)}) copy-start(f32[8,128,256]{2,1,0:T(8,128)S(1)} %collective-permute-done.1.near1) | copy-start | bytes 3145732
  11.7 17.1 %collective-permute-start.3 = (f32[1048,128]{1,0:T(8,128)S(1)}, f32[1048,128]{1,0:T(8,128)S(1)}, u32[]{:S(2)}, u32[]{:S(2)}) collective-permute-start(f32[1048,128]{1,0:T(8,128)S(1)} %pad_maximum_fusion), channel_id=1, source_target_pairs={{0,2},{1,3},{2,0},{3,1},{4,6},{5,7},{6,4},{7,5},{8,10},{9,11},{10,... | collective-permute-start | bytes 1609736 | tf_op jit(solution)/shard_map/ppermute | solution.py:567
  13.5 15.3 %collective-permute-start.2 = (f32[536,128]{1,0:T(8,128)S(1)}, f32[536,128]{1,0:T(8,128)S(1)}, u32[]{:S(2)}, u32[]{:S(2)}) collective-permute-start(f32[536,128]{1,0:T(8,128)S(1)} %pad_maximum_fusion.7), channel_id=1, source_target_pairs={{0,1},{1,0},{2,3},{3,2},{4,5},{5,4},{6,7},{7,6},{8,9},{9,8},{10,11... | collective-permute-start | bytes 823304 | tf_op jit(solution)/shard_map/ppermute | solution.py:567
  13.5 10.0 %collective-permute-start.6 = (f32[2,128,256]{2,1,0:T(8,128)S(1)}, f32[2,128,256]{2,1,0:T(8,128)S(1)}, u32[]{:S(2)}, u32[]{:S(2)}) collective-permute-start(f32[2,128,256]{2,1,0:T(8,128)S(1)} %collective-permute-done.fa0), channel_id=1, source_target_pairs={{0,12},{1,13},{2,14},{3,15},{4,8},{5,9},{6,10},{7,11},{8,4},{9,5},... | collective-permute-start | bytes 786440 | tf_op jit(solution)/shard_map/ppermute | solution.py:567
  16.0 12.8 %collective-permute-start.5 = (f32[2,128,256]{2,1,0:T(8,128)S(1)}, f32[2,128,256]{2,1,0:T(8,128)S(1)}, u32[]{:S(2)}, u32[]{:S(2)}) collective-permute-start(f32[2,128,256]{2,1,0:T(8,128)S(1)} %collective-permute-done.fa0), channel_id=1, source_target_pairs={{0,8},{1,9},{2,10},{3,11},{4,12},{5,13},{6,14},{7,15},{8,0},{9,1},... | collective-permute-start | bytes 786440 | tf_op jit(solution)/shard_map/ppermute | solution.py:567
  16.5 12.4 %collective-permute-start.4 = (f32[2,128,256]{2,1,0:T(8,128)S(1)}, f32[2,128,256]{2,1,0:T(8,128)S(1)}, u32[]{:S(2)}, u32[]{:S(2)}) collective-permute-start(f32[2,128,256]{2,1,0:T(8,128)S(1)} %collective-permute-done.fa0), channel_id=1, source_target_pairs={{0,4},{1,5},{2,6},{3,7},{4,0},{5,1},{6,2},{7,3},{8,12},{9,13},{10,... | collective-permute-start | bytes 786440 | tf_op jit(solution)/shard_map/ppermute | solution.py:567
  28.9 3.5 %collective-permute-start.7 = (f32[1048,128]{1,0:T(8,128)S(1)}, f32[1048,128]{1,0:T(8,128)S(1)}, u32[]{:S(2)}, u32[]{:S(2)}) collective-permute-start(f32[1048,128]{1,0:T(8,128)S(1)} %collective-permute-done.3.x2), channel_id=1, source_target_pairs={{0,1},{1,0},{2,3},{3,2},{4,5},{5,4},{6,7},{7,6},{8,9},{9,8},{10,11... | collective-permute-start | bytes 1609736 | tf_op jit(solution)/shard_map/ppermute | solution.py:567
  29.0 2.3 %collective-permute-start.8 = (f32[2,128,256]{2,1,0:T(8,128)S(1)}, f32[2,128,256]{2,1,0:T(8,128)S(1)}, u32[]{:S(2)}, u32[]{:S(2)}) collective-permute-start(f32[2,128,256]{2,1,0:T(8,128)S(1)} %collective-permute-done.fa0), channel_id=1, source_target_pairs={{0,1},{1,0},{2,3},{3,2},{4,5},{5,4},{6,7},{7,6},{8,9},{9,8},{10,11... | collective-permute-start | bytes 786440 | tf_op jit(solution)/shard_map/ppermute | solution.py:567
  29.5 2.2 %collective-permute-start.9 = (f32[2,128,256]{2,1,0:T(8,128)S(1)}, f32[2,128,256]{2,1,0:T(8,128)S(1)}, u32[]{:S(2)}, u32[]{:S(2)}) collective-permute-start(f32[2,128,256]{2,1,0:T(8,128)S(1)} %collective-permute-done.4.fa1), channel_id=1, source_target_pairs={{0,1},{1,0},{2,3},{3,2},{4,5},{5,4},{6,7},{7,6},{8,9},{9,8},{10,11... | collective-permute-start | bytes 786440 | tf_op jit(solution)/shard_map/ppermute | solution.py:567
  29.5 2.5 %collective-permute-start.10 = (f32[2,128,256]{2,1,0:T(8,128)S(1)}, f32[2,128,256]{2,1,0:T(8,128)S(1)}, u32[]{:S(2)}, u32[]{:S(2)}) collective-permute-start(f32[2,128,256]{2,1,0:T(8,128)S(1)} %collective-permute-done.5.fa2), channel_id=1, source_target_pairs={{0,1},{1,0},{2,3},{3,2},{4,5},{5,4},{6,7},{7,6},{8,9},{9,8},{10,11... | collective-permute-start | bytes 786440 | tf_op jit(solution)/shard_map/ppermute | solution.py:567
  30.0 2.4 %collective-permute-start.11 = (f32[2,128,256]{2,1,0:T(8,128)S(1)}, f32[2,128,256]{2,1,0:T(8,128)S(1)}, u32[]{:S(2)}, u32[]{:S(2)}) collective-permute-start(f32[2,128,256]{2,1,0:T(8,128)S(1)} %collective-permute-done.6.fa3), channel_id=1, source_target_pairs={{0,1},{1,0},{2,3},{3,2},{4,5},{5,4},{6,7},{7,6},{8,9},{9,8},{10,11... | collective-permute-start | bytes 786440 | tf_op jit(solution)/shard_map/ppermute | solution.py:567
  53.2 2.4 %collective-permute-start.12 = (f32[16,40,256]{2,1,0:T(8,128)}, f32[16,40,256]{2,1,0:T(8,128)S(1)}, u32[]{:S(2)}, u32[]{:S(2)}) collective-permute-start(f32[16,40,256]{2,1,0:T(8,128)} %get-tuple-element.97), channel_id=1, source_target_pairs={{0,1},{1,0},{2,3},{3,2},{4,5},{5,4},{6,7},{7,6},{8,9},{9,8},{10,11... | collective-permute-start | bytes 1966088 | tf_op jit(solution)/shard_map/ppermute | solution.py:567
  53.4 3.4 %collective-permute-start.13 = (f32[16,40,256]{2,1,0:T(8,128)}, f32[16,40,256]{2,1,0:T(8,128)S(1)}, u32[]{:S(2)}, u32[]{:S(2)}) collective-permute-start(f32[16,40,256]{2,1,0:T(8,128)} %get-tuple-element.99), channel_id=1, source_target_pairs={{0,1},{1,0},{2,3},{3,2},{4,5},{5,4},{6,7},{7,6},{8,9},{9,8},{10,11... | collective-permute-start | bytes 1966088 | tf_op jit(solution)/shard_map/ppermute | solution.py:567
  57.0 9.8 %collective-permute-start.16 = (f32[2,4,40,256]{3,2,1,0:T(8,128)S(1)}, f32[2,4,40,256]{3,2,1,0:T(8,128)S(1)}, u32[]{:S(2)}, u32[]{:S(2)}) collective-permute-start(f32[2,4,40,256]{3,2,1,0:T(8,128)S(1)} %bitcast.109), channel_id=1, source_target_pairs={{0,4},{1,5},{2,6},{3,7},{4,0},{5,1},{6,2},{7,3},{8,12},{9,13},{10,... | collective-permute-start | bytes 983048 | tf_op jit(solution)/shard_map/ppermute | solution.py:567
  58.5 9.8 %collective-permute-start.18 = (f32[2,4,40,256]{3,2,1,0:T(8,128)S(1)}, f32[2,4,40,256]{3,2,1,0:T(8,128)S(1)}, u32[]{:S(2)}, u32[]{:S(2)}) collective-permute-start(f32[2,4,40,256]{3,2,1,0:T(8,128)S(1)} %get-tuple-element.110), channel_id=1, source_target_pairs={{0,2},{1,3},{2,0},{3,1},{4,6},{5,7},{6,4},{7,5},{8,10},{9,11},{10,... | collective-permute-start | bytes 983048 | tf_op jit(solution)/shard_map/ppermute | solution.py:567
  66.0 8.3 %collective-permute-start.14 = (f32[2,8,64,256]{3,2,1,0:T(8,128)}, f32[2,8,64,256]{3,2,1,0:T(8,128)S(1)}, u32[]{:S(2)}, u32[]{:S(2)}) collective-permute-start(f32[2,8,64,256]{3,2,1,0:T(8,128)} %get-tuple-element.104), channel_id=1, source_target_pairs={{0,1},{1,0},{2,3},{3,2},{4,5},{5,4},{6,7},{7,6},{8,9},{9,8},{10,11... | collective-permute-start | bytes 3145736 | tf_op jit(solution)/shard_map/ppermute | solution.py:567
  66.1 8.5 %collective-permute-start.15 = (f32[2,8,64,256]{3,2,1,0:T(8,128)}, f32[2,8,64,256]{3,2,1,0:T(8,128)S(1)}, u32[]{:S(2)}, u32[]{:S(2)}) collective-permute-start(f32[2,8,64,256]{3,2,1,0:T(8,128)} %get-tuple-element.106), channel_id=1, source_target_pairs={{0,1},{1,0},{2,3},{3,2},{4,5},{5,4},{6,7},{7,6},{8,9},{9,8},{10,11... | collective-permute-start | bytes 3145736 | tf_op jit(solution)/shard_map/ppermute | solution.py:567
  66.9 6.0 %collective-permute-start.17 = (f32[4,40,256]{2,1,0:T(8,128)S(1)}, f32[4,40,256]{2,1,0:T(8,128)S(1)}, u32[]{:S(2)}, u32[]{:S(2)}) collective-permute-start(f32[4,40,256]{2,1,0:T(8,128)S(1)} %slice_bitcast_fusion.10), channel_id=1, source_target_pairs={{0,2},{1,3},{2,0},{3,1},{4,6},{5,7},{6,4},{7,5},{8,10},{9,11},{10,... | collective-permute-start | bytes 491528 | tf_op jit(solution)/shard_map/ppermute | solution.py:567
  68.3 6.0 %collective-permute-start.19 = (f32[4,40,256]{2,1,0:T(8,128)S(1)}, f32[4,40,256]{2,1,0:T(8,128)S(1)}, u32[]{:S(2)}, u32[]{:S(2)}) collective-permute-start(f32[4,40,256]{2,1,0:T(8,128)S(1)} %slice_bitcast_fusion.8), channel_id=1, source_target_pairs={{0,4},{1,5},{2,6},{3,7},{4,0},{5,1},{6,2},{7,3},{8,12},{9,13},{10,... | collective-permute-start | bytes 491528 | tf_op jit(solution)/shard_map/ppermute | solution.py:567
  75.9 5.8 %collective-permute-start.24 = (f32[80,256]{1,0:T(8,128)S(1)}, f32[80,256]{1,0:T(8,128)S(1)}, u32[]{:S(2)}, u32[]{:S(2)}) collective-permute-start(f32[80,256]{1,0:T(8,128)S(1)} %get-tuple-element.169), channel_id=1, source_target_pairs={{0,8},{1,9},{2,10},{3,11},{4,12},{5,13},{6,14},{7,15},{8,0},{9,1},... | collective-permute-start | bytes 245768 | tf_op jit(solution)/shard_map/ppermute | solution.py:567
  77.5 6.6 %collective-permute-start.26 = (f32[80,256]{1,0:T(8,128)S(1)}, f32[80,256]{1,0:T(8,128)S(1)}, u32[]{:S(2)}, u32[]{:S(2)}) collective-permute-start(f32[80,256]{1,0:T(8,128)S(1)} %get-tuple-element.170), channel_id=1, source_target_pairs={{0,24},{1,25},{2,26},{3,27},{4,28},{5,29},{6,30},{7,31},{8,16},{9,... | collective-permute-start | bytes 245768 | tf_op jit(solution)/shard_map/ppermute | solution.py:567
  80.0 6.9 %collective-permute-start.25 = (f32[80,256]{1,0:T(8,128)S(1)}, f32[80,256]{1,0:T(8,128)S(1)}, u32[]{:S(2)}, u32[]{:S(2)}) collective-permute-start(f32[80,256]{1,0:T(8,128)S(1)} %get-tuple-element.171), channel_id=1, source_target_pairs={{0,16},{1,17},{2,18},{3,19},{4,20},{5,21},{6,22},{7,23},{8,24},{9,... | collective-permute-start | bytes 245768 | tf_op jit(solution)/shard_map/ppermute | solution.py:567
  80.1 12.5 %collective-permute-start.20 = (f32[2,4,64,256]{3,2,1,0:T(8,128)S(1)}, f32[2,4,64,256]{3,2,1,0:T(8,128)S(1)}, u32[]{:S(2)}, u32[]{:S(2)}) collective-permute-start(f32[2,4,64,256]{3,2,1,0:T(8,128)S(1)} %bitcast.108), channel_id=1, source_target_pairs={{0,2},{1,3},{2,0},{3,1},{4,6},{5,7},{6,4},{7,5},{8,10},{9,11},{10,... | collective-permute-start | bytes 1572872 | tf_op jit(solution)/shard_map/ppermute | solution.py:567
  80.6 12.8 %collective-permute-start.22 = (f32[2,4,64,256]{3,2,1,0:T(8,128)S(1)}, f32[2,4,64,256]{3,2,1,0:T(8,128)S(1)}, u32[]{:S(2)}, u32[]{:S(2)}) collective-permute-start(f32[2,4,64,256]{3,2,1,0:T(8,128)S(1)} %get-tuple-element.114), channel_id=1, source_target_pairs={{0,4},{1,5},{2,6},{3,7},{4,0},{5,1},{6,2},{7,3},{8,12},{9,13},{10,... | collective-permute-start | bytes 1572872 | tf_op jit(solution)/shard_map/ppermute | solution.py:567
  88.2 7.4 %collective-permute-start.28 = (f32[80,256]{1,0:T(8,128)S(1)}, f32[80,256]{1,0:T(8,128)S(1)}, u32[]{:S(2)}, u32[]{:S(2)}) collective-permute-start(f32[80,256]{1,0:T(8,128)S(1)} %broadcast_multiply_fusion), channel_id=1, source_target_pairs={{0,16},{1,17},{2,18},{3,19},{4,20},{5,21},{6,22},{7,23},{8,24},{9,... | collective-permute-start | bytes 245768 | tf_op jit(solution)/shard_map/ppermute | solution.py:567
  88.9 6.7 %collective-permute-start.27 = (f32[80,256]{1,0:T(8,128)S(1)}, f32[80,256]{1,0:T(8,128)S(1)}, u32[]{:S(2)}, u32[]{:S(2)}) collective-permute-start(f32[80,256]{1,0:T(8,128)S(1)} %broadcast_multiply_fusion), channel_id=1, source_target_pairs={{0,8},{1,9},{2,10},{3,11},{4,12},{5,13},{6,14},{7,15},{8,0},{9,1},... | collective-permute-start | bytes 245768 | tf_op jit(solution)/shard_map/ppermute | solution.py:567
  91.2 6.2 %collective-permute-start.29 = (f32[80,256]{1,0:T(8,128)S(1)}, f32[80,256]{1,0:T(8,128)S(1)}, u32[]{:S(2)}, u32[]{:S(2)}) collective-permute-start(f32[80,256]{1,0:T(8,128)S(1)} %broadcast_multiply_fusion), channel_id=1, source_target_pairs={{0,24},{1,25},{2,26},{3,27},{4,28},{5,29},{6,30},{7,31},{8,16},{9,... | collective-permute-start | bytes 245768 | tf_op jit(solution)/shard_map/ppermute | solution.py:567
  92.6 14.4 %copy-start.16 = (f32[2,128,256]{2,1,0:T(8,128)S(1)}, f32[2,128,256]{2,1,0:T(8,128)}, u32[]{:S(2)}) copy-start(f32[2,128,256]{2,1,0:T(8,128)} %copy-done.15) | copy-start | bytes 786436
  92.6 14.4 %copy-start.18 = (f32[2,128,256]{2,1,0:T(8,128)S(1)}, f32[2,128,256]{2,1,0:T(8,128)}, u32[]{:S(2)}) copy-start(f32[2,128,256]{2,1,0:T(8,128)} %copy-done.17) | copy-start | bytes 786436
  92.6 14.4 %copy-start.20 = (f32[2,128,256]{2,1,0:T(8,128)S(1)}, f32[2,128,256]{2,1,0:T(8,128)}, u32[]{:S(2)}) copy-start(f32[2,128,256]{2,1,0:T(8,128)} %copy-done.19) | copy-start | bytes 786436
  92.7 14.4 %copy-start.22 = (f32[24,512]{1,0:T(8,128)S(1)}, f32[24,512]{1,0:T(8,128)}, u32[]{:S(2)}) copy-start(f32[24,512]{1,0:T(8,128)} %get-tuple-element.120.glog) | copy-start | bytes 147460
  92.7 14.3 %copy-start.12 = (f32[2,128,256]{2,1,0:T(8,128)S(1)}, f32[2,128,256]{2,1,0:T(8,128)}, u32[]{:S(2)}) copy-start(f32[2,128,256]{2,1,0:T(8,128)} %copy-done.11) | copy-start | bytes 786436
  92.8 14.3 %copy-start.14 = (f32[2,128,256]{2,1,0:T(8,128)S(1)}, f32[2,128,256]{2,1,0:T(8,128)}, u32[]{:S(2)}) copy-start(f32[2,128,256]{2,1,0:T(8,128)} %copy-done.13) | copy-start | bytes 786436
  92.8 6.9 %collective-permute-start.21 = (f32[4,64,256]{2,1,0:T(8,128)S(1)}, f32[4,64,256]{2,1,0:T(8,128)S(1)}, u32[]{:S(2)}, u32[]{:S(2)}) collective-permute-start(f32[4,64,256]{2,1,0:T(8,128)S(1)} %slice_bitcast_fusion.6), channel_id=1, source_target_pairs={{0,4},{1,5},{2,6},{3,7},{4,0},{5,1},{6,2},{7,3},{8,12},{9,13},{10,... | collective-permute-start | bytes 786440 | tf_op jit(solution)/shard_map/ppermute | solution.py:567
  93.5 13.6 %copy-start.4 = (f32[8,128,256]{2,1,0:T(8,128)S(1)}, f32[8,128,256]{2,1,0:T(8,128)}, u32[]{:S(2)}) copy-start(f32[8,128,256]{2,1,0:T(8,128)} %copy-done.3) | copy-start | bytes 3145732
  93.5 13.6 %copy-start.8 = (f32[2,128,256]{2,1,0:T(8,128)S(1)}, f32[2,128,256]{2,1,0:T(8,128)}, u32[]{:S(2)}) copy-start(f32[2,128,256]{2,1,0:T(8,128)} %copy-done.7) | copy-start | bytes 786436
  93.5 13.6 %copy-start.10 = (f32[2,128,256]{2,1,0:T(8,128)S(1)}, f32[2,128,256]{2,1,0:T(8,128)}, u32[]{:S(2)}) copy-start(f32[2,128,256]{2,1,0:T(8,128)} %copy-done.9) | copy-start | bytes 786436
  93.5 13.5 %copy-start.2 = (f32[8,128,256]{2,1,0:T(8,128)S(1)}, f32[8,128,256]{2,1,0:T(8,128)}, u32[]{:S(2)}) copy-start(f32[8,128,256]{2,1,0:T(8,128)} %near0.3) | copy-start | bytes 3145732
  93.6 6.6 %collective-permute-start.23 = (f32[4,64,256]{2,1,0:T(8,128)S(1)}, f32[4,64,256]{2,1,0:T(8,128)S(1)}, u32[]{:S(2)}, u32[]{:S(2)}) collective-permute-start(f32[4,64,256]{2,1,0:T(8,128)S(1)} %slice_bitcast_fusion.4), channel_id=1, source_target_pairs={{0,2},{1,3},{2,0},{3,1},{4,6},{5,7},{6,4},{7,5},{8,10},{9,11},{10,... | collective-permute-start | bytes 786440 | tf_op jit(solution)/shard_map/ppermute | solution.py:567
  97.4 9.7 %copy-start.6 = (f32[2,128,256]{2,1,0:T(8,128)S(1)}, f32[2,128,256]{2,1,0:T(8,128)}, u32[]{:S(2)}) copy-start(f32[2,128,256]{2,1,0:T(8,128)} %copy-done.5) | copy-start | bytes 786436
  97.5 9.6 %copy-start = (bf16[8,256,512]{2,1,0:T(8,128)(2,1)S(1)}, bf16[8,256,512]{2,1,0:T(8,128)(2,1)}, u32[]{:S(2)}) copy-start(bf16[8,256,512]{2,1,0:T(8,128)(2,1)} %get-tuple-element.101.gf_high_in) | copy-start | bytes 6291460
  97.5 9.6 %copy-start.1 = (bf16[8,256,512]{2,1,0:T(8,128)(2,1)S(1)}, bf16[8,256,512]{2,1,0:T(8,128)(2,1)}, u32[]{:S(2)}) copy-start(bf16[8,256,512]{2,1,0:T(8,128)(2,1)} %get-tuple-element.121.gf_low_in) | copy-start | bytes 6291460
  97.5 9.6 %copy-start.21 = (f32[24,512]{1,0:T(8,128)S(1)}, f32[24,512]{1,0:T(8,128)}, u32[]{:S(2)}) copy-start(f32[24,512]{1,0:T(8,128)} %get-tuple-element.119.gate_all) | copy-start | bytes 147460
  100.3 12.4 %collective-permute-start.30 = (f32[128,256]{1,0:T(8,128)S(1)}, f32[128,256]{1,0:T(8,128)S(1)}, u32[]{:S(2)}, u32[]{:S(2)}) collective-permute-start(f32[128,256]{1,0:T(8,128)S(1)} %get-tuple-element.162), channel_id=1, source_target_pairs={{0,8},{1,9},{2,10},{3,11},{4,12},{5,13},{6,14},{7,15},{8,0},{9,1},... | collective-permute-start | bytes 393224 | tf_op jit(solution)/shard_map/ppermute | solution.py:567
  101.5 11.2 %collective-permute-start.32 = (f32[128,256]{1,0:T(8,128)S(1)}, f32[128,256]{1,0:T(8,128)S(1)}, u32[]{:S(2)}, u32[]{:S(2)}) collective-permute-start(f32[128,256]{1,0:T(8,128)S(1)} %get-tuple-element.163), channel_id=1, source_target_pairs={{0,24},{1,25},{2,26},{3,27},{4,28},{5,29},{6,30},{7,31},{8,16},{9,... | collective-permute-start | bytes 393224 | tf_op jit(solution)/shard_map/ppermute | solution.py:567
  104.0 8.8 %collective-permute-start.31 = (f32[128,256]{1,0:T(8,128)S(1)}, f32[128,256]{1,0:T(8,128)S(1)}, u32[]{:S(2)}, u32[]{:S(2)}) collective-permute-start(f32[128,256]{1,0:T(8,128)S(1)} %get-tuple-element.164), channel_id=1, source_target_pairs={{0,16},{1,17},{2,18},{3,19},{4,20},{5,21},{6,22},{7,23},{8,24},{9,... | collective-permute-start | bytes 393224 | tf_op jit(solution)/shard_map/ppermute | solution.py:567
  104.0 8.7 %collective-permute-start.34 = (f32[4,40,256]{2,1,0:T(8,128)S(1)}, f32[4,40,256]{2,1,0:T(8,128)S(1)}, u32[]{:S(2)}, u32[]{:S(2)}) collective-permute-start(f32[4,40,256]{2,1,0:T(8,128)S(1)} %get-tuple-element.167), channel_id=1, source_target_pairs={{0,4},{1,5},{2,6},{3,7},{4,0},{5,1},{6,2},{7,3},{8,12},{9,13},{10,... | collective-permute-start | bytes 491528 | tf_op jit(solution)/shard_map/ppermute | solution.py:567
  105.4 7.4 %collective-permute-start.33 = (f32[4,40,256]{2,1,0:T(8,128)S(1)}, f32[4,40,256]{2,1,0:T(8,128)S(1)}, u32[]{:S(2)}, u32[]{:S(2)}) collective-permute-start(f32[4,40,256]{2,1,0:T(8,128)S(1)} %get-tuple-element.168), channel_id=1, source_target_pairs={{0,2},{1,3},{2,0},{3,1},{4,6},{5,7},{6,4},{7,5},{8,10},{9,11},{10,... | collective-permute-start | bytes 491528 | tf_op jit(solution)/shard_map/ppermute | solution.py:567
  112.9 8.7 %collective-permute-start.35 = (f32[2,4,40,256]{3,2,1,0:T(8,128)S(1)}, f32[2,4,40,256]{3,2,1,0:T(8,128)S(1)}, u32[]{:S(2)}, u32[]{:S(2)}) collective-permute-start(f32[2,4,40,256]{3,2,1,0:T(8,128)S(1)} %pad_maximum_fusion.5.a0), channel_id=1, source_target_pairs={{0,4},{1,5},{2,6},{3,7},{4,0},{5,1},{6,2},{7,3},{8,12},{9,13},{10,... | collective-permute-start | bytes 983048 | tf_op jit(solution)/shard_map/ppermute | solution.py:567
  114.4 8.3 %collective-permute-start.36 = (f32[2,4,40,256]{3,2,1,0:T(8,128)S(1)}, f32[2,4,40,256]{3,2,1,0:T(8,128)S(1)}, u32[]{:S(2)}, u32[]{:S(2)}) collective-permute-start(f32[2,4,40,256]{3,2,1,0:T(8,128)S(1)} %pad_maximum_fusion.6.a1), channel_id=1, source_target_pairs={{0,2},{1,3},{2,0},{3,1},{4,6},{5,7},{6,4},{7,5},{8,10},{9,11},{10,... | collective-permute-start | bytes 983048 | tf_op jit(solution)/shard_map/ppermute | solution.py:567
  114.9 8.2 %collective-permute-start.46 = (f32[128,256]{1,0:T(8,128)S(1)}, f32[128,256]{1,0:T(8,128)S(1)}, u32[]{:S(2)}, u32[]{:S(2)}) collective-permute-start(f32[128,256]{1,0:T(8,128)S(1)} %fusion.6.a0), channel_id=1, source_target_pairs={{0,24},{1,25},{2,26},{3,27},{4,28},{5,29},{6,30},{7,31},{8,16},{9,... | collective-permute-start | bytes 393224 | tf_op jit(solution)/shard_map/ppermute | solution.py:567
  116.7 9.8 %collective-permute-start.45 = (f32[128,256]{1,0:T(8,128)S(1)}, f32[128,256]{1,0:T(8,128)S(1)}, u32[]{:S(2)}, u32[]{:S(2)}) collective-permute-start(f32[128,256]{1,0:T(8,128)S(1)} %fusion.6.a0), channel_id=1, source_target_pairs={{0,16},{1,17},{2,18},{3,19},{4,20},{5,21},{6,22},{7,23},{8,24},{9,... | collective-permute-start | bytes 393224 | tf_op jit(solution)/shard_map/ppermute | solution.py:567
  117.5 9.0 %collective-permute-start.44 = (f32[128,256]{1,0:T(8,128)S(1)}, f32[128,256]{1,0:T(8,128)S(1)}, u32[]{:S(2)}, u32[]{:S(2)}) collective-permute-start(f32[128,256]{1,0:T(8,128)S(1)} %fusion.6.a0), channel_id=1, source_target_pairs={{0,8},{1,9},{2,10},{3,11},{4,12},{5,13},{6,14},{7,15},{8,0},{9,1},... | collective-permute-start | bytes 393224 | tf_op jit(solution)/shard_map/ppermute | solution.py:567
  121.5 5.6 %collective-permute-start.41 = (f32[512,128]{1,0:T(8,128)S(1)}, f32[512,128]{1,0:T(8,128)S(1)}, u32[]{:S(2)}, u32[]{:S(2)}) collective-permute-start(f32[512,128]{1,0:T(8,128)S(1)} %get-tuple-element.136), channel_id=1, source_target_pairs={{0,1},{1,0},{2,3},{3,2},{4,5},{5,4},{6,7},{7,6},{8,9},{9,8},{10,11... | collective-permute-start | bytes 786440 | tf_op jit(solution)/shard_map/ppermute | solution.py:567
  122.7 9.2 %collective-permute-start.42 = (f32[512,128]{1,0:T(8,128)S(1)}, f32[512,128]{1,0:T(8,128)S(1)}, u32[]{:S(2)}, u32[]{:S(2)}) collective-permute-start(f32[512,128]{1,0:T(8,128)S(1)} %get-tuple-element.137), channel_id=1, source_target_pairs={{0,2},{1,3},{2,0},{3,1},{4,6},{5,7},{6,4},{7,5},{8,10},{9,11},{10,... | collective-permute-start | bytes 786440 | tf_op jit(solution)/shard_map/ppermute | solution.py:567
  123.1 11.0 %collective-permute-start.43 = (f32[512,128]{1,0:T(8,128)S(1)}, f32[512,128]{1,0:T(8,128)S(1)}, u32[]{:S(2)}, u32[]{:S(2)}) collective-permute-start(f32[512,128]{1,0:T(8,128)S(1)} %get-tuple-element.138), channel_id=1, source_target_pairs={{0,3},{1,2},{2,1},{3,0},{4,7},{5,6},{6,5},{7,4},{8,11},{9,10},{10,... | collective-permute-start | bytes 786440 | tf_op jit(solution)/shard_map/ppermute | solution.py:567
  126.5 13.9 %collective-permute-start.47 = (f32[4,128,256]{2,1,0:T(8,128)S(1)}, f32[4,128,256]{2,1,0:T(8,128)S(1)}, u32[]{:S(2)}, u32[]{:S(2)}) collective-permute-start(f32[4,128,256]{2,1,0:T(8,128)S(1)} %pad_maximum_fusion.2), channel_id=1, source_target_pairs={{0,4},{1,5},{2,6},{3,7},{4,0},{5,1},{6,2},{7,3},{8,12},{9,13},{10,... | collective-permute-start | bytes 1572872 | tf_op jit(solution)/shard_map/ppermute | solution.py:567
  127.1 10.9 %collective-permute-start.37 = (f32[2,4,40,256]{3,2,1,0:T(8,128)S(1)}, f32[2,4,40,256]{3,2,1,0:T(8,128)S(1)}, u32[]{:S(2)}, u32[]{:S(2)}) collective-permute-start(f32[2,4,40,256]{3,2,1,0:T(8,128)S(1)} %pad_maximum_fusion.5.a0), channel_id=1, source_target_pairs={{0,1},{1,0},{2,3},{3,2},{4,5},{5,4},{6,7},{7,6},{8,9},{9,8},{10,11... | collective-permute-start | bytes 983048 | tf_op jit(solution)/shard_map/ppermute | solution.py:567
  127.1 10.9 %collective-permute-start.38 = (f32[2,4,40,256]{3,2,1,0:T(8,128)S(1)}, f32[2,4,40,256]{3,2,1,0:T(8,128)S(1)}, u32[]{:S(2)}, u32[]{:S(2)}) collective-permute-start(f32[2,4,40,256]{3,2,1,0:T(8,128)S(1)} %pad_maximum_fusion.6.a1), channel_id=1, source_target_pairs={{0,1},{1,0},{2,3},{3,2},{4,5},{5,4},{6,7},{7,6},{8,9},{9,8},{10,11... | collective-permute-start | bytes 983048 | tf_op jit(solution)/shard_map/ppermute | solution.py:567
  132.0 6.0 %collective-permute-start.39 = (f32[2,4,40,256]{3,2,1,0:T(8,128)S(1)}, f32[2,4,40,256]{3,2,1,0:T(8,128)S(1)}, u32[]{:S(2)}, u32[]{:S(2)}) collective-permute-start(f32[2,4,40,256]{3,2,1,0:T(8,128)S(1)} %collective-permute-done.35.a2), channel_id=1, source_target_pairs={{0,1},{1,0},{2,3},{3,2},{4,5},{5,4},{6,7},{7,6},{8,9},{9,8},{10,11... | collective-permute-start | bytes 983048 | tf_op jit(solution)/shard_map/ppermute | solution.py:567
  134.2 3.9 %collective-permute-start.40 = (f32[2,4,40,256]{3,2,1,0:T(8,128)S(1)}, f32[2,4,40,256]{3,2,1,0:T(8,128)S(1)}, u32[]{:S(2)}, u32[]{:S(2)}) collective-permute-start(f32[2,4,40,256]{3,2,1,0:T(8,128)S(1)} %collective-permute-done.36.a3), channel_id=1, source_target_pairs={{0,1},{1,0},{2,3},{3,2},{4,5},{5,4},{6,7},{7,6},{8,9},{9,8},{10,11... | collective-permute-start | bytes 983048 | tf_op jit(solution)/shard_map/ppermute | solution.py:567
  (16 other events, 63.1 us)

commit v6 on v5

--- a/solution.py
+++ b/solution.py
@@ -14,7 +14,7 @@
 VMEM = pltpu.VMEM
 PARAMS = pltpu.CompilerParams(vmem_limit_bytes=58 * 1024 * 1024)
 MEDIUM = pltpu.CompilerParams(vmem_limit_bytes=24 * 1024 * 1024)
-SMALL = pltpu.CompilerParams(vmem_limit_bytes=12 * 1024 * 1024)
+SMALL = pltpu.CompilerParams(vmem_limit_bytes=14 * 1024 * 1024)
 NN, TN, NT = (1, 0), (0, 0), (1, 1)
 
 
@@ -440,7 +440,7 @@
 
 
 def finish_second_kernel(
-    place, a0, a1, a2, a3, b0, b1, b2, b3, gw2, gtf, ggw, ggb, gb1, gb2, gtb, gto, gtob, loss, parts, rest
+    place, factor, a0, a1, a2, a3, b0, b1, b2, b3, g0, g1, g2, g3, gw2, gtf, ggw, ggb, gb1, gb2, gtb, gto, gtob, loss, out, parts, rest
 ):
     me, field = place[0], place[1]
     hidden = gw2.shape[1]
@@ -484,6 +484,9 @@
         gto[k : k + 1] = rest[misc + at // 2 : misc + at // 2 + 1, (at % 2) * tower : (at % 2 + 1) * tower]
     gtob[...] = rest[misc + tasks : misc + tasks + 1, 0:tasks]
     loss[...] = rest[misc + tasks : misc + tasks + 1, tasks : tasks + 1]
+    rows = g0.shape[0]
+    for k, ref in enumerate((g0, g1, g2, g3)):
+        out[pl.ds(pl.multiple_of((field ^ k) * rows, 8), rows), :] = ref[...] * factor[...]
 
 
 def place_near_kernel(place, a0, a1, a2, a3, out, sems):
@@ -502,13 +505,6 @@
         copy.start()
     for copy in copies:
         copy.wait()
-
-
-def finish_inputs_kernel(place, factor, g0, g1, g2, g3, out):
-    field = place[0]
-    rows = g0.shape[0]
-    for k, ref in enumerate((g0, g1, g2, g3)):
-        out[pl.ds(pl.multiple_of((field ^ k) * rows, 8), rows), :] = ref[...] * factor[...]
 
 
 def whole():
@@ -782,23 +778,15 @@
             like((tasks, tower)),
             like((1, tasks)),
             like((1, 1)),
+            like((all_rows, cols)),
         ),
-        in_specs=[scalars()] + [whole()] * 8,
-        out_specs=[whole()] * 10,
+        in_specs=[scalars()] + [whole()] * 13,
+        out_specs=[whole()] * 11,
         scratch_shapes=[VMEM((32, 16, width), F32), VMEM((480, width), F32)],
         compiler_params=SMALL,
-    )(jnp.stack([me5, field]), *s_near, *s_far)
+    )(jnp.stack([me5, field]), factor, *s_near, *s_far, g0, g1, g2, g3)
     grad_w_second, grad_tower_first, grad_gate_weight, grad_gate_bias = seconds[:4]
-    grad_b_first, grad_b_second, grad_tower_bias, grad_tower_out, grad_out_bias, loss = seconds[4:]
-
-    grad_examples = pl.pallas_call(
-        finish_inputs_kernel,
-        name="finish_inputs",
-        out_shape=like((all_rows, cols)),
-        in_specs=[scalars()] + [whole()] * 5,
-        out_specs=whole(),
-        compiler_params=SMALL,
-    )(field.reshape(1), factor, g0, g1, g2, g3)
+    grad_b_first, grad_b_second, grad_tower_bias, grad_tower_out, grad_out_bias, loss, grad_examples = seconds[4:]
 
     begun = pl.pallas_call(
         place_near_kernel,

time: 142 us -> 141 us (level)
  transfers between devices with their start and end apart: 48 -> 48, of which waited for: 23 -> 24; matrix products, arithmetic and copies ran while one was open for 5% -> 5% of each run, Pallas kernels for 12% -> 11%
where the time goes in v6:
time: 141 us
  waiting for transfers between devices  49 us (35%)
  starting transfers between devices  43 us (30%)
  Pallas kernels  36.9 us (26%)
  local copies, waits for them, and re-layouts  6.95 us (5%)
  between operations  2.9 us (2%)
  other arithmetic  2.27 us (2%)
    ppermute x48, waiting for transfers between devices, move(): return lax.ppermute(value, ('dp', 'field'), pairs)  49 us
    ppermute x48, starting transfers between devices, move(): return lax.ppermute(value, ('dp', 'field'), pairs)  43 us
    pallas_call x1, Pallas kernels, per_device(): pl.pallas_call(middle_kernel, name='middle', out_shape=(like((4 * cols, r...  19.9 us
    pallas_call x1, Pallas kernels, per_device(): pl.pallas_call(first_kernel, name='first', out_shape=tuple((like((2, 8, c...  7.02 us
    pallas_call x1, Pallas kernels, per_device(): pl.pallas_call(inputs_kernel, name='inputs', out_shape=tuple((like((rows,...  5.56 us
  transfers between devices with their start and end apart: 48, of which 24 were waited for; matrix products, arithmetic and copies ran while one was open for 5% of the time, Pallas kernels for 11%

profile of v6, /device:TPU:0, one launch (start us, length us, event | category | flops | bytes accessed | tf_op | source)
XLA Modules:
  0.0 141.0 jit_solution(2685151130078497910)
XLA Ops:
  0.7 0.5 collective-permute-start.1
  1.2 1.0 constant_dynamic-slice_fusion.4
  2.2 2.6 %collective-permute-start = (f32[2,128,256]{2,1,0:T(8,128)S(1)}, f32[2,128,256]{2,1,0:T(8,128)S(1)}, u32[]{:S(2)}, u32[]{:S(2)}) collective-permute-start(f32[2,128,256]{2,1,0:T(8,128)S(1)} %constant_dynamic-slice_fusion.4), channel_id=1, source_target_pairs={{0,2},{1,3},{2,0},{3,1},{4,6},{5,7},{6,4},{7,5},{8,10},{9,11},{10,... | collective-permute-start | bytes 786440 | tf_op jit(solution)/shard_map/ppermute | solution.py:563
  4.8 2.0 %constant_dynamic-slice_fusion = (f32[512,128]{1,0:T(8,128)}, f32[512,128]{1,0:T(8,128)S(1)}, f32[512,128]{1,0:T(8,128)S(1)}, f32[512,128]{1,0:T(8,128)S(1)}) fusion(f32[2048,128]{1,0:T(8,128)} %param.14, s32[]{:T(128)S(6)} %select_n.19, s32[]{:T(128)S(6)} %select_n.17, s32[]{:T(128)S(6)} %select_n.16, s32[]{:T(128)S(6)} %select_n.18), kind=kLoop, calls=%fused_computation.38 | loop fusion | bytes 2097168 | tf_op jit(solution)/shard_map/dynamic_slice | solution.py:584
  7.4 0.6 reshape.55.domain
  8.0 0.6 stack.73.place
  8.7 3.1 %collective-permute-done.fa0 = f32[2,128,256]{2,1,0:T(8,128)S(1)} collective-permute-done((f32[2,128,256]{2,1,0:T(8,128)S(1)}, f32[2,128,256]{2,1,0:T(8,128)S(1)}, u32[]{:S(2)}, u32[]{:S(2)}) %collective-permute-start) | collective-permute-done | bytes 262176 | tf_op jit(solution)/shard_map/ppermute | solution.py:563
  11.7 1.8 %collective-permute-start.3 = (f32[1048,128]{1,0:T(8,128)S(1)}, f32[1048,128]{1,0:T(8,128)S(1)}, u32[]{:S(2)}, u32[]{:S(2)}) collective-permute-start(f32[1048,128]{1,0:T(8,128)S(1)} %pad_maximum_fusion), channel_id=1, source_target_pairs={{0,2},{1,3},{2,0},{3,1},{4,6},{5,7},{6,4},{7,5},{8,10},{9,11},{10,... | collective-permute-start | bytes 1609736 | tf_op jit(solution)/shard_map/ppermute | solution.py:563
  13.5 2.5 %collective-permute-start.6 = (f32[2,128,256]{2,1,0:T(8,128)S(1)}, f32[2,128,256]{2,1,0:T(8,128)S(1)}, u32[]{:S(2)}, u32[]{:S(2)}) collective-permute-start(f32[2,128,256]{2,1,0:T(8,128)S(1)} %collective-permute-done.fa0), channel_id=1, source_target_pairs={{0,12},{1,13},{2,14},{3,15},{4,8},{5,9},{6,10},{7,11},{8,4},{9,5},... | collective-permute-start | bytes 786440 | tf_op jit(solution)/shard_map/ppermute | solution.py:563
  16.0 0.4 collective-permute-start.5
  16.5 0.5 collective-permute-start.4
  17.0 6.6 %collective-permute-done.6.fa3 = f32[2,128,256]{2,1,0:T(8,128)S(1)} collective-permute-done((f32[2,128,256]{2,1,0:T(8,128)S(1)}, f32[2,128,256]{2,1,0:T(8,128)S(1)}, u32[]{:S(2)}, u32[]{:S(2)}) %collective-permute-start.6) | collective-permute-done | bytes 262176 | tf_op jit(solution)/shard_map/ppermute | solution.py:563
  23.6 5.3 %collective-permute-done.5.fa2 = f32[2,128,256]{2,1,0:T(8,128)S(1)} collective-permute-done((f32[2,128,256]{2,1,0:T(8,128)S(1)}, f32[2,128,256]{2,1,0:T(8,128)S(1)}, u32[]{:S(2)}, u32[]{:S(2)}) %collective-permute-start.5) | collective-permute-done | bytes 262176 | tf_op jit(solution)/shard_map/ppermute | solution.py:563
  29.0 0.5 collective-permute-start.8
  30.0 1.2 collective-permute-done.8.fb0
  33.3 19.9 %middle.1 = (bf16[512,512]{1,0:T(8,128)(2,1)}, bf16[512,512]{1,0:T(8,128)(2,1)}, bf16[8,256,512]{2,1,0:T(8,128)(2,1)}, bf16[8,256,512]{2,1,0:T(8,128)(2,1)}, f32...) custom-call(s32[5]{0:T(128)} %stack.73.place, ...), custom_call_target="tpu_custom_call" | custom-call | tf_op jit(solution)/shard_map/middle/pallas_call | solution.py:604
  53.8 1.8 %collective-permute-done.12 = f32[16,40,256]{2,1,0:T(8,128)S(1)} collective-permute-done((f32[16,40,256]{2,1,0:T(8,128)}, f32[16,40,256]{2,1,0:T(8,128)S(1)}, u32[]{:S(2)}, u32[]{:S(2)}) %collective-permute-start.12) | collective-permute-done | bytes 655392 | tf_op jit(solution)/shard_map/ppermute | solution.py:563
  55.6 1.2 add.98
  57.0 1.5 %collective-permute-start.16 = (f32[2,4,40,256]{3,2,1,0:T(8,128)S(1)}, f32[2,4,40,256]{3,2,1,0:T(8,128)S(1)}, u32[]{:S(2)}, u32[]{:S(2)}) collective-permute-start(f32[2,4,40,256]{3,2,1,0:T(8,128)S(1)} %bitcast.109), channel_id=1, source_target_pairs={{0,4},{1,5},{2,6},{3,7},{4,0},{5,1},{6,2},{7,3},{8,12},{9,13},{10,... | collective-permute-start | bytes 983048 | tf_op jit(solution)/shard_map/ppermute | solution.py:563
  58.5 0.5 collective-permute-start.18
  59.0 7.0 %first.1 = (f32[2,8,64,256]{3,2,1,0:T(8,128)}, f32[2,8,64,256]{3,2,1,0:T(8,128)}, f32[2,8,64,256]{3,2,1,0:T(8,128)}, f32[2,8,64,256]{3,2,1,0:T(8,128)}) custom-call(s32[1]{0:T(128)} %bitcast.2.place, bf16[512,512]{1,0:T(8,128)(2,1)} %get-tuple-element.95.xt_high_in, bf16[512,512]{1,0:T(8,128)(2,1)} %get-tuple-element.96.xt_low_in, ...), custom_call_target="tpu_custom_call" | custom-call | bytes 1048576 | tf_op jit(solution)/shard_map/first/pallas_call | solution.py:692
  66.1 0.5 collective-permute-start.15
  66.9 1.3 collective-permute-start.17
  68.3 0.7 collective-permute-start.19
  69.0 3.9 %collective-permute-done.17 = f32[4,40,256]{2,1,0:T(8,128)S(1)} collective-permute-done((f32[4,40,256]{2,1,0:T(8,128)S(1)}, f32[4,40,256]{2,1,0:T(8,128)S(1)}, u32[]{:S(2)}, u32[]{:S(2)}) %collective-permute-start.17) | collective-permute-done | bytes 163872 | tf_op jit(solution)/shard_map/ppermute | solution.py:563
  72.9 1.3 collective-permute-done.19
  74.6 1.0 copy-done.24
  75.9 1.6 %collective-permute-start.20 = (f32[80,256]{1,0:T(8,128)S(1)}, f32[80,256]{1,0:T(8,128)S(1)}, u32[]{:S(2)}, u32[]{:S(2)}) collective-permute-start(f32[80,256]{1,0:T(8,128)S(1)} %get-tuple-element.171), channel_id=1, source_target_pairs={{0,8},{1,9},{2,10},{3,11},{4,12},{5,13},{6,14},{7,15},{8,0},{9,1},... | collective-permute-start | bytes 245768 | tf_op jit(solution)/shard_map/ppermute | solution.py:563
  77.5 2.5 %collective-permute-start.22 = (f32[80,256]{1,0:T(8,128)S(1)}, f32[80,256]{1,0:T(8,128)S(1)}, u32[]{:S(2)}, u32[]{:S(2)}) collective-permute-start(f32[80,256]{1,0:T(8,128)S(1)} %get-tuple-element.172), channel_id=1, source_target_pairs={{0,24},{1,25},{2,26},{3,27},{4,28},{5,29},{6,30},{7,31},{8,16},{9,... | collective-permute-start | bytes 245768 | tf_op jit(solution)/shard_map/ppermute | solution.py:563
  80.1 0.5 collective-permute-start.23
  80.6 1.0 collective-permute-start.25
  81.7 2.5 %collective-permute-done.22 = f32[80,256]{1,0:T(8,128)S(1)} collective-permute-done((f32[80,256]{1,0:T(8,128)S(1)}, f32[80,256]{1,0:T(8,128)S(1)}, u32[]{:S(2)}, u32[]{:S(2)}) %collective-permute-start.22) | collective-permute-done | bytes 81952 | tf_op jit(solution)/shard_map/ppermute | solution.py:563
  84.2 2.7 %collective-permute-done.21 = f32[80,256]{1,0:T(8,128)S(1)} collective-permute-done((f32[80,256]{1,0:T(8,128)S(1)}, f32[80,256]{1,0:T(8,128)S(1)}, u32[]{:S(2)}, u32[]{:S(2)}) %collective-permute-start.21) | collective-permute-done | bytes 81952 | tf_op jit(solution)/shard_map/ppermute | solution.py:563
  86.9 0.5 slice.124
  88.2 0.7 collective-permute-start.28
  88.9 2.3 %collective-permute-start.27 = (f32[80,256]{1,0:T(8,128)S(1)}, f32[80,256]{1,0:T(8,128)S(1)}, u32[]{:S(2)}, u32[]{:S(2)}) collective-permute-start(f32[80,256]{1,0:T(8,128)S(1)} %broadcast_multiply_fusion), channel_id=1, source_target_pairs={{0,8},{1,9},{2,10},{3,11},{4,12},{5,13},{6,14},{7,15},{8,0},{9,1},... | collective-permute-start | bytes 245768 | tf_op jit(solution)/shard_map/ppermute | solution.py:563
  91.2 1.4 %collective-permute-start.29 = (f32[80,256]{1,0:T(8,128)S(1)}, f32[80,256]{1,0:T(8,128)S(1)}, u32[]{:S(2)}, u32[]{:S(2)}) collective-permute-start(f32[80,256]{1,0:T(8,128)S(1)} %broadcast_multiply_fusion), channel_id=1, source_target_pairs={{0,24},{1,25},{2,26},{3,27},{4,28},{5,29},{6,30},{7,31},{8,16},{9,... | collective-permute-start | bytes 245768 | tf_op jit(solution)/shard_map/ppermute | solution.py:563
  92.8 0.7 collective-permute-start.24
  93.6 0.8 collective-permute-start.26
  94.3 1.2 collective-permute-done.28
  95.5 1.9 %collective-permute-done.29 = f32[80,256]{1,0:T(8,128)S(1)} collective-permute-done((f32[80,256]{1,0:T(8,128)S(1)}, f32[80,256]{1,0:T(8,128)S(1)}, u32[]{:S(2)}, u32[]{:S(2)}) %collective-permute-start.29) | collective-permute-done | bytes 81952 | tf_op jit(solution)/shard_map/ppermute | solution.py:563
  97.5 2.2 %collective-permute-done.24 = f32[4,64,256]{2,1,0:T(8,128)S(1)} collective-permute-done((f32[4,64,256]{2,1,0:T(8,128)S(1)}, f32[4,64,256]{2,1,0:T(8,128)S(1)}, u32[]{:S(2)}, u32[]{:S(2)}) %collective-permute-start.24) | collective-permute-done | bytes 262176 | tf_op jit(solution)/shard_map/ppermute | solution.py:563
  99.7 0.5 collective-permute-done.26
  100.3 1.2 collective-permute-start.30
  101.5 2.5 %collective-permute-start.32 = (f32[128,256]{1,0:T(8,128)S(1)}, f32[128,256]{1,0:T(8,128)S(1)}, u32[]{:S(2)}, u32[]{:S(2)}) collective-permute-start(f32[128,256]{1,0:T(8,128)S(1)} %get-tuple-element.165), channel_id=1, source_target_pairs={{0,24},{1,25},{2,26},{3,27},{4,28},{5,29},{6,30},{7,31},{8,16},{9,... | collective-permute-start | bytes 393224 | tf_op jit(solution)/shard_map/ppermute | solution.py:563
  104.0 1.4 collective-permute-start.34
  105.4 1.6 %collective-permute-start.33 = (f32[4,40,256]{2,1,0:T(8,128)S(1)}, f32[4,40,256]{2,1,0:T(8,128)S(1)}, u32[]{:S(2)}, u32[]{:S(2)}) collective-permute-start(f32[4,40,256]{2,1,0:T(8,128)S(1)} %get-tuple-element.170), channel_id=1, source_target_pairs={{0,2},{1,3},{2,0},{3,1},{4,6},{5,7},{6,4},{7,5},{8,10},{9,11},{10,... | collective-permute-start | bytes 491528 | tf_op jit(solution)/shard_map/ppermute | solution.py:563
  107.1 5.6 %inputs.1 = (f32[512,128]{1,0:T(8,128)S(1)}, f32[512,128]{1,0:T(8,128)S(1)}, f32[512,128]{1,0:T(8,128)S(1)}, f32[512,128]{1,0:T(8,128)S(1)}) custom-call(s32[5]{0:T(128)S(1)} %copy-done.23, f32[24,512]{1,0:T(8,128)S(1)} %copy-done.21, f32[24,512]{1,0:T(8,128)S(1)} %copy-done.22, bf16[8,256,512]{2,1,0:T(8,128)(2,1)S(1)} %copy-done, ...), custom_call_target="tpu_custom_call" | custom-call | bytes 1048576 | tf_op jit(solution)/shard_map/inputs/pallas_call | solution.py:733
  112.9 1.6 %collective-permute-start.35 = (f32[2,4,40,256]{3,2,1,0:T(8,128)S(1)}, f32[2,4,40,256]{3,2,1,0:T(8,128)S(1)}, u32[]{:S(2)}, u32[]{:S(2)}) collective-permute-start(f32[2,4,40,256]{3,2,1,0:T(8,128)S(1)} %pad_maximum_fusion.5.a0), channel_id=1, source_target_pairs={{0,4},{1,5},{2,6},{3,7},{4,0},{5,1},{6,2},{7,3},{8,12},{9,13},{10,... | collective-permute-start | bytes 983048 | tf_op jit(solution)/shard_map/ppermute | solution.py:563
  114.4 0.5 collective-permute-start.36
  114.9 1.8 %collective-permute-start.46 = (f32[128,256]{1,0:T(8,128)S(1)}, f32[128,256]{1,0:T(8,128)S(1)}, u32[]{:S(2)}, u32[]{:S(2)}) collective-permute-start(f32[128,256]{1,0:T(8,128)S(1)} %fusion.6.a0), channel_id=1, source_target_pairs={{0,24},{1,25},{2,26},{3,27},{4,28},{5,29},{6,30},{7,31},{8,16},{9,... | collective-permute-start | bytes 393224 | tf_op jit(solution)/shard_map/ppermute | solution.py:563
  116.7 0.8 collective-permute-start.45
  117.5 1.8 %collective-permute-start.44 = (f32[128,256]{1,0:T(8,128)S(1)}, f32[128,256]{1,0:T(8,128)S(1)}, u32[]{:S(2)}, u32[]{:S(2)}) collective-permute-start(f32[128,256]{1,0:T(8,128)S(1)} %fusion.6.a0), channel_id=1, source_target_pairs={{0,8},{1,9},{2,10},{3,11},{4,12},{5,13},{6,14},{7,15},{8,0},{9,1},... | collective-permute-start | bytes 393224 | tf_op jit(solution)/shard_map/ppermute | solution.py:563
  119.3 2.3 %collective-permute-done.35.a2 = f32[2,4,40,256]{3,2,1,0:T(8,128)S(1)} collective-permute-done((f32[2,4,40,256]{3,2,1,0:T(8,128)S(1)}, f32[2,4,40,256]{3,2,1,0:T(8,128)S(1)}, u32[]{:S(2)}, u32[]{:S(2)}) %collective-permute-start.35) | collective-permute-done | bytes 327712 | tf_op jit(solution)/shard_map/ppermute | solution.py:563
  121.5 1.2 collective-permute-done.36.a3
  123.4 3.1 %collective-permute-done.45.a2 = f32[128,256]{1,0:T(8,128)S(1)} collective-permute-done((f32[128,256]{1,0:T(8,128)S(1)}, f32[128,256]{1,0:T(8,128)S(1)}, u32[]{:S(2)}, u32[]{:S(2)}) %collective-permute-start.45) | collective-permute-done | bytes 131104 | tf_op jit(solution)/shard_map/ppermute | solution.py:563
  126.5 0.6 collective-permute-start.47
  127.1 0.5 collective-permute-start.38
  127.6 4.4 %collective-permute-done.42.g2 = f32[512,128]{1,0:T(8,128)S(1)} collective-permute-done((f32[512,128]{1,0:T(8,128)S(1)}, f32[512,128]{1,0:T(8,128)S(1)}, u32[]{:S(2)}, u32[]{:S(2)}) %collective-permute-start.42) | collective-permute-done | bytes 262176 | tf_op jit(solution)/shard_map/ppermute | solution.py:563
  132.0 2.2 %collective-permute-done.43.g3 = f32[512,128]{1,0:T(8,128)S(1)} collective-permute-done((f32[512,128]{1,0:T(8,128)S(1)}, f32[512,128]{1,0:T(8,128)S(1)}, u32[]{:S(2)}, u32[]{:S(2)}) %collective-permute-start.43) | collective-permute-done | bytes 262176 | tf_op jit(solution)/shard_map/ppermute | solution.py:563
  134.2 1.8 %collective-permute-start.40 = (f32[2,4,40,256]{3,2,1,0:T(8,128)S(1)}, f32[2,4,40,256]{3,2,1,0:T(8,128)S(1)}, u32[]{:S(2)}, u32[]{:S(2)}) collective-permute-start(f32[2,4,40,256]{3,2,1,0:T(8,128)S(1)} %collective-permute-done.36.a3), channel_id=1, source_target_pairs={{0,1},{1,0},{2,3},{3,2},{4,5},{5,4},{6,7},{7,6},{8,9},{9,8},{10,11... | collective-permute-start | bytes 983048 | tf_op jit(solution)/shard_map/ppermute | solution.py:563
  136.1 0.8 place_near.1.begun
  137.3 2.7 %finish_second.1 = (f32[8,256,256]{2,1,0:T(8,128)}, f32[3,256,128]{2,1,0:T(8,128)}, f32[3,8,128]{2,1,0:T(8,128)}, f32[16,24]{1,0:T(8,128)}, f32[8,256]{1,0:T(8,1...) custom-call(s32[2]{0:T(128)S(1)} %pad_add_fusion.place, ...), custom_call_target="tpu_custom_call" | custom-call | tf_op jit(solution)/shard_map/finish_second/pallas_call | solution.py:767
  140.0 0.8 place_far.1
  (143 shorter events, 6.3 us)
Async XLA Ops:
  0.7 11.1 %collective-permute-start.1 = (f32[8,128,256]{2,1,0:T(8,128)}, f32[8,128,256]{2,1,0:T(8,128)S(1)}, u32[]{:S(2)}, u32[]{:S(2)}) collective-permute-start(f32[8,128,256]{2,1,0:T(8,128)} %near0.3), channel_id=1, source_target_pairs={{0,1},{1,0},{2,3},{3,2},{4,5},{5,4},{6,7},{7,6},{8,9},{9,8},{10,11... | collective-permute-start | bytes 3145736 | tf_op jit(solution)/shard_map/ppermute | solution.py:563
  2.2 9.6 %collective-permute-start = (f32[2,128,256]{2,1,0:T(8,128)S(1)}, f32[2,128,256]{2,1,0:T(8,128)S(1)}, u32[]{:S(2)}, u32[]{:S(2)}) collective-permute-start(f32[2,128,256]{2,1,0:T(8,128)S(1)} %constant_dynamic-slice_fusion.4), channel_id=1, source_target_pairs={{0,2},{1,3},{2,0},{3,1},{4,6},{5,7},{6,4},{7,5},{8,10},{9,11},{10,... | collective-permute-start | bytes 786440 | tf_op jit(solution)/shard_map/ppermute | solution.py:563
  11.7 20.7 %copy-start.5 = (f32[2,128,256]{2,1,0:T(8,128)}, f32[2,128,256]{2,1,0:T(8,128)S(1)}, u32[]{:S(2)}) copy-start(f32[2,128,256]{2,1,0:T(8,128)S(1)} %collective-permute-done.fa0) | copy-start | bytes 786436
  11.7 20.7 %copy-start.3 = (f32[8,128,256]{2,1,0:T(8,128)}, f32[8,128,256]{2,1,0:T(8,128)S(1)}, u32[]{:S(2)}) copy-start(f32[8,128,256]{2,1,0:T(8,128)S(1)} %collective-permute-done.1.near1) | copy-start | bytes 3145732
  11.7 17.1 %collective-permute-start.3 = (f32[1048,128]{1,0:T(8,128)S(1)}, f32[1048,128]{1,0:T(8,128)S(1)}, u32[]{:S(2)}, u32[]{:S(2)}) collective-permute-start(f32[1048,128]{1,0:T(8,128)S(1)} %pad_maximum_fusion), channel_id=1, source_target_pairs={{0,2},{1,3},{2,0},{3,1},{4,6},{5,7},{6,4},{7,5},{8,10},{9,11},{10,... | collective-permute-start | bytes 1609736 | tf_op jit(solution)/shard_map/ppermute | solution.py:563
  13.5 15.3 %collective-permute-start.2 = (f32[536,128]{1,0:T(8,128)S(1)}, f32[536,128]{1,0:T(8,128)S(1)}, u32[]{:S(2)}, u32[]{:S(2)}) collective-permute-start(f32[536,128]{1,0:T(8,128)S(1)} %pad_maximum_fusion.7), channel_id=1, source_target_pairs={{0,1},{1,0},{2,3},{3,2},{4,5},{5,4},{6,7},{7,6},{8,9},{9,8},{10,11... | collective-permute-start | bytes 823304 | tf_op jit(solution)/shard_map/ppermute | solution.py:563
  13.5 10.0 %collective-permute-start.6 = (f32[2,128,256]{2,1,0:T(8,128)S(1)}, f32[2,128,256]{2,1,0:T(8,128)S(1)}, u32[]{:S(2)}, u32[]{:S(2)}) collective-permute-start(f32[2,128,256]{2,1,0:T(8,128)S(1)} %collective-permute-done.fa0), channel_id=1, source_target_pairs={{0,12},{1,13},{2,14},{3,15},{4,8},{5,9},{6,10},{7,11},{8,4},{9,5},... | collective-permute-start | bytes 786440 | tf_op jit(solution)/shard_map/ppermute | solution.py:563
  16.0 12.8 %collective-permute-start.5 = (f32[2,128,256]{2,1,0:T(8,128)S(1)}, f32[2,128,256]{2,1,0:T(8,128)S(1)}, u32[]{:S(2)}, u32[]{:S(2)}) collective-permute-start(f32[2,128,256]{2,1,0:T(8,128)S(1)} %collective-permute-done.fa0), channel_id=1, source_target_pairs={{0,8},{1,9},{2,10},{3,11},{4,12},{5,13},{6,14},{7,15},{8,0},{9,1},... | collective-permute-start | bytes 786440 | tf_op jit(solution)/shard_map/ppermute | solution.py:563
  16.5 12.4 %collective-permute-start.4 = (f32[2,128,256]{2,1,0:T(8,128)S(1)}, f32[2,128,256]{2,1,0:T(8,128)S(1)}, u32[]{:S(2)}, u32[]{:S(2)}) collective-permute-start(f32[2,128,256]{2,1,0:T(8,128)S(1)} %collective-permute-done.fa0), channel_id=1, source_target_pairs={{0,4},{1,5},{2,6},{3,7},{4,0},{5,1},{6,2},{7,3},{8,12},{9,13},{10,... | collective-permute-start | bytes 786440 | tf_op jit(solution)/shard_map/ppermute | solution.py:563
  28.9 3.5 %collective-permute-start.7 = (f32[1048,128]{1,0:T(8,128)S(1)}, f32[1048,128]{1,0:T(8,128)S(1)}, u32[]{:S(2)}, u32[]{:S(2)}) collective-permute-start(f32[1048,128]{1,0:T(8,128)S(1)} %collective-permute-done.3.x2), channel_id=1, source_target_pairs={{0,1},{1,0},{2,3},{3,2},{4,5},{5,4},{6,7},{7,6},{8,9},{9,8},{10,11... | collective-permute-start | bytes 1609736 | tf_op jit(solution)/shard_map/ppermute | solution.py:563
  29.0 2.3 %collective-permute-start.8 = (f32[2,128,256]{2,1,0:T(8,128)S(1)}, f32[2,128,256]{2,1,0:T(8,128)S(1)}, u32[]{:S(2)}, u32[]{:S(2)}) collective-permute-start(f32[2,128,256]{2,1,0:T(8,128)S(1)} %collective-permute-done.fa0), channel_id=1, source_target_pairs={{0,1},{1,0},{2,3},{3,2},{4,5},{5,4},{6,7},{7,6},{8,9},{9,8},{10,11... | collective-permute-start | bytes 786440 | tf_op jit(solution)/shard_map/ppermute | solution.py:563
  29.5 2.2 %collective-permute-start.9 = (f32[2,128,256]{2,1,0:T(8,128)S(1)}, f32[2,128,256]{2,1,0:T(8,128)S(1)}, u32[]{:S(2)}, u32[]{:S(2)}) collective-permute-start(f32[2,128,256]{2,1,0:T(8,128)S(1)} %collective-permute-done.4.fa1), channel_id=1, source_target_pairs={{0,1},{1,0},{2,3},{3,2},{4,5},{5,4},{6,7},{7,6},{8,9},{9,8},{10,11... | collective-permute-start | bytes 786440 | tf_op jit(solution)/shard_map/ppermute | solution.py:563
  29.5 2.5 %collective-permute-start.10 = (f32[2,128,256]{2,1,0:T(8,128)S(1)}, f32[2,128,256]{2,1,0:T(8,128)S(1)}, u32[]{:S(2)}, u32[]{:S(2)}) collective-permute-start(f32[2,128,256]{2,1,0:T(8,128)S(1)} %collective-permute-done.5.fa2), channel_id=1, source_target_pairs={{0,1},{1,0},{2,3},{3,2},{4,5},{5,4},{6,7},{7,6},{8,9},{9,8},{10,11... | collective-permute-start | bytes 786440 | tf_op jit(solution)/shard_map/ppermute | solution.py:563
  30.0 2.4 %collective-permute-start.11 = (f32[2,128,256]{2,1,0:T(8,128)S(1)}, f32[2,128,256]{2,1,0:T(8,128)S(1)}, u32[]{:S(2)}, u32[]{:S(2)}) collective-permute-start(f32[2,128,256]{2,1,0:T(8,128)S(1)} %collective-permute-done.6.fa3), channel_id=1, source_target_pairs={{0,1},{1,0},{2,3},{3,2},{4,5},{5,4},{6,7},{7,6},{8,9},{9,8},{10,11... | collective-permute-start | bytes 786440 | tf_op jit(solution)/shard_map/ppermute | solution.py:563
  53.2 2.4 %collective-permute-start.12 = (f32[16,40,256]{2,1,0:T(8,128)}, f32[16,40,256]{2,1,0:T(8,128)S(1)}, u32[]{:S(2)}, u32[]{:S(2)}) collective-permute-start(f32[16,40,256]{2,1,0:T(8,128)} %get-tuple-element.98), channel_id=1, source_target_pairs={{0,1},{1,0},{2,3},{3,2},{4,5},{5,4},{6,7},{7,6},{8,9},{9,8},{10,11... | collective-permute-start | bytes 1966088 | tf_op jit(solution)/shard_map/ppermute | solution.py:563
  53.4 3.4 %collective-permute-start.13 = (f32[16,40,256]{2,1,0:T(8,128)}, f32[16,40,256]{2,1,0:T(8,128)S(1)}, u32[]{:S(2)}, u32[]{:S(2)}) collective-permute-start(f32[16,40,256]{2,1,0:T(8,128)} %get-tuple-element.100), channel_id=1, source_target_pairs={{0,1},{1,0},{2,3},{3,2},{4,5},{5,4},{6,7},{7,6},{8,9},{9,8},{10,11... | collective-permute-start | bytes 1966088 | tf_op jit(solution)/shard_map/ppermute | solution.py:563
  57.0 9.8 %collective-permute-start.16 = (f32[2,4,40,256]{3,2,1,0:T(8,128)S(1)}, f32[2,4,40,256]{3,2,1,0:T(8,128)S(1)}, u32[]{:S(2)}, u32[]{:S(2)}) collective-permute-start(f32[2,4,40,256]{3,2,1,0:T(8,128)S(1)} %bitcast.109), channel_id=1, source_target_pairs={{0,4},{1,5},{2,6},{3,7},{4,0},{5,1},{6,2},{7,3},{8,12},{9,13},{10,... | collective-permute-start | bytes 983048 | tf_op jit(solution)/shard_map/ppermute | solution.py:563
  58.5 9.8 %collective-permute-start.18 = (f32[2,4,40,256]{3,2,1,0:T(8,128)S(1)}, f32[2,4,40,256]{3,2,1,0:T(8,128)S(1)}, u32[]{:S(2)}, u32[]{:S(2)}) collective-permute-start(f32[2,4,40,256]{3,2,1,0:T(8,128)S(1)} %get-tuple-element.111), channel_id=1, source_target_pairs={{0,2},{1,3},{2,0},{3,1},{4,6},{5,7},{6,4},{7,5},{8,10},{9,11},{10,... | collective-permute-start | bytes 983048 | tf_op jit(solution)/shard_map/ppermute | solution.py:563
  66.0 8.3 %collective-permute-start.14 = (f32[2,8,64,256]{3,2,1,0:T(8,128)}, f32[2,8,64,256]{3,2,1,0:T(8,128)S(1)}, u32[]{:S(2)}, u32[]{:S(2)}) collective-permute-start(f32[2,8,64,256]{3,2,1,0:T(8,128)} %get-tuple-element.105), channel_id=1, source_target_pairs={{0,1},{1,0},{2,3},{3,2},{4,5},{5,4},{6,7},{7,6},{8,9},{9,8},{10,11... | collective-permute-start | bytes 3145736 | tf_op jit(solution)/shard_map/ppermute | solution.py:563
  66.1 8.5 %collective-permute-start.15 = (f32[2,8,64,256]{3,2,1,0:T(8,128)}, f32[2,8,64,256]{3,2,1,0:T(8,128)S(1)}, u32[]{:S(2)}, u32[]{:S(2)}) collective-permute-start(f32[2,8,64,256]{3,2,1,0:T(8,128)} %get-tuple-element.107), channel_id=1, source_target_pairs={{0,1},{1,0},{2,3},{3,2},{4,5},{5,4},{6,7},{7,6},{8,9},{9,8},{10,11... | collective-permute-start | bytes 3145736 | tf_op jit(solution)/shard_map/ppermute | solution.py:563
  66.9 6.0 %collective-permute-start.17 = (f32[4,40,256]{2,1,0:T(8,128)S(1)}, f32[4,40,256]{2,1,0:T(8,128)S(1)}, u32[]{:S(2)}, u32[]{:S(2)}) collective-permute-start(f32[4,40,256]{2,1,0:T(8,128)S(1)} %slice_bitcast_fusion.10), channel_id=1, source_target_pairs={{0,2},{1,3},{2,0},{3,1},{4,6},{5,7},{6,4},{7,5},{8,10},{9,11},{10,... | collective-permute-start | bytes 491528 | tf_op jit(solution)/shard_map/ppermute | solution.py:563
  68.3 6.0 %collective-permute-start.19 = (f32[4,40,256]{2,1,0:T(8,128)S(1)}, f32[4,40,256]{2,1,0:T(8,128)S(1)}, u32[]{:S(2)}, u32[]{:S(2)}) collective-permute-start(f32[4,40,256]{2,1,0:T(8,128)S(1)} %slice_bitcast_fusion.8), channel_id=1, source_target_pairs={{0,4},{1,5},{2,6},{3,7},{4,0},{5,1},{6,2},{7,3},{8,12},{9,13},{10,... | collective-permute-start | bytes 491528 | tf_op jit(solution)/shard_map/ppermute | solution.py:563
  75.9 5.8 %collective-permute-start.20 = (f32[80,256]{1,0:T(8,128)S(1)}, f32[80,256]{1,0:T(8,128)S(1)}, u32[]{:S(2)}, u32[]{:S(2)}) collective-permute-start(f32[80,256]{1,0:T(8,128)S(1)} %get-tuple-element.171), channel_id=1, source_target_pairs={{0,8},{1,9},{2,10},{3,11},{4,12},{5,13},{6,14},{7,15},{8,0},{9,1},... | collective-permute-start | bytes 245768 | tf_op jit(solution)/shard_map/ppermute | solution.py:563
  77.5 6.6 %collective-permute-start.22 = (f32[80,256]{1,0:T(8,128)S(1)}, f32[80,256]{1,0:T(8,128)S(1)}, u32[]{:S(2)}, u32[]{:S(2)}) collective-permute-start(f32[80,256]{1,0:T(8,128)S(1)} %get-tuple-element.172), channel_id=1, source_target_pairs={{0,24},{1,25},{2,26},{3,27},{4,28},{5,29},{6,30},{7,31},{8,16},{9,... | collective-permute-start | bytes 245768 | tf_op jit(solution)/shard_map/ppermute | solution.py:563
  80.0 6.9 %collective-permute-start.21 = (f32[80,256]{1,0:T(8,128)S(1)}, f32[80,256]{1,0:T(8,128)S(1)}, u32[]{:S(2)}, u32[]{:S(2)}) collective-permute-start(f32[80,256]{1,0:T(8,128)S(1)} %get-tuple-element.173), channel_id=1, source_target_pairs={{0,16},{1,17},{2,18},{3,19},{4,20},{5,21},{6,22},{7,23},{8,24},{9,... | collective-permute-start | bytes 245768 | tf_op jit(solution)/shard_map/ppermute | solution.py:563
  80.1 12.5 %collective-permute-start.23 = (f32[2,4,64,256]{3,2,1,0:T(8,128)S(1)}, f32[2,4,64,256]{3,2,1,0:T(8,128)S(1)}, u32[]{:S(2)}, u32[]{:S(2)}) collective-permute-start(f32[2,4,64,256]{3,2,1,0:T(8,128)S(1)} %bitcast.108), channel_id=1, source_target_pairs={{0,2},{1,3},{2,0},{3,1},{4,6},{5,7},{6,4},{7,5},{8,10},{9,11},{10,... | collective-permute-start | bytes 1572872 | tf_op jit(solution)/shard_map/ppermute | solution.py:563
  80.6 12.8 %collective-permute-start.25 = (f32[2,4,64,256]{3,2,1,0:T(8,128)S(1)}, f32[2,4,64,256]{3,2,1,0:T(8,128)S(1)}, u32[]{:S(2)}, u32[]{:S(2)}) collective-permute-start(f32[2,4,64,256]{3,2,1,0:T(8,128)S(1)} %get-tuple-element.116), channel_id=1, source_target_pairs={{0,4},{1,5},{2,6},{3,7},{4,0},{5,1},{6,2},{7,3},{8,12},{9,13},{10,... | collective-permute-start | bytes 1572872 | tf_op jit(solution)/shard_map/ppermute | solution.py:563
  88.2 7.4 %collective-permute-start.28 = (f32[80,256]{1,0:T(8,128)S(1)}, f32[80,256]{1,0:T(8,128)S(1)}, u32[]{:S(2)}, u32[]{:S(2)}) collective-permute-start(f32[80,256]{1,0:T(8,128)S(1)} %broadcast_multiply_fusion), channel_id=1, source_target_pairs={{0,16},{1,17},{2,18},{3,19},{4,20},{5,21},{6,22},{7,23},{8,24},{9,... | collective-permute-start | bytes 245768 | tf_op jit(solution)/shard_map/ppermute | solution.py:563
  88.9 6.7 %collective-permute-start.27 = (f32[80,256]{1,0:T(8,128)S(1)}, f32[80,256]{1,0:T(8,128)S(1)}, u32[]{:S(2)}, u32[]{:S(2)}) collective-permute-start(f32[80,256]{1,0:T(8,128)S(1)} %broadcast_multiply_fusion), channel_id=1, source_target_pairs={{0,8},{1,9},{2,10},{3,11},{4,12},{5,13},{6,14},{7,15},{8,0},{9,1},... | collective-permute-start | bytes 245768 | tf_op jit(solution)/shard_map/ppermute | solution.py:563
  91.2 6.2 %collective-permute-start.29 = (f32[80,256]{1,0:T(8,128)S(1)}, f32[80,256]{1,0:T(8,128)S(1)}, u32[]{:S(2)}, u32[]{:S(2)}) collective-permute-start(f32[80,256]{1,0:T(8,128)S(1)} %broadcast_multiply_fusion), channel_id=1, source_target_pairs={{0,24},{1,25},{2,26},{3,27},{4,28},{5,29},{6,30},{7,31},{8,16},{9,... | collective-permute-start | bytes 245768 | tf_op jit(solution)/shard_map/ppermute | solution.py:563
  92.6 14.4 %copy-start.16 = (f32[2,128,256]{2,1,0:T(8,128)S(1)}, f32[2,128,256]{2,1,0:T(8,128)}, u32[]{:S(2)}) copy-start(f32[2,128,256]{2,1,0:T(8,128)} %copy-done.15) | copy-start | bytes 786436
  92.6 14.4 %copy-start.18 = (f32[2,128,256]{2,1,0:T(8,128)S(1)}, f32[2,128,256]{2,1,0:T(8,128)}, u32[]{:S(2)}) copy-start(f32[2,128,256]{2,1,0:T(8,128)} %copy-done.17) | copy-start | bytes 786436
  92.6 14.4 %copy-start.20 = (f32[2,128,256]{2,1,0:T(8,128)S(1)}, f32[2,128,256]{2,1,0:T(8,128)}, u32[]{:S(2)}) copy-start(f32[2,128,256]{2,1,0:T(8,128)} %copy-done.19) | copy-start | bytes 786436
  92.7 14.4 %copy-start.22 = (f32[24,512]{1,0:T(8,128)S(1)}, f32[24,512]{1,0:T(8,128)}, u32[]{:S(2)}) copy-start(f32[24,512]{1,0:T(8,128)} %get-tuple-element.121.glog) | copy-start | bytes 147460
  92.7 14.3 %copy-start.12 = (f32[2,128,256]{2,1,0:T(8,128)S(1)}, f32[2,128,256]{2,1,0:T(8,128)}, u32[]{:S(2)}) copy-start(f32[2,128,256]{2,1,0:T(8,128)} %copy-done.11) | copy-start | bytes 786436
  92.8 14.3 %copy-start.14 = (f32[2,128,256]{2,1,0:T(8,128)S(1)}, f32[2,128,256]{2,1,0:T(8,128)}, u32[]{:S(2)}) copy-start(f32[2,128,256]{2,1,0:T(8,128)} %copy-done.13) | copy-start | bytes 786436
  92.8 6.9 %collective-permute-start.24 = (f32[4,64,256]{2,1,0:T(8,128)S(1)}, f32[4,64,256]{2,1,0:T(8,128)S(1)}, u32[]{:S(2)}, u32[]{:S(2)}) collective-permute-start(f32[4,64,256]{2,1,0:T(8,128)S(1)} %slice_bitcast_fusion.6), channel_id=1, source_target_pairs={{0,4},{1,5},{2,6},{3,7},{4,0},{5,1},{6,2},{7,3},{8,12},{9,13},{10,... | collective-permute-start | bytes 786440 | tf_op jit(solution)/shard_map/ppermute | solution.py:563
  93.5 13.6 %copy-start.4 = (f32[8,128,256]{2,1,0:T(8,128)S(1)}, f32[8,128,256]{2,1,0:T(8,128)}, u32[]{:S(2)}) copy-start(f32[8,128,256]{2,1,0:T(8,128)} %copy-done.3) | copy-start | bytes 3145732
  93.5 13.6 %copy-start.8 = (f32[2,128,256]{2,1,0:T(8,128)S(1)}, f32[2,128,256]{2,1,0:T(8,128)}, u32[]{:S(2)}) copy-start(f32[2,128,256]{2,1,0:T(8,128)} %copy-done.7) | copy-start | bytes 786436
  93.5 13.6 %copy-start.10 = (f32[2,128,256]{2,1,0:T(8,128)S(1)}, f32[2,128,256]{2,1,0:T(8,128)}, u32[]{:S(2)}) copy-start(f32[2,128,256]{2,1,0:T(8,128)} %copy-done.9) | copy-start | bytes 786436
  93.5 13.5 %copy-start.2 = (f32[8,128,256]{2,1,0:T(8,128)S(1)}, f32[8,128,256]{2,1,0:T(8,128)}, u32[]{:S(2)}) copy-start(f32[8,128,256]{2,1,0:T(8,128)} %near0.3) | copy-start | bytes 3145732
  93.6 6.6 %collective-permute-start.26 = (f32[4,64,256]{2,1,0:T(8,128)S(1)}, f32[4,64,256]{2,1,0:T(8,128)S(1)}, u32[]{:S(2)}, u32[]{:S(2)}) collective-permute-start(f32[4,64,256]{2,1,0:T(8,128)S(1)} %slice_bitcast_fusion.4), channel_id=1, source_target_pairs={{0,2},{1,3},{2,0},{3,1},{4,6},{5,7},{6,4},{7,5},{8,10},{9,11},{10,... | collective-permute-start | bytes 786440 | tf_op jit(solution)/shard_map/ppermute | solution.py:563
  97.4 9.7 %copy-start.6 = (f32[2,128,256]{2,1,0:T(8,128)S(1)}, f32[2,128,256]{2,1,0:T(8,128)}, u32[]{:S(2)}) copy-start(f32[2,128,256]{2,1,0:T(8,128)} %copy-done.5) | copy-start | bytes 786436
  97.5 9.6 %copy-start = (bf16[8,256,512]{2,1,0:T(8,128)(2,1)S(1)}, bf16[8,256,512]{2,1,0:T(8,128)(2,1)}, u32[]{:S(2)}) copy-start(bf16[8,256,512]{2,1,0:T(8,128)(2,1)} %get-tuple-element.102.gf_high_in) | copy-start | bytes 6291460
  97.5 9.6 %copy-start.1 = (bf16[8,256,512]{2,1,0:T(8,128)(2,1)S(1)}, bf16[8,256,512]{2,1,0:T(8,128)(2,1)}, u32[]{:S(2)}) copy-start(bf16[8,256,512]{2,1,0:T(8,128)(2,1)} %get-tuple-element.122.gf_low_in) | copy-start | bytes 6291460
  97.5 9.6 %copy-start.21 = (f32[24,512]{1,0:T(8,128)S(1)}, f32[24,512]{1,0:T(8,128)}, u32[]{:S(2)}) copy-start(f32[24,512]{1,0:T(8,128)} %get-tuple-element.120.gate_all) | copy-start | bytes 147460
  100.3 12.4 %collective-permute-start.30 = (f32[128,256]{1,0:T(8,128)S(1)}, f32[128,256]{1,0:T(8,128)S(1)}, u32[]{:S(2)}, u32[]{:S(2)}) collective-permute-start(f32[128,256]{1,0:T(8,128)S(1)} %get-tuple-element.164), channel_id=1, source_target_pairs={{0,8},{1,9},{2,10},{3,11},{4,12},{5,13},{6,14},{7,15},{8,0},{9,1},... | collective-permute-start | bytes 393224 | tf_op jit(solution)/shard_map/ppermute | solution.py:563
  101.5 11.2 %collective-permute-start.32 = (f32[128,256]{1,0:T(8,128)S(1)}, f32[128,256]{1,0:T(8,128)S(1)}, u32[]{:S(2)}, u32[]{:S(2)}) collective-permute-start(f32[128,256]{1,0:T(8,128)S(1)} %get-tuple-element.165), channel_id=1, source_target_pairs={{0,24},{1,25},{2,26},{3,27},{4,28},{5,29},{6,30},{7,31},{8,16},{9,... | collective-permute-start | bytes 393224 | tf_op jit(solution)/shard_map/ppermute | solution.py:563
  104.0 8.8 %collective-permute-start.31 = (f32[128,256]{1,0:T(8,128)S(1)}, f32[128,256]{1,0:T(8,128)S(1)}, u32[]{:S(2)}, u32[]{:S(2)}) collective-permute-start(f32[128,256]{1,0:T(8,128)S(1)} %get-tuple-element.166), channel_id=1, source_target_pairs={{0,16},{1,17},{2,18},{3,19},{4,20},{5,21},{6,22},{7,23},{8,24},{9,... | collective-permute-start | bytes 393224 | tf_op jit(solution)/shard_map/ppermute | solution.py:563
  104.0 8.7 %collective-permute-start.34 = (f32[4,40,256]{2,1,0:T(8,128)S(1)}, f32[4,40,256]{2,1,0:T(8,128)S(1)}, u32[]{:S(2)}, u32[]{:S(2)}) collective-permute-start(f32[4,40,256]{2,1,0:T(8,128)S(1)} %get-tuple-element.169), channel_id=1, source_target_pairs={{0,4},{1,5},{2,6},{3,7},{4,0},{5,1},{6,2},{7,3},{8,12},{9,13},{10,... | collective-permute-start | bytes 491528 | tf_op jit(solution)/shard_map/ppermute | solution.py:563
  105.4 7.4 %collective-permute-start.33 = (f32[4,40,256]{2,1,0:T(8,128)S(1)}, f32[4,40,256]{2,1,0:T(8,128)S(1)}, u32[]{:S(2)}, u32[]{:S(2)}) collective-permute-start(f32[4,40,256]{2,1,0:T(8,128)S(1)} %get-tuple-element.170), channel_id=1, source_target_pairs={{0,2},{1,3},{2,0},{3,1},{4,6},{5,7},{6,4},{7,5},{8,10},{9,11},{10,... | collective-permute-start | bytes 491528 | tf_op jit(solution)/shard_map/ppermute | solution.py:563
  112.9 8.7 %collective-permute-start.35 = (f32[2,4,40,256]{3,2,1,0:T(8,128)S(1)}, f32[2,4,40,256]{3,2,1,0:T(8,128)S(1)}, u32[]{:S(2)}, u32[]{:S(2)}) collective-permute-start(f32[2,4,40,256]{3,2,1,0:T(8,128)S(1)} %pad_maximum_fusion.5.a0), channel_id=1, source_target_pairs={{0,4},{1,5},{2,6},{3,7},{4,0},{5,1},{6,2},{7,3},{8,12},{9,13},{10,... | collective-permute-start | bytes 983048 | tf_op jit(solution)/shard_map/ppermute | solution.py:563
  114.4 8.3 %collective-permute-start.36 = (f32[2,4,40,256]{3,2,1,0:T(8,128)S(1)}, f32[2,4,40,256]{3,2,1,0:T(8,128)S(1)}, u32[]{:S(2)}, u32[]{:S(2)}) collective-permute-start(f32[2,4,40,256]{3,2,1,0:T(8,128)S(1)} %pad_maximum_fusion.6.a1), channel_id=1, source_target_pairs={{0,2},{1,3},{2,0},{3,1},{4,6},{5,7},{6,4},{7,5},{8,10},{9,11},{10,... | collective-permute-start | bytes 983048 | tf_op jit(solution)/shard_map/ppermute | solution.py:563
  114.9 8.2 %collective-permute-start.46 = (f32[128,256]{1,0:T(8,128)S(1)}, f32[128,256]{1,0:T(8,128)S(1)}, u32[]{:S(2)}, u32[]{:S(2)}) collective-permute-start(f32[128,256]{1,0:T(8,128)S(1)} %fusion.6.a0), channel_id=1, source_target_pairs={{0,24},{1,25},{2,26},{3,27},{4,28},{5,29},{6,30},{7,31},{8,16},{9,... | collective-permute-start | bytes 393224 | tf_op jit(solution)/shard_map/ppermute | solution.py:563
  116.7 9.8 %collective-permute-start.45 = (f32[128,256]{1,0:T(8,128)S(1)}, f32[128,256]{1,0:T(8,128)S(1)}, u32[]{:S(2)}, u32[]{:S(2)}) collective-permute-start(f32[128,256]{1,0:T(8,128)S(1)} %fusion.6.a0), channel_id=1, source_target_pairs={{0,16},{1,17},{2,18},{3,19},{4,20},{5,21},{6,22},{7,23},{8,24},{9,... | collective-permute-start | bytes 393224 | tf_op jit(solution)/shard_map/ppermute | solution.py:563
  117.5 9.0 %collective-permute-start.44 = (f32[128,256]{1,0:T(8,128)S(1)}, f32[128,256]{1,0:T(8,128)S(1)}, u32[]{:S(2)}, u32[]{:S(2)}) collective-permute-start(f32[128,256]{1,0:T(8,128)S(1)} %fusion.6.a0), channel_id=1, source_target_pairs={{0,8},{1,9},{2,10},{3,11},{4,12},{5,13},{6,14},{7,15},{8,0},{9,1},... | collective-permute-start | bytes 393224 | tf_op jit(solution)/shard_map/ppermute | solution.py:563
  121.5 5.6 %collective-permute-start.41 = (f32[512,128]{1,0:T(8,128)S(1)}, f32[512,128]{1,0:T(8,128)S(1)}, u32[]{:S(2)}, u32[]{:S(2)}) collective-permute-start(f32[512,128]{1,0:T(8,128)S(1)} %get-tuple-element.136), channel_id=1, source_target_pairs={{0,1},{1,0},{2,3},{3,2},{4,5},{5,4},{6,7},{7,6},{8,9},{9,8},{10,11... | collective-permute-start | bytes 786440 | tf_op jit(solution)/shard_map/ppermute | solution.py:563
  122.7 9.2 %collective-permute-start.42 = (f32[512,128]{1,0:T(8,128)S(1)}, f32[512,128]{1,0:T(8,128)S(1)}, u32[]{:S(2)}, u32[]{:S(2)}) collective-permute-start(f32[512,128]{1,0:T(8,128)S(1)} %get-tuple-element.137), channel_id=1, source_target_pairs={{0,2},{1,3},{2,0},{3,1},{4,6},{5,7},{6,4},{7,5},{8,10},{9,11},{10,... | collective-permute-start | bytes 786440 | tf_op jit(solution)/shard_map/ppermute | solution.py:563
  123.1 11.0 %collective-permute-start.43 = (f32[512,128]{1,0:T(8,128)S(1)}, f32[512,128]{1,0:T(8,128)S(1)}, u32[]{:S(2)}, u32[]{:S(2)}) collective-permute-start(f32[512,128]{1,0:T(8,128)S(1)} %get-tuple-element.138), channel_id=1, source_target_pairs={{0,3},{1,2},{2,1},{3,0},{4,7},{5,6},{6,5},{7,4},{8,11},{9,10},{10,... | collective-permute-start | bytes 786440 | tf_op jit(solution)/shard_map/ppermute | solution.py:563
  126.5 13.4 %collective-permute-start.47 = (f32[4,128,256]{2,1,0:T(8,128)S(1)}, f32[4,128,256]{2,1,0:T(8,128)S(1)}, u32[]{:S(2)}, u32[]{:S(2)}) collective-permute-start(f32[4,128,256]{2,1,0:T(8,128)S(1)} %pad_maximum_fusion.2), channel_id=1, source_target_pairs={{0,4},{1,5},{2,6},{3,7},{4,0},{5,1},{6,2},{7,3},{8,12},{9,13},{10,... | collective-permute-start | bytes 1572872 | tf_op jit(solution)/shard_map/ppermute | solution.py:563
  127.1 9.8 %collective-permute-start.37 = (f32[2,4,40,256]{3,2,1,0:T(8,128)S(1)}, f32[2,4,40,256]{3,2,1,0:T(8,128)S(1)}, u32[]{:S(2)}, u32[]{:S(2)}) collective-permute-start(f32[2,4,40,256]{3,2,1,0:T(8,128)S(1)} %pad_maximum_fusion.5.a0), channel_id=1, source_target_pairs={{0,1},{1,0},{2,3},{3,2},{4,5},{5,4},{6,7},{7,6},{8,9},{9,8},{10,11... | collective-permute-start | bytes 983048 | tf_op jit(solution)/shard_map/ppermute | solution.py:563
  127.1 9.8 %collective-permute-start.38 = (f32[2,4,40,256]{3,2,1,0:T(8,128)S(1)}, f32[2,4,40,256]{3,2,1,0:T(8,128)S(1)}, u32[]{:S(2)}, u32[]{:S(2)}) collective-permute-start(f32[2,4,40,256]{3,2,1,0:T(8,128)S(1)} %pad_maximum_fusion.6.a1), channel_id=1, source_target_pairs={{0,1},{1,0},{2,3},{3,2},{4,5},{5,4},{6,7},{7,6},{8,9},{9,8},{10,11... | collective-permute-start | bytes 983048 | tf_op jit(solution)/shard_map/ppermute | solution.py:563
  132.0 4.9 %collective-permute-start.39 = (f32[2,4,40,256]{3,2,1,0:T(8,128)S(1)}, f32[2,4,40,256]{3,2,1,0:T(8,128)S(1)}, u32[]{:S(2)}, u32[]{:S(2)}) collective-permute-start(f32[2,4,40,256]{3,2,1,0:T(8,128)S(1)} %collective-permute-done.35.a2), channel_id=1, source_target_pairs={{0,1},{1,0},{2,3},{3,2},{4,5},{5,4},{6,7},{7,6},{8,9},{9,8},{10,11... | collective-permute-start | bytes 983048 | tf_op jit(solution)/shard_map/ppermute | solution.py:563
  134.2 3.1 %collective-permute-start.40 = (f32[2,4,40,256]{3,2,1,0:T(8,128)S(1)}, f32[2,4,40,256]{3,2,1,0:T(8,128)S(1)}, u32[]{:S(2)}, u32[]{:S(2)}) collective-permute-start(f32[2,4,40,256]{3,2,1,0:T(8,128)S(1)} %collective-permute-done.36.a3), channel_id=1, source_target_pairs={{0,1},{1,0},{2,3},{3,2},{4,5},{5,4},{6,7},{7,6},{8,9},{9,8},{10,11... | collective-permute-start | bytes 983048 | tf_op jit(solution)/shard_map/ppermute | solution.py:563
  (16 other events, 63.1 us)

commit v7 on v5

--- a/solution.py
+++ b/solution.py
@@ -162,7 +162,7 @@
     tower_cols = tower_rows[...].T
     for load in loads[0:2]:
         load.wait()
-    ahead = 4
+    ahead = 6
     for n in range(ahead):
         begun[n] = dot3(split(near_in[order[n]]), (xt_high[0 : 2 * cols], xt_low[0 : 2 * cols]), TN)
     for load in loads[2:]:
@@ -629,7 +629,7 @@
         + [whole()] * 4,
         out_specs=[anywhere()] * 4 + [whole()] * 2 + [anywhere()] * 4,
         scratch_shapes=[
-            VMEM((4, hidden, rows), F32),
+            VMEM((8, hidden, rows), F32),
             VMEM((4, rows + units, cols), F32),
             VMEM((experts, 2 * cols, hidden), F32),
             VMEM((experts, 2 * cols, hidden), F32),

time: 142 us -> 142 us (level)
  no operation moved by 1% of the time
where the time goes in v7:
time: 142 us; the launch traced here: 141 us
  waiting for transfers between devices  48.6 us (34%)
  starting transfers between devices  42.9 us (30%)
  Pallas kernels  37.5 us (26%)
  local copies, waits for them, and re-layouts  6.95 us (5%)
  between operations  2.9 us (2%)
  other arithmetic  2.27 us (2%)
    ppermute x48, waiting for transfers between devices, move(): return lax.ppermute(value, ('dp', 'field'), pairs)  48.6 us
    ppermute x48, starting transfers between devices, move(): return lax.ppermute(value, ('dp', 'field'), pairs)  42.9 us
    pallas_call x1, Pallas kernels, per_device(): pl.pallas_call(middle_kernel, name='middle', out_shape=(like((4 * cols, r...  19.8 us
    pallas_call x1, Pallas kernels, per_device(): pl.pallas_call(first_kernel, name='first', out_shape=tuple((like((2, 8, c...  7.02 us
    pallas_call x1, Pallas kernels, per_device(): pl.pallas_call(inputs_kernel, name='inputs', out_shape=tuple((like((rows,...  5.56 us
  transfers between devices with their start and end apart: 48, of which 23 were waited for; matrix products, arithmetic and copies ran while one was open for 5% of the time, Pallas kernels for 12%

profile of v7, /device:TPU:0, one launch (start us, length us, event | category | flops | bytes accessed | tf_op | source)
XLA Modules:
  0.0 141.2 jit_solution(12909154228704228850)
XLA Ops:
  0.7 0.5 collective-permute-start.1
  1.2 1.0 constant_dynamic-slice_fusion.4
  2.2 2.6 %collective-permute-start = (f32[2,128,256]{2,1,0:T(8,128)S(1)}, f32[2,128,256]{2,1,0:T(8,128)S(1)}, u32[]{:S(2)}, u32[]{:S(2)}) collective-permute-start(f32[2,128,256]{2,1,0:T(8,128)S(1)} %constant_dynamic-slice_fusion.4), channel_id=1, source_target_pairs={{0,2},{1,3},{2,0},{3,1},{4,6},{5,7},{6,4},{7,5},{8,10},{9,11},{10,... | collective-permute-start | bytes 786440 | tf_op jit(solution)/shard_map/ppermute | solution.py:567
  4.8 2.0 %constant_dynamic-slice_fusion = (f32[512,128]{1,0:T(8,128)}, f32[512,128]{1,0:T(8,128)S(1)}, f32[512,128]{1,0:T(8,128)S(1)}, f32[512,128]{1,0:T(8,128)S(1)}) fusion(f32[2048,128]{1,0:T(8,128)} %param.14, s32[]{:T(128)S(6)} %select_n.19, s32[]{:T(128)S(6)} %select_n.17, s32[]{:T(128)S(6)} %select_n.16, s32[]{:T(128)S(6)} %select_n.18), kind=kLoop, calls=%fused_computation.38 | loop fusion | bytes 2097168 | tf_op jit(solution)/shard_map/dynamic_slice | solution.py:588
  7.4 0.6 reshape.56.domain
  8.0 0.6 stack.73.place
  8.7 3.1 %collective-permute-done.fa0 = f32[2,128,256]{2,1,0:T(8,128)S(1)} collective-permute-done((f32[2,128,256]{2,1,0:T(8,128)S(1)}, f32[2,128,256]{2,1,0:T(8,128)S(1)}, u32[]{:S(2)}, u32[]{:S(2)}) %collective-permute-start) | collective-permute-done | bytes 262176 | tf_op jit(solution)/shard_map/ppermute | solution.py:567
  11.7 1.8 %collective-permute-start.3 = (f32[1048,128]{1,0:T(8,128)S(1)}, f32[1048,128]{1,0:T(8,128)S(1)}, u32[]{:S(2)}, u32[]{:S(2)}) collective-permute-start(f32[1048,128]{1,0:T(8,128)S(1)} %pad_maximum_fusion), channel_id=1, source_target_pairs={{0,2},{1,3},{2,0},{3,1},{4,6},{5,7},{6,4},{7,5},{8,10},{9,11},{10,... | collective-permute-start | bytes 1609736 | tf_op jit(solution)/shard_map/ppermute | solution.py:567
  13.5 2.5 %collective-permute-start.6 = (f32[2,128,256]{2,1,0:T(8,128)S(1)}, f32[2,128,256]{2,1,0:T(8,128)S(1)}, u32[]{:S(2)}, u32[]{:S(2)}) collective-permute-start(f32[2,128,256]{2,1,0:T(8,128)S(1)} %collective-permute-done.fa0), channel_id=1, source_target_pairs={{0,12},{1,13},{2,14},{3,15},{4,8},{5,9},{6,10},{7,11},{8,4},{9,5},... | collective-permute-start | bytes 786440 | tf_op jit(solution)/shard_map/ppermute | solution.py:567
  16.5 0.5 collective-permute-start.4
  17.0 6.6 %collective-permute-done.6.fa3 = f32[2,128,256]{2,1,0:T(8,128)S(1)} collective-permute-done((f32[2,128,256]{2,1,0:T(8,128)S(1)}, f32[2,128,256]{2,1,0:T(8,128)S(1)}, u32[]{:S(2)}, u32[]{:S(2)}) %collective-permute-start.6) | collective-permute-done | bytes 262176 | tf_op jit(solution)/shard_map/ppermute | solution.py:567
  23.6 5.3 %collective-permute-done.5.fa2 = f32[2,128,256]{2,1,0:T(8,128)S(1)} collective-permute-done((f32[2,128,256]{2,1,0:T(8,128)S(1)}, f32[2,128,256]{2,1,0:T(8,128)S(1)}, u32[]{:S(2)}, u32[]{:S(2)}) %collective-permute-start.5) | collective-permute-done | bytes 262176 | tf_op jit(solution)/shard_map/ppermute | solution.py:567
  29.0 0.5 collective-permute-start.8
  30.0 1.2 collective-permute-done.8.fb0
  33.3 19.8 %middle.1 = (bf16[512,512]{1,0:T(8,128)(2,1)}, bf16[512,512]{1,0:T(8,128)(2,1)}, bf16[8,256,512]{2,1,0:T(8,128)(2,1)}, bf16[8,256,512]{2,1,0:T(8,128)(2,1)}, f32...) custom-call(s32[5]{0:T(128)} %stack.73.place, ...), custom_call_target="tpu_custom_call" | custom-call | tf_op jit(solution)/shard_map/middle/pallas_call | solution.py:608
  53.7 1.8 %collective-permute-done.12 = f32[16,40,256]{2,1,0:T(8,128)S(1)} collective-permute-done((f32[16,40,256]{2,1,0:T(8,128)}, f32[16,40,256]{2,1,0:T(8,128)S(1)}, u32[]{:S(2)}, u32[]{:S(2)}) %collective-permute-start.12) | collective-permute-done | bytes 655392 | tf_op jit(solution)/shard_map/ppermute | solution.py:567
  55.4 1.2 add.98
  56.8 1.5 %collective-permute-start.16 = (f32[2,4,40,256]{3,2,1,0:T(8,128)S(1)}, f32[2,4,40,256]{3,2,1,0:T(8,128)S(1)}, u32[]{:S(2)}, u32[]{:S(2)}) collective-permute-start(f32[2,4,40,256]{3,2,1,0:T(8,128)S(1)} %bitcast.109), channel_id=1, source_target_pairs={{0,4},{1,5},{2,6},{3,7},{4,0},{5,1},{6,2},{7,3},{8,12},{9,13},{10,... | collective-permute-start | bytes 983048 | tf_op jit(solution)/shard_map/ppermute | solution.py:567
  58.3 0.5 collective-permute-start.18
  58.8 7.0 %first.1 = (f32[2,8,64,256]{3,2,1,0:T(8,128)}, f32[2,8,64,256]{3,2,1,0:T(8,128)}, f32[2,8,64,256]{3,2,1,0:T(8,128)}, f32[2,8,64,256]{3,2,1,0:T(8,128)}) custom-call(s32[1]{0:T(128)} %bitcast.2.place, bf16[512,512]{1,0:T(8,128)(2,1)} %get-tuple-element.94.xt_high_in, bf16[512,512]{1,0:T(8,128)(2,1)} %get-tuple-element.95.xt_low_in, ...), custom_call_target="tpu_custom_call" | custom-call | bytes 1048576 | tf_op jit(solution)/shard_map/first/pallas_call | solution.py:696
  65.9 0.5 collective-permute-start.15
  66.7 1.3 collective-permute-start.17
  68.1 0.7 collective-permute-start.19
  68.8 3.9 %collective-permute-done.17 = f32[4,40,256]{2,1,0:T(8,128)S(1)} collective-permute-done((f32[4,40,256]{2,1,0:T(8,128)S(1)}, f32[4,40,256]{2,1,0:T(8,128)S(1)}, u32[]{:S(2)}, u32[]{:S(2)}) %collective-permute-start.17) | collective-permute-done | bytes 163872 | tf_op jit(solution)/shard_map/ppermute | solution.py:567
  72.8 1.3 collective-permute-done.19
  74.5 1.0 copy-done.24
  75.7 1.6 %collective-permute-start.24 = (f32[80,256]{1,0:T(8,128)S(1)}, f32[80,256]{1,0:T(8,128)S(1)}, u32[]{:S(2)}, u32[]{:S(2)}) collective-permute-start(f32[80,256]{1,0:T(8,128)S(1)} %get-tuple-element.169), channel_id=1, source_target_pairs={{0,8},{1,9},{2,10},{3,11},{4,12},{5,13},{6,14},{7,15},{8,0},{9,1},... | collective-permute-start | bytes 245768 | tf_op jit(solution)/shard_map/ppermute | solution.py:567
  77.3 2.5 %collective-permute-start.26 = (f32[80,256]{1,0:T(8,128)S(1)}, f32[80,256]{1,0:T(8,128)S(1)}, u32[]{:S(2)}, u32[]{:S(2)}) collective-permute-start(f32[80,256]{1,0:T(8,128)S(1)} %get-tuple-element.170), channel_id=1, source_target_pairs={{0,24},{1,25},{2,26},{3,27},{4,28},{5,29},{6,30},{7,31},{8,16},{9,... | collective-permute-start | bytes 245768 | tf_op jit(solution)/shard_map/ppermute | solution.py:567
  79.9 0.5 collective-permute-start.20
  80.4 1.0 collective-permute-start.22
  81.5 2.5 %collective-permute-done.26 = f32[80,256]{1,0:T(8,128)S(1)} collective-permute-done((f32[80,256]{1,0:T(8,128)S(1)}, f32[80,256]{1,0:T(8,128)S(1)}, u32[]{:S(2)}, u32[]{:S(2)}) %collective-permute-start.26) | collective-permute-done | bytes 81952 | tf_op jit(solution)/shard_map/ppermute | solution.py:567
  84.0 2.7 %collective-permute-done.25 = f32[80,256]{1,0:T(8,128)S(1)} collective-permute-done((f32[80,256]{1,0:T(8,128)S(1)}, f32[80,256]{1,0:T(8,128)S(1)}, u32[]{:S(2)}, u32[]{:S(2)}) %collective-permute-start.25) | collective-permute-done | bytes 81952 | tf_op jit(solution)/shard_map/ppermute | solution.py:567
  86.8 0.5 slice.128
  88.0 0.7 collective-permute-start.28
  88.7 2.3 %collective-permute-start.27 = (f32[80,256]{1,0:T(8,128)S(1)}, f32[80,256]{1,0:T(8,128)S(1)}, u32[]{:S(2)}, u32[]{:S(2)}) collective-permute-start(f32[80,256]{1,0:T(8,128)S(1)} %broadcast_multiply_fusion), channel_id=1, source_target_pairs={{0,8},{1,9},{2,10},{3,11},{4,12},{5,13},{6,14},{7,15},{8,0},{9,1},... | collective-permute-start | bytes 245768 | tf_op jit(solution)/shard_map/ppermute | solution.py:567
  91.0 1.4 %collective-permute-start.29 = (f32[80,256]{1,0:T(8,128)S(1)}, f32[80,256]{1,0:T(8,128)S(1)}, u32[]{:S(2)}, u32[]{:S(2)}) collective-permute-start(f32[80,256]{1,0:T(8,128)S(1)} %broadcast_multiply_fusion), channel_id=1, source_target_pairs={{0,24},{1,25},{2,26},{3,27},{4,28},{5,29},{6,30},{7,31},{8,16},{9,... | collective-permute-start | bytes 245768 | tf_op jit(solution)/shard_map/ppermute | solution.py:567
  92.6 0.7 collective-permute-start.21
  93.4 0.7 collective-permute-start.23
  94.2 1.2 collective-permute-done.28
  95.4 1.9 %collective-permute-done.29 = f32[80,256]{1,0:T(8,128)S(1)} collective-permute-done((f32[80,256]{1,0:T(8,128)S(1)}, f32[80,256]{1,0:T(8,128)S(1)}, u32[]{:S(2)}, u32[]{:S(2)}) %collective-permute-start.29) | collective-permute-done | bytes 81952 | tf_op jit(solution)/shard_map/ppermute | solution.py:567
  97.3 2.2 %collective-permute-done.21 = f32[4,64,256]{2,1,0:T(8,128)S(1)} collective-permute-done((f32[4,64,256]{2,1,0:T(8,128)S(1)}, f32[4,64,256]{2,1,0:T(8,128)S(1)}, u32[]{:S(2)}, u32[]{:S(2)}) %collective-permute-start.21) | collective-permute-done | bytes 262176 | tf_op jit(solution)/shard_map/ppermute | solution.py:567
  99.5 0.5 collective-permute-done.23
  100.1 1.2 collective-permute-start.30
  101.3 2.5 %collective-permute-start.32 = (f32[128,256]{1,0:T(8,128)S(1)}, f32[128,256]{1,0:T(8,128)S(1)}, u32[]{:S(2)}, u32[]{:S(2)}) collective-permute-start(f32[128,256]{1,0:T(8,128)S(1)} %get-tuple-element.163), channel_id=1, source_target_pairs={{0,24},{1,25},{2,26},{3,27},{4,28},{5,29},{6,30},{7,31},{8,16},{9,... | collective-permute-start | bytes 393224 | tf_op jit(solution)/shard_map/ppermute | solution.py:567
  103.9 1.3 collective-permute-start.34
  105.2 1.6 %collective-permute-start.33 = (f32[4,40,256]{2,1,0:T(8,128)S(1)}, f32[4,40,256]{2,1,0:T(8,128)S(1)}, u32[]{:S(2)}, u32[]{:S(2)}) collective-permute-start(f32[4,40,256]{2,1,0:T(8,128)S(1)} %get-tuple-element.168), channel_id=1, source_target_pairs={{0,2},{1,3},{2,0},{3,1},{4,6},{5,7},{6,4},{7,5},{8,10},{9,11},{10,... | collective-permute-start | bytes 491528 | tf_op jit(solution)/shard_map/ppermute | solution.py:567
  107.0 5.6 %inputs.1 = (f32[512,128]{1,0:T(8,128)S(1)}, f32[512,128]{1,0:T(8,128)S(1)}, f32[512,128]{1,0:T(8,128)S(1)}, f32[512,128]{1,0:T(8,128)S(1)}) custom-call(s32[5]{0:T(128)S(1)} %copy-done.23, f32[24,512]{1,0:T(8,128)S(1)} %copy-done.21, f32[24,512]{1,0:T(8,128)S(1)} %copy-done.22, bf16[8,256,512]{2,1,0:T(8,128)(2,1)S(1)} %copy-done, ...), custom_call_target="tpu_custom_call" | custom-call | bytes 1048576 | tf_op jit(solution)/shard_map/inputs/pallas_call | solution.py:737
  112.7 1.6 %collective-permute-start.35 = (f32[2,4,40,256]{3,2,1,0:T(8,128)S(1)}, f32[2,4,40,256]{3,2,1,0:T(8,128)S(1)}, u32[]{:S(2)}, u32[]{:S(2)}) collective-permute-start(f32[2,4,40,256]{3,2,1,0:T(8,128)S(1)} %pad_maximum_fusion.5.a0), channel_id=1, source_target_pairs={{0,4},{1,5},{2,6},{3,7},{4,0},{5,1},{6,2},{7,3},{8,12},{9,13},{10,... | collective-permute-start | bytes 983048 | tf_op jit(solution)/shard_map/ppermute | solution.py:567
  114.2 0.5 collective-permute-start.36
  114.7 1.8 %collective-permute-start.46 = (f32[128,256]{1,0:T(8,128)S(1)}, f32[128,256]{1,0:T(8,128)S(1)}, u32[]{:S(2)}, u32[]{:S(2)}) collective-permute-start(f32[128,256]{1,0:T(8,128)S(1)} %fusion.6.a0), channel_id=1, source_target_pairs={{0,24},{1,25},{2,26},{3,27},{4,28},{5,29},{6,30},{7,31},{8,16},{9,... | collective-permute-start | bytes 393224 | tf_op jit(solution)/shard_map/ppermute | solution.py:567
  116.5 0.8 collective-permute-start.45
  117.3 1.8 %collective-permute-start.44 = (f32[128,256]{1,0:T(8,128)S(1)}, f32[128,256]{1,0:T(8,128)S(1)}, u32[]{:S(2)}, u32[]{:S(2)}) collective-permute-start(f32[128,256]{1,0:T(8,128)S(1)} %fusion.6.a0), channel_id=1, source_target_pairs={{0,8},{1,9},{2,10},{3,11},{4,12},{5,13},{6,14},{7,15},{8,0},{9,1},... | collective-permute-start | bytes 393224 | tf_op jit(solution)/shard_map/ppermute | solution.py:567
  119.1 2.2 %collective-permute-done.35.a2 = f32[2,4,40,256]{3,2,1,0:T(8,128)S(1)} collective-permute-done((f32[2,4,40,256]{3,2,1,0:T(8,128)S(1)}, f32[2,4,40,256]{3,2,1,0:T(8,128)S(1)}, u32[]{:S(2)}, u32[]{:S(2)}) %collective-permute-start.35) | collective-permute-done | bytes 327712 | tf_op jit(solution)/shard_map/ppermute | solution.py:567
  121.3 1.2 collective-permute-done.36.a3
  123.2 3.1 %collective-permute-done.45.a2 = f32[128,256]{1,0:T(8,128)S(1)} collective-permute-done((f32[128,256]{1,0:T(8,128)S(1)}, f32[128,256]{1,0:T(8,128)S(1)}, u32[]{:S(2)}, u32[]{:S(2)}) %collective-permute-start.45) | collective-permute-done | bytes 131104 | tf_op jit(solution)/shard_map/ppermute | solution.py:567
  126.3 0.6 collective-permute-start.47
  126.9 0.5 collective-permute-start.38
  127.4 4.4 %collective-permute-done.42.g2 = f32[512,128]{1,0:T(8,128)S(1)} collective-permute-done((f32[512,128]{1,0:T(8,128)S(1)}, f32[512,128]{1,0:T(8,128)S(1)}, u32[]{:S(2)}, u32[]{:S(2)}) %collective-permute-start.42) | collective-permute-done | bytes 262176 | tf_op jit(solution)/shard_map/ppermute | solution.py:567
  131.8 2.1 %collective-permute-done.43.g3 = f32[512,128]{1,0:T(8,128)S(1)} collective-permute-done((f32[512,128]{1,0:T(8,128)S(1)}, f32[512,128]{1,0:T(8,128)S(1)}, u32[]{:S(2)}, u32[]{:S(2)}) %collective-permute-start.43) | collective-permute-done | bytes 262176 | tf_op jit(solution)/shard_map/ppermute | solution.py:567
  133.9 1.9 %collective-permute-start.40 = (f32[2,4,40,256]{3,2,1,0:T(8,128)S(1)}, f32[2,4,40,256]{3,2,1,0:T(8,128)S(1)}, u32[]{:S(2)}, u32[]{:S(2)}) collective-permute-start(f32[2,4,40,256]{3,2,1,0:T(8,128)S(1)} %collective-permute-done.36.a3), channel_id=1, source_target_pairs={{0,1},{1,0},{2,3},{3,2},{4,5},{5,4},{6,7},{7,6},{8,9},{9,8},{10,11... | collective-permute-start | bytes 983048 | tf_op jit(solution)/shard_map/ppermute | solution.py:567
  135.9 0.8 place_near.1.begun
  136.7 1.1 finish_inputs.1
  137.8 2.4 %finish_second.1 = (f32[8,256,256]{2,1,0:T(8,128)}, f32[3,256,128]{2,1,0:T(8,128)}, f32[3,8,128]{2,1,0:T(8,128)}, f32[16,24]{1,0:T(8,128)}, f32[8,256]{1,0:T(8,1...) custom-call(s32[2]{0:T(128)S(1)} %pad_add_fusion.place, ...), custom_call_target="tpu_custom_call" | custom-call | tf_op jit(solution)/shard_map/finish_second/pallas_call | solution.py:771
  140.2 0.8 place_far.1
  (144 shorter events, 6.4 us)
Async XLA Ops:
  0.7 11.1 %collective-permute-start.1 = (f32[8,128,256]{2,1,0:T(8,128)}, f32[8,128,256]{2,1,0:T(8,128)S(1)}, u32[]{:S(2)}, u32[]{:S(2)}) collective-permute-start(f32[8,128,256]{2,1,0:T(8,128)} %near0.3), channel_id=1, source_target_pairs={{0,1},{1,0},{2,3},{3,2},{4,5},{5,4},{6,7},{7,6},{8,9},{9,8},{10,11... | collective-permute-start | bytes 3145736 | tf_op jit(solution)/shard_map/ppermute | solution.py:567
  2.2 9.6 %collective-permute-start = (f32[2,128,256]{2,1,0:T(8,128)S(1)}, f32[2,128,256]{2,1,0:T(8,128)S(1)}, u32[]{:S(2)}, u32[]{:S(2)}) collective-permute-start(f32[2,128,256]{2,1,0:T(8,128)S(1)} %constant_dynamic-slice_fusion.4), channel_id=1, source_target_pairs={{0,2},{1,3},{2,0},{3,1},{4,6},{5,7},{6,4},{7,5},{8,10},{9,11},{10,... | collective-permute-start | bytes 786440 | tf_op jit(solution)/shard_map/ppermute | solution.py:567
  11.7 20.7 %copy-start.5 = (f32[2,128,256]{2,1,0:T(8,128)}, f32[2,128,256]{2,1,0:T(8,128)S(1)}, u32[]{:S(2)}) copy-start(f32[2,128,256]{2,1,0:T(8,128)S(1)} %collective-permute-done.fa0) | copy-start | bytes 786436
  11.7 20.7 %copy-start.3 = (f32[8,128,256]{2,1,0:T(8,128)}, f32[8,128,256]{2,1,0:T(8,128)S(1)}, u32[]{:S(2)}) copy-start(f32[8,128,256]{2,1,0:T(8,128)S(1)} %collective-permute-done.1.near1) | copy-start | bytes 3145732
  11.7 17.1 %collective-permute-start.3 = (f32[1048,128]{1,0:T(8,128)S(1)}, f32[1048,128]{1,0:T(8,128)S(1)}, u32[]{:S(2)}, u32[]{:S(2)}) collective-permute-start(f32[1048,128]{1,0:T(8,128)S(1)} %pad_maximum_fusion), channel_id=1, source_target_pairs={{0,2},{1,3},{2,0},{3,1},{4,6},{5,7},{6,4},{7,5},{8,10},{9,11},{10,... | collective-permute-start | bytes 1609736 | tf_op jit(solution)/shard_map/ppermute | solution.py:567
  13.5 15.3 %collective-permute-start.2 = (f32[536,128]{1,0:T(8,128)S(1)}, f32[536,128]{1,0:T(8,128)S(1)}, u32[]{:S(2)}, u32[]{:S(2)}) collective-permute-start(f32[536,128]{1,0:T(8,128)S(1)} %pad_maximum_fusion.7), channel_id=1, source_target_pairs={{0,1},{1,0},{2,3},{3,2},{4,5},{5,4},{6,7},{7,6},{8,9},{9,8},{10,11... | collective-permute-start | bytes 823304 | tf_op jit(solution)/shard_map/ppermute | solution.py:567
  13.5 10.0 %collective-permute-start.6 = (f32[2,128,256]{2,1,0:T(8,128)S(1)}, f32[2,128,256]{2,1,0:T(8,128)S(1)}, u32[]{:S(2)}, u32[]{:S(2)}) collective-permute-start(f32[2,128,256]{2,1,0:T(8,128)S(1)} %collective-permute-done.fa0), channel_id=1, source_target_pairs={{0,12},{1,13},{2,14},{3,15},{4,8},{5,9},{6,10},{7,11},{8,4},{9,5},... | collective-permute-start | bytes 786440 | tf_op jit(solution)/shard_map/ppermute | solution.py:567
  16.0 12.8 %collective-permute-start.5 = (f32[2,128,256]{2,1,0:T(8,128)S(1)}, f32[2,128,256]{2,1,0:T(8,128)S(1)}, u32[]{:S(2)}, u32[]{:S(2)}) collective-permute-start(f32[2,128,256]{2,1,0:T(8,128)S(1)} %collective-permute-done.fa0), channel_id=1, source_target_pairs={{0,8},{1,9},{2,10},{3,11},{4,12},{5,13},{6,14},{7,15},{8,0},{9,1},... | collective-permute-start | bytes 786440 | tf_op jit(solution)/shard_map/ppermute | solution.py:567
  16.5 12.4 %collective-permute-start.4 = (f32[2,128,256]{2,1,0:T(8,128)S(1)}, f32[2,128,256]{2,1,0:T(8,128)S(1)}, u32[]{:S(2)}, u32[]{:S(2)}) collective-permute-start(f32[2,128,256]{2,1,0:T(8,128)S(1)} %collective-permute-done.fa0), channel_id=1, source_target_pairs={{0,4},{1,5},{2,6},{3,7},{4,0},{5,1},{6,2},{7,3},{8,12},{9,13},{10,... | collective-permute-start | bytes 786440 | tf_op jit(solution)/shard_map/ppermute | solution.py:567
  28.9 3.5 %collective-permute-start.7 = (f32[1048,128]{1,0:T(8,128)S(1)}, f32[1048,128]{1,0:T(8,128)S(1)}, u32[]{:S(2)}, u32[]{:S(2)}) collective-permute-start(f32[1048,128]{1,0:T(8,128)S(1)} %collective-permute-done.3.x2), channel_id=1, source_target_pairs={{0,1},{1,0},{2,3},{3,2},{4,5},{5,4},{6,7},{7,6},{8,9},{9,8},{10,11... | collective-permute-start | bytes 1609736 | tf_op jit(solution)/shard_map/ppermute | solution.py:567
  29.0 2.3 %collective-permute-start.8 = (f32[2,128,256]{2,1,0:T(8,128)S(1)}, f32[2,128,256]{2,1,0:T(8,128)S(1)}, u32[]{:S(2)}, u32[]{:S(2)}) collective-permute-start(f32[2,128,256]{2,1,0:T(8,128)S(1)} %collective-permute-done.fa0), channel_id=1, source_target_pairs={{0,1},{1,0},{2,3},{3,2},{4,5},{5,4},{6,7},{7,6},{8,9},{9,8},{10,11... | collective-permute-start | bytes 786440 | tf_op jit(solution)/shard_map/ppermute | solution.py:567
  29.5 2.2 %collective-permute-start.9 = (f32[2,128,256]{2,1,0:T(8,128)S(1)}, f32[2,128,256]{2,1,0:T(8,128)S(1)}, u32[]{:S(2)}, u32[]{:S(2)}) collective-permute-start(f32[2,128,256]{2,1,0:T(8,128)S(1)} %collective-permute-done.4.fa1), channel_id=1, source_target_pairs={{0,1},{1,0},{2,3},{3,2},{4,5},{5,4},{6,7},{7,6},{8,9},{9,8},{10,11... | collective-permute-start | bytes 786440 | tf_op jit(solution)/shard_map/ppermute | solution.py:567
  29.5 2.5 %collective-permute-start.10 = (f32[2,128,256]{2,1,0:T(8,128)S(1)}, f32[2,128,256]{2,1,0:T(8,128)S(1)}, u32[]{:S(2)}, u32[]{:S(2)}) collective-permute-start(f32[2,128,256]{2,1,0:T(8,128)S(1)} %collective-permute-done.5.fa2), channel_id=1, source_target_pairs={{0,1},{1,0},{2,3},{3,2},{4,5},{5,4},{6,7},{7,6},{8,9},{9,8},{10,11... | collective-permute-start | bytes 786440 | tf_op jit(solution)/shard_map/ppermute | solution.py:567
  30.0 2.4 %collective-permute-start.11 = (f32[2,128,256]{2,1,0:T(8,128)S(1)}, f32[2,128,256]{2,1,0:T(8,128)S(1)}, u32[]{:S(2)}, u32[]{:S(2)}) collective-permute-start(f32[2,128,256]{2,1,0:T(8,128)S(1)} %collective-permute-done.6.fa3), channel_id=1, source_target_pairs={{0,1},{1,0},{2,3},{3,2},{4,5},{5,4},{6,7},{7,6},{8,9},{9,8},{10,11... | collective-permute-start | bytes 786440 | tf_op jit(solution)/shard_map/ppermute | solution.py:567
  53.1 2.4 %collective-permute-start.12 = (f32[16,40,256]{2,1,0:T(8,128)}, f32[16,40,256]{2,1,0:T(8,128)S(1)}, u32[]{:S(2)}, u32[]{:S(2)}) collective-permute-start(f32[16,40,256]{2,1,0:T(8,128)} %get-tuple-element.97), channel_id=1, source_target_pairs={{0,1},{1,0},{2,3},{3,2},{4,5},{5,4},{6,7},{7,6},{8,9},{9,8},{10,11... | collective-permute-start | bytes 1966088 | tf_op jit(solution)/shard_map/ppermute | solution.py:567
  53.3 3.4 %collective-permute-start.13 = (f32[16,40,256]{2,1,0:T(8,128)}, f32[16,40,256]{2,1,0:T(8,128)S(1)}, u32[]{:S(2)}, u32[]{:S(2)}) collective-permute-start(f32[16,40,256]{2,1,0:T(8,128)} %get-tuple-element.99), channel_id=1, source_target_pairs={{0,1},{1,0},{2,3},{3,2},{4,5},{5,4},{6,7},{7,6},{8,9},{9,8},{10,11... | collective-permute-start | bytes 1966088 | tf_op jit(solution)/shard_map/ppermute | solution.py:567
  56.8 9.8 %collective-permute-start.16 = (f32[2,4,40,256]{3,2,1,0:T(8,128)S(1)}, f32[2,4,40,256]{3,2,1,0:T(8,128)S(1)}, u32[]{:S(2)}, u32[]{:S(2)}) collective-permute-start(f32[2,4,40,256]{3,2,1,0:T(8,128)S(1)} %bitcast.109), channel_id=1, source_target_pairs={{0,4},{1,5},{2,6},{3,7},{4,0},{5,1},{6,2},{7,3},{8,12},{9,13},{10,... | collective-permute-start | bytes 983048 | tf_op jit(solution)/shard_map/ppermute | solution.py:567
  58.3 9.8 %collective-permute-start.18 = (f32[2,4,40,256]{3,2,1,0:T(8,128)S(1)}, f32[2,4,40,256]{3,2,1,0:T(8,128)S(1)}, u32[]{:S(2)}, u32[]{:S(2)}) collective-permute-start(f32[2,4,40,256]{3,2,1,0:T(8,128)S(1)} %get-tuple-element.110), channel_id=1, source_target_pairs={{0,2},{1,3},{2,0},{3,1},{4,6},{5,7},{6,4},{7,5},{8,10},{9,11},{10,... | collective-permute-start | bytes 983048 | tf_op jit(solution)/shard_map/ppermute | solution.py:567
  65.8 8.3 %collective-permute-start.14 = (f32[2,8,64,256]{3,2,1,0:T(8,128)}, f32[2,8,64,256]{3,2,1,0:T(8,128)S(1)}, u32[]{:S(2)}, u32[]{:S(2)}) collective-permute-start(f32[2,8,64,256]{3,2,1,0:T(8,128)} %get-tuple-element.104), channel_id=1, source_target_pairs={{0,1},{1,0},{2,3},{3,2},{4,5},{5,4},{6,7},{7,6},{8,9},{9,8},{10,11... | collective-permute-start | bytes 3145736 | tf_op jit(solution)/shard_map/ppermute | solution.py:567
  65.9 8.5 %collective-permute-start.15 = (f32[2,8,64,256]{3,2,1,0:T(8,128)}, f32[2,8,64,256]{3,2,1,0:T(8,128)S(1)}, u32[]{:S(2)}, u32[]{:S(2)}) collective-permute-start(f32[2,8,64,256]{3,2,1,0:T(8,128)} %get-tuple-element.106), channel_id=1, source_target_pairs={{0,1},{1,0},{2,3},{3,2},{4,5},{5,4},{6,7},{7,6},{8,9},{9,8},{10,11... | collective-permute-start | bytes 3145736 | tf_op jit(solution)/shard_map/ppermute | solution.py:567
  66.7 6.0 %collective-permute-start.17 = (f32[4,40,256]{2,1,0:T(8,128)S(1)}, f32[4,40,256]{2,1,0:T(8,128)S(1)}, u32[]{:S(2)}, u32[]{:S(2)}) collective-permute-start(f32[4,40,256]{2,1,0:T(8,128)S(1)} %slice_bitcast_fusion.10), channel_id=1, source_target_pairs={{0,2},{1,3},{2,0},{3,1},{4,6},{5,7},{6,4},{7,5},{8,10},{9,11},{10,... | collective-permute-start | bytes 491528 | tf_op jit(solution)/shard_map/ppermute | solution.py:567
  68.1 6.0 %collective-permute-start.19 = (f32[4,40,256]{2,1,0:T(8,128)S(1)}, f32[4,40,256]{2,1,0:T(8,128)S(1)}, u32[]{:S(2)}, u32[]{:S(2)}) collective-permute-start(f32[4,40,256]{2,1,0:T(8,128)S(1)} %slice_bitcast_fusion.8), channel_id=1, source_target_pairs={{0,4},{1,5},{2,6},{3,7},{4,0},{5,1},{6,2},{7,3},{8,12},{9,13},{10,... | collective-permute-start | bytes 491528 | tf_op jit(solution)/shard_map/ppermute | solution.py:567
  75.7 5.8 %collective-permute-start.24 = (f32[80,256]{1,0:T(8,128)S(1)}, f32[80,256]{1,0:T(8,128)S(1)}, u32[]{:S(2)}, u32[]{:S(2)}) collective-permute-start(f32[80,256]{1,0:T(8,128)S(1)} %get-tuple-element.169), channel_id=1, source_target_pairs={{0,8},{1,9},{2,10},{3,11},{4,12},{5,13},{6,14},{7,15},{8,0},{9,1},... | collective-permute-start | bytes 245768 | tf_op jit(solution)/shard_map/ppermute | solution.py:567
  77.3 6.6 %collective-permute-start.26 = (f32[80,256]{1,0:T(8,128)S(1)}, f32[80,256]{1,0:T(8,128)S(1)}, u32[]{:S(2)}, u32[]{:S(2)}) collective-permute-start(f32[80,256]{1,0:T(8,128)S(1)} %get-tuple-element.170), channel_id=1, source_target_pairs={{0,24},{1,25},{2,26},{3,27},{4,28},{5,29},{6,30},{7,31},{8,16},{9,... | collective-permute-start | bytes 245768 | tf_op jit(solution)/shard_map/ppermute | solution.py:567
  79.8 6.9 %collective-permute-start.25 = (f32[80,256]{1,0:T(8,128)S(1)}, f32[80,256]{1,0:T(8,128)S(1)}, u32[]{:S(2)}, u32[]{:S(2)}) collective-permute-start(f32[80,256]{1,0:T(8,128)S(1)} %get-tuple-element.171), channel_id=1, source_target_pairs={{0,16},{1,17},{2,18},{3,19},{4,20},{5,21},{6,22},{7,23},{8,24},{9,... | collective-permute-start | bytes 245768 | tf_op jit(solution)/shard_map/ppermute | solution.py:567
  79.9 12.5 %collective-permute-start.20 = (f32[2,4,64,256]{3,2,1,0:T(8,128)S(1)}, f32[2,4,64,256]{3,2,1,0:T(8,128)S(1)}, u32[]{:S(2)}, u32[]{:S(2)}) collective-permute-start(f32[2,4,64,256]{3,2,1,0:T(8,128)S(1)} %bitcast.108), channel_id=1, source_target_pairs={{0,2},{1,3},{2,0},{3,1},{4,6},{5,7},{6,4},{7,5},{8,10},{9,11},{10,... | collective-permute-start | bytes 1572872 | tf_op jit(solution)/shard_map/ppermute | solution.py:567
  80.4 12.8 %collective-permute-start.22 = (f32[2,4,64,256]{3,2,1,0:T(8,128)S(1)}, f32[2,4,64,256]{3,2,1,0:T(8,128)S(1)}, u32[]{:S(2)}, u32[]{:S(2)}) collective-permute-start(f32[2,4,64,256]{3,2,1,0:T(8,128)S(1)} %get-tuple-element.114), channel_id=1, source_target_pairs={{0,4},{1,5},{2,6},{3,7},{4,0},{5,1},{6,2},{7,3},{8,12},{9,13},{10,... | collective-permute-start | bytes 1572872 | tf_op jit(solution)/shard_map/ppermute | solution.py:567
  88.0 7.4 %collective-permute-start.28 = (f32[80,256]{1,0:T(8,128)S(1)}, f32[80,256]{1,0:T(8,128)S(1)}, u32[]{:S(2)}, u32[]{:S(2)}) collective-permute-start(f32[80,256]{1,0:T(8,128)S(1)} %broadcast_multiply_fusion), channel_id=1, source_target_pairs={{0,16},{1,17},{2,18},{3,19},{4,20},{5,21},{6,22},{7,23},{8,24},{9,... | collective-permute-start | bytes 245768 | tf_op jit(solution)/shard_map/ppermute | solution.py:567
  88.7 6.7 %collective-permute-start.27 = (f32[80,256]{1,0:T(8,128)S(1)}, f32[80,256]{1,0:T(8,128)S(1)}, u32[]{:S(2)}, u32[]{:S(2)}) collective-permute-start(f32[80,256]{1,0:T(8,128)S(1)} %broadcast_multiply_fusion), channel_id=1, source_target_pairs={{0,8},{1,9},{2,10},{3,11},{4,12},{5,13},{6,14},{7,15},{8,0},{9,1},... | collective-permute-start | bytes 245768 | tf_op jit(solution)/shard_map/ppermute | solution.py:567
  91.0 6.2 %collective-permute-start.29 = (f32[80,256]{1,0:T(8,128)S(1)}, f32[80,256]{1,0:T(8,128)S(1)}, u32[]{:S(2)}, u32[]{:S(2)}) collective-permute-start(f32[80,256]{1,0:T(8,128)S(1)} %broadcast_multiply_fusion), channel_id=1, source_target_pairs={{0,24},{1,25},{2,26},{3,27},{4,28},{5,29},{6,30},{7,31},{8,16},{9,... | collective-permute-start | bytes 245768 | tf_op jit(solution)/shard_map/ppermute | solution.py:567
  92.4 14.4 %copy-start.16 = (f32[2,128,256]{2,1,0:T(8,128)S(1)}, f32[2,128,256]{2,1,0:T(8,128)}, u32[]{:S(2)}) copy-start(f32[2,128,256]{2,1,0:T(8,128)} %copy-done.15) | copy-start | bytes 786436
  92.5 14.4 %copy-start.18 = (f32[2,128,256]{2,1,0:T(8,128)S(1)}, f32[2,128,256]{2,1,0:T(8,128)}, u32[]{:S(2)}) copy-start(f32[2,128,256]{2,1,0:T(8,128)} %copy-done.17) | copy-start | bytes 786436
  92.5 14.4 %copy-start.20 = (f32[2,128,256]{2,1,0:T(8,128)S(1)}, f32[2,128,256]{2,1,0:T(8,128)}, u32[]{:S(2)}) copy-start(f32[2,128,256]{2,1,0:T(8,128)} %copy-done.19) | copy-start | bytes 786436
  92.5 14.4 %copy-start.22 = (f32[24,512]{1,0:T(8,128)S(1)}, f32[24,512]{1,0:T(8,128)}, u32[]{:S(2)}) copy-start(f32[24,512]{1,0:T(8,128)} %get-tuple-element.120.glog) | copy-start | bytes 147460
  92.6 14.3 %copy-start.12 = (f32[2,128,256]{2,1,0:T(8,128)S(1)}, f32[2,128,256]{2,1,0:T(8,128)}, u32[]{:S(2)}) copy-start(f32[2,128,256]{2,1,0:T(8,128)} %copy-done.11) | copy-start | bytes 786436
  92.6 14.3 %copy-start.14 = (f32[2,128,256]{2,1,0:T(8,128)S(1)}, f32[2,128,256]{2,1,0:T(8,128)}, u32[]{:S(2)}) copy-start(f32[2,128,256]{2,1,0:T(8,128)} %copy-done.13) | copy-start | bytes 786436
  92.6 6.9 %collective-permute-start.21 = (f32[4,64,256]{2,1,0:T(8,128)S(1)}, f32[4,64,256]{2,1,0:T(8,128)S(1)}, u32[]{:S(2)}, u32[]{:S(2)}) collective-permute-start(f32[4,64,256]{2,1,0:T(8,128)S(1)} %slice_bitcast_fusion.6), channel_id=1, source_target_pairs={{0,4},{1,5},{2,6},{3,7},{4,0},{5,1},{6,2},{7,3},{8,12},{9,13},{10,... | collective-permute-start | bytes 786440 | tf_op jit(solution)/shard_map/ppermute | solution.py:567
  93.3 13.6 %copy-start.4 = (f32[8,128,256]{2,1,0:T(8,128)S(1)}, f32[8,128,256]{2,1,0:T(8,128)}, u32[]{:S(2)}) copy-start(f32[8,128,256]{2,1,0:T(8,128)} %copy-done.3) | copy-start | bytes 3145732
  93.3 13.6 %copy-start.8 = (f32[2,128,256]{2,1,0:T(8,128)S(1)}, f32[2,128,256]{2,1,0:T(8,128)}, u32[]{:S(2)}) copy-start(f32[2,128,256]{2,1,0:T(8,128)} %copy-done.7) | copy-start | bytes 786436
  93.3 13.6 %copy-start.10 = (f32[2,128,256]{2,1,0:T(8,128)S(1)}, f32[2,128,256]{2,1,0:T(8,128)}, u32[]{:S(2)}) copy-start(f32[2,128,256]{2,1,0:T(8,128)} %copy-done.9) | copy-start | bytes 786436
  93.4 13.5 %copy-start.2 = (f32[8,128,256]{2,1,0:T(8,128)S(1)}, f32[8,128,256]{2,1,0:T(8,128)}, u32[]{:S(2)}) copy-start(f32[8,128,256]{2,1,0:T(8,128)} %near0.3) | copy-start | bytes 3145732
  93.4 6.6 %collective-permute-start.23 = (f32[4,64,256]{2,1,0:T(8,128)S(1)}, f32[4,64,256]{2,1,0:T(8,128)S(1)}, u32[]{:S(2)}, u32[]{:S(2)}) collective-permute-start(f32[4,64,256]{2,1,0:T(8,128)S(1)} %slice_bitcast_fusion.4), channel_id=1, source_target_pairs={{0,2},{1,3},{2,0},{3,1},{4,6},{5,7},{6,4},{7,5},{8,10},{9,11},{10,... | collective-permute-start | bytes 786440 | tf_op jit(solution)/shard_map/ppermute | solution.py:567
  97.3 9.7 %copy-start.6 = (f32[2,128,256]{2,1,0:T(8,128)S(1)}, f32[2,128,256]{2,1,0:T(8,128)}, u32[]{:S(2)}) copy-start(f32[2,128,256]{2,1,0:T(8,128)} %copy-done.5) | copy-start | bytes 786436
  97.3 9.6 %copy-start = (bf16[8,256,512]{2,1,0:T(8,128)(2,1)S(1)}, bf16[8,256,512]{2,1,0:T(8,128)(2,1)}, u32[]{:S(2)}) copy-start(bf16[8,256,512]{2,1,0:T(8,128)(2,1)} %get-tuple-element.101.gf_high_in) | copy-start | bytes 6291460
  97.3 9.6 %copy-start.1 = (bf16[8,256,512]{2,1,0:T(8,128)(2,1)S(1)}, bf16[8,256,512]{2,1,0:T(8,128)(2,1)}, u32[]{:S(2)}) copy-start(bf16[8,256,512]{2,1,0:T(8,128)(2,1)} %get-tuple-element.121.gf_low_in) | copy-start | bytes 6291460
  97.3 9.6 %copy-start.21 = (f32[24,512]{1,0:T(8,128)S(1)}, f32[24,512]{1,0:T(8,128)}, u32[]{:S(2)}) copy-start(f32[24,512]{1,0:T(8,128)} %get-tuple-element.119.gate_all) | copy-start | bytes 147460
  100.1 12.4 %collective-permute-start.30 = (f32[128,256]{1,0:T(8,128)S(1)}, f32[128,256]{1,0:T(8,128)S(1)}, u32[]{:S(2)}, u32[]{:S(2)}) collective-permute-start(f32[128,256]{1,0:T(8,128)S(1)} %get-tuple-element.162), channel_id=1, source_target_pairs={{0,8},{1,9},{2,10},{3,11},{4,12},{5,13},{6,14},{7,15},{8,0},{9,1},... | collective-permute-start | bytes 393224 | tf_op jit(solution)/shard_map/ppermute | solution.py:567
  101.3 11.2 %collective-permute-start.32 = (f32[128,256]{1,0:T(8,128)S(1)}, f32[128,256]{1,0:T(8,128)S(1)}, u32[]{:S(2)}, u32[]{:S(2)}) collective-permute-start(f32[128,256]{1,0:T(8,128)S(1)} %get-tuple-element.163), channel_id=1, source_target_pairs={{0,24},{1,25},{2,26},{3,27},{4,28},{5,29},{6,30},{7,31},{8,16},{9,... | collective-permute-start | bytes 393224 | tf_op jit(solution)/shard_map/ppermute | solution.py:567
  103.8 8.7 %collective-permute-start.31 = (f32[128,256]{1,0:T(8,128)S(1)}, f32[128,256]{1,0:T(8,128)S(1)}, u32[]{:S(2)}, u32[]{:S(2)}) collective-permute-start(f32[128,256]{1,0:T(8,128)S(1)} %get-tuple-element.164), channel_id=1, source_target_pairs={{0,16},{1,17},{2,18},{3,19},{4,20},{5,21},{6,22},{7,23},{8,24},{9,... | collective-permute-start | bytes 393224 | tf_op jit(solution)/shard_map/ppermute | solution.py:567
  103.9 8.7 %collective-permute-start.34 = (f32[4,40,256]{2,1,0:T(8,128)S(1)}, f32[4,40,256]{2,1,0:T(8,128)S(1)}, u32[]{:S(2)}, u32[]{:S(2)}) collective-permute-start(f32[4,40,256]{2,1,0:T(8,128)S(1)} %get-tuple-element.167), channel_id=1, source_target_pairs={{0,4},{1,5},{2,6},{3,7},{4,0},{5,1},{6,2},{7,3},{8,12},{9,13},{10,... | collective-permute-start | bytes 491528 | tf_op jit(solution)/shard_map/ppermute | solution.py:567
  105.2 7.4 %collective-permute-start.33 = (f32[4,40,256]{2,1,0:T(8,128)S(1)}, f32[4,40,256]{2,1,0:T(8,128)S(1)}, u32[]{:S(2)}, u32[]{:S(2)}) collective-permute-start(f32[4,40,256]{2,1,0:T(8,128)S(1)} %get-tuple-element.168), channel_id=1, source_target_pairs={{0,2},{1,3},{2,0},{3,1},{4,6},{5,7},{6,4},{7,5},{8,10},{9,11},{10,... | collective-permute-start | bytes 491528 | tf_op jit(solution)/shard_map/ppermute | solution.py:567
  112.7 8.7 %collective-permute-start.35 = (f32[2,4,40,256]{3,2,1,0:T(8,128)S(1)}, f32[2,4,40,256]{3,2,1,0:T(8,128)S(1)}, u32[]{:S(2)}, u32[]{:S(2)}) collective-permute-start(f32[2,4,40,256]{3,2,1,0:T(8,128)S(1)} %pad_maximum_fusion.5.a0), channel_id=1, source_target_pairs={{0,4},{1,5},{2,6},{3,7},{4,0},{5,1},{6,2},{7,3},{8,12},{9,13},{10,... | collective-permute-start | bytes 983048 | tf_op jit(solution)/shard_map/ppermute | solution.py:567
  114.2 8.3 %collective-permute-start.36 = (f32[2,4,40,256]{3,2,1,0:T(8,128)S(1)}, f32[2,4,40,256]{3,2,1,0:T(8,128)S(1)}, u32[]{:S(2)}, u32[]{:S(2)}) collective-permute-start(f32[2,4,40,256]{3,2,1,0:T(8,128)S(1)} %pad_maximum_fusion.6.a1), channel_id=1, source_target_pairs={{0,2},{1,3},{2,0},{3,1},{4,6},{5,7},{6,4},{7,5},{8,10},{9,11},{10,... | collective-permute-start | bytes 983048 | tf_op jit(solution)/shard_map/ppermute | solution.py:567
  114.7 8.2 %collective-permute-start.46 = (f32[128,256]{1,0:T(8,128)S(1)}, f32[128,256]{1,0:T(8,128)S(1)}, u32[]{:S(2)}, u32[]{:S(2)}) collective-permute-start(f32[128,256]{1,0:T(8,128)S(1)} %fusion.6.a0), channel_id=1, source_target_pairs={{0,24},{1,25},{2,26},{3,27},{4,28},{5,29},{6,30},{7,31},{8,16},{9,... | collective-permute-start | bytes 393224 | tf_op jit(solution)/shard_map/ppermute | solution.py:567
  116.5 9.8 %collective-permute-start.45 = (f32[128,256]{1,0:T(8,128)S(1)}, f32[128,256]{1,0:T(8,128)S(1)}, u32[]{:S(2)}, u32[]{:S(2)}) collective-permute-start(f32[128,256]{1,0:T(8,128)S(1)} %fusion.6.a0), channel_id=1, source_target_pairs={{0,16},{1,17},{2,18},{3,19},{4,20},{5,21},{6,22},{7,23},{8,24},{9,... | collective-permute-start | bytes 393224 | tf_op jit(solution)/shard_map/ppermute | solution.py:567
  117.3 9.0 %collective-permute-start.44 = (f32[128,256]{1,0:T(8,128)S(1)}, f32[128,256]{1,0:T(8,128)S(1)}, u32[]{:S(2)}, u32[]{:S(2)}) collective-permute-start(f32[128,256]{1,0:T(8,128)S(1)} %fusion.6.a0), channel_id=1, source_target_pairs={{0,8},{1,9},{2,10},{3,11},{4,12},{5,13},{6,14},{7,15},{8,0},{9,1},... | collective-permute-start | bytes 393224 | tf_op jit(solution)/shard_map/ppermute | solution.py:567
  121.3 5.6 %collective-permute-start.41 = (f32[512,128]{1,0:T(8,128)S(1)}, f32[512,128]{1,0:T(8,128)S(1)}, u32[]{:S(2)}, u32[]{:S(2)}) collective-permute-start(f32[512,128]{1,0:T(8,128)S(1)} %get-tuple-element.136), channel_id=1, source_target_pairs={{0,1},{1,0},{2,3},{3,2},{4,5},{5,4},{6,7},{7,6},{8,9},{9,8},{10,11... | collective-permute-start | bytes 786440 | tf_op jit(solution)/shard_map/ppermute | solution.py:567
  122.6 9.2 %collective-permute-start.42 = (f32[512,128]{1,0:T(8,128)S(1)}, f32[512,128]{1,0:T(8,128)S(1)}, u32[]{:S(2)}, u32[]{:S(2)}) collective-permute-start(f32[512,128]{1,0:T(8,128)S(1)} %get-tuple-element.137), channel_id=1, source_target_pairs={{0,2},{1,3},{2,0},{3,1},{4,6},{5,7},{6,4},{7,5},{8,10},{9,11},{10,... | collective-permute-start | bytes 786440 | tf_op jit(solution)/shard_map/ppermute | solution.py:567
  122.9 11.0 %collective-permute-start.43 = (f32[512,128]{1,0:T(8,128)S(1)}, f32[512,128]{1,0:T(8,128)S(1)}, u32[]{:S(2)}, u32[]{:S(2)}) collective-permute-start(f32[512,128]{1,0:T(8,128)S(1)} %get-tuple-element.138), channel_id=1, source_target_pairs={{0,3},{1,2},{2,1},{3,0},{4,7},{5,6},{6,5},{7,4},{8,11},{9,10},{10,... | collective-permute-start | bytes 786440 | tf_op jit(solution)/shard_map/ppermute | solution.py:567
  126.3 13.9 %collective-permute-start.47 = (f32[4,128,256]{2,1,0:T(8,128)S(1)}, f32[4,128,256]{2,1,0:T(8,128)S(1)}, u32[]{:S(2)}, u32[]{:S(2)}) collective-permute-start(f32[4,128,256]{2,1,0:T(8,128)S(1)} %pad_maximum_fusion.2), channel_id=1, source_target_pairs={{0,4},{1,5},{2,6},{3,7},{4,0},{5,1},{6,2},{7,3},{8,12},{9,13},{10,... | collective-permute-start | bytes 1572872 | tf_op jit(solution)/shard_map/ppermute | solution.py:567
  126.9 10.9 %collective-permute-start.37 = (f32[2,4,40,256]{3,2,1,0:T(8,128)S(1)}, f32[2,4,40,256]{3,2,1,0:T(8,128)S(1)}, u32[]{:S(2)}, u32[]{:S(2)}) collective-permute-start(f32[2,4,40,256]{3,2,1,0:T(8,128)S(1)} %pad_maximum_fusion.5.a0), channel_id=1, source_target_pairs={{0,1},{1,0},{2,3},{3,2},{4,5},{5,4},{6,7},{7,6},{8,9},{9,8},{10,11... | collective-permute-start | bytes 983048 | tf_op jit(solution)/shard_map/ppermute | solution.py:567
  126.9 10.9 %collective-permute-start.38 = (f32[2,4,40,256]{3,2,1,0:T(8,128)S(1)}, f32[2,4,40,256]{3,2,1,0:T(8,128)S(1)}, u32[]{:S(2)}, u32[]{:S(2)}) collective-permute-start(f32[2,4,40,256]{3,2,1,0:T(8,128)S(1)} %pad_maximum_fusion.6.a1), channel_id=1, source_target_pairs={{0,1},{1,0},{2,3},{3,2},{4,5},{5,4},{6,7},{7,6},{8,9},{9,8},{10,11... | collective-permute-start | bytes 983048 | tf_op jit(solution)/shard_map/ppermute | solution.py:567
  131.8 6.0 %collective-permute-start.39 = (f32[2,4,40,256]{3,2,1,0:T(8,128)S(1)}, f32[2,4,40,256]{3,2,1,0:T(8,128)S(1)}, u32[]{:S(2)}, u32[]{:S(2)}) collective-permute-start(f32[2,4,40,256]{3,2,1,0:T(8,128)S(1)} %collective-permute-done.35.a2), channel_id=1, source_target_pairs={{0,1},{1,0},{2,3},{3,2},{4,5},{5,4},{6,7},{7,6},{8,9},{9,8},{10,11... | collective-permute-start | bytes 983048 | tf_op jit(solution)/shard_map/ppermute | solution.py:567
  133.9 3.9 %collective-permute-start.40 = (f32[2,4,40,256]{3,2,1,0:T(8,128)S(1)}, f32[2,4,40,256]{3,2,1,0:T(8,128)S(1)}, u32[]{:S(2)}, u32[]{:S(2)}) collective-permute-start(f32[2,4,40,256]{3,2,1,0:T(8,128)S(1)} %collective-permute-done.36.a3), channel_id=1, source_target_pairs={{0,1},{1,0},{2,3},{3,2},{4,5},{5,4},{6,7},{7,6},{8,9},{9,8},{10,11... | collective-permute-start | bytes 983048 | tf_op jit(solution)/shard_map/ppermute | solution.py:567
  (16 other events, 63.0 us)
